TPU v7x, 32 devices: a whole 2x2x4 slice. The times are simulated.
32 devices in a mesh: dp: 16 (over z, y, core), mp: 2 (over x).
Axes of the slice: x: 2, y: 2, z: 4, core: 2. Of those that a mesh axis runs over, the one named last changes fastest.
Arguments:
- inputs: bfloat16 [2, 16, 1024, 1472], P(None, 'dp', 'mp'), may hold values from -6 to 6
- cotangent: bfloat16 [2, 16, 1024, 1472], P(None, 'dp', 'mp'), may hold values from -6 to 6
- segments: int32 [2, 16, 1024], P(None, 'dp'), may hold values from 0 to 3, never falling along the last dimension, each value on 1 to 512 neighbouring positions
- rel_bucket: int32 [2047], replicated, may hold values from 0 to 31
- head_order: int32 [6], replicated, may hold values from 0 to 5, each once
- rel_table: float32 [32, 6], replicated, may hold values from -4 to 4
- norm1_gain: float32 [1472], replicated, may hold values from 0.1 to 1.9
- norm2_gain: float32 [1472], replicated, may hold values from 0.1 to 1.9
- w_query: bfloat16 [1472, 384], P('dp'), may hold values from -0.0390625 to 0.0390625
- w_key: bfloat16 [1472, 384], P('dp'), may hold values from -0.15625 to 0.15625
- w_value: bfloat16 [1472, 384], P('dp'), may hold values from -0.15625 to 0.15625
- output_weight: bfloat16 [384, 1472], P(None, 'dp'), may hold values from -1.25 to 1.25
- w_gate: bfloat16 [1472, 3584], P('dp', 'mp'), may hold values from -0.15625 to 0.15625
- w_up: bfloat16 [1472, 3584], P('dp', 'mp'), may hold values from -0.15625 to 0.15625
- w_down: bfloat16 [3584, 1472], P('mp', 'dp'), may hold values from -0.125 to 0.125
Outputs:
- outputs: bfloat16 [2, 16, 1024, 1472], P(None, 'dp', 'mp')
- grad_inputs: bfloat16 [2, 16, 1024, 1472], P(None, 'dp', 'mp')
- grad_rel: float32 [32, 6], replicated
- grad_norm1: float32 [1472], replicated
- grad_norm2: float32 [1472], replicated
- grad_query: float32 [1472, 384], P('dp')
- grad_key: float32 [1472, 384], P('dp')
- grad_value: float32 [1472, 384], P('dp')
- grad_out: float32 [384, 1472], P(None, 'dp')
- grad_gate: float32 [1472, 3584], P('dp', 'mp')
- grad_up: float32 [1472, 3584], P('dp', 'mp')
- grad_down: float32 [3584, 1472], P('mp', 'dp')
Inputs may be any that keep to these rules, and one draw needn't show every extreme that they name: `segments`: ids never fall along a row; a document has 1 to 512 bytes. `head_order`: a permutation of the heads.
All inputs are finite; a program needn't handle non-finite values.
Results may differ from a plain program's by a relative error of at most 0.023.
Values may be sent and summed in bfloat16 or wider, within the bound.
No kernel may reach another device: no remote copies, remote signals or barrier semaphores. Data moves between devices by JAX's collectives and lax.ppermute only.
A program may use at most 320 MiB of HBM per device.

v0:
```python
import jax
import jax.numpy as jnp
from jax import lax
from jax.sharding import PartitionSpec as P

EPSILON = 1e-06
TOP_PRECISION = lax.Precision.HIGHEST
GELU_SCALE = 0.7978845608028654


def gelu_tanh(values):
    return (
        0.5 * values * (1.0 + jnp.tanh(GELU_SCALE * (values + 0.044715 * values * values * values)))
    )


def rms_scale(values, gain):
    return values * lax.rsqrt(jnp.mean(values * values, axis=-1, keepdims=True) + EPSILON) * gain


def own_slots(weight_matrix, slot_dim, head_count, per_device, model_size, model_place):
    width = weight_matrix.shape[slot_dim] // head_count
    padding = [(0, 0), (0, 0)]
    padding[slot_dim] = (0, (per_device * model_size - head_count) * width)
    padded = jnp.pad(weight_matrix, padding)
    before_dims = list(padded.shape[:slot_dim])
    after_dims = list(padded.shape[slot_dim + 1 :])
    split = padded.reshape(before_dims + [per_device, model_size, width] + after_dims)
    picked = lax.dynamic_index_in_dim(split, model_place, slot_dim + 1, keepdims=False)
    return picked.reshape(before_dims + [per_device * width] + after_dims)


def spread_slots(gradient, slot_dim, head_count, per_device, model_size, model_place):
    width = gradient.shape[slot_dim] // per_device
    before_dims = list(gradient.shape[:slot_dim])
    after_dims = list(gradient.shape[slot_dim + 1 :])
    pieces = gradient.reshape(before_dims + [per_device, 1, width] + after_dims)
    canvas = jnp.zeros(before_dims + [per_device, model_size, width] + after_dims, gradient.dtype)
    filled = lax.dynamic_update_slice_in_dim(canvas, pieces, model_place, slot_dim + 1)
    merged = filled.reshape(before_dims + [per_device * model_size * width] + after_dims)
    return lax.slice_in_dim(merged, 0, head_count * width, axis=slot_dim)


def fetch_weights(weights, head_count, per_device, model_size, model_place):
    gathered = (
        lax.all_gather(weights[0], "dp", axis=0, tiled=True),
        lax.all_gather(weights[1], "dp", axis=0, tiled=True),
        lax.all_gather(weights[2], "dp", axis=0, tiled=True),
        lax.all_gather(weights[3], "dp", axis=1, tiled=True),
        lax.all_gather(weights[4], "dp", axis=0, tiled=True),
        lax.all_gather(weights[5], "dp", axis=0, tiled=True),
        lax.all_gather(weights[6], "dp", axis=1, tiled=True),
    )
    return (
        own_slots(gathered[0], 1, head_count, per_device, model_size, model_place),
        own_slots(gathered[1], 1, head_count, per_device, model_size, model_place),
        own_slots(gathered[2], 1, head_count, per_device, model_size, model_place),
        own_slots(gathered[3], 0, head_count, per_device, model_size, model_place),
        gathered[4],
        gathered[5],
        gathered[6],
    )


def shard_grads(gradients):
    shards = (
        lax.psum_scatter(
            gradients[0].astype(jnp.bfloat16), "dp", scatter_dimension=0, tiled=True
        ).astype(jnp.float32),
        lax.psum_scatter(
            gradients[1].astype(jnp.bfloat16), "dp", scatter_dimension=0, tiled=True
        ).astype(jnp.float32),
        lax.psum_scatter(
            gradients[2].astype(jnp.bfloat16), "dp", scatter_dimension=0, tiled=True
        ).astype(jnp.float32),
        lax.psum_scatter(
            gradients[3].astype(jnp.bfloat16), "dp", scatter_dimension=1, tiled=True
        ).astype(jnp.float32),
        lax.psum_scatter(
            gradients[4].astype(jnp.bfloat16), "dp", scatter_dimension=0, tiled=True
        ).astype(jnp.float32),
        lax.psum_scatter(
            gradients[5].astype(jnp.bfloat16), "dp", scatter_dimension=0, tiled=True
        ).astype(jnp.float32),
        lax.psum_scatter(
            gradients[6].astype(jnp.bfloat16), "dp", scatter_dimension=1, tiled=True
        ).astype(jnp.float32),
    )
    return tuple(shards)


def skew_bias(offsets_bias, start, block_rows, length):
    span = length + block_rows - 1
    window = lax.dynamic_slice_in_dim(offsets_bias, length - block_rows - start, span, 1)
    padded = jnp.pad(window, ((0, 0), (0, 1)))
    slot_count = padded.shape[0]
    tiled = jnp.broadcast_to(padded[:, None, :], (slot_count, block_rows, span + 1))
    tiled = tiled.reshape(slot_count, block_rows * (span + 1))
    shifted = lax.slice_in_dim(tiled, block_rows - 1, block_rows - 1 + block_rows * span, axis=1)
    return shifted.reshape(slot_count, block_rows, span)[:, :, :length]


def unskew_add(offsets_sum, grad_scores, start):
    slot_count, block_rows, length = grad_scores.shape
    span = length + block_rows - 1
    widened = jnp.pad(grad_scores.astype(jnp.float32), ((0, 0), (0, 0), (0, block_rows - 1)))
    widened = widened.reshape(slot_count, block_rows * span)
    placed = jnp.pad(widened, ((0, 0), (block_rows - 1, 1))).reshape(
        slot_count, block_rows, span + 1
    )
    diagonal = jnp.sum(placed, axis=1)[:, :span]
    begin = length - block_rows - start
    current = lax.dynamic_slice_in_dim(offsets_sum, begin, span, 1)
    return lax.dynamic_update_slice_in_dim(offsets_sum, current + diagonal, begin, 1)


def block_scores(query_block, keys, seg_block, seg_ids, offsets_bias, start):
    block_rows = query_block.shape[0]
    length = keys.shape[0]
    bias_block = skew_bias(offsets_bias, start, block_rows, length)
    scores = (
        jnp.einsum("ihe,the->hit", query_block, keys, preferred_element_type=jnp.float32)
        + bias_block
    )
    same_doc = seg_block[:, None] == seg_ids[None, :]
    return jnp.where(same_doc[None], scores, -1e30)


def attend_row(queries, keys, values, seg_ids, offsets_bias):
    length, slot_count, head_size = queries.shape
    block_rows = min(512, length)
    starts = jnp.arange(length // block_rows, dtype=jnp.int32) * block_rows

    def one_block(start):
        query_block = lax.dynamic_slice_in_dim(queries, start, block_rows, 0)
        seg_block = lax.dynamic_slice_in_dim(seg_ids, start, block_rows, 0)
        scores = block_scores(query_block, keys, seg_block, seg_ids, offsets_bias, start)
        highest = jnp.max(scores, axis=-1, keepdims=True)
        exp_terms = jnp.exp(scores - highest)
        norm_sum = jnp.sum(exp_terms, axis=-1, keepdims=True)
        attn_probs = (exp_terms / norm_sum).astype(jnp.bfloat16)
        context_rows = jnp.einsum(
            "hit,the->ihe", attn_probs, values, preferred_element_type=jnp.float32
        )
        return (context_rows.astype(jnp.bfloat16), (highest + jnp.log(norm_sum))[:, :, 0])

    context_rows, log_sums = lax.map(one_block, starts)
    return (context_rows.reshape(length, slot_count, head_size), log_sums)


def attend_grads(queries, keys, values, seg_ids, offsets_bias, log_sums, grad_context):
    length, slot_count, head_size = queries.shape
    block_rows = min(512, length)
    starts = jnp.arange(length // block_rows, dtype=jnp.int32) * block_rows

    def one_block(carry, item):
        keys_sum, values_sum, offsets_sum = carry
        start, log_block = item
        query_block = lax.dynamic_slice_in_dim(queries, start, block_rows, 0)
        seg_block = lax.dynamic_slice_in_dim(seg_ids, start, block_rows, 0)
        grad_block = lax.dynamic_slice_in_dim(grad_context, start, block_rows, 0)
        scores = block_scores(query_block, keys, seg_block, seg_ids, offsets_bias, start)
        attn_probs = jnp.exp(scores - log_block[:, :, None])
        grad_probs = jnp.einsum(
            "ihe,the->hit", grad_block, values, preferred_element_type=jnp.float32
        )
        delta = jnp.sum(attn_probs * grad_probs, axis=-1, keepdims=True)
        grad_scores = (attn_probs * (grad_probs - delta)).astype(jnp.bfloat16)
        query_grad = jnp.einsum(
            "hit,the->ihe", grad_scores, keys, preferred_element_type=jnp.float32
        )
        keys_sum = keys_sum + jnp.einsum(
            "hit,ihe->the", grad_scores, query_block, preferred_element_type=jnp.float32
        )
        values_sum = values_sum + jnp.einsum(
            "hit,ihe->the",
            attn_probs.astype(jnp.bfloat16),
            grad_block,
            preferred_element_type=jnp.float32,
        )
        offsets_sum = unskew_add(offsets_sum, grad_scores, start)
        return ((keys_sum, values_sum, offsets_sum), query_grad.astype(jnp.bfloat16))

    initial = (
        jnp.zeros((length, slot_count, head_size), jnp.float32),
        jnp.zeros((length, slot_count, head_size), jnp.float32),
        jnp.zeros((slot_count, 2 * length - 1), jnp.float32),
    )
    (keys_sum, values_sum, offsets_sum), query_blocks = lax.scan(
        one_block, initial, (starts, log_sums)
    )
    return (
        query_blocks.reshape(length, slot_count, head_size),
        keys_sum.astype(jnp.bfloat16),
        values_sum.astype(jnp.bfloat16),
        offsets_sum,
    )


def body(
    inputs,
    cotangent,
    segments,
    rel_bucket,
    head_order,
    rel_table,
    norm1_gain,
    norm2_gain,
    w_query,
    w_key,
    w_value,
    output_weight,
    w_gate,
    w_up,
    w_down,
):
    micro_count = inputs.shape[0]
    model_size = lax.axis_size("mp")
    model_place = lax.axis_index("mp")
    bucket_count, head_count = rel_table.shape
    head_size = w_query.shape[1] // head_count
    per_device = -(-head_count // model_size)
    slot_width = per_device * head_size
    slot_ids = model_place + model_size * jnp.arange(per_device, dtype=jnp.int32)
    slot_live = (slot_ids < head_count).astype(jnp.float32)
    slot_head = jnp.take(head_order, jnp.minimum(slot_ids, head_count - 1))
    bucket_hot = (rel_bucket[:, None] == jnp.arange(bucket_count, dtype=jnp.int32)[None, :]).astype(
        jnp.float32
    )
    head_hot = (slot_head[:, None] == jnp.arange(head_count, dtype=jnp.int32)[None, :]).astype(
        jnp.float32
    )
    head_hot = head_hot * slot_live[:, None]
    offset_table = jnp.dot(bucket_hot, rel_table, precision=TOP_PRECISION)
    offsets_bias = jnp.dot(head_hot, offset_table.T, precision=TOP_PRECISION)
    weights = (w_query, w_key, w_value, output_weight, w_gate, w_up, w_down)
    width_rows = w_query.shape[0]
    shard_sums = (
        jnp.zeros((width_rows, slot_width), jnp.float32),
        jnp.zeros((width_rows, slot_width), jnp.float32),
        jnp.zeros((width_rows, slot_width), jnp.float32),
        jnp.zeros((slot_width, width_rows), jnp.float32),
        jnp.zeros(w_gate.shape, jnp.float32),
        jnp.zeros(w_up.shape, jnp.float32),
        jnp.zeros(w_down.shape, jnp.float32),
    )
    norm1_sum = jnp.zeros(norm1_gain.shape, jnp.float32)
    norm2_sum = jnp.zeros(norm2_gain.shape, jnp.float32)
    rel_sum = jnp.zeros(rel_table.shape, jnp.float32)
    outputs = []
    grad_inputs = []
    for micro_step in range(micro_count):
        current = fetch_weights(weights, head_count, per_device, model_size, model_place)
        query_own, key_own, value_own, out_own, gate_full, up_full, down_full = current
        layer_in = inputs[micro_step].astype(jnp.float32)
        row_count = layer_in.shape[0]
        seg_rows = segments[micro_step]
        length = seg_rows.shape[1]
        normalized_rows = lax.all_gather(
            rms_scale(layer_in, norm1_gain).astype(jnp.bfloat16), "mp", axis=1, tiled=True
        )

        def project(weight_matrix):
            mixed_heads = jnp.einsum(
                "rld,dc->rlc", normalized_rows, weight_matrix, preferred_element_type=jnp.float32
            )
            return mixed_heads.astype(jnp.bfloat16).reshape(
                row_count, length, per_device, head_size
            )

        queries = project(query_own)
        keys = project(key_own)
        values = project(value_own)
        context_rows, log_sums = lax.map(
            lambda item: attend_row(item[0], item[1], item[2], item[3], offsets_bias),
            (queries, keys, values, seg_rows),
        )
        context_rows = context_rows.reshape(row_count, length, slot_width)
        attn_part = jnp.einsum(
            "rlc,cd->rld", context_rows, out_own, preferred_element_type=jnp.float32
        )
        attention_output = lax.psum_scatter(
            attn_part.astype(jnp.bfloat16), "mp", scatter_dimension=1, tiled=True
        ).astype(jnp.float32)
        middle = layer_in + attention_output
        normed_two = lax.all_gather(
            rms_scale(middle, norm2_gain).astype(jnp.bfloat16), "mp", axis=1, tiled=True
        )
        gate = jnp.einsum("rld,df->rlf", normed_two, gate_full, preferred_element_type=jnp.float32)
        upward = jnp.einsum("rld,df->rlf", normed_two, up_full, preferred_element_type=jnp.float32)
        hidden = (gelu_tanh(gate) * upward).astype(jnp.bfloat16)
        ffn_part = jnp.einsum("rlf,fd->rld", hidden, down_full, preferred_element_type=jnp.float32)
        ffn_out = lax.psum_scatter(
            ffn_part.astype(jnp.bfloat16), "mp", scatter_dimension=1, tiled=True
        ).astype(jnp.float32)
        outputs.append((middle + ffn_out).astype(jnp.bfloat16))
        grad_top = cotangent[micro_step].astype(jnp.float32)
        grad_ffn = lax.all_gather(cotangent[micro_step], "mp", axis=1, tiled=True)
        grad_hidden = jnp.einsum(
            "rld,fd->rlf", grad_ffn, down_full, preferred_element_type=jnp.float32
        )
        _, gelu_pull = jax.vjp(lambda gate_in, up_in: gelu_tanh(gate_in) * up_in, gate, upward)
        grad_gate_wide, grad_up_wide = gelu_pull(grad_hidden)
        grad_gate_in = grad_gate_wide.astype(jnp.bfloat16)
        grad_up_in = grad_up_wide.astype(jnp.bfloat16)
        back_two = jnp.einsum(
            "rlf,df->rld", grad_gate_in, gate_full, preferred_element_type=jnp.float32
        ) + jnp.einsum("rlf,df->rld", grad_up_in, up_full, preferred_element_type=jnp.float32)
        grad_normed_two = lax.psum_scatter(
            back_two.astype(jnp.bfloat16), "mp", scatter_dimension=1, tiled=True
        ).astype(jnp.float32)
        _, norm_two_pull = jax.vjp(rms_scale, middle, norm2_gain)
        grad_mid_norm, grad_gain_two = norm_two_pull(grad_normed_two)
        grad_middle = grad_top + grad_mid_norm
        grad_attn = lax.all_gather(grad_middle.astype(jnp.bfloat16), "mp", axis=1, tiled=True)
        grad_context = jnp.einsum(
            "rld,cd->rlc", grad_attn, out_own, preferred_element_type=jnp.float32
        )
        grad_context = grad_context.astype(jnp.bfloat16).reshape(
            row_count, length, per_device, head_size
        )
        grad_queries, grad_keys, grad_values, offset_grads = lax.map(
            lambda item: attend_grads(
                item[0], item[1], item[2], item[3], offsets_bias, item[4], item[5]
            ),
            (queries, keys, values, seg_rows, log_sums, grad_context),
        )
        flat_queries = grad_queries.reshape(row_count, length, slot_width)
        flat_keys = grad_keys.reshape(row_count, length, slot_width)
        flat_values = grad_values.reshape(row_count, length, slot_width)
        back_one = (
            jnp.einsum("rlc,dc->rld", flat_queries, query_own, preferred_element_type=jnp.float32)
            + jnp.einsum("rlc,dc->rld", flat_keys, key_own, preferred_element_type=jnp.float32)
            + jnp.einsum("rlc,dc->rld", flat_values, value_own, preferred_element_type=jnp.float32)
        )
        grad_normed_one = lax.psum_scatter(
            back_one.astype(jnp.bfloat16), "mp", scatter_dimension=1, tiled=True
        ).astype(jnp.float32)
        _, norm_one_pull = jax.vjp(rms_scale, layer_in, norm1_gain)
        grad_in_norm, grad_gain_one = norm_one_pull(grad_normed_one)
        grad_inputs.append((grad_middle + grad_in_norm).astype(jnp.bfloat16))
        offsets_total = jnp.sum(offset_grads, axis=0)
        bucket_part = jnp.dot(bucket_hot.T, offsets_total.T, precision=TOP_PRECISION)
        rel_sum = rel_sum + jnp.dot(bucket_part, head_hot, precision=TOP_PRECISION)
        norm1_sum = norm1_sum + grad_gain_one
        norm2_sum = norm2_sum + grad_gain_two
        micro_grads = (
            jnp.einsum(
                "rld,rlc->dc", normalized_rows, flat_queries, preferred_element_type=jnp.float32
            ),
            jnp.einsum(
                "rld,rlc->dc", normalized_rows, flat_keys, preferred_element_type=jnp.float32
            ),
            jnp.einsum(
                "rld,rlc->dc", normalized_rows, flat_values, preferred_element_type=jnp.float32
            ),
            jnp.einsum("rlc,rld->cd", context_rows, grad_attn, preferred_element_type=jnp.float32),
            jnp.einsum("rld,rlf->df", normed_two, grad_gate_in, preferred_element_type=jnp.float32),
            jnp.einsum("rld,rlf->df", normed_two, grad_up_in, preferred_element_type=jnp.float32),
            jnp.einsum("rlf,rld->fd", hidden, grad_ffn, preferred_element_type=jnp.float32),
        )
        scattered = shard_grads(micro_grads)
        shard_sums = tuple((total + piece for total, piece in zip(shard_sums, scattered)))
    shard_query, shard_key, shard_value, shard_out, shard_gate, shard_up, shard_down = shard_sums
    wide_query = spread_slots(shard_query, 1, head_count, per_device, model_size, model_place)
    wide_key = spread_slots(shard_key, 1, head_count, per_device, model_size, model_place)
    wide_value = spread_slots(shard_value, 1, head_count, per_device, model_size, model_place)
    wide_out = spread_slots(shard_out, 0, head_count, per_device, model_size, model_place)
    grad_query, grad_key, grad_value, grad_out = (
        lax.psum(wide_query.astype(jnp.bfloat16), "mp").astype(jnp.float32),
        lax.psum(wide_key.astype(jnp.bfloat16), "mp").astype(jnp.float32),
        lax.psum(wide_value.astype(jnp.bfloat16), "mp").astype(jnp.float32),
        lax.psum(wide_out.astype(jnp.bfloat16), "mp").astype(jnp.float32),
    )
    grad_norm1, grad_norm2, grad_rel = lax.psum((norm1_sum, norm2_sum, rel_sum), ("dp", "mp"))
    return (
        jnp.stack(outputs),
        jnp.stack(grad_inputs),
        grad_rel,
        grad_norm1,
        grad_norm2,
        grad_query,
        grad_key,
        grad_value,
        grad_out,
        shard_gate,
        shard_up,
        shard_down,
    )


def solution(mesh):
    placed = (
        P(None, "dp", "mp", None),
        P(None, "dp", "mp", None),
        P(None, "dp", None),
        P(),
        P(),
        P(),
        P(),
        P(),
        P("dp", None),
        P("dp", None),
        P("dp", None),
        P(None, "dp"),
        P("dp", "mp"),
        P("dp", "mp"),
        P("mp", "dp"),
    )
    return jax.shard_map(
        body,
        mesh=mesh,
        in_specs=placed,
        out_specs=(
            P(None, "dp", "mp", None),
            P(None, "dp", "mp", None),
            P(),
            P(),
            P(),
            P("dp", None),
            P("dp", None),
            P("dp", None),
            P(None, "dp"),
            P("dp", "mp"),
            P("dp", "mp"),
            P("mp", "dp"),
        ),
        check_vma=False,
    )
```

profile of v0, /device:TPU:0, one launch (start us, length us, event | category | flops | bytes accessed | tf_op | source)
XLA Modules:
  0.0 2344.6 jit_solution(4331366458660081787)
XLA Ops:
  18.7 32.8 %all-gather.47.cloned.1.call-done = bf16[16,92,384]{2,1,0:T(8,128)(2,1)} async-done(((bf16[1,92,384]{2,1,0:T(8,128)(2,1)}), bf16[16,92,384]{2,1,0:T(8,128)(2,1)}) %all-gather.47.cloned.1.call-update) | async-done | bytes 1130512 | tf_op jit(solution)/shard_map/all_gather | solution.py:49
  54.1 37.0 %all-gather.45.cloned.1.call-done = bf16[16,92,384]{2,1,0:T(8,128)(2,1)} async-done(((bf16[1,92,384]{2,1,0:T(8,128)(2,1)}), bf16[16,92,384]{2,1,0:T(8,128)(2,1)}) %all-gather.45.cloned.1.call-update) | async-done | bytes 1130512 | tf_op jit(solution)/shard_map/all_gather | solution.py:48
  96.1 34.7 %all-gather.43.cloned.1.call-done = bf16[16,92,384]{2,1,0:T(8,128)(2,1)} async-done(((bf16[1,92,384]{2,1,0:T(8,128)(2,1)}), bf16[16,92,384]{2,1,0:T(8,128)(2,1)}) %all-gather.43.cloned.1.call-update) | async-done | bytes 1130512 | tf_op jit(solution)/shard_map/all_gather | solution.py:47
  135.7 34.5 %all-gather.41.cloned.1.call-done = bf16[16,92,384]{2,1,0:T(8,128)(2,1)} async-done(((bf16[1,92,384]{2,1,0:T(8,128)(2,1)}), bf16[16,92,384]{2,1,0:T(8,128)(2,1)}) %all-gather.41.cloned.1.call-update) | async-done | bytes 1130512 | tf_op jit(solution)/shard_map/all_gather | solution.py:46
  178.9 35.8 %all-gather.25.cloned.1.call-done = bf16[1,1024,1472]{1,2,0:T(8,128)(2,1)} async-done(((bf16[1,512,1472]{1,2,0:T(8,128)(2,1)}), bf16[1,1024,1472]{1,2,0:T(8,128)(2,1)}) %all-gather.25.cloned.1.call-update) | async-done | bytes 3014672 | tf_op jit(solution)/shard_map/all_gather | solution.py:259
  219.2 141.3 %while.110 = (s32[]{:T(128)}, bf16[2,512,3,64]{1,3,2,0:T(8,128)(2,1)S(1)}, f32[2,3,512]{2,1,0:T(4,128)S(1)}, s32[2]{0:T(128)S(1)}, s32[1024]{0:T(1024)S(1)}, /*i...) while((s32[]{:T(128)}, ...), condition=%wide.region_4.5_spmd, body=%wide.region_1.4_spmd.sunk | while | flops 415857152 | bytes 112453840 | solution.py:147
  225.0 19.9 copy.94
  295.3 19.9 copy.94
  369.4 143.8 %while.111 = (s32[]{:T(128)}, bf16[2,512,3,64]{1,3,2,0:T(8,128)(2,1)S(1)}, f32[2,3,512]{2,1,0:T(4,128)S(1)}, s32[2]{0:T(128)S(1)}, s32[1024]{0:T(1024)S(1)}, /*i...) while((s32[]{:T(128)}, ...), condition=%wide.region_12.13_spmd, body=%wide.region_9.12_spmd.sunk | while | flops 415857152 | bytes 112453840 | solution.py:147
  448.1 19.9 copy.95
  519.3 39.9 %reduce-scatter.39.cloned.1.call-done = bf16[1,512,1472]{1,2,0:T(8,128)(2,1)} async-done(((bf16[1,1024,1472]{1,2,0:T(8,128)(2,1)}), bf16[1,512,1472]{1,2,0:T(8,128)(2,1)}) %reduce-scatter.39.cloned.1.call-update) | async-done | bytes 1507344 | tf_op jit(solution)/shard_map/reduce_scatter | solution.py:282
  570.2 48.8 %all-gather.49.cloned.1.call-done = bf16[16,92,1792]{2,1,0:T(8,128)(2,1)} async-done(((bf16[1,92,1792]{2,1,0:T(8,128)(2,1)}), bf16[16,92,1792]{2,1,0:T(8,128)(2,1)}) %all-gather.49.cloned.1.call-update) | async-done | bytes 5275664 | tf_op jit(solution)/shard_map/all_gather | solution.py:50
  626.5 50.6 %all-gather.51.cloned.1.call-done = bf16[16,92,1792]{2,1,0:T(8,128)(2,1)} async-done(((bf16[1,92,1792]{2,1,0:T(8,128)(2,1)}), bf16[16,92,1792]{2,1,0:T(8,128)(2,1)}) %all-gather.51.cloned.1.call-update) | async-done | bytes 5275664 | tf_op jit(solution)/shard_map/all_gather | solution.py:51
  684.6 50.8 %all-gather.53.cloned.1.call-done = bf16[16,92,1792]{2,1,0:T(8,128)(2,1)} async-done(((bf16[1,92,1792]{2,1,0:T(8,128)(2,1)}), bf16[16,92,1792]{2,1,0:T(8,128)(2,1)}) %all-gather.53.cloned.1.call-update) | async-done | bytes 5275664 | tf_op jit(solution)/shard_map/all_gather | solution.py:52
  743.1 36.4 %all-gather.31.cloned.1.call-done = bf16[1,1024,1472]{1,2,0:T(8,128)(2,1)} async-done(((bf16[1,512,1472]{1,2,0:T(8,128)(2,1)}), bf16[1,1024,1472]{1,2,0:T(8,128)(2,1)}) %all-gather.31.cloned.1.call-update) | async-done | bytes 3014672 | tf_op jit(solution)/shard_map/all_gather | solution.py:286
  801.4 23.1 all-gather.39.cloned.1.call-done
  824.5 20.9 multiply_convert_fusion.2
  892.2 22.6 all-gather.37.cloned.1.call-done
  914.9 20.7 multiply_convert_fusion.3
  1009.9 38.3 %reduce-scatter.41.cloned.1.call-done = bf16[1,512,1472]{1,2,0:T(8,128)(2,1)} async-done(((bf16[1,1024,1472]{1,2,0:T(8,128)(2,1)}), bf16[1,512,1472]{1,2,0:T(8,128)(2,1)}) %reduce-scatter.41.cloned.1.call-update) | async-done | bytes 1507344 | tf_op jit(solution)/shard_map/reduce_scatter | solution.py:293
  1102.6 239.2 %while.113 = (s32[]{:T(128)}, f32[1024,3,64]{0,2,1:T(8,128)}, f32[1024,3,64]{0,2,1:T(8,128)}, f32[3,2047]{1,0:T(4,128)S(1)}, bf16[2,512,3,64]{1,3,2,0:T(8,128)(2...) while((s32[]{:T(128)}, f32[1024,3,64]{0,2,1:T(8,128)}, ...), condition=%wide.region_29.30_spmd.clone, body=%wide.region_26.29_spmd.clone.sunk | while | flops 1026914816 | bytes 236184112 | solution.py:189
  1134.2 19.9 copy.99
  1242.7 19.9 copy.99
  1347.8 246.5 %while.112 = (s32[]{:T(128)}, f32[1024,3,64]{0,2,1:T(8,128)}, f32[1024,3,64]{0,2,1:T(8,128)}, f32[3,2047]{1,0:T(4,128)S(1)}, bf16[2,512,3,64]{1,3,2,0:T(8,128)(2...) while((s32[]{:T(128)}, f32[1024,3,64]{0,2,1:T(8,128)}, ...), condition=%wide.region_21.22_spmd.clone, body=%wide.region_18.21_spmd.clone.sunk | while | flops 1026914816 | bytes 236184112 | solution.py:189
  1378.6 19.9 copy.97
  1487.1 19.9 copy.97
  1615.8 368.2 %fusion.252 = (bf16[96,192]{1,0:T(8,128)(2,1)S(1)}, bf16[96,192]{1,0:T(8,128)(2,1)S(1)}, bf16[96,192]{1,0:T(8,128)(2,1)S(1)}, bf16[96,192]{1,0:T(8,128)(2,1)S(1)...) fusion(bf16[1472,192]{1,0:T(8,128)(2,1)} %fusion.179, ...), kind=kCustom, calls=%all-reduce-scatter.12 | all-reduce-scatter fusion | flops 18284544 | bytes 37331456
  1987.8 28.8 %collective-permute-start.4 = (bf16[60,192]{1,0:T(8,128)(2,1)}, bf16[60,192]{1,0:T(8,128)(2,1)}, u32[]{:S(2)}, u32[]{:S(2)}) collective-permute-start(bf16[60,192]{1,0:T(8,128)(2,1)} %slice.108), channel_id=1, source_target_pairs={{0,2},{2,4},{4,6},{6,8},{8,10},{10,12},{12,14},{14,16},{16,18},{18... | collective-permute-start | bytes 69128
  2064.9 61.9 %all-reduce.41.cloned.1.call-done = (bf16[192,1472]{1,0:T(8,128)(2,1)}, bf16[192,1472]{1,0:T(8,128)(2,1)}) async-done(((bf16[192,1472]{1,0:T(8,128)(2,1)}, bf16[192,1472]{1,0:T(8,128)(2,1)}), (bf16[192,1472]{1,0:T(8,128)(2,1)}, bf16[192,1472]{1,0:T(8,128)(2,1)})) %all-reduce.41.cloned.1.call-update) | async-done | bytes 1130512
  2211.2 34.2 %reduce-scatter.49.cloned.1.call-done = bf16[1,512,1472]{1,2,0:T(8,128)(2,1)} async-done(((bf16[1,1024,1472]{1,2,0:T(8,128)(2,1)}), bf16[1,512,1472]{1,2,0:T(8,128)(2,1)}) %reduce-scatter.49.cloned.1.call-update) | async-done | bytes 1507344 | tf_op jit(solution)/shard_map/reduce_scatter | solution.py:336
  2254.0 35.5 %reduce-scatter.37.cloned.1.call-done = bf16[1,512,1472]{1,2,0:T(8,128)(2,1)} async-done(((bf16[1,1024,1472]{1,2,0:T(8,128)(2,1)}), bf16[1,512,1472]{1,2,0:T(8,128)(2,1)}) %reduce-scatter.37.cloned.1.call-update) | async-done | bytes 1507344 | tf_op jit(solution)/shard_map/reduce_scatter | solution.py:293
  2297.8 39.8 %all-reduce.34 = (f32[32,6]{0,1:T(8,128)}, f32[1472]{0:T(1024)}, f32[1472]{0:T(1024)}) all-reduce(f32[32,6]{0,1:T(8,128)S(1)} %convolution_add_fusion, f32[1472]{0:T(1024)S(1)} %add.497, f32[1472]{0:T(1024)S(1)} %add.498), channel_id=1, replica_groups=mesh['dp'=16,'mp'=2] {'dp','mp'}, use_global_device_ids=true, to_apply=%region_32.33 | all-reduce | flops 3136 | bytes 25088 | tf_op jit(solution)/shard_map/psum | solution.py:375
  (743 shorter events, 1010.2 us)
Async XLA Ops:
  7.2 44.3 %all-gather.47.cloned.1.call-start = ((), (), s32[]{:S(2)}) async-start(), calls=%async_computation.27 | async-start | bytes 1253376 | tf_op jit(solution)/shard_map/all_gather | solution.py:49
  8.0 83.2 %all-gather.45.cloned.1.call-start = ((), (), s32[]{:S(2)}) async-start(), calls=%async_computation.26 | async-start | bytes 1253376 | tf_op jit(solution)/shard_map/all_gather | solution.py:48
  8.7 122.1 %all-gather.43.cloned.1.call-start = ((), (), s32[]{:S(2)}) async-start(), calls=%async_computation.25 | async-start | bytes 1253376 | tf_op jit(solution)/shard_map/all_gather | solution.py:47
  9.4 160.8 %all-gather.41.cloned.1.call-start = ((), (), s32[]{:S(2)}) async-start(), calls=%async_computation.24 | async-start | bytes 1253376 | tf_op jit(solution)/shard_map/all_gather | solution.py:46
  10.0 204.7 %all-gather.25.cloned.1.call-start = ((), (), s32[]{:S(2)}) async-start(), calls=%async_computation.8 | async-start | bytes 4521984 | tf_op jit(solution)/shard_map/all_gather | solution.py:259
  15.6 349.0 %all-gather.29.cloned.1.call-start = ((), (), s32[]{:S(2)}) async-start(), calls=%async_computation.12 | async-start | bytes 4521984 | tf_op jit(solution)/shard_map/all_gather | solution.py:259
  16.1 503.2 %reduce-scatter.35.cloned.1.call-start = ((), (), s32[]{:S(2)}) async-start(), calls=%async_computation.9 | async-start | bytes 4521984 | tf_op jit(solution)/shard_map/reduce_scatter | solution.py:282
  364.5 194.7 %reduce-scatter.39.cloned.1.call-start = ((), (), s32[]{:S(2)}) async-start(), calls=%async_computation.13 | async-start | bytes 4521984 | tf_op jit(solution)/shard_map/reduce_scatter | solution.py:282
  517.2 101.8 %all-gather.49.cloned.1.call-start = ((), (), s32[]{:S(2)}) async-start(), calls=%async_computation.28 | async-start | bytes 5849088 | tf_op jit(solution)/shard_map/all_gather | solution.py:50
  517.9 159.2 %all-gather.51.cloned.1.call-start = ((), (), s32[]{:S(2)}) async-start(), calls=%async_computation.29 | async-start | bytes 5849088 | tf_op jit(solution)/shard_map/all_gather | solution.py:51
  518.5 216.9 %all-gather.53.cloned.1.call-start = ((), (), s32[]{:S(2)}) async-start(), calls=%async_computation.30 | async-start | bytes 5849088 | tf_op jit(solution)/shard_map/all_gather | solution.py:52
  519.3 260.2 %all-gather.31.cloned.1.call-start = ((), (), s32[]{:S(2)}) async-start(), calls=%async_computation.14 | async-start | bytes 4521984 | tf_op jit(solution)/shard_map/all_gather | solution.py:286
  565.2 259.3 %all-gather.39.cloned.1.call-start = ((), (), s32[]{:S(2)}) async-start(), calls=%async_computation.23 | async-start | bytes 4521984 | tf_op jit(solution)/shard_map/all_gather | solution.py:298
  568.9 301.0 %all-gather.27.cloned.1.call-start = ((), (), s32[]{:S(2)}) async-start(), calls=%async_computation.10 | async-start | bytes 4521984 | tf_op jit(solution)/shard_map/all_gather | solution.py:286
  569.5 345.3 %all-gather.37.cloned.1.call-start = ((), (), s32[]{:S(2)}) async-start(), calls=%async_computation.22 | async-start | bytes 4521984 | tf_op jit(solution)/shard_map/all_gather | solution.py:298
  570.1 422.8 %reduce-scatter.47.cloned.1.call-start = ((), (), s32[]{:S(2)}) async-start(), calls=%async_computation.19 | async-start | bytes 4521984 | tf_op jit(solution)/shard_map/reduce_scatter | solution.py:309
  864.8 139.4 %reduce-scatter.43.cloned.1.call-start = ((), (), s32[]{:S(2)}) async-start(), calls=%async_computation.16 | async-start | bytes 4521984 | tf_op jit(solution)/shard_map/reduce_scatter | solution.py:309
  954.9 93.3 %reduce-scatter.41.cloned.1.call-start = ((), (), s32[]{:S(2)}) async-start(), calls=%async_computation.15 | async-start | bytes 4521984 | tf_op jit(solution)/shard_map/reduce_scatter | solution.py:293
  965.1 134.0 %all-gather.35.cloned.1.call-start = ((), (), s32[]{:S(2)}) async-start(), calls=%async_computation.20 | async-start | bytes 4521984 | tf_op jit(solution)/shard_map/all_gather | solution.py:315
  1055.5 288.7 %all-gather.33.cloned.1.call-start = ((), (), s32[]{:S(2)}) async-start(), calls=%async_computation.17 | async-start | bytes 4521984 | tf_op jit(solution)/shard_map/all_gather | solution.py:315
  1080.5 1046.3 %all-reduce.41.cloned.1.call-start = ((), (), s32[]{:S(2)}) async-start(), calls=%async_computation.31 | async-start | bytes 2359296
  1987.8 45.3 %collective-permute-start.4 = (bf16[60,192]{1,0:T(8,128)(2,1)}, bf16[60,192]{1,0:T(8,128)(2,1)}, u32[]{:S(2)}, u32[]{:S(2)}) collective-permute-start(bf16[60,192]{1,0:T(8,128)(2,1)} %slice.108), channel_id=1, source_target_pairs={{0,2},{2,4},{4,6},{6,8},{8,10},{10,12},{12,14},{14,16},{16,18},{18... | collective-permute-start | bytes 69128
  2016.6 25.5 %collective-permute-start.5 = (bf16[60,192]{1,0:T(8,128)(2,1)}, bf16[60,192]{1,0:T(8,128)(2,1)}, u32[]{:S(2)}, u32[]{:S(2)}) collective-permute-start(bf16[60,192]{1,0:T(8,128)(2,1)} %slice.109), channel_id=1, source_target_pairs={{0,2},{2,4},{4,6},{6,8},{8,10},{10,12},{12,14},{14,16},{16,18},{18... | collective-permute-start | bytes 69128
  2021.0 25.3 %collective-permute-start.2 = (bf16[60,192]{1,0:T(8,128)(2,1)}, bf16[60,192]{1,0:T(8,128)(2,1)}, u32[]{:S(2)}, u32[]{:S(2)}) collective-permute-start(bf16[60,192]{1,0:T(8,128)(2,1)} %slice.106), channel_id=1, source_target_pairs={{0,2},{2,4},{4,6},{6,8},{8,10},{10,12},{12,14},{14,16},{16,18},{18... | collective-permute-start | bytes 69128
  2023.0 27.6 %collective-permute-start.3 = (bf16[60,192]{1,0:T(8,128)(2,1)}, bf16[60,192]{1,0:T(8,128)(2,1)}, u32[]{:S(2)}, u32[]{:S(2)}) collective-permute-start(bf16[60,192]{1,0:T(8,128)(2,1)} %slice.107), channel_id=1, source_target_pairs={{0,2},{2,4},{4,6},{6,8},{8,10},{10,12},{12,14},{14,16},{16,18},{18... | collective-permute-start | bytes 69128
  2024.9 27.3 %collective-permute-start = (bf16[60,192]{1,0:T(8,128)(2,1)}, bf16[60,192]{1,0:T(8,128)(2,1)}, u32[]{:S(2)}, u32[]{:S(2)}) collective-permute-start(bf16[60,192]{1,0:T(8,128)(2,1)} %slice.104), channel_id=1, source_target_pairs={{0,2},{2,4},{4,6},{6,8},{8,10},{10,12},{12,14},{14,16},{16,18},{18... | collective-permute-start | bytes 69128
  2033.0 171.4 %all-reduce.43.cloned.1.call-start = ((), (), s32[]{:S(2)}) async-start(), calls=%async_computation.32 | async-start | bytes 786432 | tf_op jit(solution)/shard_map/psum | solution.py:370
  2033.1 26.3 %collective-permute-start.1 = (bf16[60,192]{1,0:T(8,128)(2,1)}, bf16[60,192]{1,0:T(8,128)(2,1)}, u32[]{:S(2)}, u32[]{:S(2)}) collective-permute-start(bf16[60,192]{1,0:T(8,128)(2,1)} %slice.105), channel_id=1, source_target_pairs={{0,2},{2,4},{4,6},{6,8},{8,10},{10,12},{12,14},{14,16},{16,18},{18... | collective-permute-start | bytes 69128
  2128.5 82.6 %reduce-scatter.45.cloned.1.call-start = ((), (), s32[]{:S(2)}) async-start(), calls=%async_computation.18 | async-start | bytes 4521984 | tf_op jit(solution)/shard_map/reduce_scatter | solution.py:336
  2135.9 109.4 %reduce-scatter.49.cloned.1.call-start = ((), (), s32[]{:S(2)}) async-start(), calls=%async_computation.21 | async-start | bytes 4521984 | tf_op jit(solution)/shard_map/reduce_scatter | solution.py:336
  2140.8 148.7 %reduce-scatter.37.cloned.1.call-start = ((), (), s32[]{:S(2)}) async-start(), calls=%async_computation.11 | async-start | bytes 4521984 | tf_op jit(solution)/shard_map/reduce_scatter | solution.py:293
  2168.1 25.3 %collective-permute-start.7 = (bf16[60,1792]{1,0:T(8,128)(2,1)}, bf16[60,1792]{1,0:T(8,128)(2,1)}, u32[]{:S(2)}, u32[]{:S(2)}) collective-permute-start(bf16[60,1792]{1,0:T(8,128)(2,1)} %slice.111), channel_id=1, source_target_pairs={{0,2},{2,4},{4,6},{6,8},{8,10},{10,12},{12,14},{14,16},{16,18},{18... | collective-permute-start | bytes 645128
  (177 other events, 2830.4 us)
Sparse Core Ops, SparseCore 0:
  10.3 41.1 all-gather.46
  53.8 37.3 all-gather.44
  93.4 37.3 all-gather.42
  132.9 37.3 all-gather.40
  172.2 42.4 all-gather.24
  216.7 43.4 all-gather.28
  364.6 41.9 reduce-scatter.34
  517.3 41.8 reduce-scatter.38
  561.5 57.3 all-gather.48
  621.1 55.9 all-gather.50
  679.4 55.9 all-gather.52
  737.4 42.0 all-gather.30
  781.0 43.4 all-gather.38
  826.5 43.4 all-gather.26
  871.4 43.4 all-gather.36
  917.5 41.9 reduce-scatter.46
  962.2 41.8 reduce-scatter.42
  1006.3 41.9 reduce-scatter.40
  1055.6 43.4 all-gather.34
  1101.1 43.4 all-gather.32
  2033.2 93.5 all-reduce.40
  2130.5 25.2 all-reduce.42
  2158.7 41.9 reduce-scatter.44
  2203.4 41.8 reduce-scatter.48
  2247.6 41.9 reduce-scatter.36
where the time goes:
time: 2360 us; the launch traced here: 2340 us
  local copies, waits for them, and re-layouts  684 us (29%)
  waiting for transfers between devices  658 us (28%)
  blocking collectives  408 us (17%)
  matrix products  333 us (14%)
  other arithmetic  100 us (4%)
  loops' own time  82.6 us (4%)
  starting transfers between devices  61.1 us (3%)
    unnamed x1, blocking collectives  368 us
    while x124, local copies, waits for them, and re-layouts  317 us
    reshape x8, local copies, waits for them, and re-layouts, skew_bias(): return shifted.reshape(slot_count, block_rows, span)[:, :, :length]  125 us
    unnamed x292, local copies, waits for them, and re-layouts  87 us
    reduce_scatter x2, waiting for transfers between devices, body(): lax.psum_scatter(ffn_part.astype(jnp.bfloat16), 'mp', scatter_dimension=1...  73.8 us
    slice x8, local copies, waits for them, and re-layouts, skew_bias(): lax.slice_in_dim(tiled, block_rows - 1, block_rows - 1 + block_rows * spa...  69.1 us
    unnamed x38, waiting for transfers between devices  68.2 us
    another operation x2, loops' own time, attend_grads(): lax.scan(one_block, initial, (starts, log_sums))  65.5 us
  transfers between devices with their start and end apart: 37, of which 19 were waited for; matrix products, arithmetic and copies ran while one was open for 36% of the time, Pallas kernels for 0%

commit v1 on v0

v1 whole, which is shorter than its diff:
```python
import functools

import jax
import jax.numpy as jnp
from jax import lax
from jax.experimental import pallas as pl
from jax.experimental.pallas import tpu as pltpu
from jax.sharding import PartitionSpec as P

EPSILON = 1e-06
TOP_PRECISION = lax.Precision.HIGHEST
GELU_SCALE = 0.7978845608028654
BF16 = jnp.bfloat16
F32 = jnp.float32
NEGATIVE = -1e30
VMEM_BYTES = 56 * 1024 * 1024


def swap_dp(array, mask):
    count = lax.axis_size("dp")
    return lax.ppermute(array, "dp", [(i, i ^ mask) for i in range(count)])


def swap_mp(array, mask):
    count = lax.axis_size("mp")
    return lax.ppermute(array, "mp", [(i, i ^ mask) for i in range(count)])


def place(pieces, index, axis):
    first = pieces[0]
    shape = first.shape[:axis] + (len(pieces),) + first.shape[axis:]
    whole = jnp.zeros(shape, first.dtype)
    for k, piece in enumerate(pieces):
        whole = lax.dynamic_update_index_in_dim(
            whole, jnp.expand_dims(piece, axis), index ^ k, axis
        )
    return whole


def pick(array, index, axis):
    return lax.dynamic_index_in_dim(array, index, axis, keepdims=False)


def add_low(*terms):
    total = terms[0].astype(F32)
    for term in terms[1:]:
        total = total + term.astype(F32)
    return total.astype(BF16)


def bias_kernel(window_ref, table_ref):
    block = table_ref.shape[-1]
    wide = jnp.broadcast_to(window_ref[0, 0], (block, 2 * block))
    rolled = pltpu.roll(wide, block + 1, 1, stride=1, stride_axis=0)
    table_ref[0, 0] = rolled[:, :block]


def bias_table(windows, block):
    heads, count = windows.shape[:2]
    return pl.pallas_call(
        bias_kernel,
        grid=(heads, count),
        in_specs=[pl.BlockSpec((1, 1, 1, 2 * block), lambda j, e: (j, e, 0, 0))],
        out_specs=pl.BlockSpec((1, 1, block, block), lambda j, e: (j, e, 0, 0)),
        out_shape=jax.ShapeDtypeStruct((heads, count, block, block), F32),
        name="bias_table",
    )(windows)


def transposed(value):
    return jnp.transpose(value.astype(F32), (1, 0)).astype(BF16)


def halves(value_t, half):
    zero = jnp.zeros((half, value_t.shape[1]), value_t.dtype)
    return (
        jnp.concatenate([value_t[:half], zero], axis=0),
        jnp.concatenate([zero, value_t[half:]], axis=0),
    )


def dot_nn(left, right):
    return lax.dot_general(left, right, (((1,), (0,)), ((), ())), preferred_element_type=F32)


def attend_kernel(sources, block, half, info_ref, q_ref, *refs):
    kv_refs = refs[: 2 * sources]
    segq_ref, segk_ref, table_ref, ctx_ref, lse_ref = refs[2 * sources : 2 * sources + 5]
    s_scr, m_scr, l_scr, acc_scr, vt_scr = refs[2 * sources + 5 :]
    length = q_ref.shape[1]
    q_blocks = length // block
    k_blocks = q_blocks * sources
    place_x = info_ref[0]
    step = pl.program_id(1)
    for s in range(sources):
        vt_scr[:, s * length : (s + 1) * length] = transposed(kv_refs[2 * s + 1][0])
    for qb in range(q_blocks):
        rows = pl.ds(qb * block, block)
        q_heads = halves(transposed(q_ref[0, rows, :]), half)
        seg_q = segq_ref[0, :, rows]
        m_scr[...] = jnp.full(m_scr.shape, NEGATIVE, F32)
        l_scr[...] = jnp.zeros(l_scr.shape, F32)
        acc_scr[...] = jnp.zeros(acc_scr.shape, F32)
        for kb in range(k_blocks):
            s, lb = divmod(kb, q_blocks)
            live = info_ref[1 + (step * q_blocks + qb) * k_blocks + kb]

            @pl.when(live != 0)
            def _(s=s, lb=lb, kb=kb):
                entry = k_blocks - 1 - ((place_x ^ s) * q_blocks + lb - place_x * q_blocks - qb)
                keys = kv_refs[2 * s][0, pl.ds(lb * block, block), :]
                kept = segk_ref[0, pl.ds(kb * block, block), :] == seg_q
                for h in range(2):
                    score = dot_nn(keys, q_heads[h]) + table_ref[h, entry]
                    score = jnp.where(kept, score, NEGATIVE)
                    s_scr[h, kb] = score
                    m_scr[h] = jnp.maximum(m_scr[h], jnp.max(score, axis=0, keepdims=True))

        for kb in range(k_blocks):
            live = info_ref[1 + (step * q_blocks + qb) * k_blocks + kb]

            @pl.when(live != 0)
            def _(kb=kb):
                for h in range(2):
                    prob = jnp.exp(s_scr[h, kb] - m_scr[h])
                    l_scr[h] += jnp.sum(prob, axis=0, keepdims=True)
                    values_t = vt_scr[h * half : (h + 1) * half, kb * block : (kb + 1) * block]
                    acc_scr[h * half : (h + 1) * half] += dot_nn(values_t, prob.astype(BF16))

        for h in range(2):
            lse_ref[0, 0, h : h + 1, rows] = m_scr[h] + jnp.log(l_scr[h])
        context = jnp.concatenate(
            [acc_scr[:half] / l_scr[0], acc_scr[half:] / l_scr[1]], axis=0
        )
        ctx_ref[0, rows, :] = jnp.transpose(context, (1, 0)).astype(BF16)


def grad_kernel(sources, block, half, info_ref, q_ref, *refs):
    kv_refs = refs[: 2 * sources]
    refs = refs[2 * sources :]
    segq_ref, segk_ref, table_ref, ctx_ref, lse_ref, gctx_ref = refs[:6]
    dq_ref, gbias_ref = refs[6:8]
    dkv_refs = refs[8 : 8 + sources]
    dk_scr, dv_scr, dq_scr, kt_scr, db_scr = refs[8 + sources :]
    length = q_ref.shape[1]
    q_blocks = length // block
    k_blocks = q_blocks * sources
    place_x = info_ref[0]
    step = pl.program_id(1)
    lane = lax.broadcasted_iota(jnp.int32, (block, 2 * half), 1)

    @pl.when(step == 0)
    def _():
        db_scr[...] = jnp.zeros(db_scr.shape, F32)

    for s in range(sources):
        kt_scr[:, s * length : (s + 1) * length] = transposed(kv_refs[2 * s][0])
    dk_scr[...] = jnp.zeros(dk_scr.shape, F32)
    dv_scr[...] = jnp.zeros(dv_scr.shape, F32)
    for qb in range(q_blocks):
        rows = pl.ds(qb * block, block)
        query = q_ref[0, rows, :]
        grad_out = gctx_ref[0, rows, :]
        grad_out_t = jnp.transpose(grad_out.astype(F32), (1, 0))
        context_t = jnp.transpose(ctx_ref[0, rows, :].astype(F32), (1, 0))
        product = grad_out_t * context_t
        deltas = (
            jnp.sum(product[:half], axis=0, keepdims=True),
            jnp.sum(product[half:], axis=0, keepdims=True),
        )
        q_heads = halves(transposed(query), half)
        g_heads = halves(grad_out_t.astype(BF16), half)
        zero = jnp.zeros(query.shape, BF16)
        q_lanes = (jnp.where(lane < half, query, zero), jnp.where(lane < half, zero, query))
        g_lanes = (
            jnp.where(lane < half, grad_out, zero),
            jnp.where(lane < half, zero, grad_out),
        )
        seg_q = segq_ref[0, :, rows]
        dq_scr[...] = jnp.zeros(dq_scr.shape, F32)
        for kb in range(k_blocks):
            s, lb = divmod(kb, q_blocks)
            live = info_ref[1 + (step * q_blocks + qb) * k_blocks + kb]

            @pl.when(live != 0)
            def _(s=s, lb=lb, kb=kb):
                entry = k_blocks - 1 - ((place_x ^ s) * q_blocks + lb - place_x * q_blocks - qb)
                keys = kv_refs[2 * s][0, pl.ds(lb * block, block), :]
                values = kv_refs[2 * s + 1][0, pl.ds(lb * block, block), :]
                kept = segk_ref[0, pl.ds(kb * block, block), :] == seg_q
                key_rows = pl.ds(kb * block, block)
                key_grad = dk_scr[key_rows, :]
                value_grad = dv_scr[key_rows, :]
                for h in range(2):
                    score = dot_nn(keys, q_heads[h]) + table_ref[h, entry]
                    score = jnp.where(kept, score, NEGATIVE)
                    prob = jnp.exp(score - lse_ref[0, 0, h : h + 1, rows])
                    grad_prob = dot_nn(values, g_heads[h])
                    grad_score = prob * (grad_prob - deltas[h])
                    db_scr[h, entry] += grad_score
                    low = grad_score.astype(BF16)
                    key_grad = key_grad + dot_nn(low, q_lanes[h])
                    value_grad = value_grad + dot_nn(prob.astype(BF16), g_lanes[h])
                    keys_t = kt_scr[h * half : (h + 1) * half, kb * block : (kb + 1) * block]
                    dq_scr[h * half : (h + 1) * half] += dot_nn(keys_t, low)
                dk_scr[key_rows, :] = key_grad
                dv_scr[key_rows, :] = value_grad

        dq_ref[0, rows, :] = jnp.transpose(dq_scr[...], (1, 0)).astype(BF16)
    for s in range(sources):
        dkv_refs[s][0, 0] = dk_scr[s * length : (s + 1) * length, :].astype(BF16)
        dkv_refs[s][0, 1] = dv_scr[s * length : (s + 1) * length, :].astype(BF16)

    @pl.when(step == pl.num_programs(1) - 1)
    def _():
        for h in range(2):
            for entry in range(2 * k_blocks - 1):
                tile = db_scr[h, entry]
                tile = jnp.concatenate([tile, jnp.zeros_like(tile)], axis=1)
                count = block
                while count > 8:
                    count //= 2
                    tile = pltpu.roll(tile[:count], count, 1) + tile[count:]
                total = tile[7:8]
                for t in range(7):
                    total = total + pltpu.roll(tile[t : t + 1], 7 - t, 1)
                gbias_ref[h, entry] = total


def attention_specs(sources, length, block, pairs, width):
    k_blocks = length * sources // block
    entries = 2 * k_blocks - 1

    def column(offset):
        return pl.BlockSpec((1, length, width), lambda p, m, info: (m, 0, p + offset))

    kv_specs = [column(pairs), column(2 * pairs)]
    for _ in range(sources - 1):
        kv_specs += [column(0), column(pairs)]
    seg_specs = [
        pl.BlockSpec((1, 1, length), lambda p, m, info: (m, 0, 0)),
        pl.BlockSpec((1, length * sources, 1), lambda p, m, info: (m, 0, 0)),
    ]
    table_spec = pl.BlockSpec((2, entries, block, block), lambda p, m, info: (p, 0, 0, 0))
    lse_spec = pl.BlockSpec((1, 1, 8, length), lambda p, m, info: (m, p, 0, 0))
    return k_blocks, entries, column, kv_specs, seg_specs, table_spec, lse_spec


def kv_operands(qkv, others):
    operands = [qkv, qkv]
    for other in others:
        operands += [other, other]
    return operands


def attend(info, qkv, others, seg_q, seg_k, table, block, head_size):
    micro, length, total = qkv.shape
    sources = 1 + len(others)
    width = 2 * head_size
    pairs = total // (3 * width)
    k_blocks, entries, column, kv_specs, seg_specs, table_spec, lse_spec = attention_specs(
        sources, length, block, pairs, width
    )
    return pl.pallas_call(
        functools.partial(attend_kernel, sources, block, head_size),
        grid_spec=pltpu.PrefetchScalarGridSpec(
            num_scalar_prefetch=1,
            grid=(pairs, micro),
            in_specs=[column(0)] + kv_specs + seg_specs + [table_spec],
            out_specs=[column(0), lse_spec],
            scratch_shapes=[
                pltpu.VMEM((2, k_blocks, block, block), F32),
                pltpu.VMEM((2, 1, block), F32),
                pltpu.VMEM((2, 1, block), F32),
                pltpu.VMEM((width, block), F32),
                pltpu.VMEM((width, length * sources), BF16),
            ],
        ),
        out_shape=[
            jax.ShapeDtypeStruct((micro, length, pairs * width), BF16),
            jax.ShapeDtypeStruct((micro, pairs, 8, length), F32),
        ],
        compiler_params=pltpu.CompilerParams(vmem_limit_bytes=VMEM_BYTES),
        name="attend",
    )(info, qkv, *kv_operands(qkv, others), seg_q, seg_k, table)


def attend_grads(info, qkv, others, seg_q, seg_k, table, context, lse, grad_context, block, head_size):
    micro, length, total = qkv.shape
    sources = 1 + len(others)
    width = 2 * head_size
    pairs = total // (3 * width)
    k_blocks, entries, column, kv_specs, seg_specs, table_spec, lse_spec = attention_specs(
        sources, length, block, pairs, width
    )
    dkv_spec = pl.BlockSpec((1, 2, length, width), lambda p, m, info: (m, 0, 0, p))
    results = pl.pallas_call(
        functools.partial(grad_kernel, sources, block, head_size),
        grid_spec=pltpu.PrefetchScalarGridSpec(
            num_scalar_prefetch=1,
            grid=(pairs, micro),
            in_specs=[column(0)]
            + kv_specs
            + seg_specs
            + [table_spec, column(0), lse_spec, column(0)],
            out_specs=[
                column(0),
                pl.BlockSpec((2, entries, 1, 2 * block), lambda p, m, info: (p, 0, 0, 0)),
            ]
            + [dkv_spec] * sources,
            scratch_shapes=[
                pltpu.VMEM((length * sources, width), F32),
                pltpu.VMEM((length * sources, width), F32),
                pltpu.VMEM((width, block), F32),
                pltpu.VMEM((width, length * sources), BF16),
                pltpu.VMEM((2, entries, block, block), F32),
            ],
        ),
        out_shape=[
            jax.ShapeDtypeStruct((micro, length, pairs * width), BF16),
            jax.ShapeDtypeStruct((2 * pairs, entries, 1, 2 * block), F32),
        ]
        + [jax.ShapeDtypeStruct((micro, 2, length, pairs * width), BF16)] * sources,
        compiler_params=pltpu.CompilerParams(vmem_limit_bytes=VMEM_BYTES),
        name="attend_grads",
    )(
        info,
        qkv,
        *kv_operands(qkv, others),
        seg_q,
        seg_k,
        table,
        context,
        lse,
        grad_context,
    )
    return results[0], results[1], results[2:]


def gather_attention(shard, z, y, core, x):
    dp, mp = lax.axis_size("dp"), lax.axis_size("mp")
    depth = dp // 4
    rows, columns = shard.shape
    part = columns // (2 * mp)
    split = shard.reshape(rows, mp, 2, part)
    own_x = pick(split, x, 1)
    kept = pick(own_x, core, 1)
    got = swap_dp(pick(own_x, 1 - core, 1), 1)
    piece = place([kept, got], core, 0).reshape(2 * rows, part)
    column_y = place([piece] + [swap_dp(piece, 4 * k) for k in range(1, depth)], z, 0)
    both = place([column_y, swap_dp(column_y, 2)], y, 1)
    full = both.reshape(dp * rows, part)
    all_x = place([full] + [swap_mp(full, k) for k in range(1, mp)], x, 0)
    all_core = place([all_x, swap_dp(all_x, 1)], core, 1)
    return jnp.transpose(all_core, (2, 0, 1, 3)).reshape(dp * rows, columns)


def scatter_attention(grads, z, y, core, x):
    dp, mp = lax.axis_size("dp"), lax.axis_size("mp")
    depth = dp // 4
    wide, columns = grads.shape
    rows = wide // dp
    part = columns // (2 * mp)
    split = grads.reshape(wide, mp, 2, part)
    mine = add_low(pick(split, core, 2), swap_dp(pick(split, 1 - core, 2), 1))
    own = add_low(
        pick(mine, x, 1), *[swap_mp(pick(mine, x ^ k, 1), k) for k in range(1, mp)]
    ).reshape(depth, 2, 2 * rows, part)
    half = add_low(pick(own, y, 1), swap_dp(pick(own, 1 - y, 1), 2))
    piece = add_low(
        pick(half, z, 0), *[swap_dp(pick(half, z ^ k, 0), 4 * k) for k in range(1, depth)]
    )
    all_x = place([piece] + [swap_mp(piece, k) for k in range(1, mp)], x, 0)
    split_rows = all_x.reshape(mp, 2, rows, part)
    kept = pick(split_rows, core, 1)
    got = swap_dp(pick(split_rows, 1 - core, 1), 1)
    both = place([kept, got], core, 1)
    return jnp.transpose(both, (2, 0, 1, 3)).reshape(rows, columns)


def gather_ffn(piece, z, y, x_last):
    dp, mp = lax.axis_size("dp"), lax.axis_size("mp")
    depth = dp // 4
    kinds, rows, units = piece.shape
    column_y = place([piece] + [swap_dp(piece, 4 * k) for k in range(1, depth)], z, 1)
    if x_last:
        both = place([column_y, swap_dp(column_y, 2)], y, 2)
        full = both.reshape(kinds, dp // 2 * rows, units)
        return jnp.concatenate([full] + [swap_mp(full, k) for k in range(1, mp)], axis=2)
    wide = jnp.concatenate([column_y] + [swap_mp(column_y, k) for k in range(1, mp)], axis=3)
    both = place([wide, swap_dp(wide, 2)], y, 2)
    return both.reshape(kinds, dp // 2 * rows, mp * units)


def scatter_ffn(grads, z, y, x_last):
    dp, mp = lax.axis_size("dp"), lax.axis_size("mp")
    depth = dp // 4
    kinds, wide, total = grads.shape
    rows, units = wide // (dp // 2), total // mp
    own = grads.reshape(kinds, depth, 2, rows, mp, units)

    def sum_y(part):
        return add_low(pick(part, y, 2), swap_dp(pick(part, 1 - y, 2), 2))

    def sum_x(part):
        return add_low(part[..., 0, :], *[swap_mp(part[..., k, :], k) for k in range(1, mp)])

    half = sum_y(sum_x(own)) if x_last else sum_x(sum_y(own))
    return add_low(
        pick(half, z, 1), *[swap_dp(pick(half, z ^ k, 1), 4 * k) for k in range(1, depth)]
    )


def norm_factor(values):
    return lax.rsqrt(jnp.mean(values * values, axis=-1, keepdims=True) + EPSILON)


def norm_grads(values, factor, gain, grad):
    scaled = values * factor
    lifted = grad * gain
    inner = jnp.mean(lifted * scaled, axis=-1, keepdims=True)
    return factor * (lifted - scaled * inner), jnp.sum(grad * scaled, axis=0)


def matmul(left, right):
    return jnp.einsum("td,df->tf", left, right, preferred_element_type=F32)


def matmul_t(left, right):
    return jnp.einsum("tf,df->td", left, right, preferred_element_type=F32)


def outer(left, right):
    return jnp.einsum("td,tf->df", left, right, preferred_element_type=F32)


def body(
    inputs,
    cotangent,
    segments,
    rel_bucket,
    head_order,
    rel_table,
    norm1_gain,
    norm2_gain,
    w_query,
    w_key,
    w_value,
    output_weight,
    w_gate,
    w_up,
    w_down,
):
    mp = lax.axis_size("mp")
    x = lax.axis_index("mp")
    dp_place = lax.axis_index("dp")
    core, y, z = dp_place & 1, (dp_place >> 1) & 1, dp_place >> 2
    micro, rows, own_length, model = inputs.shape
    groups = micro * rows
    length = own_length * mp
    bucket_count, head_count = rel_table.shape
    inner = w_query.shape[1]
    head_size = inner // head_count
    block = min(256, own_length)
    q_blocks, k_blocks = own_length // block, length // block
    tokens = groups * own_length

    attention_shard = jnp.concatenate(
        [w_query, w_key, w_value, jnp.transpose(output_weight)], axis=1
    )
    attention_full = gather_attention(attention_shard, z, y, core, x)
    w_qkv, w_out_t = attention_full[:, : 3 * inner], attention_full[:, 3 * inner :]

    own_rows, own_units = w_gate.shape
    half_units = own_units // 2
    ffn_shard = jnp.stack([w_gate, w_up, jnp.transpose(w_down)])
    ffn_split = ffn_shard.reshape(3, own_rows, 2, half_units)
    kept = pick(ffn_split, core, 2)
    got = swap_dp(pick(ffn_split, 1 - core, 2), 1)
    ffn_piece = place([kept, got], core, 1).reshape(3, 2 * own_rows, half_units)
    first_units = half_units * 3 // 7
    chunks = (
        gather_ffn(ffn_piece[:, :, :first_units], z, y, True),
        gather_ffn(ffn_piece[:, :, first_units:], z, y, False),
    )

    bucket_rev = jnp.concatenate([rel_bucket[::-1], jnp.full((1,), -1, jnp.int32)])
    bucket_hot = (bucket_rev[:, None] == jnp.arange(bucket_count, dtype=jnp.int32)[None, :]).astype(F32)
    head_hot = (head_order[:, None] == jnp.arange(head_count, dtype=jnp.int32)[None, :]).astype(F32)
    offset_table = jnp.dot(bucket_hot, rel_table, precision=TOP_PRECISION)
    offset_bias = jnp.dot(head_hot, offset_table.T, precision=TOP_PRECISION)
    bias_blocks = offset_bias.reshape(head_count, 2 * k_blocks, block)
    windows = jnp.concatenate([bias_blocks[:, :-1], bias_blocks[:, 1:]], axis=2)
    table = bias_table(windows[:, :, None, :], block)

    seg_flat = segments.reshape(groups, length)
    seg_q = lax.dynamic_slice_in_dim(seg_flat, x * own_length, own_length, 1)
    seg_parts = seg_flat.reshape(groups, mp, own_length)
    seg_k = jnp.concatenate([pick(seg_parts, x ^ k, 1) for k in range(mp)], axis=1)
    q_edges = seg_q.reshape(groups, q_blocks, block)
    k_edges = seg_k.reshape(groups, k_blocks, block)
    live = (q_edges[:, :, None, 0] <= k_edges[:, None, :, -1]) & (
        k_edges[:, None, :, 0] <= q_edges[:, :, None, -1]
    )
    info = jnp.concatenate([x.reshape(1).astype(jnp.int32), live.reshape(-1).astype(jnp.int32)])
    seg_q_row = seg_q.reshape(groups, 1, own_length)
    seg_k_column = seg_k.reshape(groups, length, 1)

    layer_in = inputs.reshape(tokens, model).astype(F32)
    factor1 = norm_factor(layer_in)
    normed1 = (layer_in * factor1 * norm1_gain).astype(BF16)
    qkv = matmul(normed1, w_qkv).astype(BF16).reshape(groups, own_length, 3 * inner)
    own_kv = qkv[:, :, inner:]
    others = [swap_mp(own_kv, k) for k in range(1, mp)]
    context, lse = attend(info, qkv, others, seg_q_row, seg_k_column, table, block, head_size)
    context_flat = context.reshape(tokens, inner)
    middle = layer_in + matmul_t(context_flat, w_out_t)
    factor2 = norm_factor(middle)
    normed2 = (middle * factor2 * norm2_gain).astype(BF16)

    cot = cotangent.reshape(tokens, model)
    normed2_both = jnp.concatenate([normed2, swap_dp(normed2, 1)], axis=0)
    cot_both = jnp.concatenate([cot, swap_dp(cot, 1)], axis=0)
    ffn_sum = None
    back_sum = None
    reduced = []
    for chunk, weights in enumerate(chunks):
        gate = matmul(normed2_both, weights[0])
        upward = matmul(normed2_both, weights[1])
        grad_hidden = matmul(cot_both, weights[2])
        tanh = jnp.tanh(GELU_SCALE * (gate + 0.044715 * gate * gate * gate))
        gelu = 0.5 * gate * (1.0 + tanh)
        slope = 0.5 * (1.0 + tanh) + 0.5 * gate * (1.0 - tanh * tanh) * GELU_SCALE * (
            1.0 + 3.0 * 0.044715 * gate * gate
        )
        hidden = (gelu * upward).astype(BF16)
        grad_gate_in = (grad_hidden * upward * slope).astype(BF16)
        grad_up_in = (grad_hidden * gelu).astype(BF16)
        ffn_part = matmul_t(hidden, weights[2])
        back_part = matmul_t(grad_gate_in, weights[0]) + matmul_t(grad_up_in, weights[1])
        ffn_sum = ffn_part if ffn_sum is None else ffn_sum + ffn_part
        back_sum = back_part if back_sum is None else back_sum + back_part
        grads = jnp.stack(
            [
                outer(normed2_both, grad_gate_in).astype(BF16),
                outer(normed2_both, grad_up_in).astype(BF16),
                outer(cot_both, hidden).astype(BF16),
            ]
        )
        reduced.append(scatter_ffn(grads, z, y, chunk == 0))
    ffn_low = ffn_sum.astype(BF16)
    back_low = back_sum.astype(BF16)
    grad_normed2 = back_low[:tokens].astype(F32) + swap_dp(back_low[tokens:], 1).astype(F32)
    ffn_out = ffn_low[:tokens].astype(F32) + swap_dp(ffn_low[tokens:], 1).astype(F32)
    outputs = (middle + ffn_out).astype(BF16)

    grad_mid_norm, grad_gain2 = norm_grads(middle, factor2, norm2_gain, grad_normed2)
    grad_middle = cot.astype(F32) + grad_mid_norm
    grad_attn = grad_middle.astype(BF16)
    grad_context = matmul(grad_attn, w_out_t).astype(BF16)
    grad_q, bias_grads, dkv = attend_grads(
        info,
        qkv,
        others,
        seg_q_row,
        seg_k_column,
        table,
        context,
        lse,
        grad_context.reshape(groups, own_length, inner),
        block,
        head_size,
    )
    grad_kv = add_low(dkv[0], *[swap_mp(dkv[k], k) for k in range(1, mp)])
    grad_qkv = jnp.concatenate(
        [
            grad_q.reshape(tokens, inner),
            grad_kv[:, 0].reshape(tokens, inner),
            grad_kv[:, 1].reshape(tokens, inner),
        ],
        axis=1,
    )
    grad_normed1 = matmul_t(grad_qkv, w_qkv)
    grad_in_norm, grad_gain1 = norm_grads(layer_in, factor1, norm1_gain, grad_normed1)
    grad_inputs = (grad_middle + grad_in_norm).astype(BF16)
    attention_grads = jnp.concatenate(
        [outer(normed1, grad_qkv).astype(BF16), outer(grad_attn, context_flat).astype(BF16)], axis=1
    )
    attention_sum = scatter_attention(attention_grads, z, y, core, x).astype(F32)

    ffn_sums = jnp.concatenate(reduced, axis=2).reshape(3, 2, own_rows, half_units)
    kept = pick(ffn_sums, core, 1)
    got = swap_dp(pick(ffn_sums, 1 - core, 1), 1)
    ffn_grads = place([kept, got], core, 2).reshape(3, own_rows, own_units).astype(F32)

    bias_flat = bias_grads[:, :, 0, :]
    left = jnp.pad(bias_flat[:, :, :block], ((0, 0), (0, 1), (0, 0)))
    right = jnp.pad(bias_flat[:, :, block:], ((0, 0), (1, 0), (0, 0)))
    offsets_total = (left + right).reshape(head_count, 2 * k_blocks * block)
    bucket_part = jnp.dot(bucket_hot.T, offsets_total.T, precision=TOP_PRECISION)
    rel_part = jnp.dot(bucket_part, head_hot, precision=TOP_PRECISION)
    grad_norm1, grad_norm2, grad_rel = lax.psum((grad_gain1, grad_gain2, rel_part), ("dp", "mp"))
    shape = inputs.shape
    return (
        outputs.reshape(shape),
        grad_inputs.reshape(shape),
        grad_rel,
        grad_norm1,
        grad_norm2,
        attention_sum[:, :inner],
        attention_sum[:, inner : 2 * inner],
        attention_sum[:, 2 * inner : 3 * inner],
        jnp.transpose(attention_sum[:, 3 * inner :]),
        ffn_grads[0],
        ffn_grads[1],
        jnp.transpose(ffn_grads[2]),
    )


def solution(mesh):
    return jax.shard_map(
        body,
        mesh=mesh,
        in_specs=(
            P(None, "dp", "mp", None),
            P(None, "dp", "mp", None),
            P(None, "dp", None),
            P(),
            P(),
            P(),
            P(),
            P(),
            P("dp", None),
            P("dp", None),
            P("dp", None),
            P(None, "dp"),
            P("dp", "mp"),
            P("dp", "mp"),
            P("mp", "dp"),
        ),
        out_specs=(
            P(None, "dp", "mp", None),
            P(None, "dp", "mp", None),
            P(),
            P(),
            P(),
            P("dp", None),
            P("dp", None),
            P("dp", None),
            P(None, "dp"),
            P("dp", "mp"),
            P("dp", "mp"),
            P("mp", "dp"),
        ),
        check_vma=False,
    )
```

time: 2360 us -> 990 us (0.42)
  waiting for transfers between devices: 658 us -> 208 us
  local copies, waits for them, and re-layouts: 684 us -> 258 us
  blocking collectives: 408 us -> 41.1 us
  matrix products: 333 us -> 238 us
  loops' own time: 82.6 us -> 0 us
  Pallas kernels: 0 us -> 75.6 us
  starting transfers between devices: 61.1 us -> 112 us
  other arithmetic: 100 us -> 50.9 us
    all_gather x15 -> x0, waiting for transfers between devices: 431 us -> none  [the longest x1 50.8 us: fetch_weights(): lax.all_gather(weights[6], 'dp', axis=1, tiled=True)]
    unnamed x1 -> x0, blocking collectives: 368 us -> none
    while x128 -> x0, local copies, waits for them, and re-layouts: 321 us -> none
    ppermute x0 -> x43, waiting for transfers between devices: none -> 208 us  [the longest x34 199 us: swap_dp(): return lax.ppermute(array, 'dp', [(i, i ^ mask) for i in range(count)])]
    reduce_scatter x8 -> x0, waiting for transfers between devices: 159 us -> none  [the longest x2 73.8 us: body(): lax.psum_scatter(ffn_part.astype(jnp.bfloat16), 'mp', scatter_dimension=1...]
    reshape x15 -> x10, local copies, waits for them, and re-layouts: 163 us -> 22.6 us  [the longest x1 10.1 us: scatter_attention(): split = grads.reshape(wide, mp, 2, part)]
    ppermute x0 -> x43, starting transfers between devices: none -> 112 us  [the longest x34 102 us: swap_dp(): return lax.ppermute(array, 'dp', [(i, i ^ mask) for i in range(count)])]
    dot_general x73 -> x26, matrix products: 331 us -> 236 us  [the longest x8 89.1 us: matmul(): return jnp.einsum('td,df->tf', left, right, preferred_element_type=F32)]
  transfers between devices with their start and end apart: 37 -> 43, of which waited for: 19 -> 16; matrix products, arithmetic and copies ran while one was open for 36% -> 45% of each run, Pallas kernels for 0% -> 8%
where the time goes in v1:
time: 990 us; the launch traced here: 985 us
  local copies, waits for them, and re-layouts  258 us (26%)
  matrix products  238 us (24%)
  waiting for transfers between devices  208 us (21%)
  starting transfers between devices  112 us (11%)
  Pallas kernels  75.6 us (8%)
  other arithmetic  50.9 us (5%)
  blocking collectives  41.1 us (4%)
    ppermute x34, waiting for transfers between devices, swap_dp(): return lax.ppermute(array, 'dp', [(i, i ^ mask) for i in range(count)])  199 us
    ppermute x34, starting transfers between devices, swap_dp(): return lax.ppermute(array, 'dp', [(i, i ^ mask) for i in range(count)])  102 us
    dot_general x8, matrix products, matmul(): return jnp.einsum('td,df->tf', left, right, preferred_element_type=F32)  89.1 us
    dot_general x8, matrix products, matmul_t(): return jnp.einsum('tf,df->td', left, right, preferred_element_type=F32)  85.9 us
    unnamed x168, local copies, waits for them, and re-layouts  60.2 us
    dot_general x8, matrix products, outer(): return jnp.einsum('td,tf->df', left, right, preferred_element_type=F32)  60.1 us
    dynamic_update_slice x30, local copies, waits for them, and re-layouts, place(): lax.dynamic_update_index_in_dim(whole, jnp.expand_dims(piece, axis), inde...  48.9 us
    another operation x8, local copies, waits for them, and re-layouts, body(): jnp.stack([outer(normed2_both, grad_gate_in).astype(BF16), outer(normed2_...  45.6 us
  transfers between devices with their start and end apart: 43, of which 16 were waited for; matrix products, arithmetic and copies ran while one was open for 45% of the time, Pallas kernels for 8%

profile of v1, /device:TPU:0, one launch (start us, length us, event | category | flops | bytes accessed | tf_op | source)
XLA Modules:
  0.0 984.9 jit_solution(13043943030346119694)
XLA Ops:
  9.7 12.0 %copy.128 = bf16[2,1,512,1472]{2,0,3,1:T(2,128)(2,1)S(1)} copy(bf16[2,1,512,1472]{2,3,1,0:T(8,128)(2,1)S(1)} %copy-done.16) | data formatting | bytes 6029312 | tf_op args[1]
  37.1 10.1 %collective-permute-done.2 = bf16[184,384]{1,0:T(8,128)(2,1)S(1)} collective-permute-done((bf16[184,384]{1,0:T(8,128)(2,1)S(1)}, bf16[184,384]{1,0:T(8,128)(2,1)S(1)}, u32[]{:S(2)}, u32[]{:S(2)}) %collective-permute-start.2) | collective-permute-done | bytes 141344 | tf_op jit(solution)/shard_map/ppermute | solution.py:21
  67.4 11.0 %collective-permute-done.15 = bf16[3,184,512]{2,1,0:T(8,128)(2,1)S(1)} collective-permute-done((bf16[3,184,512]{2,1,0:T(8,128)(2,1)S(1)}, bf16[3,184,512]{2,1,0:T(8,128)(2,1)S(1)}, u32[]{:S(2)}, u32[]{:S(2)}) %collective-permute-start.15) | collective-permute-done | bytes 565280 | tf_op jit(solution)/shard_map/ppermute | solution.py:21
  78.4 17.7 %collective-permute-done.16 = bf16[3,184,512]{2,1,0:T(8,128)(2,1)S(1)} collective-permute-done((bf16[3,184,512]{2,1,0:T(8,128)(2,1)S(1)}, bf16[3,184,512]{2,1,0:T(8,128)(2,1)S(1)}, u32[]{:S(2)}, u32[]{:S(2)}) %collective-permute-start.16) | collective-permute-done | bytes 565280 | tf_op jit(solution)/shard_map/ppermute | solution.py:21
  99.0 11.7 %copy.109 = f32[2,1,512,1472]{2,0,3,1:T(2,128)S(1)} copy(bf16[2,1,512,1472]{2,3,1,0:T(8,128)(2,1)S(1)} %copy-done.10) | data formatting | bytes 9043968 | tf_op jit(solution)/shard_map/convert_element_type | solution.py:509
  115.0 10.5 %collective-permute-start.10 = (bf16[3,184,384]{2,1,0:T(8,128)(2,1)S(1)}, bf16[3,184,384]{2,1,0:T(8,128)(2,1)S(1)}, u32[]{:S(2)}, u32[]{:S(2)}) collective-permute-start(bf16[3,184,384]{2,1,0:T(8,128)(2,1)S(1)} %slice.165), channel_id=1, source_target_pairs={{0,8},{2,10},{4,12},{6,14},{8,0},{10,2},{12,4},{14,6},{16,24},{18,... | collective-permute-start | bytes 1271816 | tf_op jit(solution)/shard_map/ppermute | solution.py:21
  128.9 16.0 %collective-permute-done.10 = bf16[3,184,384]{2,1,0:T(8,128)(2,1)S(1)} collective-permute-done((bf16[3,184,384]{2,1,0:T(8,128)(2,1)S(1)}, bf16[3,184,384]{2,1,0:T(8,128)(2,1)S(1)}, u32[]{:S(2)}, u32[]{:S(2)}) %collective-permute-start.10) | collective-permute-done | bytes 423968 | tf_op jit(solution)/shard_map/ppermute | solution.py:21
  148.4 10.0 %collective-permute-done.12 = bf16[3,184,384]{2,1,0:T(8,128)(2,1)S(1)} collective-permute-done((bf16[3,184,384]{2,1,0:T(8,128)(2,1)S(1)}, bf16[3,184,384]{2,1,0:T(8,128)(2,1)S(1)}, u32[]{:S(2)}, u32[]{:S(2)}) %collective-permute-start.12) | collective-permute-done | bytes 423968 | tf_op jit(solution)/shard_map/ppermute | solution.py:21
  190.2 22.2 %bias_table.1.refs_6_ = f32[6,7,256,256]{3,2,1,0:T(8,128)} custom-call(f32[6,7,1,512]{3,2,1,0:T(1,128)} %broadcast_in_dim.157.window_ref), custom_call_target="tpu_custom_call" | custom-call | tf_op jit(solution)/shard_map/bias_table/pallas_call | solution.py:60
  236.7 18.7 %attend.1 = (bf16[2,512,384]{2,1,0:T(8,128)(2,1)}, f32[2,3,8,512]{3,2,1,0:T(8,128)}) custom-call(s32[17]{0:T(128)} %pad_add_fusion.2.info_ref, bf16[2,512,1152]{2,1,0:T(8,128)(2,1)} %bitcast.284, bf16[2,512,1152]{2,1,0:T(8,128)(2,1)} %bitcast.285, bf16[2,512,1152]{2,1,0:T(8,128)(2,1)} %bitcast.286, ...), custom_call_target="tpu_custom_call" | custom-call | tf_op jit(solution)/shard_map/attend/pallas_call | solution.py:264
  262.1 32.3 %collective-permute-done.19 = bf16[3,4,184,1024]{3,2,1,0:T(8,128)(2,1)} collective-permute-done((bf16[3,4,184,1024]{3,2,1,0:T(8,128)(2,1)}, bf16[3,4,184,1024]{3,2,1,0:T(8,128)(2,1)}, u32[]{:S(2)}, u32[]{:S(2)}) %collective-permute-start.19) | collective-permute-done | bytes 4522016 | tf_op jit(solution)/shard_map/ppermute | solution.py:21
  299.4 13.0 %fusion.82 = f32[2048,1024]{1,0:T(8,128)} fusion(bf16[2048,1472]{0,1:T(8,128)(2,1)} %constant_dynamic-update-slice_fusion.3, bf16[1472,1024]{1,0:T(8,128)(2,1)S(1)} %bitcast.321), kind=kOutput, calls=%fused_computation.228 | convolution fusion | flops 6174015488 | bytes 17432576 | tf_op jit(solution)/shard_map/td,df->tf/dot_general | solution.py:426
  312.5 9.8 fusion.71
  322.2 20.8 %fusion.7 = (bf16[2048,1024]{1,0:T(8,128)(2,1)}, bf16[2048,1024]{1,0:T(8,128)(2,1)}, bf16[2048,1024]{1,0:T(8,128)(2,1)}) fusion(f32[2048,1024]{1,0:T(8,128)} %fusion.82, f32[2048,1024]{1,0:T(8,128)} %fusion.71, bf16[1472,1024]{1,0:T(8,128)(2,1)} %bitcast.317, bf16[1024,1472]{0,1:T(8,128)(2,1)} %copy-done.45, bf16[1024,1472]{0,1:T(8,128)(2,1)S(1)} %multiply_convert_fusion.4), kind=kOutput, calls=%fused_computation.14 | convolution fusion | flops 6238502912 | bytes 38404096 | tf_op jit(solution)/shard_map/td,df->tf/dot_general | solution.py:426
  343.1 12.1 %fusion.81 = f32[2048,1472]{0,1:T(8,128)} fusion(bf16[2048,1024]{1,0:T(8,128)(2,1)} %get-tuple-element.93, bf16[1472,1024]{1,0:T(8,128)(2,1)} %bitcast.322), kind=kOutput, calls=%fused_computation.227 | convolution fusion | flops 6174015488 | bytes 19267584 | tf_op jit(solution)/shard_map/tf,df->td/dot_general | solution.py:430
  355.2 10.0 %convolution_convert_fusion.1 = bf16[1472,1024]{1,0:T(8,128)(2,1)} fusion(bf16[2048,1472]{0,1:T(8,128)(2,1)} %constant_dynamic-update-slice_fusion.3, bf16[2048,1024]{1,0:T(8,128)(2,1)S(1)} %copy-done.55), kind=kOutput, calls=%fused_computation.59 | convolution fusion | flops 6175522816 | bytes 13238272 | tf_op jit(solution)/shard_map/td,tf->df/dot_general | solution.py:434
  372.2 10.0 %fusion.65 = f32[2048,768]{1,0:T(8,128)} fusion(bf16[3,1472,384]{2,1,0:T(8,128)(2,1)} %bitcast.37, bf16[3,1472,384]{2,1,0:T(8,128)(2,1)} %collective-permute-done.14, bf16[1024,1472]{0,1:T(8,128)(2,1)S(1)} %copy-done.46, bf16[1024,1472]{0,1:T(8,128)(2,1)S(1)} %multiply_convert_fusion.4), kind=kOutput, calls=%fused_computation.215 | convolution fusion | flops 4647092224 | bytes 19103744 | tf_op jit(solution)/shard_map/td,df->tf/dot_general | solution.py:426
  382.2 15.1 %multiply_convert_fusion.2 = (bf16[2048,768]{1,0:T(8,128)(2,1)S(1)}, bf16[2048,768]{1,0:T(8,128)(2,1)}, bf16[2048,768]{1,0:T(8,128)(2,1)}) fusion(f32[2048,768]{1,0:T(8,128)} %fusion.65, f32[2048,768]{1,0:T(8,128)S(1)} %fusion.69, bf16[2048,1472]{0,1:T(8,128)(2,1)} %constant_dynamic-update-slice_fusion.3, ...), kind=kOutput, calls=%fused_computation.32 | convolution fusion | flops 4674355200 | bytes 34832384 | tf_op jit(solution)/shard_map/td,df->tf/dot_general | solution.py:426
  409.5 9.9 %convolution_convert_fusion.7 = bf16[1472,768]{1,0:T(8,128)(2,1)} fusion(bf16[2048,768]{1,0:T(8,128)(2,1)} %get-tuple-element.95, bf16[1024,1472]{0,1:T(8,128)(2,1)} %copy-done.45, bf16[1024,1472]{0,1:T(8,128)(2,1)} %copy-done.17), kind=kOutput, calls=%fused_computation.69 | convolution fusion | flops 4643700736 | bytes 11436032 | tf_op jit(solution)/shard_map/td,tf->df/dot_general | solution.py:434
  468.2 12.0 %fusion.83 = f32[2048,1472]{0,1:T(8,128)} fusion(bf16[2048,1024]{1,0:T(8,128)(2,1)} %get-tuple-element.92, bf16[1472,1024]{1,0:T(8,128)(2,1)} %bitcast.320), kind=kOutput, calls=%fused_computation.229 | convolution fusion | flops 6174015488 | bytes 19267584 | tf_op jit(solution)/shard_map/tf,df->td/dot_general | solution.py:430
  499.1 18.5 %add_convert_fusion = bf16[2048,1472]{0,1:T(8,128)(2,1)} fusion(f32[2048,1472]{0,1:T(8,128)} %fusion.83, f32[2048,1472]{0,1:T(8,128)} %fusion.63, f32[2048,1472]{0,1:T(8,128)} %fusion.67, bf16[2048,1024]{1,0:T(8,128)(2,1)} %get-tuple-element.91, bf16[1472,1024]{1,0:T(8,128)(2,1)} %bitcast.318), kind=kOutput, calls=%fused_computation.2 | convolution fusion | flops 6186074112 | bytes 49414144 | tf_op jit(solution)/shard_map/tf,df->td/dot_general | solution.py:430
  521.6 10.1 %add_convert_fusion.1 = bf16[2048,1472]{0,1:T(8,128)(2,1)} fusion(f32[2048,1472]{0,1:T(8,128)} %fusion.81, bf16[2048,768]{1,0:T(8,128)(2,1)S(1)} %copy-done.54, bf16[3,1472,384]{2,1,0:T(8,128)(2,1)} %collective-permute-done.14, bf16[3,1472,384]{2,1,0:T(8,128)(2,1)} %bitcast.37), kind=kOutput, calls=%fused_computation.3 | convolution fusion | flops 4641062912 | bytes 28016640 | tf_op jit(solution)/shard_map/tf,df->td/dot_general | solution.py:430
  534.6 11.2 %convolution_convert_fusion.2 = bf16[1472,1024]{1,0:T(8,128)(2,1)} fusion(bf16[2048,1024]{1,0:T(8,128)(2,1)} %get-tuple-element.92, bf16[1024,1472]{0,1:T(8,128)(2,1)} %copy-done.45, bf16[1024,1472]{0,1:T(8,128)(2,1)S(1)} %copy-done.18), kind=kOutput, calls=%fused_computation.60 | convolution fusion | flops 6187581440 | bytes 13238272 | tf_op jit(solution)/shard_map/td,tf->df/dot_general | solution.py:434
  561.3 34.8 %attend_grads.1 = (bf16[2,512,384]{2,1,0:T(8,128)(2,1)}, f32[6,7,1,512]{3,2,1,0:T(1,128)}, bf16[2,2,512,384]{3,2,1,0:T(8,128)(2,1)}, bf16[2,2,512,384]{3,2,1,0:T(8,128)(2,1)}) custom-call(s32[17]{0:T(128)} %pad_add_fusion.2.info_ref, bf16[2,512,1152]{2,1,0:T(8,128)(2,1)} %bitcast.287, bf16[2,512,1152]{2,1,0:T(8,128)(2,1)} %bitcast.288, ...), custom_call_target="tpu_custom_call" | custom-call | tf_op jit(solution)/shard_map/attend_grads/pallas_call | solution.py:297
  647.6 10.1 %reshape.238 = bf16[1472,2,2,384]{3,2,1,0:T(2,128)(2,1)} reshape(bf16[1472,1536]{1,0:T(8,128)(2,1)} %pad_maximum_fusion.2) | data formatting | bytes 9043968 | tf_op jit(solution)/shard_map/reshape | solution.py:364
  657.7 11.7 %constant_dynamic-slice_fusion.2 = (bf16[1472,2,1,384]{3,2,1,0:T(2,128)(2,1)}, bf16[1472,2,1,384]{3,2,1,0:T(2,128)(2,1)S(1)}) fusion(bf16[1472,2,2,384]{3,2,1,0:T(2,128)(2,1)} %reshape.238, s32[]{:T(128)S(6)} %select_n.129, s32[]{:T(128)S(6)} %select_n.131), kind=kLoop, calls=%fused_computation.176 | loop fusion | bytes 9043976 | tf_op jit(solution)/shard_map/jit(dynamic_index_in_dim)/dynamic_slice | solution.py:41
  685.7 49.8 %collective-permute-done.37 = bf16[3,4,184,2,512]{4,2,1,0,3:T(8,128)(2,1)} collective-permute-done((bf16[3,4,184,2,512]{4,2,1,0,3:T(8,128)(2,1)}, bf16[3,4,184,2,512]{4,2,1,0,3:T(8,128)(2,1)}, u32[]{:S(2)}, u32[]{:S(2)}) %collective-permute-start.37) | collective-permute-done | bytes 4522016 | tf_op jit(solution)/shard_map/ppermute | solution.py:21
  746.5 10.7 %multiply_reduce_fusion.1 = (f32[1472]{0:T(1024)}, f32[1024]{0:T(1024)S(1)}, f32[1024,1472]{0,1:T(8,128)}) fusion(f32[1024,1472]{0,1:T(8,128)S(1)} %bitcast.300, f32[1024]{0:T(1024)S(1)} %bitcast.344, f32[1472]{0:T(1024)S(1)} %copy-done.37, bf16[1472,1536]{0,1:T(8,128)(2,1)} %bitcast.314, bf16[1024,384]{1,0:T(8,128)(2,1)} %bitcast.330, ...), kind=kOutput, calls=%fused_computation.36 | convolution fusion | flops 3489003008 | bytes 17976832 | tf_op jit(solution)/shard_map/tf,df->td/dot_general | solution.py:430
  803.7 22.2 %collective-permute-start.40 = (bf16[3,184,512]{2,1,0:T(8,128)(2,1)S(1)}, bf16[3,184,512]{2,1,0:T(8,128)(2,1)S(1)}, u32[]{:S(2)}, u32[]{:S(2)}) collective-permute-start(bf16[3,184,512]{2,1,0:T(8,128)(2,1)S(1)} %get-tuple-element.106), channel_id=1, source_target_pairs={{0,16},{2,18},{4,20},{6,22},{8,24},{10,26},{12,28},{14,30},{16,0},... | collective-permute-start | bytes 1695752 | tf_op jit(solution)/shard_map/ppermute | solution.py:21
  827.4 31.5 %collective-permute-done.40 = bf16[3,184,512]{2,1,0:T(8,128)(2,1)S(1)} collective-permute-done((bf16[3,184,512]{2,1,0:T(8,128)(2,1)S(1)}, bf16[3,184,512]{2,1,0:T(8,128)(2,1)S(1)}, u32[]{:S(2)}, u32[]{:S(2)}) %collective-permute-start.40) | collective-permute-done | bytes 565280 | tf_op jit(solution)/shard_map/ppermute | solution.py:21
  860.3 12.1 %collective-permute-start.27 = (bf16[184,384]{1,0:T(8,128)(2,1)}, bf16[184,384]{1,0:T(8,128)(2,1)S(1)}, u32[]{:S(2)}, u32[]{:S(2)}) collective-permute-start(bf16[184,384]{1,0:T(8,128)(2,1)} %get-tuple-element.123), channel_id=1, source_target_pairs={{0,8},{2,10},{4,12},{6,14},{8,0},{10,2},{12,4},{14,6},{16,24},{18,... | collective-permute-start | bytes 423944 | tf_op jit(solution)/shard_map/ppermute | solution.py:21
  906.2 41.1 %all-reduce.2 = (f32[32,6]{0,1:T(8,128)}, f32[1472]{0:T(1024)}, f32[1472]{0:T(1024)}) all-reduce(f32[32,6]{0,1:T(8,128)S(1)} %copy-done.42, f32[1472]{0:T(1024)S(1)} %copy-done.41, f32[1472]{0:T(1024)S(1)} %get-tuple-element.72), channel_id=1, replica_groups=mesh['dp'=16,'mp'=2] {'dp','mp'}, use_global_device_ids=true, to_apply=%region_4.5 | all-reduce | flops 3136 | bytes 25088 | tf_op jit(solution)/shard_map/psum | solution.py:602
  (405 shorter events, 434.1 us)
Async XLA Ops:
  2.2 27.8 %collective-permute-start = (bf16[92,384]{1,0:T(8,128)(2,1)S(1)}, bf16[92,384]{1,0:T(8,128)(2,1)S(1)}, u32[]{:S(2)}, u32[]{:S(2)}) collective-permute-start(bf16[92,384]{1,0:T(8,128)(2,1)S(1)} %bitcast.340), channel_id=1, source_target_pairs={{0,2},{2,0},{4,6},{6,4},{8,10},{10,8},{12,14},{14,12},{16,18},{18,... | collective-permute-start | bytes 211976 | tf_op jit(solution)/shard_map/ppermute | solution.py:21
  9.6 41.4 %collective-permute-start.9 = (bf16[3,92,896]{2,1,0:T(8,128)(2,1)}, bf16[3,92,896]{2,1,0:T(8,128)(2,1)}, u32[]{:S(2)}, u32[]{:S(2)}) collective-permute-start(bf16[3,92,896]{2,1,0:T(8,128)(2,1)} %bitcast.277), channel_id=1, source_target_pairs={{0,2},{2,0},{4,6},{6,4},{8,10},{10,8},{12,14},{14,12},{16,18},{18,... | collective-permute-start | bytes 1483784 | tf_op jit(solution)/shard_map/ppermute | solution.py:21
  24.2 201.3 %collective-permute-start.21 = (bf16[1024,1472]{0,1:T(8,128)(2,1)}, bf16[1024,1472]{0,1:T(8,128)(2,1)}, u32[]{:S(2)}, u32[]{:S(2)}) collective-permute-start(bf16[1024,1472]{0,1:T(8,128)(2,1)} %bitcast.143), channel_id=1, source_target_pairs={{0,2},{2,0},{4,6},{6,4},{8,10},{10,8},{12,14},{14,12},{16,18},{18,... | collective-permute-start | bytes 9043976 | tf_op jit(solution)/shard_map/ppermute | solution.py:21
  52.4 26.0 %collective-permute-start.15 = (bf16[3,184,512]{2,1,0:T(8,128)(2,1)S(1)}, bf16[3,184,512]{2,1,0:T(8,128)(2,1)S(1)}, u32[]{:S(2)}, u32[]{:S(2)}) collective-permute-start(bf16[3,184,512]{2,1,0:T(8,128)(2,1)S(1)} %slice.170), channel_id=1, source_target_pairs={{0,8},{2,10},{4,12},{6,14},{8,0},{10,2},{12,4},{14,6},{16,24},{18,... | collective-permute-start | bytes 1695752 | tf_op jit(solution)/shard_map/ppermute | solution.py:21
  55.3 40.9 %collective-permute-start.16 = (bf16[3,184,512]{2,1,0:T(8,128)(2,1)S(1)}, bf16[3,184,512]{2,1,0:T(8,128)(2,1)S(1)}, u32[]{:S(2)}, u32[]{:S(2)}) collective-permute-start(bf16[3,184,512]{2,1,0:T(8,128)(2,1)S(1)} %slice.170), channel_id=1, source_target_pairs={{0,16},{2,18},{4,20},{6,22},{8,24},{10,26},{12,28},{14,30},{16,0},... | collective-permute-start | bytes 1695752 | tf_op jit(solution)/shard_map/ppermute | solution.py:21
  56.4 39.8 %collective-permute-start.17 = (bf16[3,184,512]{2,1,0:T(8,128)(2,1)S(1)}, bf16[3,184,512]{2,1,0:T(8,128)(2,1)S(1)}, u32[]{:S(2)}, u32[]{:S(2)}) collective-permute-start(bf16[3,184,512]{2,1,0:T(8,128)(2,1)S(1)} %slice.170), channel_id=1, source_target_pairs={{0,24},{2,26},{4,28},{6,30},{8,16},{10,18},{12,20},{14,22},{16,8},... | collective-permute-start | bytes 1695752 | tf_op jit(solution)/shard_map/ppermute | solution.py:21
  61.6 36.2 %collective-permute-start.5 = (bf16[1472,384]{1,0:T(8,128)(2,1)}, bf16[1472,384]{1,0:T(8,128)(2,1)S(1)}, u32[]{:S(2)}, u32[]{:S(2)}) collective-permute-start(bf16[1472,384]{1,0:T(8,128)(2,1)} %bitcast.10), channel_id=1, source_target_pairs={{0,1},{1,0},{2,3},{3,2},{4,5},{5,4},{6,7},{7,6},{8,9},{9,8},{10,11... | collective-permute-start | bytes 3391496 | tf_op jit(solution)/shard_map/ppermute | solution.py:26
  96.3 67.7 %collective-permute-start.18 = (bf16[3,4,184,512]{3,2,1,0:T(8,128)(2,1)S(1)}, bf16[3,4,184,512]{3,2,1,0:T(8,128)(2,1)}, u32[]{:S(2)}, u32[]{:S(2)}) collective-permute-start(bf16[3,4,184,512]{3,2,1,0:T(8,128)(2,1)S(1)} %bitcast_dynamic-update-slice_fusion.5), channel_id=1, source_target_pairs={{0,1},{1,0},{2,3},{3,2},{4,5},{5,4},{6,7},{7,6},{8,9},{9,8},{10,11... | collective-permute-start | bytes 6782984 | tf_op jit(solution)/shard_map/ppermute | solution.py:26
  99.0 71.6 %collective-permute-start.6 = (bf16[2,1472,384]{2,1,0:T(8,128)(2,1)}, bf16[2,1472,384]{2,1,0:T(8,128)(2,1)}, u32[]{:S(2)}, u32[]{:S(2)}) collective-permute-start(bf16[2,1472,384]{2,1,0:T(8,128)(2,1)} %bitcast_dynamic-update-slice_fusion.4), channel_id=1, source_target_pairs={{0,2},{2,0},{4,6},{6,4},{8,10},{10,8},{12,14},{14,12},{16,18},{18,... | collective-permute-start | bytes 6782984 | tf_op jit(solution)/shard_map/ppermute | solution.py:21
  115.0 29.9 %collective-permute-start.10 = (bf16[3,184,384]{2,1,0:T(8,128)(2,1)S(1)}, bf16[3,184,384]{2,1,0:T(8,128)(2,1)S(1)}, u32[]{:S(2)}, u32[]{:S(2)}) collective-permute-start(bf16[3,184,384]{2,1,0:T(8,128)(2,1)S(1)} %slice.165), channel_id=1, source_target_pairs={{0,8},{2,10},{4,12},{6,14},{8,0},{10,2},{12,4},{14,6},{16,24},{18,... | collective-permute-start | bytes 1271816 | tf_op jit(solution)/shard_map/ppermute | solution.py:21
  159.2 61.9 %collective-permute-start.13 = (bf16[3,4,184,384]{3,2,1,0:T(8,128)(2,1)}, bf16[3,4,184,384]{3,2,1,0:T(8,128)(2,1)}, u32[]{:S(2)}, u32[]{:S(2)}) collective-permute-start(bf16[3,4,184,384]{3,2,1,0:T(8,128)(2,1)} %bitcast_dynamic-update-slice_fusion.13), channel_id=1, source_target_pairs={{0,4},{2,6},{4,0},{6,2},{8,12},{10,14},{12,8},{14,10},{16,20},{18,... | collective-permute-start | bytes 5087240 | tf_op jit(solution)/shard_map/ppermute | solution.py:21
  168.3 126.1 %collective-permute-start.19 = (bf16[3,4,184,1024]{3,2,1,0:T(8,128)(2,1)}, bf16[3,4,184,1024]{3,2,1,0:T(8,128)(2,1)}, u32[]{:S(2)}, u32[]{:S(2)}) collective-permute-start(bf16[3,4,184,1024]{3,2,1,0:T(8,128)(2,1)} %pad_maximum_fusion.1), channel_id=1, source_target_pairs={{0,4},{2,6},{4,0},{6,2},{8,12},{10,14},{12,8},{14,10},{16,20},{18,... | collective-permute-start | bytes 13565960 | tf_op jit(solution)/shard_map/ppermute | solution.py:21
  187.1 49.7 %collective-permute-start.7 = (bf16[2,512,768]{2,1,0:T(8,128)(2,1)}, bf16[2,512,768]{2,1,0:T(8,128)(2,1)}, u32[]{:S(2)}, u32[]{:S(2)}) collective-permute-start(bf16[2,512,768]{2,1,0:T(8,128)(2,1)} %slice.161), channel_id=1, source_target_pairs={{0,1},{1,0},{2,3},{3,2},{4,5},{5,4},{6,7},{7,6},{8,9},{9,8},{10,11... | collective-permute-start | bytes 4718600 | tf_op jit(solution)/shard_map/ppermute | solution.py:26
  223.9 141.2 %collective-permute-start.14 = (bf16[3,1472,384]{2,1,0:T(8,128)(2,1)}, bf16[3,1472,384]{2,1,0:T(8,128)(2,1)}, u32[]{:S(2)}, u32[]{:S(2)}) collective-permute-start(bf16[3,1472,384]{2,1,0:T(8,128)(2,1)} %bitcast.37), channel_id=1, source_target_pairs={{0,1},{1,0},{2,3},{3,2},{4,5},{5,4},{6,7},{7,6},{8,9},{9,8},{10,11... | collective-permute-start | bytes 10174472 | tf_op jit(solution)/shard_map/ppermute | solution.py:26
  262.1 50.4 %collective-permute-start.8 = (bf16[1024,1472]{0,1:T(8,128)(2,1)S(1)}, bf16[1024,1472]{0,1:T(8,128)(2,1)S(1)}, u32[]{:S(2)}, u32[]{:S(2)}) collective-permute-start(bf16[1024,1472]{0,1:T(8,128)(2,1)S(1)} %multiply_convert_fusion.4), channel_id=1, source_target_pairs={{0,2},{2,0},{4,6},{6,4},{8,10},{10,8},{12,14},{14,12},{16,18},{18,... | collective-permute-start | bytes 9043976 | tf_op jit(solution)/shard_map/ppermute | solution.py:21
  451.5 228.9 %collective-permute-start.32 = (bf16[3,4,2,184,384]{4,3,2,1,0:T(8,128)(2,1)}, bf16[3,4,2,184,384]{4,3,2,1,0:T(8,128)(2,1)}, u32[]{:S(2)}, u32[]{:S(2)}) collective-permute-start(bf16[3,4,2,184,384]{4,3,2,1,0:T(8,128)(2,1)} %slice_bitcast_fusion), channel_id=1, source_target_pairs={{0,1},{1,0},{2,3},{3,2},{4,5},{5,4},{6,7},{7,6},{8,9},{9,8},{10,11... | collective-permute-start | bytes 10174472 | tf_op jit(solution)/shard_map/ppermute | solution.py:26
  521.6 24.2 %collective-permute-start.22 = (bf16[1024,1472]{0,1:T(8,128)(2,1)}, bf16[1024,1472]{0,1:T(8,128)(2,1)S(1)}, u32[]{:S(2)}, u32[]{:S(2)}) collective-permute-start(bf16[1024,1472]{0,1:T(8,128)(2,1)} %slice.177), channel_id=1, source_target_pairs={{0,2},{2,0},{4,6},{6,4},{8,10},{10,8},{12,14},{14,12},{16,18},{18,... | collective-permute-start | bytes 9043976 | tf_op jit(solution)/shard_map/ppermute | solution.py:21
  596.0 42.4 %collective-permute-start.23 = (bf16[2,2,512,384]{3,2,1,0:T(8,128)(2,1)}, bf16[2,2,512,384]{3,2,1,0:T(8,128)(2,1)}, u32[]{:S(2)}, u32[]{:S(2)}) collective-permute-start(bf16[2,2,512,384]{3,2,1,0:T(8,128)(2,1)} %get-tuple-element.22), channel_id=1, source_target_pairs={{0,1},{1,0},{2,3},{3,2},{4,5},{5,4},{6,7},{7,6},{8,9},{9,8},{10,11... | collective-permute-start | bytes 4718600 | tf_op jit(solution)/shard_map/ppermute | solution.py:26
  628.9 106.5 %collective-permute-start.37 = (bf16[3,4,184,2,512]{4,2,1,0,3:T(8,128)(2,1)}, bf16[3,4,184,2,512]{4,2,1,0,3:T(8,128)(2,1)}, u32[]{:S(2)}, u32[]{:S(2)}) collective-permute-start(bf16[3,4,184,2,512]{4,2,1,0,3:T(8,128)(2,1)} %dynamic-slice_bitcast_fusion), channel_id=1, source_target_pairs={{0,4},{2,6},{4,0},{6,2},{8,12},{10,14},{12,8},{14,10},{16,20},{18,... | collective-permute-start | bytes 13565960 | tf_op jit(solution)/shard_map/ppermute | solution.py:21
  671.1 71.8 %collective-permute-start.24 = (bf16[1472,2,384]{2,0,1:T(8,128)(2,1)}, bf16[1472,2,384]{2,0,1:T(8,128)(2,1)}, u32[]{:S(2)}, u32[]{:S(2)}) collective-permute-start(bf16[1472,2,384]{2,0,1:T(8,128)(2,1)} %bitcast.276), channel_id=1, source_target_pairs={{0,2},{2,0},{4,6},{6,4},{8,10},{10,8},{12,14},{14,12},{16,18},{18,... | collective-permute-start | bytes 6782984 | tf_op jit(solution)/shard_map/ppermute | solution.py:21
  685.7 79.1 %collective-permute-start.33 = (bf16[3,4,184,384]{3,2,1,0:T(8,128)(2,1)}, bf16[3,4,184,384]{3,2,1,0:T(8,128)(2,1)S(1)}, u32[]{:S(2)}, u32[]{:S(2)}) collective-permute-start(bf16[3,4,184,384]{3,2,1,0:T(8,128)(2,1)} %dynamic-slice_bitcast_fusion.1), channel_id=1, source_target_pairs={{0,4},{2,6},{4,0},{6,2},{8,12},{10,14},{12,8},{14,10},{16,20},{18,... | collective-permute-start | bytes 5087240 | tf_op jit(solution)/shard_map/ppermute | solution.py:21
  742.1 49.6 %collective-permute-start.38 = (bf16[3,4,184,512]{3,2,1,0:T(8,128)(2,1)}, bf16[3,4,184,512]{3,2,1,0:T(8,128)(2,1)}, u32[]{:S(2)}, u32[]{:S(2)}) collective-permute-start(bf16[3,4,184,512]{3,2,1,0:T(8,128)(2,1)} %slice_bitcast_fusion.2), channel_id=1, source_target_pairs={{0,1},{1,0},{2,3},{3,2},{4,5},{5,4},{6,7},{7,6},{8,9},{9,8},{10,11... | collective-permute-start | bytes 6782984 | tf_op jit(solution)/shard_map/ppermute | solution.py:26
  745.2 58.5 %collective-permute-start.25 = (bf16[1472,384]{1,0:T(8,128)(2,1)S(1)}, bf16[1472,384]{1,0:T(8,128)(2,1)S(1)}, u32[]{:S(2)}, u32[]{:S(2)}) collective-permute-start(bf16[1472,384]{1,0:T(8,128)(2,1)S(1)} %dynamic-slice_bitcast_fusion.2), channel_id=1, source_target_pairs={{0,1},{1,0},{2,3},{3,2},{4,5},{5,4},{6,7},{7,6},{8,9},{9,8},{10,11... | collective-permute-start | bytes 3391496 | tf_op jit(solution)/shard_map/ppermute | solution.py:26
  765.3 61.0 %collective-permute-start.34 = (bf16[3,184,384]{2,1,0:T(8,128)(2,1)S(1)}, bf16[3,184,384]{2,1,0:T(8,128)(2,1)S(1)}, u32[]{:S(2)}, u32[]{:S(2)}) collective-permute-start(bf16[3,184,384]{2,1,0:T(8,128)(2,1)S(1)} %get-tuple-element.110), channel_id=1, source_target_pairs={{0,8},{2,10},{4,12},{6,14},{8,0},{10,2},{12,4},{14,6},{16,24},{18,... | collective-permute-start | bytes 1271816 | tf_op jit(solution)/shard_map/ppermute | solution.py:21
  774.2 52.2 %collective-permute-start.35 = (bf16[3,184,384]{2,1,0:T(8,128)(2,1)S(1)}, bf16[3,184,384]{2,1,0:T(8,128)(2,1)S(1)}, u32[]{:S(2)}, u32[]{:S(2)}) collective-permute-start(bf16[3,184,384]{2,1,0:T(8,128)(2,1)S(1)} %get-tuple-element.112), channel_id=1, source_target_pairs={{0,16},{2,18},{4,20},{6,22},{8,24},{10,26},{12,28},{14,30},{16,0},... | collective-permute-start | bytes 1271816 | tf_op jit(solution)/shard_map/ppermute | solution.py:21
  782.0 45.2 %collective-permute-start.36 = (bf16[3,184,384]{2,1,0:T(8,128)(2,1)S(1)}, bf16[3,184,384]{2,1,0:T(8,128)(2,1)S(1)}, u32[]{:S(2)}, u32[]{:S(2)}) collective-permute-start(bf16[3,184,384]{2,1,0:T(8,128)(2,1)S(1)} %get-tuple-element.111), channel_id=1, source_target_pairs={{0,24},{2,26},{4,28},{6,30},{8,16},{10,18},{12,20},{14,22},{16,8},... | collective-permute-start | bytes 1271816 | tf_op jit(solution)/shard_map/ppermute | solution.py:21
  794.0 33.3 %collective-permute-start.39 = (bf16[3,184,512]{2,1,0:T(8,128)(2,1)S(1)}, bf16[3,184,512]{2,1,0:T(8,128)(2,1)S(1)}, u32[]{:S(2)}, u32[]{:S(2)}) collective-permute-start(bf16[3,184,512]{2,1,0:T(8,128)(2,1)S(1)} %get-tuple-element.104), channel_id=1, source_target_pairs={{0,8},{2,10},{4,12},{6,14},{8,0},{10,2},{12,4},{14,6},{16,24},{18,... | collective-permute-start | bytes 1695752 | tf_op jit(solution)/shard_map/ppermute | solution.py:21
  803.7 55.1 %collective-permute-start.40 = (bf16[3,184,512]{2,1,0:T(8,128)(2,1)S(1)}, bf16[3,184,512]{2,1,0:T(8,128)(2,1)S(1)}, u32[]{:S(2)}, u32[]{:S(2)}) collective-permute-start(bf16[3,184,512]{2,1,0:T(8,128)(2,1)S(1)} %get-tuple-element.106), channel_id=1, source_target_pairs={{0,16},{2,18},{4,20},{6,22},{8,24},{10,26},{12,28},{14,30},{16,0},... | collective-permute-start | bytes 1695752 | tf_op jit(solution)/shard_map/ppermute | solution.py:21
  826.3 32.6 %collective-permute-start.41 = (bf16[3,184,512]{2,1,0:T(8,128)(2,1)S(1)}, bf16[3,184,512]{2,1,0:T(8,128)(2,1)S(1)}, u32[]{:S(2)}, u32[]{:S(2)}) collective-permute-start(bf16[3,184,512]{2,1,0:T(8,128)(2,1)S(1)} %get-tuple-element.105), channel_id=1, source_target_pairs={{0,24},{2,26},{4,28},{6,30},{8,16},{10,18},{12,20},{14,22},{16,8},... | collective-permute-start | bytes 1695752 | tf_op jit(solution)/shard_map/ppermute | solution.py:21
  826.5 32.9 %collective-permute-start.26 = (bf16[4,184,384]{2,1,0:T(8,128)(2,1)S(1)}, bf16[4,184,384]{2,1,0:T(8,128)(2,1)S(1)}, u32[]{:S(2)}, u32[]{:S(2)}) collective-permute-start(bf16[4,184,384]{2,1,0:T(8,128)(2,1)S(1)} %dynamic-slice_bitcast_fusion.6), channel_id=1, source_target_pairs={{0,4},{2,6},{4,0},{6,2},{8,12},{10,14},{12,8},{14,10},{16,20},{18,... | collective-permute-start | bytes 1695752 | tf_op jit(solution)/shard_map/ppermute | solution.py:21
  875.9 82.0 %collective-permute-start.42 = (bf16[3,92,896]{2,1,0:T(8,128)(2,1)}, bf16[3,92,896]{2,1,0:T(8,128)(2,1)}, u32[]{:S(2)}, u32[]{:S(2)}) collective-permute-start(bf16[3,92,896]{2,1,0:T(8,128)(2,1)} %get-tuple-element.115), channel_id=1, source_target_pairs={{0,2},{2,0},{4,6},{6,4},{8,10},{10,8},{12,14},{14,12},{16,18},{18,... | collective-permute-start | bytes 1483784 | tf_op jit(solution)/shard_map/ppermute | solution.py:21
  887.6 82.2 %collective-permute-start.30 = (bf16[184,384]{1,0:T(8,128)(2,1)}, bf16[184,384]{1,0:T(8,128)(2,1)}, u32[]{:S(2)}, u32[]{:S(2)}) collective-permute-start(bf16[184,384]{1,0:T(8,128)(2,1)} %get-tuple-element.84), channel_id=1, source_target_pairs={{0,1},{1,0},{2,3},{3,2},{4,5},{5,4},{6,7},{7,6},{8,9},{9,8},{10,11... | collective-permute-start | bytes 423944 | tf_op jit(solution)/shard_map/ppermute | solution.py:26
  (81 other events, 1131.0 us)

commit v2 on v1

v2 whole, which is shorter than its diff:
```python
import functools

import jax
import jax.numpy as jnp
from jax import lax
from jax.experimental import pallas as pl
from jax.experimental.pallas import tpu as pltpu
from jax.sharding import PartitionSpec as P

EPSILON = 1e-06
TOP_PRECISION = lax.Precision.HIGHEST
GELU_SCALE = 0.7978845608028654
GELU_CUBE = 0.044715
BF16 = jnp.bfloat16
F32 = jnp.float32
NEGATIVE = -1e30
VMEM_BYTES = 60 * 1024 * 1024
LANES = 128


def swap_dp(array, mask):
    count = lax.axis_size("dp")
    return lax.ppermute(array, "dp", [(i, i ^ mask) for i in range(count)])


def swap_mp(array, mask):
    count = lax.axis_size("mp")
    return lax.ppermute(array, "mp", [(i, i ^ mask) for i in range(count)])


def pick(array, index, axis):
    return lax.dynamic_index_in_dim(array, index, axis, keepdims=False)


def add_low(*terms):
    total = terms[0].astype(F32)
    for term in terms[1:]:
        total = total + term.astype(F32)
    return total.astype(BF16)


def either(flag, first, second):
    return jnp.where(flag == 0, first, second)


def gather_quads(piece):
    depth, mp = lax.axis_size("dp") // 4, lax.axis_size("mp")
    kinds, rows, columns = piece.shape
    parts = [piece] + [swap_dp(piece, 4 * k) for k in range(1, depth)]
    own = jnp.stack(parts, axis=1).reshape(kinds, depth * rows, columns)
    half = depth * rows // 2
    over_y = swap_dp(own, 2)
    quads = [(own, over_y)]
    for k in range(1, mp):
        over_x = swap_mp(own, k)
        quads.append(
            (over_x, swap_mp(over_y[:, :half], k), swap_dp(over_x[:, half:], 2))
        )
    return quads


def scatter_quads(quads):
    depth = lax.axis_size("dp") // 4
    own, to_y = quads[0]
    kinds, wide, columns = own.shape
    half = wide // 2
    low = to_y[:, :half]
    high = to_y[:, half:]
    terms = [own]
    for k, (to_x, first, second) in enumerate(quads[1:], 1):
        low = add_low(low, swap_mp(first, k))
        to_x = jnp.concatenate(
            [to_x[:, :half], add_low(to_x[:, half:], swap_dp(second, 2))], axis=1
        )
        terms.append(swap_mp(to_x, k))
    terms.append(swap_dp(jnp.concatenate([low, high], axis=1), 2))
    total = add_low(*terms).reshape(kinds, depth, wide // depth, columns)
    return add_low(total[:, 0], *[swap_dp(total[:, k], 4 * k) for k in range(1, depth)])


def sum_all(values):
    mask = 1
    while mask < lax.axis_size("dp"):
        values = values + swap_dp(values, mask)
        mask *= 2
    mask = 1
    while mask < lax.axis_size("mp"):
        values = values + swap_mp(values, mask)
        mask *= 2
    return values


def call(kernel, name, grid, in_specs, out_specs, out_shape, operands, flops=0, scratch=(), scalars=0):
    moved = sum(a.size * a.dtype.itemsize for a in operands)
    moved += sum(s.size * s.dtype.itemsize for s in out_shape)
    return pl.pallas_call(
        kernel,
        grid_spec=pltpu.PrefetchScalarGridSpec(
            num_scalar_prefetch=scalars,
            grid=grid,
            in_specs=in_specs,
            out_specs=out_specs,
            scratch_shapes=list(scratch),
        ),
        out_shape=out_shape,
        compiler_params=pltpu.CompilerParams(vmem_limit_bytes=VMEM_BYTES),
        cost_estimate=pl.CostEstimate(flops=flops, bytes_accessed=moved, transcendentals=0),
        name=name,
    )(*operands)


def whole(shape):
    return pl.BlockSpec(shape, lambda *_: (0,) * len(shape), pipeline_mode=pl.Buffered(1))


def slab(*shape):
    return pl.BlockSpec((1,) + shape, lambda m, *_: (m,) + (0,) * len(shape))


def dot_nn(left, right):
    return lax.dot_general(left, right, (((1,), (0,)), ((), ())), preferred_element_type=F32)


def dot_tn(left, right):
    return lax.dot_general(left, right, (((0,), (0,)), ((), ())), preferred_element_type=F32)


def dot_nt(left, right):
    return lax.dot_general(left, right, (((1,), (1,)), ((), ())), preferred_element_type=F32)


def transposed(value):
    return jnp.transpose(value.astype(F32), (1, 0)).astype(BF16)


def block_of(place, position, depth):
    z, y = place // 2, place % 2
    return (z ^ (position % depth)) * 2 + (y ^ (position // depth))


def reorder_kernel(outward, info_ref, in_ref, out_ref):
    blocks = in_ref.shape[1]
    for p in range(blocks):
        chip = block_of(info_ref[0], p, blocks // 2)
        if outward:
            out_ref[0, chip] = in_ref[0, p]
        else:
            out_ref[0, p] = in_ref[0, chip]


def reorder(array, place, blocks, outward):
    groups, wide, length = array.shape
    split = array.reshape(groups, blocks, wide // blocks, length)
    spec = slab(blocks, wide // blocks, length)
    return call(
        functools.partial(reorder_kernel, outward),
        "reorder",
        (groups,),
        [spec],
        [spec],
        [jax.ShapeDtypeStruct(split.shape, array.dtype)],
        [place, split],
        scalars=1,
    )[0].reshape(groups, wide, length)


def bias_kernel(window_ref, table_ref):
    count, block = table_ref.shape[1], table_ref.shape[-1]
    for entry in range(count):
        wide = jnp.broadcast_to(window_ref[0, entry], (block, 2 * block))
        rolled = pltpu.roll(wide, block + 1, 1, stride=1, stride_axis=0)
        table_ref[0, entry] = rolled[:, :block]


def bias_table(windows, block):
    heads, count = windows.shape[:2]
    return call(
        bias_kernel,
        "bias_table",
        (heads,),
        [slab(count, 1, 2 * block)],
        [slab(count, block, block)],
        [jax.ShapeDtypeStruct((heads, count, block, block), F32)],
        [windows],
    )[0]


def project_kernel(x_ref, gain_ref, w_ref, normed_ref, q_ref, kv_ref):
    values = x_ref[0].astype(F32)
    factor = lax.rsqrt(jnp.mean(values * values, axis=0, keepdims=True) + EPSILON)
    normed = (values * factor * gain_ref[...]).astype(BF16)
    normed_ref[0] = normed
    inner = q_ref.shape[1]
    q_ref[0] = dot_tn(w_ref[0], normed).astype(BF16)
    kv_ref[0, :inner] = dot_tn(w_ref[1], normed).astype(BF16)
    kv_ref[0, inner:] = dot_tn(w_ref[2], normed).astype(BF16)


def project(x, gain, weights):
    groups, wide, length = x.shape
    inner = weights.shape[2]
    return call(
        project_kernel,
        "project",
        (groups,),
        [slab(wide, length), whole((wide, 1)), whole(weights.shape)],
        [slab(wide, length), slab(inner, length), slab(2 * inner, length)],
        [
            jax.ShapeDtypeStruct((groups, wide, length), BF16),
            jax.ShapeDtypeStruct((groups, inner, length), BF16),
            jax.ShapeDtypeStruct((groups, 2 * inner, length), BF16),
        ],
        [x, gain, weights],
        flops=6 * groups * wide * length * inner,
    )


def middle_kernel(x_ref, context_ref, w_ref, gain_ref, middle_ref, normed_ref):
    values = x_ref[0].astype(F32) + dot_nn(w_ref[3], context_ref[0])
    middle_ref[0] = values
    factor = lax.rsqrt(jnp.mean(values * values, axis=0, keepdims=True) + EPSILON)
    normed_ref[0] = (values * factor * gain_ref[...]).astype(BF16)


def middle_layer(x, context, weights, gain):
    groups, wide, length = x.shape
    inner = weights.shape[2]
    return call(
        middle_kernel,
        "middle",
        (groups,),
        [slab(wide, length), slab(inner, length), whole(weights.shape), whole((wide, 1))],
        [slab(wide, length), slab(wide, length)],
        [
            jax.ShapeDtypeStruct((groups, wide, length), F32),
            jax.ShapeDtypeStruct((groups, wide, length), BF16),
        ],
        [x, context, weights, gain],
        flops=2 * groups * wide * length * inner,
    )


def lifted_grads(values, gain, grad):
    factor = lax.rsqrt(jnp.mean(values * values, axis=0, keepdims=True) + EPSILON)
    scaled = values * factor
    lifted = grad * gain
    inner = jnp.mean(lifted * scaled, axis=0, keepdims=True)
    return factor * (lifted - scaled * inner), jnp.sum(grad * scaled, axis=1, keepdims=True)


def turn_kernel(
    middle_ref, cot_ref, ffn0_ref, ffn1_ref, back0_ref, back1_ref, gain_ref, w_ref,
    out_ref, grad_ref, low_ref, context_ref, gain_grad_ref,
):
    middle = middle_ref[0]
    out_ref[0] = (middle + ffn0_ref[0].astype(F32) + ffn1_ref[0].astype(F32)).astype(BF16)
    grad = back0_ref[0].astype(F32) + back1_ref[0].astype(F32)
    normed_grad, gain_grad = lifted_grads(middle, gain_ref[...], grad)
    gain_grad_ref[0] = gain_grad
    total = cot_ref[0].astype(F32) + normed_grad
    grad_ref[0] = total
    low = total.astype(BF16)
    low_ref[0] = low
    context_ref[0] = dot_tn(w_ref[3], low).astype(BF16)


def turn(middle, cot, ffn, back, gain, weights):
    groups, wide, length = middle.shape
    inner = weights.shape[2]
    big = slab(wide, length)
    return call(
        turn_kernel,
        "turn",
        (groups,),
        [big] * 6 + [whole((wide, 1)), whole(weights.shape)],
        [big, big, big, slab(inner, length), slab(wide, 1)],
        [
            jax.ShapeDtypeStruct((groups, wide, length), BF16),
            jax.ShapeDtypeStruct((groups, wide, length), F32),
            jax.ShapeDtypeStruct((groups, wide, length), BF16),
            jax.ShapeDtypeStruct((groups, inner, length), BF16),
            jax.ShapeDtypeStruct((groups, wide, 1), F32),
        ],
        [middle, cot, *ffn, *back, gain, weights],
        flops=2 * groups * wide * length * inner,
    )


def attention_weights_kernel(normed_ref, low_ref, context_ref, dq_ref, dkv_ref, out_ref, sum_scr):
    step = pl.program_id(0)
    inner = dq_ref.shape[1]
    terms = (
        (normed_ref, dq_ref[0]),
        (normed_ref, dkv_ref[0, :inner]),
        (normed_ref, dkv_ref[0, inner:]),
        (low_ref, context_ref[0]),
    )
    for r, (left_ref, right) in enumerate(terms):
        product = dot_nt(left_ref[0], right)

        @pl.when(step == 0)
        def _(r=r, product=product):
            sum_scr[r] = product

        @pl.when(step > 0)
        def _(r=r, product=product):
            sum_scr[r] += product

    @pl.when(step == pl.num_programs(0) - 1)
    def _():
        out_ref[...] = sum_scr[...].astype(BF16)


def attention_weight_grads(normed, low, context, dq, dkv):
    groups, wide, length = normed.shape
    inner = context.shape[1]
    return call(
        attention_weights_kernel,
        "attention_weight_grads",
        (groups,),
        [slab(wide, length), slab(wide, length)]
        + [slab(inner, length), slab(inner, length), slab(2 * inner, length)],
        [whole((4, wide, inner))],
        [jax.ShapeDtypeStruct((4, wide, inner), BF16)],
        [normed, low, context, dq, dkv],
        flops=8 * groups * wide * length * inner,
        scratch=[pltpu.VMEM((4, wide, inner), F32)],
    )[0]


def input_kernel(x_ref, grad_ref, dq_ref, dkv_ref, gain_ref, w_ref, out_ref, gain_grad_ref):
    inner = dq_ref.shape[1]
    grad = (
        dot_nn(w_ref[0], dq_ref[0])
        + dot_nn(w_ref[1], dkv_ref[0, :inner])
        + dot_nn(w_ref[2], dkv_ref[0, inner:])
    )
    normed_grad, gain_grad = lifted_grads(x_ref[0].astype(F32), gain_ref[...], grad)
    gain_grad_ref[0] = gain_grad
    out_ref[0] = (grad_ref[0] + normed_grad).astype(BF16)


def input_grads(x, grad, dq, dkv, gain, weights):
    groups, wide, length = x.shape
    inner = weights.shape[2]
    return call(
        input_kernel,
        "input_grads",
        (groups,),
        [slab(wide, length), slab(wide, length), slab(inner, length), slab(2 * inner, length)]
        + [whole((wide, 1)), whole(weights.shape)],
        [slab(wide, length), slab(wide, 1)],
        [
            jax.ShapeDtypeStruct((groups, wide, length), BF16),
            jax.ShapeDtypeStruct((groups, wide, 1), F32),
        ],
        [x, grad, dq, dkv, gain, weights],
        flops=6 * groups * wide * length * inner,
    )


def halves(value_t, half):
    zero = jnp.zeros((half, value_t.shape[1]), value_t.dtype)
    return (
        jnp.concatenate([value_t[:half], zero], axis=0),
        jnp.concatenate([zero, value_t[half:]], axis=0),
    )


def attend_kernel(sources, block, half, info_ref, q_ref, *refs):
    kv_refs = refs[: 2 * sources]
    segq_ref, segk_ref, table_ref, ctx_ref, lse_ref = refs[2 * sources : 2 * sources + 5]
    s_scr, m_scr, l_scr, acc_scr, k_scr = refs[2 * sources + 5 :]
    length = q_ref.shape[2]
    q_blocks = length // block
    k_blocks = q_blocks * sources
    place_x = info_ref[0]
    step = pl.program_id(1)
    for s in range(sources):
        k_scr[s * length : (s + 1) * length, :] = transposed(kv_refs[2 * s][0])
    for qb in range(q_blocks):
        rows = pl.ds(qb * block, block)
        q_heads = halves(q_ref[0, :, rows], half)
        seg_q = segq_ref[0, :, rows]
        m_scr[...] = jnp.full(m_scr.shape, NEGATIVE, F32)
        l_scr[...] = jnp.zeros(l_scr.shape, F32)
        acc_scr[...] = jnp.zeros(acc_scr.shape, F32)
        for kb in range(k_blocks):
            s, lb = divmod(kb, q_blocks)
            live = info_ref[1 + (step * q_blocks + qb) * k_blocks + kb]

            @pl.when(live != 0)
            def _(s=s, lb=lb, kb=kb):
                entry = k_blocks - 1 - ((place_x ^ s) * q_blocks + lb - place_x * q_blocks - qb)
                keys = k_scr[pl.ds(kb * block, block), :]
                kept = segk_ref[0, pl.ds(kb * block, block), :] == seg_q
                for h in range(2):
                    score = dot_nn(keys, q_heads[h]) + table_ref[h, entry]
                    score = jnp.where(kept, score, NEGATIVE)
                    s_scr[h, kb] = score
                    m_scr[h] = jnp.maximum(m_scr[h], jnp.max(score, axis=0, keepdims=True))

        for kb in range(k_blocks):
            s, lb = divmod(kb, q_blocks)
            live = info_ref[1 + (step * q_blocks + qb) * k_blocks + kb]

            @pl.when(live != 0)
            def _(s=s, lb=lb, kb=kb):
                for h in range(2):
                    prob = jnp.exp(s_scr[h, kb] - m_scr[h])
                    l_scr[h] += jnp.sum(prob, axis=0, keepdims=True)
                    values_t = kv_refs[2 * s + 1][
                        0, h * half : (h + 1) * half, lb * block : (lb + 1) * block
                    ]
                    acc_scr[h * half : (h + 1) * half] += dot_nn(values_t, prob.astype(BF16))

        for h in range(2):
            lse_ref[0, 0, h : h + 1, rows] = m_scr[h] + jnp.log(l_scr[h])
            ctx_ref[0, h * half : (h + 1) * half, rows] = (
                acc_scr[h * half : (h + 1) * half] / l_scr[h]
            ).astype(BF16)


def grad_kernel(sources, block, half, info_ref, q_ref, *refs):
    kv_refs = refs[: 2 * sources]
    refs = refs[2 * sources :]
    segq_ref, segk_ref, table_ref, ctx_ref, lse_ref, gctx_ref = refs[:6]
    dq_ref, gbias_ref = refs[6:8]
    dkv_refs = refs[8 : 8 + sources]
    dk_scr, dv_scr, dq_scr, k_scr, v_scr, db_scr = refs[8 + sources :]
    length = q_ref.shape[2]
    q_blocks = length // block
    k_blocks = q_blocks * sources
    place_x = info_ref[0]
    step = pl.program_id(1)
    lane = lax.broadcasted_iota(jnp.int32, (block, 2 * half), 1)

    @pl.when(step == 0)
    def _():
        db_scr[...] = jnp.zeros(db_scr.shape, F32)

    for s in range(sources):
        k_scr[s * length : (s + 1) * length, :] = transposed(kv_refs[2 * s][0])
        v_scr[s * length : (s + 1) * length, :] = transposed(kv_refs[2 * s + 1][0])
    dk_scr[...] = jnp.zeros(dk_scr.shape, F32)
    dv_scr[...] = jnp.zeros(dv_scr.shape, F32)
    for qb in range(q_blocks):
        rows = pl.ds(qb * block, block)
        query_t = q_ref[0, :, rows]
        grad_out_t = gctx_ref[0, :, rows]
        product = grad_out_t.astype(F32) * ctx_ref[0, :, rows].astype(F32)
        deltas = (
            jnp.sum(product[:half], axis=0, keepdims=True),
            jnp.sum(product[half:], axis=0, keepdims=True),
        )
        q_heads = halves(query_t, half)
        g_heads = halves(grad_out_t, half)
        query, grad_out = transposed(query_t), transposed(grad_out_t)
        zero = jnp.zeros(query.shape, BF16)
        q_lanes = (jnp.where(lane < half, query, zero), jnp.where(lane < half, zero, query))
        g_lanes = (
            jnp.where(lane < half, grad_out, zero),
            jnp.where(lane < half, zero, grad_out),
        )
        seg_q = segq_ref[0, :, rows]
        dq_scr[...] = jnp.zeros(dq_scr.shape, F32)
        for kb in range(k_blocks):
            s, lb = divmod(kb, q_blocks)
            live = info_ref[1 + (step * q_blocks + qb) * k_blocks + kb]

            @pl.when(live != 0)
            def _(s=s, lb=lb, kb=kb):
                entry = k_blocks - 1 - ((place_x ^ s) * q_blocks + lb - place_x * q_blocks - qb)
                key_rows = pl.ds(kb * block, block)
                keys = k_scr[key_rows, :]
                values = v_scr[key_rows, :]
                kept = segk_ref[0, key_rows, :] == seg_q
                key_grad = dk_scr[key_rows, :]
                value_grad = dv_scr[key_rows, :]
                for h in range(2):
                    score = dot_nn(keys, q_heads[h]) + table_ref[h, entry]
                    score = jnp.where(kept, score, NEGATIVE)
                    prob = jnp.exp(score - lse_ref[0, 0, h : h + 1, rows])
                    grad_prob = dot_nn(values, g_heads[h])
                    grad_score = prob * (grad_prob - deltas[h])
                    db_scr[h, entry] += grad_score
                    low = grad_score.astype(BF16)
                    key_grad = key_grad + dot_nn(low, q_lanes[h])
                    value_grad = value_grad + dot_nn(prob.astype(BF16), g_lanes[h])
                    keys_t = kv_refs[2 * s][
                        0, h * half : (h + 1) * half, lb * block : (lb + 1) * block
                    ]
                    dq_scr[h * half : (h + 1) * half] += dot_nn(keys_t, low)
                dk_scr[key_rows, :] = key_grad
                dv_scr[key_rows, :] = value_grad

        dq_ref[0, :, rows] = dq_scr[...].astype(BF16)
    for s in range(sources):
        rows = slice(s * length, (s + 1) * length)
        dkv_refs[s][0, 0] = jnp.transpose(dk_scr[rows, :], (1, 0)).astype(BF16)
        dkv_refs[s][0, 1] = jnp.transpose(dv_scr[rows, :], (1, 0)).astype(BF16)

    @pl.when(step == pl.num_programs(1) - 1)
    def _():
        for h in range(2):
            for entry in range(2 * k_blocks - 1):
                tile = db_scr[h, entry]
                tile = jnp.concatenate([tile, jnp.zeros_like(tile)], axis=1)
                count = block
                while count > 8:
                    count //= 2
                    tile = pltpu.roll(tile[:count], count, 1) + tile[count:]
                total = tile[7:8]
                for t in range(7):
                    total = total + pltpu.roll(tile[t : t + 1], 7 - t, 1)
                gbias_ref[h, entry] = total


def attention_specs(sources, length, block, pairs, width):
    k_blocks = length * sources // block
    entries = 2 * k_blocks - 1

    def rows(offset):
        return pl.BlockSpec((1, width, length), lambda p, m, info: (m, p + offset, 0))

    kv_specs = [rows(0), rows(pairs)] * sources
    seg_specs = [
        pl.BlockSpec((1, 1, length), lambda p, m, info: (m, 0, 0)),
        pl.BlockSpec((1, length * sources, 1), lambda p, m, info: (m, 0, 0)),
    ]
    table_spec = pl.BlockSpec((2, entries, block, block), lambda p, m, info: (p, 0, 0, 0))
    lse_spec = pl.BlockSpec((1, 1, 8, length), lambda p, m, info: (m, p, 0, 0))
    return k_blocks, entries, rows, kv_specs, seg_specs, table_spec, lse_spec


def attend(info, q, kvs, seg_q, seg_k, table, block, head_size):
    micro, inner, length = q.shape
    sources = len(kvs)
    width = 2 * head_size
    pairs = inner // width
    k_blocks, entries, rows, kv_specs, seg_specs, table_spec, lse_spec = attention_specs(
        sources, length, block, pairs, width
    )
    return call(
        functools.partial(attend_kernel, sources, block, head_size),
        "attend",
        (pairs, micro),
        [rows(0)] + kv_specs + seg_specs + [table_spec],
        [rows(0), lse_spec],
        [
            jax.ShapeDtypeStruct((micro, inner, length), BF16),
            jax.ShapeDtypeStruct((micro, pairs, 8, length), F32),
        ],
        [info, q, *[kv for kv in kvs for _ in range(2)], seg_q, seg_k, table],
        flops=16 * micro * inner * length * length * sources,
        scratch=[
            pltpu.VMEM((2, k_blocks, block, block), F32),
            pltpu.VMEM((2, 1, block), F32),
            pltpu.VMEM((2, 1, block), F32),
            pltpu.VMEM((width, block), F32),
            pltpu.VMEM((length * sources, width), BF16),
        ],
        scalars=1,
    )


def attend_grads(info, q, kvs, seg_q, seg_k, table, context, lse, grad_context, block, head_size):
    micro, inner, length = q.shape
    sources = len(kvs)
    width = 2 * head_size
    pairs = inner // width
    k_blocks, entries, rows, kv_specs, seg_specs, table_spec, lse_spec = attention_specs(
        sources, length, block, pairs, width
    )
    dkv_spec = pl.BlockSpec((1, 2, width, length), lambda p, m, info: (m, 0, p, 0))
    results = call(
        functools.partial(grad_kernel, sources, block, head_size),
        "attend_grads",
        (pairs, micro),
        [rows(0)] + kv_specs + seg_specs + [table_spec, rows(0), lse_spec, rows(0)],
        [
            rows(0),
            pl.BlockSpec((2, entries, 1, 2 * block), lambda p, m, info: (p, 0, 0, 0)),
        ]
        + [dkv_spec] * sources,
        [
            jax.ShapeDtypeStruct((micro, inner, length), BF16),
            jax.ShapeDtypeStruct((2 * pairs, entries, 1, 2 * block), F32),
        ]
        + [jax.ShapeDtypeStruct((micro, 2, inner, length), BF16)] * sources,
        [info, q, *[kv for kv in kvs for _ in range(2)], seg_q, seg_k, table]
        + [context, lse, grad_context],
        flops=32 * micro * inner * length * length * sources,
        scratch=[
            pltpu.VMEM((length * sources, width), F32),
            pltpu.VMEM((length * sources, width), F32),
            pltpu.VMEM((width, block), F32),
            pltpu.VMEM((length * sources, width), BF16),
            pltpu.VMEM((length * sources, width), BF16),
            pltpu.VMEM((2, entries, block, block), F32),
        ],
        scalars=1,
    )
    return results[0], results[1], results[2:]


def gelu_terms(gate, upward, grad_hidden):
    square = gate * gate
    tanh = jnp.tanh(GELU_SCALE * gate * (1.0 + GELU_CUBE * square))
    half = 0.5 + 0.5 * tanh
    gelu = gate * half
    slope = half + 0.5 * gate * (1.0 - tanh * tanh) * (
        GELU_SCALE + 3.0 * GELU_CUBE * GELU_SCALE * square
    )
    return (
        (gelu * upward).astype(BF16),
        (grad_hidden * upward * slope).astype(BF16),
        (grad_hidden * gelu).astype(BF16),
    )


def joined(parts, axis):
    return parts[0] if len(parts) == 1 else jnp.concatenate(parts, axis=axis)


def source_rows(refs, kind, columns):
    return joined([ref[kind][:, columns] for ref in refs], 0)


def batches_of(sources, tile):
    if tile % LANES:
        return [[s] for s in range(sources)]
    return [list(range(s, min(s + 2, sources))) for s in range(0, sources, 2)]


def split_refs(refs, counts):
    result, start = [], 0
    for count in counts:
        result.append(refs[start : start + count])
        start += count
    return result, refs[start:]


def ffn_kernel(counts, *refs):
    sources, refs = split_refs(refs, counts)
    (normed_own, normed_far, cot_own, cot_far, hid_ref, ggi_ref, gui_ref), refs = refs[:7], refs[7:]
    grads, _ = split_refs(refs, counts)
    tile = sources[0][0].shape[2]
    micro = normed_own.shape[0]
    normed = [(ref, m) for ref in (normed_own, normed_far) for m in range(micro)]
    cot = [(ref, m) for ref in (cot_own, cot_far) for m in range(micro)]
    start = 0
    for batch in batches_of(len(sources), tile):
        units = tile * len(batch)
        rows = slice(start, start + units)
        start += units
        weights = [
            joined([source_rows(sources[s], kind, slice(None)) for s in batch], 1)
            for kind in range(3)
        ]
        for g in range(2 * micro):
            ref, m = normed[g]
            gate = dot_tn(weights[0], ref[m])
            upward = dot_tn(weights[1], ref[m])
            ref, m = cot[g]
            grad_hidden = dot_tn(weights[2], ref[m])
            hidden, grad_gate, grad_up = gelu_terms(gate, upward, grad_hidden)
            hid_ref[g, rows] = hidden
            ggi_ref[g, rows] = grad_gate
            gui_ref[g, rows] = grad_up
        for kind, (left, right_ref) in enumerate(((normed, ggi_ref), (normed, gui_ref), (cot, hid_ref))):
            total = None
            for g in range(2 * micro):
                ref, m = left[g]
                product = dot_nt(ref[m], right_ref[g, rows])
                total = product if total is None else total + product
            total = total.astype(BF16)
            for n, s in enumerate(batch):
                row = 0
                for ref in grads[s]:
                    depth = ref.shape[1]
                    ref[kind] = total[row : row + depth, n * tile : (n + 1) * tile]
                    row += depth


def tile_of(columns):
    return LANES if columns % LANES == 0 else columns


def ffn_chunk(quads, normed_own, normed_far, cot_own, cot_far):
    micro, wide, length = normed_own.shape
    columns = quads[0][0].shape[2]
    tile = tile_of(columns)
    counts = [len(parts) for parts in quads]
    flat = [part for parts in quads for part in parts]
    part_specs = [
        pl.BlockSpec((3, part.shape[1], tile), lambda j: (0, 0, j)) for part in flat
    ]
    units = len(quads) * tile
    act_spec = pl.BlockSpec((2 * micro, units, length), lambda j: (0, j, 0))
    act_shape = jax.ShapeDtypeStruct((2 * micro, len(quads) * columns, length), BF16)
    results = call(
        functools.partial(ffn_kernel, counts),
        "ffn_chunk",
        (columns // tile,),
        part_specs + [whole(normed_own.shape)] * 4,
        [act_spec] * 3 + part_specs,
        [act_shape] * 3 + [jax.ShapeDtypeStruct(part.shape, BF16) for part in flat],
        [*flat, normed_own, normed_far, cot_own, cot_far],
        flops=24 * micro * length * wide * len(quads) * columns,
    )
    grads, _ = split_refs(results[3:], counts)
    return results[:3], grads


def down_kernel(layout, *refs):
    chunks = []
    for counts in layout:
        sources, refs = split_refs(refs, counts)
        acts, refs = refs[:3], refs[3:]
        chunks.append((sources, acts))
    ffn_own, ffn_far, back_own, back_far = refs
    group = pl.program_id(0)
    micro = pl.num_programs(0) // 2
    totals = [None, None]
    for sources, acts in chunks:
        columns = sources[0][0].shape[2]
        tile = tile_of(columns)
        pieces = [(j, s) for j in range(columns // tile) for s in range(len(sources))]
        if tile % LANES == 0:
            pieces = [pieces]
        else:
            pieces = [[piece] for piece in pieces]
        for kind, act, which in ((2, 0, 0), (0, 1, 1), (1, 2, 1)):
            row = 0
            for group_of in pieces:
                left = joined(
                    [
                        source_rows(sources[s], kind, slice(j * tile, (j + 1) * tile))
                        for j, s in group_of
                    ],
                    1,
                )
                right = acts[act][0, row : row + left.shape[1]]
                row += left.shape[1]
                product = dot_nn(left, right)
                totals[which] = product if totals[which] is None else totals[which] + product

    @pl.when(group < micro)
    def _():
        ffn_own[0] = totals[0].astype(BF16)
        back_own[0] = totals[1].astype(BF16)

    @pl.when(group >= micro)
    def _():
        ffn_far[0] = totals[0].astype(BF16)
        back_far[0] = totals[1].astype(BF16)


def down(chunk_quads, chunk_acts, wide):
    groups, _, length = chunk_acts[0][0].shape
    micro = groups // 2
    operands, specs, layout = [], [], []
    flops = 0
    for quads, acts in zip(chunk_quads, chunk_acts):
        layout.append([len(parts) for parts in quads])
        flat = [part for parts in quads for part in parts]
        operands += flat + list(acts)
        specs += [whole(part.shape) for part in flat]
        specs += [slab(act.shape[1], length) for act in acts]
        flops += 6 * groups * length * wide * acts[0].shape[1]
    own_spec = pl.BlockSpec((1, wide, length), lambda g: (jnp.minimum(g, micro - 1), 0, 0))
    far_spec = pl.BlockSpec((1, wide, length), lambda g: (jnp.maximum(g - micro, 0), 0, 0))
    return call(
        functools.partial(down_kernel, layout),
        "down",
        (groups,),
        specs,
        [own_spec, far_spec, own_spec, far_spec],
        [jax.ShapeDtypeStruct((micro, wide, length), BF16)] * 4,
        operands,
        flops=flops,
    )


def body(
    inputs,
    cotangent,
    segments,
    rel_bucket,
    head_order,
    rel_table,
    norm1_gain,
    norm2_gain,
    w_query,
    w_key,
    w_value,
    output_weight,
    w_gate,
    w_up,
    w_down,
):
    dp, mp = lax.axis_size("dp"), lax.axis_size("mp")
    x = lax.axis_index("mp")
    dp_place = lax.axis_index("dp")
    core, chip = dp_place & 1, dp_place >> 1
    chips, depth = dp // 2, dp // 4
    micro, rows, own_length, model = inputs.shape
    groups = micro * rows
    length = own_length * mp
    bucket_count, head_count = rel_table.shape
    inner = w_query.shape[1]
    head_size = inner // head_count
    block = min(256, own_length)
    q_blocks, k_blocks = own_length // block, length // block
    own_rows, own_units = w_gate.shape
    half_units = own_units // 2
    chip_rows = 2 * own_rows
    place = chip.reshape(1).astype(jnp.int32)

    def inward(array):
        return reorder(array, place, chips, False)

    def feature_major(array):
        return jnp.transpose(array.reshape(groups, own_length, model), (0, 2, 1))

    part = 4 * inner // (2 * mp)
    shard = jnp.concatenate([w_query, w_key, w_value, jnp.transpose(output_weight)], axis=1)
    kept = lax.dynamic_slice_in_dim(shard, (2 * x + core) * part, part, 1)
    sent = lax.dynamic_slice_in_dim(shard, (2 * x + 1 - core) * part, part, 1)
    got = swap_dp(sent, 1)
    attention_piece = either(
        core, jnp.concatenate([kept, got], axis=0), jnp.concatenate([got, kept], axis=0)
    )[None]
    attention_quads = gather_quads(attention_piece)
    near = jnp.concatenate([jnp.concatenate(parts, axis=1) for parts in attention_quads], axis=0)
    far = swap_dp(near, 1)
    parts_all = jnp.stack([near, far], axis=1).reshape(2 * mp, model, part)
    ordered = jnp.concatenate(
        [
            lax.dynamic_slice_in_dim(parts_all, (2 * x + core) ^ r, 1, 0)
            for r in range(2 * mp)
        ],
        axis=0,
    )
    attention_weights = jnp.transpose(
        ordered.reshape(4, inner // part, model, part), (0, 2, 1, 3)
    ).reshape(4, model, inner)

    ffn_shard = jnp.stack([w_gate, w_up, jnp.transpose(w_down)])
    low_half, high_half = ffn_shard[:, :, :half_units], ffn_shard[:, :, half_units:]
    kept = either(core, low_half, high_half)
    got = swap_dp(either(core, high_half, low_half), 1)
    ffn_piece = either(
        core, jnp.concatenate([kept, got], axis=1), jnp.concatenate([got, kept], axis=1)
    )
    if half_units % LANES == 0:
        first = half_units // LANES * 3 // 7 * LANES
        bounds = [0, first, half_units] if first else [0, half_units]
    else:
        bounds = [0, half_units]
    spans = list(zip(bounds[:-1], bounds[1:]))
    chunk_quads = [gather_quads(ffn_piece[:, :, a:b]) for a, b in spans]

    bucket_rev = jnp.concatenate([rel_bucket[::-1], jnp.full((1,), -1, jnp.int32)])
    bucket_hot = (bucket_rev[:, None] == jnp.arange(bucket_count, dtype=jnp.int32)[None, :]).astype(F32)
    head_hot = (head_order[:, None] == jnp.arange(head_count, dtype=jnp.int32)[None, :]).astype(F32)
    offset_table = jnp.dot(bucket_hot, rel_table, precision=TOP_PRECISION)
    offset_bias = jnp.dot(head_hot, offset_table.T, precision=TOP_PRECISION)
    bias_blocks = offset_bias.reshape(head_count, 2 * k_blocks, block)
    windows = jnp.concatenate([bias_blocks[:, :-1], bias_blocks[:, 1:]], axis=2)
    table = bias_table(windows[:, :, None, :], block)

    seg_flat = segments.reshape(groups, length)
    seg_q = lax.dynamic_slice_in_dim(seg_flat, x * own_length, own_length, 1)
    seg_parts = seg_flat.reshape(groups, mp, own_length)
    seg_k = jnp.concatenate([pick(seg_parts, x ^ k, 1) for k in range(mp)], axis=1)
    q_edges = seg_q.reshape(groups, q_blocks, block)
    k_edges = seg_k.reshape(groups, k_blocks, block)
    live = (q_edges[:, :, None, 0] <= k_edges[:, None, :, -1]) & (
        k_edges[:, None, :, 0] <= q_edges[:, :, None, -1]
    )
    info = jnp.concatenate([x.reshape(1).astype(jnp.int32), live.reshape(-1).astype(jnp.int32)])
    seg_q_row = seg_q.reshape(groups, 1, own_length)
    seg_k_column = seg_k.reshape(groups, length, 1)

    gains = inward(jnp.stack([norm1_gain, norm2_gain], axis=1)[None])[0]
    gain1, gain2 = gains[:, :1], gains[:, 1:]
    layer_in = inward(feature_major(inputs))
    cot = inward(feature_major(cotangent))
    cot_far = swap_dp(cot, 1)
    normed1, q, own_kv = project(layer_in, gain1, attention_weights)
    kvs = [own_kv] + [swap_mp(own_kv, k) for k in range(1, mp)]
    context, lse = attend(info, q, kvs, seg_q_row, seg_k_column, table, block, head_size)
    middle, normed2 = middle_layer(layer_in, context, attention_weights, gain2)
    normed2_far = swap_dp(normed2, 1)

    chunk_acts, reduced = [], []
    for quads in chunk_quads:
        acts, grads = ffn_chunk(quads, normed2, normed2_far, cot, cot_far)
        chunk_acts.append(acts)
        reduced.append(scatter_quads(grads))
    ffn_own, ffn_far, back_own, back_far = down(chunk_quads, chunk_acts, model)
    back = (back_own, swap_dp(back_far, 1))
    ffn = (ffn_own, swap_dp(ffn_far, 1))

    outputs, grad_middle, grad_attn, grad_context, gain2_grads = turn(
        middle, cot, ffn, back, gain2, attention_weights
    )
    grad_q, bias_grads, dkv = attend_grads(
        info,
        q,
        kvs,
        seg_q_row,
        seg_k_column,
        table,
        context,
        lse,
        grad_context,
        block,
        head_size,
    )
    grad_kv = add_low(dkv[0], *[swap_mp(dkv[k], k) for k in range(1, mp)])
    grad_kv = grad_kv.reshape(groups, 2 * inner, own_length)
    weight_grads = attention_weight_grads(normed1, grad_attn, context, grad_q, grad_kv)
    grad_inputs, gain1_grads = input_grads(
        layer_in, grad_middle, grad_q, grad_kv, gain1, attention_weights
    )

    by_part = jnp.transpose(
        weight_grads.reshape(4, model, inner // part, part), (0, 2, 1, 3)
    ).reshape(mp, 2, model, part)
    near = add_low(pick(by_part, core, 1), swap_dp(pick(by_part, 1 - core, 1), 1))
    half = model // 2
    quads = []
    for k in range(mp):
        matrix = pick(near, x ^ k, 0)[None]
        if k == 0:
            quads.append((matrix[:, :half], matrix[:, half:]))
        else:
            quads.append(
                (matrix[:, :half], matrix[:, half : half + half // 2], matrix[:, half + half // 2 :])
            )
    piece = scatter_quads(quads)[0]
    over_x = jnp.stack([piece] + [swap_mp(piece, k) for k in range(1, mp)])
    kept = either(core, over_x[:, :own_rows], over_x[:, own_rows:])
    got = swap_dp(either(core, over_x[:, own_rows:], over_x[:, :own_rows]), 1)
    both = jnp.stack([kept, got], axis=1).reshape(2 * mp, own_rows, part)
    final = jnp.concatenate(
        [pick(both, (2 * x + core) ^ r, 0) for r in range(2 * mp)], axis=1
    ).astype(F32)

    sums = jnp.concatenate(reduced, axis=2)
    kept = either(core, sums[:, :own_rows], sums[:, own_rows:])
    got = swap_dp(either(core, sums[:, own_rows:], sums[:, :own_rows]), 1)
    ffn_grads = either(
        core, jnp.concatenate([kept, got], axis=2), jnp.concatenate([got, kept], axis=2)
    ).astype(F32)

    bias_flat = bias_grads[:, :, 0, :]
    left = jnp.pad(bias_flat[:, :, :block], ((0, 0), (0, 1), (0, 0)))
    right = jnp.pad(bias_flat[:, :, block:], ((0, 0), (1, 0), (0, 0)))
    offsets_total = (left + right).reshape(head_count, 2 * k_blocks * block)
    bucket_part = jnp.dot(bucket_hot.T, offsets_total.T, precision=TOP_PRECISION)
    rel_part = jnp.dot(bucket_part, head_hot, precision=TOP_PRECISION)
    gain_parts = jnp.stack([jnp.sum(gain1_grads[..., 0], 0), jnp.sum(gain2_grads[..., 0], 0)], axis=1)
    gain_parts = reorder(gain_parts[None], place, chips, True)[0]
    small = jnp.concatenate([gain_parts[:, 0], gain_parts[:, 1], rel_part.reshape(-1)])
    small = sum_all(small)

    shape = inputs.shape

    def placed(array):
        array = reorder(array, place, chips, True)
        return jnp.transpose(array, (0, 2, 1)).reshape(shape)

    return (
        placed(outputs),
        placed(grad_inputs),
        small[2 * model :].reshape(rel_table.shape),
        small[:model],
        small[model : 2 * model],
        final[:, :inner],
        final[:, inner : 2 * inner],
        final[:, 2 * inner : 3 * inner],
        jnp.transpose(final[:, 3 * inner :]),
        ffn_grads[0],
        ffn_grads[1],
        jnp.transpose(ffn_grads[2]),
    )


def solution(mesh):
    return jax.shard_map(
        body,
        mesh=mesh,
        in_specs=(
            P(None, "dp", "mp", None),
            P(None, "dp", "mp", None),
            P(None, "dp", None),
            P(),
            P(),
            P(),
            P(),
            P(),
            P("dp", None),
            P("dp", None),
            P("dp", None),
            P(None, "dp"),
            P("dp", "mp"),
            P("dp", "mp"),
            P("mp", "dp"),
        ),
        out_specs=(
            P(None, "dp", "mp", None),
            P(None, "dp", "mp", None),
            P(),
            P(),
            P(),
            P("dp", None),
            P("dp", None),
            P("dp", None),
            P(None, "dp"),
            P("dp", "mp"),
            P("dp", "mp"),
            P("mp", "dp"),
        ),
        check_vma=False,
    )
```

time: 990 us -> 762 us (0.77)
  matrix products: 238 us -> 2.57 us
  local copies, waits for them, and re-layouts: 258 us -> 37.4 us
  Pallas kernels: 75.6 us -> 277 us
  waiting for transfers between devices: 208 us -> 281 us
  blocking collectives: 41.1 us -> 0 us
  starting transfers between devices: 112 us -> 94.9 us
    dot_general x24 -> x0, matrix products: 235 us -> none  [the longest x8 89.1 us: matmul(): return jnp.einsum('td,df->tf', left, right, preferred_element_type=F32)]
    pallas_call x3 -> x17, Pallas kernels: 75.6 us -> 277 us  [call(): pl.pallas_call(kernel, grid_spec=pltpu.PrefetchScalarGridSpec(num_scalar_...]
    ppermute x9 -> x16, waiting for transfers between devices: 8.54 us -> 164 us  [swap_mp(): return lax.ppermute(array, 'mp', [(i, i ^ mask) for i in range(count)])]
    ppermute x34 -> x44, waiting for transfers between devices: 199 us -> 117 us  [swap_dp(): return lax.ppermute(array, 'dp', [(i, i ^ mask) for i in range(count)])]
    unnamed x168 -> x78, local copies, waits for them, and re-layouts: 60.2 us -> 7.48 us
    dynamic_update_slice x30 -> x0, local copies, waits for them, and re-layouts: 48.9 us -> none  [place(): lax.dynamic_update_index_in_dim(whole, jnp.expand_dims(piece, axis), inde...]
    another operation x13 -> x11, local copies, waits for them, and re-layouts: 48.2 us -> 4.02 us  [the longest x3 1.34 us: body(): jnp.stack([jnp.sum(gain1_grads[..., 0], 0), jnp.sum(gain2_grads[..., 0],...]
    psum x1 -> x0, blocking collectives: 41.1 us -> none  [body(): lax.psum((grad_gain1, grad_gain2, rel_part), ('dp', 'mp'))]
  transfers between devices with their start and end apart: 43 -> 60, of which waited for: 16 -> 22; matrix products, arithmetic and copies ran while one was open for 45% -> 11% of each run, Pallas kernels for 8% -> 23%
where the time goes in v2:
time: 762 us; the launch traced here: 752 us
  waiting for transfers between devices  281 us (37%)
  Pallas kernels  277 us (36%)
  starting transfers between devices  94.9 us (12%)
  other arithmetic  56.9 us (7%)
  local copies, waits for them, and re-layouts  37.4 us (5%)
    pallas_call x17, Pallas kernels, call(): pl.pallas_call(kernel, grid_spec=pltpu.PrefetchScalarGridSpec(num_scalar_...  277 us
    ppermute x16, waiting for transfers between devices, swap_mp(): return lax.ppermute(array, 'mp', [(i, i ^ mask) for i in range(count)])  164 us
    ppermute x44, waiting for transfers between devices, swap_dp(): return lax.ppermute(array, 'dp', [(i, i ^ mask) for i in range(count)])  117 us
    ppermute x44, starting transfers between devices, swap_dp(): return lax.ppermute(array, 'dp', [(i, i ^ mask) for i in range(count)])  76.9 us
    convert_element_type x13, other arithmetic, add_low(): return total.astype(BF16)  23.7 us
    ppermute x16, starting transfers between devices, swap_mp(): return lax.ppermute(array, 'mp', [(i, i ^ mask) for i in range(count)])  18 us
  transfers between devices with their start and end apart: 60, of which 22 were waited for; matrix products, arithmetic and copies ran while one was open for 11% of the time, Pallas kernels for 23%

profile of v2, /device:TPU:0, one launch (start us, length us, event | category | flops | bytes accessed | tf_op | source)
XLA Modules:
  0.0 751.7 jit_solution(14545098541101097357)
XLA Ops:
  12.6 7.3 collective-permute-done.2
  23.1 9.8 %collective-permute-done.4 = bf16[1,736,384]{2,1,0:T(8,128)(2,1)S(1)} collective-permute-done((bf16[1,736,384]{2,1,0:T(8,128)(2,1)S(1)}, bf16[1,736,384]{2,1,0:T(8,128)(2,1)S(1)}, u32[]{:S(2)}, u32[]{:S(2)}) %collective-permute-start.4) | collective-permute-done | bytes 565280 | tf_op jit(solution)/shard_map/ppermute | solution.py:23
  42.6 5.1 maximum_maximum_fusion
  62.1 4.2 fusion.35
  71.4 8.8 %project.1 = (bf16[2,1472,512]{2,1,0:T(8,128)(2,1)}, bf16[2,384,512]{2,1,0:T(8,128)(2,1)}, bf16[2,768,512]{2,1,0:T(8,128)(2,1)}) custom-call(bf16[2,1472,512]{2,1,0:T(8,128)(2,1)} %bitcast.169, f32[1472,1]{1,0:T(8,128)} %get-tuple-element.164.gain_ref, bf16[4,1472,384]{2,1,0:T(8,128)(2,1)} %pad_maximum_fusion.1.w_ref), custom_call_target="tpu_custom_call" | custom-call | flops 3472883712 | bytes 12916480 | tf_op jit(solution)/shard_map/project/pallas_call | solution.py:96
  89.5 13.9 %collective-permute-done.11 = bf16[3,184,384]{2,1,0:T(8,128)(2,1)S(1)} collective-permute-done((bf16[3,184,384]{2,1,0:T(8,128)(2,1)S(1)}, bf16[3,184,384]{2,1,0:T(8,128)(2,1)S(1)}, u32[]{:S(2)}, u32[]{:S(2)}) %collective-permute-start.11) | collective-permute-done | bytes 423968 | tf_op jit(solution)/shard_map/ppermute | solution.py:23
  103.4 12.8 %collective-permute-done.12 = bf16[3,184,384]{2,1,0:T(8,128)(2,1)} collective-permute-done((bf16[3,184,384]{2,1,0:T(8,128)(2,1)S(1)}, bf16[3,184,384]{2,1,0:T(8,128)(2,1)}, u32[]{:S(2)}, u32[]{:S(2)}) %collective-permute-start.12) | collective-permute-done | bytes 423968 | tf_op jit(solution)/shard_map/ppermute | solution.py:23
  124.5 6.8 bias_table.1.refs_6_
  134.8 26.9 %collective-permute-done.21 = bf16[3,184,512]{2,1,0:T(8,128)(2,1)} collective-permute-done((bf16[3,184,512]{2,1,0:T(8,128)(2,1)}, bf16[3,184,512]{2,1,0:T(8,128)(2,1)}, u32[]{:S(2)}, u32[]{:S(2)}) %collective-permute-start.21) | collective-permute-done | bytes 565280 | tf_op jit(solution)/shard_map/ppermute | solution.py:23
  165.0 19.6 %attend.1 = (bf16[2,384,512]{2,1,0:T(8,128)(2,1)}, f32[2,3,8,512]{3,2,1,0:T(8,128)}) custom-call(s32[17]{0:T(128)} %pad_add_fusion.2.info_ref, bf16[2,384,512]{2,1,0:T(8,128)(2,1)} %get-tuple-element.50.q_ref, bf16[2,768,512]{2,1,0:T(8,128)(2,1)} %get-tuple-element.51.refs_0_.refs_1_, bf16[2,768,512]{2,1,0:T(8,128)(2,1)} %get-tuple-element.51.refs_0_.refs_1_, ...), custom_call_target="tpu_custom_call" | custom-call | flops 6442450944 | bytes 18985028 | tf_op jit(solution)/shard_map/attend/pallas_call | solution.py:96
  184.6 8.4 %middle.1 = (f32[2,1472,512]{2,1,0:T(8,128)}, bf16[2,1472,512]{2,1,0:T(8,128)(2,1)}) custom-call(bf16[2,1472,512]{2,1,0:T(8,128)(2,1)} %bitcast.170, bf16[2,384,512]{2,1,0:T(8,128)(2,1)} %get-tuple-element.52.context_ref.refs_7_, bf16[4,1472,384]{2,1,0:T(8,128)(2,1)} %pad_maximum_fusion.1.w_ref, f32[1472,1]{1,0:T(8,128)} %get-tuple-element.163.gain_ref), custom_call_target="tpu_custom_call" | custom-call | flops 1157627904 | bytes 17372928 | tf_op jit(solution)/shard_map/middle/pallas_call | solution.py:96
  196.3 36.6 %collective-permute-done.15.refs_2_ = bf16[3,736,384]{2,1,0:T(8,128)(2,1)S(1)} collective-permute-done((bf16[3,736,384]{2,1,0:T(8,128)(2,1)S(1)}, bf16[3,736,384]{2,1,0:T(8,128)(2,1)S(1)}, u32[]{:S(2)}, u32[]{:S(2)}) %collective-permute-start.15) | collective-permute-done | bytes 1695776 | tf_op jit(solution)/shard_map/ppermute | solution.py:28
  235.9 45.4 %collective-permute-done.24.refs_2_.refs_10_ = bf16[3,736,512]{2,1,0:T(8,128)(2,1)S(1)} collective-permute-done((bf16[3,736,512]{2,1,0:T(8,128)(2,1)S(1)}, bf16[3,736,512]{2,1,0:T(8,128)(2,1)S(1)}, u32[]{:S(2)}, u32[]{:S(2)}) %collective-permute-start.24) | collective-permute-done | bytes 2261024 | tf_op jit(solution)/shard_map/ppermute | solution.py:28
  283.0 16.4 %collective-permute-done.16.refs_3_ = bf16[3,368,384]{2,1,0:T(8,128)(2,1)S(1)} collective-permute-done((bf16[3,368,384]{2,1,0:T(8,128)(2,1)S(1)}, bf16[3,368,384]{2,1,0:T(8,128)(2,1)S(1)}, u32[]{:S(2)}, u32[]{:S(2)}) %collective-permute-start.16) | collective-permute-done | bytes 847904 | tf_op jit(solution)/shard_map/ppermute | solution.py:28
  301.3 38.4 %ffn_chunk.2 = (bf16[4,768,512]{2,1,0:T(8,128)(2,1)}, bf16[4,768,512]{2,1,0:T(8,128)(2,1)}, bf16[4,768,512]{2,1,0:T(8,128)(2,1)}, bf16[3,736,384]{2,1,0:T(8,128)...) custom-call(bf16[3,736,384]{2,1,0:T(8,128)(2,1)} %bitcast.205, ...), custom_call_target="tpu_custom_call" | custom-call | flops 27783069696 | bytes 35061760 | tf_op jit(solution)/shard_map/ffn_chunk/pallas_call | solution.py:96
  340.8 48.9 %ffn_chunk.3 = (bf16[4,1024,512]{2,1,0:T(8,128)(2,1)}, bf16[4,1024,512]{2,1,0:T(8,128)(2,1)}, bf16[4,1024,512]{2,1,0:T(8,128)(2,1)}, bf16[3,736,512]{2,1,0:T(8,1...) custom-call(bf16[3,736,512]{2,1,0:T(8,128)(2,1)} %bitcast.199, ...), custom_call_target="tpu_custom_call" | custom-call | flops 37044092928 | bytes 42729472 | tf_op jit(solution)/shard_map/ffn_chunk/pallas_call | solution.py:96
  389.7 45.6 %down.1 = (bf16[2,1472,512]{2,1,0:T(8,128)(2,1)}, bf16[2,1472,512]{2,1,0:T(8,128)(2,1)}, bf16[2,1472,512]{2,1,0:T(8,128)(2,1)}, bf16[2,1472,512]{2,1,0:T(8,128)(2,1)}) custom-call(bf16[3,736,384]{2,1,0:T(8,128)(2,1)} %bitcast.206, bf16[3,736,384]{2,1,0:T(8,128)(2,1)} %collective-permute-done.14.refs_1_, bf16[3,736,384]{2,1,0:T(8,128)(2,1)} %copy-done.17, ...), custom_call_target="tpu_custom_call" | custom-call | flops 32413581312 | bytes 49905664 | tf_op jit(solution)/shard_map/down/pallas_call | solution.py:96
  445.5 14.8 %turn.1 = (bf16[2,1472,512]{2,1,0:T(8,128)(2,1)}, f32[2,1472,512]{2,1,0:T(8,128)}, bf16[2,1472,512]{2,1,0:T(8,128)(2,1)}, bf16[2,384,512]{2,1,0:T(8,128)(2,1)}, f32[2,1472,1]{2,1,0:T(8,128)}) custom-call(f32[2,1472,512]{2,1,0:T(8,128)} %get-tuple-element.53.middle_ref, bf16[2,1472,512]{2,1,0:T(8,128)(2,1)} %bitcast.176, ...), custom_call_target="tpu_custom_call" | custom-call | flops 1157627904 | bytes 38487296 | tf_op jit(solution)/shard_map/turn/pallas_call | solution.py:96
  460.4 39.1 %attend_grads.1 = (bf16[2,384,512]{2,1,0:T(8,128)(2,1)}, f32[6,7,1,512]{3,2,1,0:T(1,128)}, bf16[2,2,384,512]{3,2,1,0:T(8,128)(2,1)}, bf16[2,2,384,512]{3,2,1,0:T(8,128)(2,1)}) custom-call(s32[17]{0:T(128)} %pad_add_fusion.2.info_ref, bf16[2,384,512]{2,1,0:T(8,128)(2,1)} %get-tuple-element.50.q_ref, bf16[2,768,512]{2,1,0:T(8,128)(2,1)} %get-tuple-element.51.refs_0_.refs_1_, ...), custom_call_target="tpu_custom_call" | custom-call | flops 12884901888 | bytes 23789636 | tf_op jit(solution)/shard_map/attend_grads/pallas_call | solution.py:96
  517.2 19.8 %collective-permute-done.29 = bf16[2,2,384,512]{3,2,1,0:T(8,128)(2,1)S(1)} collective-permute-done((bf16[2,2,384,512]{3,2,1,0:T(8,128)(2,1)}, bf16[2,2,384,512]{3,2,1,0:T(8,128)(2,1)S(1)}, u32[]{:S(2)}, u32[]{:S(2)}) %collective-permute-start.29) | collective-permute-done | bytes 1572896 | tf_op jit(solution)/shard_map/ppermute | solution.py:28
  538.6 14.4 %attention_weight_grads.1 = bf16[4,1472,384]{2,1,0:T(8,128)(2,1)} custom-call(bf16[2,1472,512]{2,1,0:T(8,128)(2,1)} %get-tuple-element.76.normed_ref, bf16[2,1472,512]{2,1,0:T(8,128)(2,1)} %get-tuple-element.77.low_ref, bf16[2,384,512]{2,1,0:T(8,128)(2,1)} %get-tuple-element.52.context_ref.refs_7_, bf16[2,384,512]{2,1,0:T(8,128)(2,1)} %get-tuple-element.69.dq_ref, ...), custom_call_target="tpu_custom_call" | custom-call | flops 4630511616 | bytes 13697024 | tf_op jit(solution)/shard_map/attention_weight_grads/pallas_call | solution.py:96
  556.2 17.2 %collective-permute-done.46 = bf16[3,736,384]{2,1,0:T(8,128)(2,1)} collective-permute-done((bf16[3,736,384]{2,1,0:T(8,128)(2,1)}, bf16[3,736,384]{2,1,0:T(8,128)(2,1)}, u32[]{:S(2)}, u32[]{:S(2)}) %collective-permute-start.46) | collective-permute-done | bytes 1695776 | tf_op jit(solution)/shard_map/ppermute | solution.py:28
  578.9 9.3 %collective-permute-start.49 = (bf16[3,184,384]{2,1,0:T(8,128)(2,1)}, bf16[3,184,384]{2,1,0:T(8,128)(2,1)}, u32[]{:S(2)}, u32[]{:S(2)}) collective-permute-start(bf16[3,184,384]{2,1,0:T(8,128)(2,1)} %get-tuple-element.152), channel_id=1, source_target_pairs={{0,8},{2,10},{4,12},{6,14},{8,0},{10,2},{12,4},{14,6},{16,24},{18,... | collective-permute-start | bytes 1271816 | tf_op jit(solution)/shard_map/ppermute | solution.py:23
  594.3 26.7 %collective-permute-done.53 = bf16[3,736,512]{2,1,0:T(8,128)(2,1)S(1)} collective-permute-done((bf16[3,736,512]{2,1,0:T(8,128)(2,1)}, bf16[3,736,512]{2,1,0:T(8,128)(2,1)S(1)}, u32[]{:S(2)}, u32[]{:S(2)}) %collective-permute-start.53) | collective-permute-done | bytes 2261024 | tf_op jit(solution)/shard_map/ppermute | solution.py:28
  621.0 4.1 collective-permute-start.51
  625.1 3.9 add_convert_fusion
  637.0 15.3 %input_grads.1 = (bf16[2,1472,512]{2,1,0:T(8,128)(2,1)}, f32[2,1472,1]{2,1,0:T(8,128)}) custom-call(bf16[2,1472,512]{2,1,0:T(8,128)(2,1)} %bitcast.171, f32[2,1472,512]{2,1,0:T(8,128)} %get-tuple-element.66.grad_ref, bf16[2,384,512]{2,1,0:T(8,128)(2,1)} %get-tuple-element.69.dq_ref, bf16[2,768,512]{2,1,0:T(8,128)(2,1)} %bitcast.184, ...), custom_call_target="tpu_custom_call" | custom-call | flops 3472883712 | bytes 18957568 | tf_op jit(solution)/shard_map/input_grads/pallas_call | solution.py:96
  659.5 9.1 %collective-permute-start.56 = (bf16[3,184,512]{2,1,0:T(8,128)(2,1)}, bf16[3,184,512]{2,1,0:T(8,128)(2,1)}, u32[]{:S(2)}, u32[]{:S(2)}) collective-permute-start(bf16[3,184,512]{2,1,0:T(8,128)(2,1)} %get-tuple-element.140), channel_id=1, source_target_pairs={{0,8},{2,10},{4,12},{6,14},{8,0},{10,2},{12,4},{14,6},{16,24},{18,... | collective-permute-start | bytes 1695752 | tf_op jit(solution)/shard_map/ppermute | solution.py:23
  681.4 12.9 %collective-permute-done.56 = bf16[3,184,512]{2,1,0:T(8,128)(2,1)} collective-permute-done((bf16[3,184,512]{2,1,0:T(8,128)(2,1)}, bf16[3,184,512]{2,1,0:T(8,128)(2,1)}, u32[]{:S(2)}, u32[]{:S(2)}) %collective-permute-start.56) | collective-permute-done | bytes 565280 | tf_op jit(solution)/shard_map/ppermute | solution.py:23
  695.2 14.6 %collective-permute-done.57 = bf16[3,184,512]{2,1,0:T(8,128)(2,1)} collective-permute-done((bf16[3,184,512]{2,1,0:T(8,128)(2,1)}, bf16[3,184,512]{2,1,0:T(8,128)(2,1)}, u32[]{:S(2)}, u32[]{:S(2)}) %collective-permute-start.57) | collective-permute-done | bytes 565280 | tf_op jit(solution)/shard_map/ppermute | solution.py:23
  711.5 12.4 %collective-permute-start.32 = (f32[3136]{0:T(1024)S(1)}, f32[3136]{0:T(1024)S(1)}, u32[]{:S(2)}, u32[]{:S(2)}) collective-permute-start(f32[3136]{0:T(1024)S(1)} %add.163), channel_id=1, source_target_pairs={{0,8},{2,10},{4,12},{6,14},{8,0},{10,2},{12,4},{14,6},{16,24},{18,... | collective-permute-start | bytes 37640 | tf_op jit(solution)/shard_map/ppermute | solution.py:23
  736.4 6.7 collective-permute-done.41
  (293 shorter events, 174.6 us)
Async XLA Ops:
  80.2 84.8 %collective-permute-start.9 = (bf16[2,768,512]{2,1,0:T(8,128)(2,1)}, bf16[2,768,512]{2,1,0:T(8,128)(2,1)}, u32[]{:S(2)}, u32[]{:S(2)}) collective-permute-start(bf16[2,768,512]{2,1,0:T(8,128)(2,1)} %get-tuple-element.51.refs_0_.refs_1_), channel_id=1, source_target_pairs={{0,1},{1,0},{2,3},{3,2},{4,5},{5,4},{6,7},{7,6},{8,9},{9,8},{10,11... | collective-permute-start | bytes 4718600 | tf_op jit(solution)/shard_map/ppermute | solution.py:28
  88.5 46.2 %collective-permute-start.20 = (bf16[3,184,512]{2,1,0:T(8,128)(2,1)}, bf16[3,184,512]{2,1,0:T(8,128)(2,1)S(1)}, u32[]{:S(2)}, u32[]{:S(2)}) collective-permute-start(bf16[3,184,512]{2,1,0:T(8,128)(2,1)} %get-tuple-element.160), channel_id=1, source_target_pairs={{0,8},{2,10},{4,12},{6,14},{8,0},{10,2},{12,4},{14,6},{16,24},{18,... | collective-permute-start | bytes 1695752 | tf_op jit(solution)/shard_map/ppermute | solution.py:23
  103.4 58.3 %collective-permute-start.21 = (bf16[3,184,512]{2,1,0:T(8,128)(2,1)}, bf16[3,184,512]{2,1,0:T(8,128)(2,1)}, u32[]{:S(2)}, u32[]{:S(2)}) collective-permute-start(bf16[3,184,512]{2,1,0:T(8,128)(2,1)} %get-tuple-element.160), channel_id=1, source_target_pairs={{0,16},{2,18},{4,20},{6,22},{8,24},{10,26},{12,28},{14,30},{16,0},... | collective-permute-start | bytes 1695752 | tf_op jit(solution)/shard_map/ppermute | solution.py:23
  116.2 45.5 %collective-permute-start.22 = (bf16[3,184,512]{2,1,0:T(8,128)(2,1)}, bf16[3,184,512]{2,1,0:T(8,128)(2,1)}, u32[]{:S(2)}, u32[]{:S(2)}) collective-permute-start(bf16[3,184,512]{2,1,0:T(8,128)(2,1)} %get-tuple-element.160), channel_id=1, source_target_pairs={{0,24},{2,26},{4,28},{6,30},{8,16},{10,18},{12,20},{14,22},{16,8},... | collective-permute-start | bytes 1695752 | tf_op jit(solution)/shard_map/ppermute | solution.py:23
  120.2 74.3 %collective-permute-start.14 = (bf16[3,736,384]{2,1,0:T(8,128)(2,1)S(1)}, bf16[3,736,384]{2,1,0:T(8,128)(2,1)}, u32[]{:S(2)}, u32[]{:S(2)}) collective-permute-start(bf16[3,736,384]{2,1,0:T(8,128)(2,1)S(1)} %bitcast.203), channel_id=1, source_target_pairs={{0,4},{2,6},{4,0},{6,2},{8,12},{10,14},{12,8},{14,10},{16,20},{18,... | collective-permute-start | bytes 5087240 | tf_op jit(solution)/shard_map/ppermute | solution.py:23
  134.7 148.2 %collective-permute-start.19 = (bf16[2,1472,512]{2,1,0:T(8,128)(2,1)}, bf16[2,1472,512]{2,1,0:T(8,128)(2,1)}, u32[]{:S(2)}, u32[]{:S(2)}) collective-permute-start(bf16[2,1472,512]{2,1,0:T(8,128)(2,1)} %bitcast.173), channel_id=1, source_target_pairs={{0,2},{2,0},{4,6},{6,4},{8,10},{10,8},{12,14},{14,12},{16,18},{18,... | collective-permute-start | bytes 9043976 | tf_op jit(solution)/shard_map/ppermute | solution.py:23
  163.4 71.1 %collective-permute-start.23 = (bf16[3,736,512]{2,1,0:T(8,128)(2,1)S(1)}, bf16[3,736,512]{2,1,0:T(8,128)(2,1)}, u32[]{:S(2)}, u32[]{:S(2)}) collective-permute-start(bf16[3,736,512]{2,1,0:T(8,128)(2,1)S(1)} %bitcast.197), channel_id=1, source_target_pairs={{0,4},{2,6},{4,0},{6,2},{8,12},{10,14},{12,8},{14,10},{16,20},{18,... | collective-permute-start | bytes 6782984 | tf_op jit(solution)/shard_map/ppermute | solution.py:23
  192.9 108.4 %collective-permute-start.18 = (bf16[2,1472,512]{2,1,0:T(8,128)(2,1)}, bf16[2,1472,512]{2,1,0:T(8,128)(2,1)}, u32[]{:S(2)}, u32[]{:S(2)}) collective-permute-start(bf16[2,1472,512]{2,1,0:T(8,128)(2,1)} %get-tuple-element.54.refs_5_), channel_id=1, source_target_pairs={{0,2},{2,0},{4,6},{6,4},{8,10},{10,8},{12,14},{14,12},{16,18},{18,... | collective-permute-start | bytes 9043976 | tf_op jit(solution)/shard_map/ppermute | solution.py:23
  192.9 39.9 %collective-permute-start.15 = (bf16[3,736,384]{2,1,0:T(8,128)(2,1)S(1)}, bf16[3,736,384]{2,1,0:T(8,128)(2,1)S(1)}, u32[]{:S(2)}, u32[]{:S(2)}) collective-permute-start(bf16[3,736,384]{2,1,0:T(8,128)(2,1)S(1)} %bitcast.204), channel_id=1, source_target_pairs={{0,1},{1,0},{2,3},{3,2},{4,5},{5,4},{6,7},{7,6},{8,9},{9,8},{10,11... | collective-permute-start | bytes 5087240 | tf_op jit(solution)/shard_map/ppermute | solution.py:28
  194.5 86.7 %collective-permute-start.24 = (bf16[3,736,512]{2,1,0:T(8,128)(2,1)S(1)}, bf16[3,736,512]{2,1,0:T(8,128)(2,1)S(1)}, u32[]{:S(2)}, u32[]{:S(2)}) collective-permute-start(bf16[3,736,512]{2,1,0:T(8,128)(2,1)S(1)} %bitcast.198), channel_id=1, source_target_pairs={{0,1},{1,0},{2,3},{3,2},{4,5},{5,4},{6,7},{7,6},{8,9},{9,8},{10,11... | collective-permute-start | bytes 6782984 | tf_op jit(solution)/shard_map/ppermute | solution.py:28
  232.8 66.6 %collective-permute-start.16 = (bf16[3,368,384]{2,1,0:T(8,128)(2,1)S(1)}, bf16[3,368,384]{2,1,0:T(8,128)(2,1)S(1)}, u32[]{:S(2)}, u32[]{:S(2)}) collective-permute-start(bf16[3,368,384]{2,1,0:T(8,128)(2,1)S(1)} %slice.275), channel_id=1, source_target_pairs={{0,1},{1,0},{2,3},{3,2},{4,5},{5,4},{6,7},{7,6},{8,9},{9,8},{10,11... | collective-permute-start | bytes 2543624 | tf_op jit(solution)/shard_map/ppermute | solution.py:28
  234.5 65.0 %collective-permute-start.17 = (bf16[3,368,384]{2,1,0:T(8,128)(2,1)S(1)}, bf16[3,368,384]{2,1,0:T(8,128)(2,1)S(1)}, u32[]{:S(2)}, u32[]{:S(2)}) collective-permute-start(bf16[3,368,384]{2,1,0:T(8,128)(2,1)S(1)} %slice.276), channel_id=1, source_target_pairs={{0,4},{2,6},{4,0},{6,2},{8,12},{10,14},{12,8},{14,10},{16,20},{18,... | collective-permute-start | bytes 2543624 | tf_op jit(solution)/shard_map/ppermute | solution.py:23
  281.3 58.5 %collective-permute-start.25 = (bf16[3,368,512]{2,1,0:T(8,128)(2,1)S(1)}, bf16[3,368,512]{2,1,0:T(8,128)(2,1)S(1)}, u32[]{:S(2)}, u32[]{:S(2)}) collective-permute-start(bf16[3,368,512]{2,1,0:T(8,128)(2,1)S(1)} %slice.278), channel_id=1, source_target_pairs={{0,1},{1,0},{2,3},{3,2},{4,5},{5,4},{6,7},{7,6},{8,9},{9,8},{10,11... | collective-permute-start | bytes 3391496 | tf_op jit(solution)/shard_map/ppermute | solution.py:28
  282.9 56.8 %collective-permute-start.26 = (bf16[3,368,512]{2,1,0:T(8,128)(2,1)S(1)}, bf16[3,368,512]{2,1,0:T(8,128)(2,1)}, u32[]{:S(2)}, u32[]{:S(2)}) collective-permute-start(bf16[3,368,512]{2,1,0:T(8,128)(2,1)S(1)} %slice.279), channel_id=1, source_target_pairs={{0,4},{2,6},{4,0},{6,2},{8,12},{10,14},{12,8},{14,10},{16,20},{18,... | collective-permute-start | bytes 3391496 | tf_op jit(solution)/shard_map/ppermute | solution.py:23
  435.9 65.2 %collective-permute-start.45 = (bf16[3,368,384]{2,1,0:T(8,128)(2,1)}, bf16[3,368,384]{2,1,0:T(8,128)(2,1)}, u32[]{:S(2)}, u32[]{:S(2)}) collective-permute-start(bf16[3,368,384]{2,1,0:T(8,128)(2,1)} %get-tuple-element.80), channel_id=1, source_target_pairs={{0,4},{2,6},{4,0},{6,2},{8,12},{10,14},{12,8},{14,10},{16,20},{18,... | collective-permute-start | bytes 2543624 | tf_op jit(solution)/shard_map/ppermute | solution.py:23
  436.0 68.6 %collective-permute-start.47 = (bf16[3,368,384]{2,1,0:T(8,128)(2,1)}, bf16[3,368,384]{2,1,0:T(8,128)(2,1)}, u32[]{:S(2)}, u32[]{:S(2)}) collective-permute-start(bf16[3,368,384]{2,1,0:T(8,128)(2,1)} %get-tuple-element.82), channel_id=1, source_target_pairs={{0,1},{1,0},{2,3},{3,2},{4,5},{5,4},{6,7},{7,6},{8,9},{9,8},{10,11... | collective-permute-start | bytes 2543624 | tf_op jit(solution)/shard_map/ppermute | solution.py:28
  438.9 68.8 %collective-permute-start.52 = (bf16[3,368,512]{2,1,0:T(8,128)(2,1)}, bf16[3,368,512]{2,1,0:T(8,128)(2,1)}, u32[]{:S(2)}, u32[]{:S(2)}) collective-permute-start(bf16[3,368,512]{2,1,0:T(8,128)(2,1)} %get-tuple-element.85), channel_id=1, source_target_pairs={{0,4},{2,6},{4,0},{6,2},{8,12},{10,14},{12,8},{14,10},{16,20},{18,... | collective-permute-start | bytes 3391496 | tf_op jit(solution)/shard_map/ppermute | solution.py:23
  442.4 70.5 %collective-permute-start.54 = (bf16[3,368,512]{2,1,0:T(8,128)(2,1)}, bf16[3,368,512]{2,1,0:T(8,128)(2,1)}, u32[]{:S(2)}, u32[]{:S(2)}) collective-permute-start(bf16[3,368,512]{2,1,0:T(8,128)(2,1)} %get-tuple-element.87), channel_id=1, source_target_pairs={{0,1},{1,0},{2,3},{3,2},{4,5},{5,4},{6,7},{7,6},{8,9},{9,8},{10,11... | collective-permute-start | bytes 3391496 | tf_op jit(solution)/shard_map/ppermute | solution.py:28
  499.5 37.5 %collective-permute-start.29 = (bf16[2,2,384,512]{3,2,1,0:T(8,128)(2,1)}, bf16[2,2,384,512]{3,2,1,0:T(8,128)(2,1)S(1)}, u32[]{:S(2)}, u32[]{:S(2)}) collective-permute-start(bf16[2,2,384,512]{3,2,1,0:T(8,128)(2,1)} %get-tuple-element.71), channel_id=1, source_target_pairs={{0,1},{1,0},{2,3},{3,2},{4,5},{5,4},{6,7},{7,6},{8,9},{9,8},{10,11... | collective-permute-start | bytes 4718600 | tf_op jit(solution)/shard_map/ppermute | solution.py:28
  504.2 69.3 %collective-permute-start.46 = (bf16[3,736,384]{2,1,0:T(8,128)(2,1)}, bf16[3,736,384]{2,1,0:T(8,128)(2,1)}, u32[]{:S(2)}, u32[]{:S(2)}) collective-permute-start(bf16[3,736,384]{2,1,0:T(8,128)(2,1)} %pad_maximum_fusion.6), channel_id=1, source_target_pairs={{0,1},{1,0},{2,3},{3,2},{4,5},{5,4},{6,7},{7,6},{8,9},{9,8},{10,11... | collective-permute-start | bytes 5087240 | tf_op jit(solution)/shard_map/ppermute | solution.py:28
  507.6 65.8 %collective-permute-start.48 = (bf16[3,736,384]{2,1,0:T(8,128)(2,1)}, bf16[3,736,384]{2,1,0:T(8,128)(2,1)}, u32[]{:S(2)}, u32[]{:S(2)}) collective-permute-start(bf16[3,736,384]{2,1,0:T(8,128)(2,1)} %pad_maximum_fusion.7), channel_id=1, source_target_pairs={{0,4},{2,6},{4,0},{6,2},{8,12},{10,14},{12,8},{14,10},{16,20},{18,... | collective-permute-start | bytes 5087240 | tf_op jit(solution)/shard_map/ppermute | solution.py:23
  511.6 109.4 %collective-permute-start.53 = (bf16[3,736,512]{2,1,0:T(8,128)(2,1)}, bf16[3,736,512]{2,1,0:T(8,128)(2,1)S(1)}, u32[]{:S(2)}, u32[]{:S(2)}) collective-permute-start(bf16[3,736,512]{2,1,0:T(8,128)(2,1)} %pad_maximum_fusion.3), channel_id=1, source_target_pairs={{0,1},{1,0},{2,3},{3,2},{4,5},{5,4},{6,7},{7,6},{8,9},{9,8},{10,11... | collective-permute-start | bytes 6782984 | tf_op jit(solution)/shard_map/ppermute | solution.py:28
  516.0 109.1 %collective-permute-start.55 = (bf16[3,736,512]{2,1,0:T(8,128)(2,1)}, bf16[3,736,512]{2,1,0:T(8,128)(2,1)}, u32[]{:S(2)}, u32[]{:S(2)}) collective-permute-start(bf16[3,736,512]{2,1,0:T(8,128)(2,1)} %pad_maximum_fusion.4), channel_id=1, source_target_pairs={{0,4},{2,6},{4,0},{6,2},{8,12},{10,14},{12,8},{14,10},{16,20},{18,... | collective-permute-start | bytes 6782984 | tf_op jit(solution)/shard_map/ppermute | solution.py:23
  556.2 74.0 %collective-permute-start.35 = (bf16[2,1472,384]{2,1,0:T(8,128)(2,1)}, bf16[2,1472,384]{2,1,0:T(8,128)(2,1)}, u32[]{:S(2)}, u32[]{:S(2)}) collective-permute-start(bf16[2,1472,384]{2,1,0:T(8,128)(2,1)} %dynamic-slice_bitcast_fusion), channel_id=1, source_target_pairs={{0,2},{2,0},{4,6},{6,4},{8,10},{10,8},{12,14},{14,12},{16,18},{18,... | collective-permute-start | bytes 6782984 | tf_op jit(solution)/shard_map/ppermute | solution.py:23
  578.9 80.6 %collective-permute-start.49 = (bf16[3,184,384]{2,1,0:T(8,128)(2,1)}, bf16[3,184,384]{2,1,0:T(8,128)(2,1)}, u32[]{:S(2)}, u32[]{:S(2)}) collective-permute-start(bf16[3,184,384]{2,1,0:T(8,128)(2,1)} %get-tuple-element.152), channel_id=1, source_target_pairs={{0,8},{2,10},{4,12},{6,14},{8,0},{10,2},{12,4},{14,6},{16,24},{18,... | collective-permute-start | bytes 1271816 | tf_op jit(solution)/shard_map/ppermute | solution.py:23
  588.2 85.1 %collective-permute-start.50 = (bf16[3,184,384]{2,1,0:T(8,128)(2,1)}, bf16[3,184,384]{2,1,0:T(8,128)(2,1)}, u32[]{:S(2)}, u32[]{:S(2)}) collective-permute-start(bf16[3,184,384]{2,1,0:T(8,128)(2,1)} %get-tuple-element.153), channel_id=1, source_target_pairs={{0,16},{2,18},{4,20},{6,22},{8,24},{10,26},{12,28},{14,30},{16,0},... | collective-permute-start | bytes 1271816 | tf_op jit(solution)/shard_map/ppermute | solution.py:23
  621.0 53.6 %collective-permute-start.51 = (bf16[3,184,384]{2,1,0:T(8,128)(2,1)}, bf16[3,184,384]{2,1,0:T(8,128)(2,1)}, u32[]{:S(2)}, u32[]{:S(2)}) collective-permute-start(bf16[3,184,384]{2,1,0:T(8,128)(2,1)} %get-tuple-element.154), channel_id=1, source_target_pairs={{0,24},{2,26},{4,28},{6,30},{8,16},{10,18},{12,20},{14,22},{16,8},... | collective-permute-start | bytes 1271816 | tf_op jit(solution)/shard_map/ppermute | solution.py:23
  659.5 34.8 %collective-permute-start.56 = (bf16[3,184,512]{2,1,0:T(8,128)(2,1)}, bf16[3,184,512]{2,1,0:T(8,128)(2,1)}, u32[]{:S(2)}, u32[]{:S(2)}) collective-permute-start(bf16[3,184,512]{2,1,0:T(8,128)(2,1)} %get-tuple-element.140), channel_id=1, source_target_pairs={{0,8},{2,10},{4,12},{6,14},{8,0},{10,2},{12,4},{14,6},{16,24},{18,... | collective-permute-start | bytes 1695752 | tf_op jit(solution)/shard_map/ppermute | solution.py:23
  668.6 41.1 %collective-permute-start.57 = (bf16[3,184,512]{2,1,0:T(8,128)(2,1)}, bf16[3,184,512]{2,1,0:T(8,128)(2,1)}, u32[]{:S(2)}, u32[]{:S(2)}) collective-permute-start(bf16[3,184,512]{2,1,0:T(8,128)(2,1)} %get-tuple-element.141), channel_id=1, source_target_pairs={{0,16},{2,18},{4,20},{6,22},{8,24},{10,26},{12,28},{14,30},{16,0},... | collective-permute-start | bytes 1695752 | tf_op jit(solution)/shard_map/ppermute | solution.py:23
  669.5 40.2 %collective-permute-start.58 = (bf16[3,184,512]{2,1,0:T(8,128)(2,1)S(1)}, bf16[3,184,512]{2,1,0:T(8,128)(2,1)}, u32[]{:S(2)}, u32[]{:S(2)}) collective-permute-start(bf16[3,184,512]{2,1,0:T(8,128)(2,1)S(1)} %get-tuple-element.142), channel_id=1, source_target_pairs={{0,24},{2,26},{4,28},{6,30},{8,16},{10,18},{12,20},{14,22},{16,8},... | collective-permute-start | bytes 1695752 | tf_op jit(solution)/shard_map/ppermute | solution.py:23
  674.6 54.1 %collective-permute-start.37 = (bf16[1,736,384]{2,1,0:T(8,128)(2,1)}, bf16[1,736,384]{2,1,0:T(8,128)(2,1)S(1)}, u32[]{:S(2)}, u32[]{:S(2)}) collective-permute-start(bf16[1,736,384]{2,1,0:T(8,128)(2,1)} %pad_maximum_fusion.10), channel_id=1, source_target_pairs={{0,1},{1,0},{2,3},{3,2},{4,5},{5,4},{6,7},{7,6},{8,9},{9,8},{10,11... | collective-permute-start | bytes 1695752 | tf_op jit(solution)/shard_map/ppermute | solution.py:28
  675.1 53.6 %collective-permute-start.39 = (bf16[1,736,384]{2,1,0:T(8,128)(2,1)}, bf16[1,736,384]{2,1,0:T(8,128)(2,1)}, u32[]{:S(2)}, u32[]{:S(2)}) collective-permute-start(bf16[1,736,384]{2,1,0:T(8,128)(2,1)} %pad_maximum_fusion.11), channel_id=1, source_target_pairs={{0,4},{2,6},{4,0},{6,2},{8,12},{10,14},{12,8},{14,10},{16,20},{18,... | collective-permute-start | bytes 1695752 | tf_op jit(solution)/shard_map/ppermute | solution.py:23
  (64 other events, 948.3 us)

commit v3 on v2

v3 whole, which is shorter than its diff:
```python
import functools

import jax
import jax.numpy as jnp
from jax import lax
from jax.experimental import pallas as pl
from jax.experimental.pallas import tpu as pltpu
from jax.sharding import PartitionSpec as P

EPSILON = 1e-06
TOP_PRECISION = lax.Precision.HIGHEST
GELU_SCALE = 0.7978845608028654
GELU_CUBE = 0.044715
BF16 = jnp.bfloat16
F32 = jnp.float32
NEGATIVE = -1e30
VMEM_BYTES = 60 * 1024 * 1024
LANES = 128
COST_SHARE = 0.05


DP = ("chip", "core")


def dp_size():
    return lax.axis_size("chip") * lax.axis_size("core")


def swap_dp(array, mask):
    return lax.ppermute(array, DP, [(i, i ^ mask) for i in range(dp_size())])


def swap_mp(array, mask):
    count = lax.axis_size("mp")
    return lax.ppermute(array, "mp", [(i, i ^ mask) for i in range(count)])


def pick(array, index, axis):
    return lax.dynamic_index_in_dim(array, index, axis, keepdims=False)


def add_low(*terms):
    total = terms[0].astype(F32)
    for term in terms[1:]:
        total = total + term.astype(F32)
    return total.astype(BF16)


def first_of(parts):
    return parts[0] if isinstance(parts, tuple) else parts


def either(flag, first, second):
    return jnp.where(flag == 0, first, second)


def hold(value, *tokens):
    return lax.optimization_barrier((value, *tokens))[0] if tokens else value


def z_masks():
    masks, mask = [], dp_size() // 2
    while mask > 2:
        masks.append(mask)
        mask //= 2
    return masks


def x_masks():
    return range(1, lax.axis_size("mp"))


def merged(parts):
    kinds, rows, columns = parts[0].shape
    return jnp.stack(parts, axis=1).reshape(kinds, len(parts) * rows, columns)


def gather_xy(own, first=(), then=()):
    own = hold(own, *first)
    return hold((swap_dp(own, 2), [swap_mp(own, k) for k in x_masks()]), *then)


def gather_corner(over_y, over_x, first=(), then=()):
    half = over_y.shape[1] // 2
    low = hold(rows_of(over_y, 0, half), *first)
    result = []
    for k, other in zip(x_masks(), over_x):
        high = hold(rows_of(other, half, half), *first)
        result.append((swap_mp(low, k), swap_dp(high, 2)))
    return hold(result, *then)


def quads_of(own, over_y, over_x, corner):
    return [(own, over_y)] + [(other, *parts) for other, parts in zip(over_x, corner)]


def scatter_corner(quads, first=(), then=()):
    own, to_y = quads[0]
    got = []
    for k, (_, low, high) in zip(x_masks(), quads[1:]):
        got.append((swap_mp(hold(low, *first), k), swap_dp(hold(high, *first), 2)))
    got = hold(got, *then)
    if len(got) == 1:
        to_y, to_x = add_corner(to_y, got[0][0], quads[1][0], got[0][1])
        return own, to_y, [to_x]
    half = own.shape[1] // 2
    low = add_low(to_y[:, :half], *[part for part, _ in got])
    to_x = [
        jnp.concatenate([parts[0][:, :half], add_low(parts[0][:, half:], part)], axis=1)
        for parts, (_, part) in zip(quads[1:], got)
    ]
    return own, jnp.concatenate([low, to_y[:, half:]], axis=1), to_x


def scatter_xy(own, to_y, to_x, then=()):
    got = [swap_dp(to_y, 2)] + [swap_mp(other, k) for k, other in zip(x_masks(), to_x)]
    return sum_rows([own, *hold(got, *then)], 2)


def scatter_z(pair, stage, then=()):
    masks = z_masks()
    mask = masks[len(masks) - 1 - stage]
    got = hold(swap_dp(pair[1], mask), *then)
    return sum_rows([pair[0], got], 1 if stage == len(masks) - 1 else 2)


def sum_all(values, late):
    mask = 1
    while mask < lax.axis_size("mp"):
        values = values + swap_mp(values, mask)
        mask *= 2
    mask = 1
    while mask < dp_size():
        values = values + swap_dp(hold(values, *late) if mask > 2 else values, mask)
        mask *= 2
    return values


def call(
    kernel, name, grid, in_specs, out_specs, out_shape, operands, flops=0, scratch=(), scalars=0, after=(),
    aliases=None,
):
    moved = sum(a.size * a.dtype.itemsize for a in operands)
    moved += sum(s.size * s.dtype.itemsize for s in out_shape)
    count = len(operands)

    def run(*refs):
        kernel(*refs[:count], *refs[count + len(after) :])

    return pl.pallas_call(
        run,
        grid_spec=pltpu.PrefetchScalarGridSpec(
            num_scalar_prefetch=scalars,
            grid=grid,
            in_specs=list(in_specs) + [pl.BlockSpec(memory_space=pl.ANY)] * len(after),
            out_specs=out_specs,
            scratch_shapes=list(scratch),
        ),
        out_shape=out_shape,
        input_output_aliases=aliases or {},
        compiler_params=pltpu.CompilerParams(vmem_limit_bytes=VMEM_BYTES),
        cost_estimate=pl.CostEstimate(
            flops=int(flops * COST_SHARE),
            bytes_accessed=int(moved * COST_SHARE),
            transcendentals=0,
        ),
        name=name,
    )(*operands, *after)


def whole(shape):
    return pl.BlockSpec(shape, lambda *_: (0,) * len(shape), pipeline_mode=pl.Buffered(1))


def slab(*shape):
    return pl.BlockSpec((1,) + shape, lambda m, *_: (m,) + (0,) * len(shape))


def columns(wide, step):
    return pl.BlockSpec((wide, step), lambda j, *_: (0, j))


def lane_step(length):
    return 256 if length % 256 == 0 else length


def dot_nn(left, right):
    return lax.dot_general(left, right, (((1,), (0,)), ((), ())), preferred_element_type=F32)


def dot_tn(left, right):
    return lax.dot_general(left, right, (((0,), (0,)), ((), ())), preferred_element_type=F32)


def dot_nt(left, right):
    return lax.dot_general(left, right, (((1,), (1,)), ((), ())), preferred_element_type=F32)


def transposed(value):
    return jnp.transpose(value.astype(F32), (1, 0)).astype(BF16)


def block_of(place, position, depth):
    z, y = place // 2, place % 2
    masks, left, mask = 0, position % depth, depth
    while mask > 1:
        mask //= 2
        masks += mask * (left % 2)
        left //= 2
    return (z ^ masks) * 2 + (y ^ (position // depth))


def reorder_kernel(outward, info_ref, in_ref, out_ref):
    blocks = out_ref.shape[0]
    for p in range(blocks):
        chip = block_of(info_ref[0], p, blocks // 2)
        if outward:
            out_ref[chip] = in_ref[0, p]
        else:
            out_ref[p] = in_ref[0, chip]


def reorder(array, group, place, blocks, outward, after=()):
    groups, wide, length = array.shape
    split = array.reshape(groups, blocks, wide // blocks, length)
    return call(
        functools.partial(reorder_kernel, outward),
        "reorder",
        (1,),
        [pl.BlockSpec((1,) + split.shape[1:], lambda *_: (group, 0, 0, 0))],
        [pl.BlockSpec(split.shape[1:], lambda *_: (0, 0, 0))],
        [jax.ShapeDtypeStruct(split.shape[1:], array.dtype)],
        [place, split],
        scalars=1,
        after=after,
    )[0].reshape(wide, length)


def bias_kernel(window_ref, table_ref):
    count, block = table_ref.shape[1], table_ref.shape[-1]
    for entry in range(count):
        wide = jnp.broadcast_to(window_ref[0, entry], (block, 2 * block))
        rolled = pltpu.roll(wide, block + 1, 1, stride=1, stride_axis=0)
        table_ref[0, entry] = rolled[:, :block]


def bias_table(windows, block, after):
    heads, count = windows.shape[:2]
    return call(
        bias_kernel,
        "bias_table",
        (heads,),
        [slab(count, 1, 2 * block)],
        [slab(count, block, block)],
        [jax.ShapeDtypeStruct((heads, count, block, block), F32)],
        [windows],
        after=after,
    )[0]


def project_kernel(counts, limit, info_ref, x_ref, gain_ref, *refs):
    matrices, (normed_ref, out_ref, kv_ref) = split_refs(refs, counts)
    first = kv_ref.shape[0] // 2
    values = x_ref[...].astype(F32)
    factor = lax.rsqrt(jnp.mean(values * values, axis=0, keepdims=True) + EPSILON)
    normed = (values * factor * gain_ref[...]).astype(BF16)
    normed_ref[...] = normed
    for r, parts in enumerate(matrices):
        place = info_ref[0] ^ r

        @pl.when(place < limit)
        def _(parts=parts, place=place):
            weights = joined([ref[0] for ref in parts], 0)
            product = dot_tn(weights, normed).astype(BF16)
            out_ref[place] = product

            @pl.when(place >= first)
            def _():
                kv_ref[place - first] = product


def project(place, x, gain, matrices, after):
    wide, length = x.shape
    part = matrices[0][0].shape[2]
    limit = len(matrices) * 3 // 4
    step = lane_step(length)
    counts = [len(parts) for parts in matrices]
    flat = [ref for parts in matrices for ref in parts]
    return call(
        functools.partial(project_kernel, counts, limit),
        "project",
        (length // step,),
        [columns(wide, step), whole((wide, 1))] + [whole(ref.shape) for ref in flat],
        [
            columns(wide, step),
            pl.BlockSpec((len(matrices), part, step), lambda j, *_: (0, 0, j)),
            pl.BlockSpec((len(matrices) // 2, part, step), lambda j, *_: (0, 0, j)),
        ],
        [
            jax.ShapeDtypeStruct((wide, length), BF16),
            jax.ShapeDtypeStruct((len(matrices), part, length), BF16),
            jax.ShapeDtypeStruct((len(matrices) // 2, part, length), BF16),
        ],
        [place, x, gain, *flat],
        flops=2 * wide * length * limit * part,
        scalars=1,
        after=after,
    )


def assemble_kernel(counts, info_ref, *refs):
    matrices, (out_ref,) = split_refs(refs, counts)
    for r, parts in enumerate(matrices):
        place, row = info_ref[0] ^ r, 0
        for ref in parts:
            rows = ref.shape[1]
            out_ref[place, row : row + rows] = ref[0]
            row += rows


def assemble(place, matrices, inner, after):
    part = matrices[0][0].shape[2]
    counts = [len(parts) for parts in matrices]
    flat = [ref for parts in matrices for ref in parts]
    wide = sum(ref.shape[1] for ref in matrices[0])
    shape = (len(matrices), wide, part)
    ordered = call(
        functools.partial(assemble_kernel, counts),
        "assemble",
        (1,),
        [whole(ref.shape) for ref in flat],
        [pl.BlockSpec(shape, lambda *_: (0, 0, 0))],
        [jax.ShapeDtypeStruct(shape, BF16)],
        [place, *flat],
        scalars=1,
        after=after,
    )[0]
    return jnp.transpose(ordered.reshape(4, inner // part, wide, part), (0, 2, 1, 3)).reshape(
        4, wide, inner
    )


def middle_kernel(x_ref, context_ref, w_ref, gain_ref, normed_ref):
    values = x_ref[...].astype(F32) + dot_nn(w_ref[0], context_ref[...])
    factor = lax.rsqrt(jnp.mean(values * values, axis=0, keepdims=True) + EPSILON)
    normed_ref[...] = (values * factor * gain_ref[...]).astype(BF16)


def out_weights(weights):
    return pl.BlockSpec(
        (1,) + weights.shape[1:], lambda *_: (3, 0, 0), pipeline_mode=pl.Buffered(1)
    )


def middle_layer(x, context, weights, gain, after):
    wide, length = x.shape
    inner = weights.shape[2]
    step = lane_step(length)
    return call(
        middle_kernel,
        "middle",
        (length // step,),
        [columns(wide, step), columns(inner, step), out_weights(weights), whole((wide, 1))],
        [columns(wide, step)],
        [jax.ShapeDtypeStruct((wide, length), BF16)],
        [x, context, weights, gain],
        flops=2 * wide * length * inner,
        after=after,
    )[0]


def lifted_grads(values, gain, grad):
    factor = lax.rsqrt(jnp.mean(values * values, axis=0, keepdims=True) + EPSILON)
    scaled = values * factor
    lifted = grad * gain
    inner = jnp.mean(lifted * scaled, axis=0, keepdims=True)
    return factor * (lifted - scaled * inner), jnp.sum(grad * scaled, axis=1, keepdims=True)


def add_up(ref, value):
    first = pl.program_id(0) == 0

    @pl.when(first)
    def _():
        ref[...] = value

    @pl.when(jnp.logical_not(first))
    def _():
        ref[...] += value


def turn_kernel(
    x_ref, context_ref, cot_ref, back0_ref, back1_ref, gain_ref, w_ref, low_ref, grad_ref, gain_grad_ref
):
    middle = x_ref[...].astype(F32) + dot_nn(w_ref[0], context_ref[...])
    grad = back0_ref[0].astype(F32) + back1_ref[0].astype(F32)
    normed_grad, gain_grad = lifted_grads(middle, gain_ref[...], grad)
    add_up(gain_grad_ref, gain_grad)
    low = (cot_ref[...].astype(F32) + normed_grad).astype(BF16)
    low_ref[...] = low
    grad_ref[...] = dot_tn(w_ref[0], low).astype(BF16)


def turn(group, x, context, cot, back, gain, weights, after):
    wide, length = x.shape
    inner = weights.shape[2]
    step = lane_step(length)
    big = columns(wide, step)
    part = pl.BlockSpec((1, wide, step), lambda j, *_: (group, 0, j))
    return call(
        turn_kernel,
        "turn",
        (length // step,),
        [big, columns(inner, step), big, part, part, whole((wide, 1)), out_weights(weights)],
        [big, columns(inner, step), pl.BlockSpec((wide, 1), lambda *_: (0, 0))],
        [
            jax.ShapeDtypeStruct((wide, length), BF16),
            jax.ShapeDtypeStruct((inner, length), BF16),
            jax.ShapeDtypeStruct((wide, 1), F32),
        ],
        [x, context, cot, *back, gain, weights],
        flops=4 * wide * length * inner,
        after=after,
    )


def put_blocks(info_ref, out_ref, values):
    if len(out_ref.shape) == 3:
        out_ref[0] = values.astype(out_ref.dtype)
        return
    blocks, rows = out_ref.shape[1:3]
    for p in range(blocks):
        chip = block_of(info_ref[0], p, blocks // 2)
        out_ref[0, chip] = values[p * rows : (p + 1) * rows].astype(out_ref.dtype)


def outward_spec(groups, wide, length, blocks, step):
    rows, steps = wide // blocks, length // step
    if rows % 8:
        spec = pl.BlockSpec((1, wide, step), lambda j, *_: (j // steps, 0, j % steps))
        return spec, jax.ShapeDtypeStruct((groups, wide, length), BF16)
    return (
        pl.BlockSpec((1, blocks, rows, step), lambda j, *_: (j // steps, 0, 0, j % steps)),
        jax.ShapeDtypeStruct((groups, blocks, rows, length), BF16),
    )


def outward(array, place, blocks):
    if array.ndim == 4:
        return array.reshape(array.shape[0], -1, array.shape[3])
    return jnp.stack([reorder(array, m, place, blocks, True) for m in range(array.shape[0])])


def group_columns(group, steps, *shape):
    def index(j, *_):
        return (0,) * (len(shape) - 1) + (jnp.clip(j - group * steps, 0, steps - 1),)

    return pl.BlockSpec(shape, index)


def in_groups(kernel, counts, steps, *refs):
    lead, each, groups = counts
    group = pl.program_id(0) // steps
    shared, rest = refs[:lead], refs[lead:]
    parts, tail = rest[: each * groups], rest[each * groups :]
    for m in range(groups):

        @pl.when(group == m)
        def _(m=m):
            kernel(*shared, *parts[each * m : each * (m + 1)], *tail)


def finish_kernel(info_ref, x_ref, context_ref, ffn0_ref, ffn1_ref, w_ref, out_ref):
    middle = x_ref[...].astype(F32) + dot_nn(w_ref[0], context_ref[...])
    total = middle + (ffn0_ref[0].astype(F32) + ffn1_ref[0].astype(F32))
    put_blocks(info_ref, out_ref, total)


def finish(place, terms, ffn, weights, blocks, after):
    wide, length = terms[0][0].shape
    inner = weights.shape[2]
    step = lane_step(length)
    groups, steps = len(terms), length // step
    spec, shape = outward_spec(groups, wide, length, blocks, step)
    specs = []
    for m in range(groups):
        specs += [group_columns(m, steps, wide, step), group_columns(m, steps, inner, step)]
    part = pl.BlockSpec((1, wide, step), lambda j, *_: (j // steps, 0, j % steps))
    result = call(
        functools.partial(in_groups, finish_kernel, (1, 2, groups), steps),
        "finish",
        (groups * steps,),
        specs + [part, part, out_weights(weights)],
        [spec],
        [shape],
        [place, *[array for term in terms for array in term], *ffn, weights],
        flops=2 * groups * wide * length * inner,
        scalars=1,
        after=after,
    )[0]
    return outward(result, place, blocks)


def outer_kernel(count, info_ref, *refs):
    out_ref = refs[-1]
    step = pl.program_id(0)
    for r in range(len(refs) // (2 * count)):
        pairs = refs[2 * count * r : 2 * count * (r + 1)]

        @pl.when(step == r)
        def _(pairs=pairs):
            total = dot_nt(pairs[0][...], matrix_of(pairs[1]))
            for m in range(1, count):
                total = total + dot_nt(pairs[2 * m][...], matrix_of(pairs[2 * m + 1]))
            out_ref[0] = total.astype(BF16)


def matrix_of(ref):
    return ref[0] if len(ref.shape) == 3 else ref[...]


def outer_products(place, roles, matrices, into, after):
    count = len(matrices[0])
    wide, length = matrices[0][0][0].shape
    low, high = roles
    operands, specs = [], []
    for left, right in [pair for pairs in matrices for pair in pairs]:
        right, number = right if isinstance(right, tuple) else (right, None)
        inner = right.shape[-2]
        operands += [left, right]
        specs.append(whole(left.shape))
        if number is None:
            specs.append(whole(right.shape))
        else:
            specs.append(
                pl.BlockSpec(
                    (1, inner, length),
                    lambda *_, n=number: (n, 0, 0),
                    pipeline_mode=pl.Buffered(1),
                )
            )

    def index(step, info):
        return (jnp.where(step == 0, low, high) ^ info[0], 0, 0)

    if into is not None:
        operands.append(into)
        specs.append(pl.BlockSpec(memory_space=pl.ANY))

    def kernel(info_ref, *refs):
        if into is not None:
            refs = refs[:-2] + refs[-1:]
        outer_kernel(count, info_ref, *refs)

    return call(
        kernel,
        "outer_products",
        (len(matrices),),
        specs,
        [pl.BlockSpec((1, wide, inner), index)],
        [jax.ShapeDtypeStruct((4, wide, inner), BF16)],
        [place, *operands],
        flops=2 * wide * inner * length * count * len(matrices),
        scalars=1,
        after=after,
        aliases=None if into is None else {len(operands): 0},
    )[0]


def input_kernel(info_ref, x_ref, low_ref, dq_ref, dkv_ref, gain_ref, w_ref, out_ref, gain_grad_ref):
    grad = (
        dot_nn(w_ref[0], dq_ref[...]) + dot_nn(w_ref[1], dkv_ref[0]) + dot_nn(w_ref[2], dkv_ref[1])
    )
    normed_grad, gain_grad = lifted_grads(x_ref[...].astype(F32), gain_ref[...], grad)
    add_up(gain_grad_ref, gain_grad)
    put_blocks(info_ref, out_ref, low_ref[...].astype(F32) + normed_grad)


def input_grads(place, terms, gain, weights, blocks, after):
    wide, length = terms[0][0].shape
    inner = weights.shape[2]
    step = lane_step(length)
    groups, steps = len(terms), length // step
    spec, shape = outward_spec(groups, wide, length, blocks, step)
    specs = []
    for m in range(groups):
        big = group_columns(m, steps, wide, step)
        specs += [big, big, group_columns(m, steps, inner, step), group_columns(m, steps, 2, inner, step)]
    result, gain_grads = call(
        functools.partial(in_groups, input_kernel, (1, 4, groups), steps),
        "input_grads",
        (groups * steps,),
        specs
        + [
            whole((wide, 1)),
            pl.BlockSpec((3,) + weights.shape[1:], lambda *_: (0, 0, 0), pipeline_mode=pl.Buffered(1)),
        ],
        [spec, pl.BlockSpec((wide, 1), lambda *_: (0, 0))],
        [shape, jax.ShapeDtypeStruct((wide, 1), F32)],
        [place, *[array for term in terms for array in term], gain, weights],
        flops=6 * groups * wide * length * inner,
        scalars=1,
        after=after,
    )
    return outward(result, place, blocks), gain_grads


def rows_kernel(in_ref, out_ref):
    out_ref[...] = in_ref[...]


def rows_of(array, start, rows):
    kinds, _, width = array.shape
    if rows % 16:
        return array[:, start : start + rows]
    return call(
        rows_kernel,
        "rows",
        (kinds,),
        [pl.BlockSpec((1, rows, width), lambda k: (k, start // rows, 0))],
        [pl.BlockSpec((1, rows, width), lambda k: (k, 0, 0))],
        [jax.ShapeDtypeStruct((kinds, rows, width), array.dtype)],
        [array],
    )[0]


def merge_kernel(first_ref, second_ref, out_ref):
    parts = [first_ref[0].astype(F32), second_ref[0].astype(F32)]
    out_ref[0] = jnp.concatenate(parts, axis=0).astype(out_ref.dtype)


def merge(first, second):
    kinds, rows, width = first.shape
    if rows % 8:
        return jnp.concatenate([first, second], axis=1)
    return call(
        merge_kernel,
        "merge",
        (kinds,),
        [slab(rows, width), slab(rows, width)],
        [slab(2 * rows, width)],
        [jax.ShapeDtypeStruct((kinds, 2 * rows, width), first.dtype)],
        [first, second],
    )[0]


def sum_kernel(count, *refs):
    total = refs[0][0].astype(F32)
    for ref in refs[1:count]:
        total = total + ref[0].astype(F32)
    row = 0
    for ref in refs[count:]:
        rows = ref.shape[1]
        ref[0] = total[row : row + rows].astype(BF16)
        row += rows


def sum_rows(terms, parts, starts=None, kinds=None, after=()):
    starts = starts or [0] * len(terms)
    kinds = kinds or terms[0].shape[0]
    rows, width = terms[0].shape[1:]
    sizes = [rows // parts] * parts if isinstance(parts, int) else list(parts)
    if sizes[0] % 8:
        total = add_low(*[term[a : a + kinds] for term, a in zip(terms, starts)])
        results, row = [], 0
        for size in sizes:
            results.append(total[:, row : row + size])
            row += size
    else:
        results = call(
            functools.partial(sum_kernel, len(terms)),
            "sum_rows",
            (kinds,),
            [pl.BlockSpec((1, rows, width), lambda k, a=a: (a + k, 0, 0)) for a in starts],
            [slab(size, width) for size in sizes],
            [jax.ShapeDtypeStruct((kinds, size, width), BF16) for size in sizes],
            terms,
            after=after,
        )
    return results[0] if len(sizes) == 1 else tuple(results)


def corner_kernel(y_ref, first_ref, x_ref, second_ref, y_out, x_out):
    y_out[...] = (y_ref[...].astype(F32) + first_ref[...].astype(F32)).astype(BF16)
    x_out[...] = (x_ref[...].astype(F32) + second_ref[...].astype(F32)).astype(BF16)


def add_corner(to_y, first, to_x, second):
    kinds, half, width = first.shape
    upper = pl.BlockSpec((1, half, width), lambda k: (k, 0, 0))
    lower = pl.BlockSpec((1, half, width), lambda k: (k, 1, 0))
    return call(
        corner_kernel,
        "add_corner",
        (kinds,),
        [upper, upper, lower, upper],
        [upper, lower],
        [jax.ShapeDtypeStruct(to_y.shape, BF16), jax.ShapeDtypeStruct(to_x.shape, BF16)],
        [to_y, first, to_x, second],
        aliases={0: 0, 2: 1},
    )


def halves(value_t, half):
    zero = jnp.zeros((half, value_t.shape[1]), value_t.dtype)
    return (
        jnp.concatenate([value_t[:half], zero], axis=0),
        jnp.concatenate([zero, value_t[half:]], axis=0),
    )


def attend_kernel(sources, block, half, info_ref, q_ref, *refs):
    kv_refs = refs[: 2 * sources]
    segq_ref, segk_ref, table_ref, ctx_ref, lse_ref = refs[2 * sources : 2 * sources + 5]
    s_scr, m_scr, l_scr, acc_scr, k_scr = refs[2 * sources + 5 :]
    length = q_ref.shape[1]
    q_blocks = length // block
    k_blocks = q_blocks * sources
    place_x = info_ref[0]
    for s in range(sources):
        k_scr[s * length : (s + 1) * length, :] = transposed(kv_refs[2 * s][...])
    for qb in range(q_blocks):
        rows = pl.ds(qb * block, block)
        q_heads = halves(q_ref[:, rows], half)
        seg_q = segq_ref[:, rows]
        m_scr[...] = jnp.full(m_scr.shape, NEGATIVE, F32)
        l_scr[...] = jnp.zeros(l_scr.shape, F32)
        acc_scr[...] = jnp.zeros(acc_scr.shape, F32)
        for kb in range(k_blocks):
            s, lb = divmod(kb, q_blocks)
            live = info_ref[1 + qb * k_blocks + kb]

            @pl.when(live != 0)
            def _(s=s, lb=lb, kb=kb):
                entry = k_blocks - 1 - ((place_x ^ s) * q_blocks + lb - place_x * q_blocks - qb)
                keys = k_scr[pl.ds(kb * block, block), :]
                kept = segk_ref[pl.ds(kb * block, block), :] == seg_q
                for h in range(2):
                    score = dot_nn(keys, q_heads[h]) + table_ref[h, entry]
                    score = jnp.where(kept, score, NEGATIVE)
                    s_scr[h, kb] = score
                    m_scr[h] = jnp.maximum(m_scr[h], jnp.max(score, axis=0, keepdims=True))

        for kb in range(k_blocks):
            s, lb = divmod(kb, q_blocks)
            live = info_ref[1 + qb * k_blocks + kb]

            @pl.when(live != 0)
            def _(s=s, lb=lb, kb=kb):
                for h in range(2):
                    prob = jnp.exp(s_scr[h, kb] - m_scr[h])
                    l_scr[h] += jnp.sum(prob, axis=0, keepdims=True)
                    values_t = kv_refs[2 * s + 1][
                        h * half : (h + 1) * half, lb * block : (lb + 1) * block
                    ]
                    acc_scr[h * half : (h + 1) * half] += dot_nn(values_t, prob.astype(BF16))

        for h in range(2):
            lse_ref[0, h : h + 1, rows] = m_scr[h] + jnp.log(l_scr[h])
            ctx_ref[h * half : (h + 1) * half, rows] = (
                acc_scr[h * half : (h + 1) * half] / l_scr[h]
            ).astype(BF16)


def grad_kernel(sources, block, half, info_ref, q_ref, *refs):
    kv_refs = refs[: 2 * sources]
    refs = refs[2 * sources :]
    segq_ref, segk_ref, table_ref, ctx_ref, lse_ref, gctx_ref = refs[:6]
    dq_ref, gbias_ref = refs[6:8]
    dkv_refs = refs[8 : 8 + sources]
    dk_scr, dv_scr, dq_scr, k_scr, v_scr, db_scr = refs[8 + sources :]
    length = q_ref.shape[1]
    q_blocks = length // block
    k_blocks = q_blocks * sources
    place_x = info_ref[0]
    lane = lax.broadcasted_iota(jnp.int32, (block, 2 * half), 1)

    db_scr[...] = jnp.zeros(db_scr.shape, F32)
    for s in range(sources):
        k_scr[s * length : (s + 1) * length, :] = transposed(kv_refs[2 * s][...])
        v_scr[s * length : (s + 1) * length, :] = transposed(kv_refs[2 * s + 1][...])
    dk_scr[...] = jnp.zeros(dk_scr.shape, F32)
    dv_scr[...] = jnp.zeros(dv_scr.shape, F32)
    for qb in range(q_blocks):
        rows = pl.ds(qb * block, block)
        query_t = q_ref[:, rows]
        grad_out_t = gctx_ref[:, rows]
        product = grad_out_t.astype(F32) * ctx_ref[:, rows].astype(F32)
        deltas = (
            jnp.sum(product[:half], axis=0, keepdims=True),
            jnp.sum(product[half:], axis=0, keepdims=True),
        )
        q_heads = halves(query_t, half)
        g_heads = halves(grad_out_t, half)
        query, grad_out = transposed(query_t), transposed(grad_out_t)
        zero = jnp.zeros(query.shape, BF16)
        q_lanes = (jnp.where(lane < half, query, zero), jnp.where(lane < half, zero, query))
        g_lanes = (
            jnp.where(lane < half, grad_out, zero),
            jnp.where(lane < half, zero, grad_out),
        )
        seg_q = segq_ref[:, rows]
        dq_scr[...] = jnp.zeros(dq_scr.shape, F32)
        for kb in range(k_blocks):
            s, lb = divmod(kb, q_blocks)
            live = info_ref[1 + qb * k_blocks + kb]

            @pl.when(live != 0)
            def _(s=s, lb=lb, kb=kb):
                entry = k_blocks - 1 - ((place_x ^ s) * q_blocks + lb - place_x * q_blocks - qb)
                key_rows = pl.ds(kb * block, block)
                keys = k_scr[key_rows, :]
                values = v_scr[key_rows, :]
                kept = segk_ref[key_rows, :] == seg_q
                key_grad = dk_scr[key_rows, :]
                value_grad = dv_scr[key_rows, :]
                for h in range(2):
                    score = dot_nn(keys, q_heads[h]) + table_ref[h, entry]
                    score = jnp.where(kept, score, NEGATIVE)
                    prob = jnp.exp(score - lse_ref[0, h : h + 1, rows])
                    grad_prob = dot_nn(values, g_heads[h])
                    grad_score = prob * (grad_prob - deltas[h])
                    db_scr[h, s, q_blocks - 1 - lb + qb] += grad_score
                    low = grad_score.astype(BF16)
                    key_grad = key_grad + dot_nn(low, q_lanes[h])
                    value_grad = value_grad + dot_nn(prob.astype(BF16), g_lanes[h])
                    keys_t = kv_refs[2 * s][
                        h * half : (h + 1) * half, lb * block : (lb + 1) * block
                    ]
                    dq_scr[h * half : (h + 1) * half] += dot_nn(keys_t, low)
                dk_scr[key_rows, :] = key_grad
                dv_scr[key_rows, :] = value_grad

        dq_ref[:, rows] = dq_scr[...].astype(BF16)
    for s in range(sources):
        rows = slice(s * length, (s + 1) * length)
        dkv_refs[s][0] = jnp.transpose(dk_scr[rows, :], (1, 0)).astype(BF16)
        dkv_refs[s][1] = jnp.transpose(dv_scr[rows, :], (1, 0)).astype(BF16)

    for h in range(2):
        for s in range(sources):
            for n in range(2 * q_blocks - 1):
                gbias_ref[h, s, n] = diagonal_sums(db_scr[h, s, n])


def diagonal_sums(tile):
    block = tile.shape[0]
    count = block
    if block == 2 * LANES:
        zero = jnp.zeros((LANES, LANES), F32)
        tile = jnp.concatenate(
            [
                tile[LANES:, :LANES],
                tile[LANES:, LANES:] + tile[:LANES, :LANES],
                tile[:LANES, LANES:],
                zero,
            ],
            axis=1,
        )
        count = LANES
    else:
        tile = jnp.concatenate([tile, jnp.zeros_like(tile)], axis=1)
    while count > 8:
        count //= 2
        tile = pltpu.roll(tile[:count], count, 1) + tile[count:]
    return tile


def attention_specs(sources, length, block, pairs, width):
    k_blocks = length * sources // block
    entries = 2 * k_blocks - 1

    def rows(offset):
        return pl.BlockSpec((width, length), lambda p, info: (p + offset, 0))

    kv_specs = [rows(pairs), rows(2 * pairs)] + [rows(0), rows(pairs)] * (sources - 1)
    seg_specs = [whole((1, length)), whole((length * sources, 1))]
    table_spec = pl.BlockSpec((2, entries, block, block), lambda p, info: (p, 0, 0, 0))
    lse_spec = pl.BlockSpec((1, 8, length), lambda p, info: (p, 0, 0))
    return k_blocks, entries, rows, kv_specs, seg_specs, table_spec, lse_spec


def attend(info, qkv, others, seg_q, seg_k, table, block, head_size, inner, after):
    length = qkv.shape[1]
    sources = 1 + len(others)
    width = 2 * head_size
    pairs = inner // width
    k_blocks, entries, rows, kv_specs, seg_specs, table_spec, lse_spec = attention_specs(
        sources, length, block, pairs, width
    )
    kvs = [qkv, qkv] + [kv for kv in others for _ in range(2)]
    return call(
        functools.partial(attend_kernel, sources, block, head_size),
        "attend",
        (pairs,),
        [rows(0)] + kv_specs + seg_specs + [table_spec],
        [rows(0), lse_spec],
        [
            jax.ShapeDtypeStruct((inner, length), BF16),
            jax.ShapeDtypeStruct((pairs, 8, length), F32),
        ],
        [info, qkv, *kvs, seg_q, seg_k, table],
        flops=16 * inner * length * length * sources,
        scratch=[
            pltpu.VMEM((2, k_blocks, block, block), F32),
            pltpu.VMEM((2, 1, block), F32),
            pltpu.VMEM((2, 1, block), F32),
            pltpu.VMEM((width, block), F32),
            pltpu.VMEM((length * sources, width), BF16),
        ],
        scalars=1,
        after=after,
    )


def attend_grads(
    info, qkv, others, seg_q, seg_k, table, context, lse, grad_context, block, head_size, after
):
    inner, length = context.shape
    sources = 1 + len(others)
    width = 2 * head_size
    pairs = inner // width
    k_blocks, entries, rows, kv_specs, seg_specs, table_spec, lse_spec = attention_specs(
        sources, length, block, pairs, width
    )
    dkv_spec = pl.BlockSpec((2, width, length), lambda p, info: (0, p, 0))
    tiles = (sources, 2 * (length // block) - 1)
    kvs = [qkv, qkv] + [kv for kv in others for _ in range(2)]
    results = call(
        functools.partial(grad_kernel, sources, block, head_size),
        "attend_grads",
        (pairs,),
        [rows(0)] + kv_specs + seg_specs + [table_spec, rows(0), lse_spec, rows(0)],
        [rows(0), pl.BlockSpec((2,) + tiles + (8, 2 * block), lambda p, info: (p, 0, 0, 0, 0))]
        + [dkv_spec] * sources,
        [
            jax.ShapeDtypeStruct((inner, length), BF16),
            jax.ShapeDtypeStruct((2 * pairs,) + tiles + (8, 2 * block), F32),
        ]
        + [jax.ShapeDtypeStruct((2, inner, length), BF16)] * sources,
        [info, qkv, *kvs, seg_q, seg_k, table, context, lse, grad_context],
        flops=32 * inner * length * length * sources,
        scratch=[
            pltpu.VMEM((length * sources, width), F32),
            pltpu.VMEM((length * sources, width), F32),
            pltpu.VMEM((width, block), F32),
            pltpu.VMEM((length * sources, width), BF16),
            pltpu.VMEM((length * sources, width), BF16),
            pltpu.VMEM((2,) + tiles + (block, block), F32),
        ],
        scalars=1,
        after=after,
    )
    return results[0], results[1], results[2:]


def gelu_terms(gate, upward, grad_hidden):
    square = gate * gate
    tanh = jnp.tanh(GELU_SCALE * gate * (1.0 + GELU_CUBE * square))
    half = 0.5 + 0.5 * tanh
    gelu = gate * half
    slope = half + 0.5 * gate * (1.0 - tanh * tanh) * (
        GELU_SCALE + 3.0 * GELU_CUBE * GELU_SCALE * square
    )
    return (
        (gelu * upward).astype(BF16),
        (grad_hidden * upward * slope).astype(BF16),
        (grad_hidden * gelu).astype(BF16),
    )


def joined(parts, axis):
    return parts[0] if len(parts) == 1 else jnp.concatenate(parts, axis=axis)


def source_rows(refs, kind, columns):
    return joined([ref[kind][:, columns] for ref in refs], 0)


def batches_of(sources, tile):
    if tile % LANES:
        return [[s] for s in range(sources)]
    return [list(range(s, min(s + 2, sources))) for s in range(0, sources, 2)]


def split_refs(refs, counts):
    result, start = [], 0
    for count in counts:
        result.append(refs[start : start + count])
        start += count
    return result, refs[start:]


def ffn_kernel(counts, groups, gathered, info_ref, *refs):
    if gathered:
        stacks, refs = refs[:3], refs[3:]
        blocks = stacks[0].shape[0] // len(counts)
        tile = stacks[0].shape[2]
    else:
        sources, refs = refs[: len(counts)], refs[len(counts) :]
        tile = sources[0].shape[2]
    acts_hbm, refs = refs[: 2 * groups], refs[2 * groups :]
    (hid_ref, ggi_ref, gui_ref, w_ref), refs = refs[:4], refs[4:]
    grads, (acts, sems) = split_refs(refs, counts)
    first = pl.program_id(0) == 0

    def fetch(n):
        return pltpu.make_async_copy(acts_hbm[n], acts.at[n], sems.at[n])

    def matrix(kind, source):
        if not gathered:
            return sources[source][kind]
        places = [
            (info_ref[1] ^ source) * blocks + block_of(info_ref[0], p, blocks // 2)
            for p in range(blocks)
        ]
        rows = [stacks[kind][place].astype(F32) for place in places]
        return jnp.concatenate(rows, axis=0).astype(BF16)

    @pl.when(first)
    def _():
        for g in range(groups):
            fetch(g).start()
            fetch(groups + g).start()

    start = 0
    for number, batch in enumerate(batches_of(len(counts), tile)):
        units = tile * len(batch)
        rows = slice(start, start + units)
        start += units
        for kind in range(3):
            w_ref[kind, :, rows] = joined([matrix(kind, s) for s in batch], 1)
        for g in range(groups):
            if number == 0:

                @pl.when(first)
                def _(g=g):
                    fetch(g).wait()
                    fetch(groups + g).wait()

            gate = dot_tn(w_ref[0, :, rows], acts[g])
            upward = dot_tn(w_ref[1, :, rows], acts[g])
            grad_hidden = dot_tn(w_ref[2, :, rows], acts[groups + g])
            hidden, grad_gate, grad_up = gelu_terms(gate, upward, grad_hidden)
            hid_ref[g, rows] = hidden
            ggi_ref[g, rows] = grad_gate
            gui_ref[g, rows] = grad_up
        for kind, (left, right_ref) in enumerate(((0, ggi_ref), (0, gui_ref), (groups, hid_ref))):
            total = None
            for g in range(groups):
                product = dot_nt(acts[left + g], right_ref[g, rows])
                total = product if total is None else total + product
            total = total.astype(BF16)
            for n, s in enumerate(batch):
                row = 0
                for ref in grads[s]:
                    depth = ref.shape[1]
                    ref[kind] = total[row : row + depth, n * tile : (n + 1) * tile]
                    row += depth


def tile_of(width):
    return LANES if width % LANES == 0 else width


def ffn_chunk(info, weights, width, normed, cot, after):
    groups = len(normed)
    wide, length = normed[0].shape
    gathered = not isinstance(weights, list)
    sources = lax.axis_size("mp")
    tile = tile_of(width)
    steps = width // tile
    half = wide // 2
    counts = [2] + [3] * (sources - 1)
    shapes = [(3, half, width)] * 2
    for _ in range(sources - 1):
        shapes += [(3, half, width)] + [(3, half // 2, width)] * 2
    if gathered:
        weight_specs = [
            pl.BlockSpec(weights.shape[:2] + (tile,), lambda j, *_, n=n: (0, 0, n * steps + j))
            for n in range(3)
        ]
        operands = [weights] * 3
    else:
        weight_specs = [pl.BlockSpec((3, wide, tile), lambda j, *_: (0, 0, j))] * sources
        operands = list(weights)
    units = sources * tile
    act_spec = pl.BlockSpec((groups, units, length), lambda j, *_: (0, j, 0))
    act_shape = jax.ShapeDtypeStruct((groups, sources * width, length), BF16)
    results = call(
        functools.partial(ffn_kernel, counts, groups, gathered),
        "ffn_chunk",
        (steps,),
        weight_specs + [pl.BlockSpec(memory_space=pl.ANY)] * (2 * groups),
        [act_spec] * 3
        + [pl.BlockSpec((3, wide, units), lambda j, *_: (0, 0, j))]
        + [pl.BlockSpec(shape[:2] + (tile,), lambda j, *_: (0, 0, j)) for shape in shapes],
        [act_shape] * 3
        + [jax.ShapeDtypeStruct((3, wide, sources * width), BF16)]
        + [jax.ShapeDtypeStruct(shape, BF16) for shape in shapes],
        [info, *operands, *normed, *cot],
        flops=12 * groups * length * wide * sources * width,
        scratch=[
            pltpu.VMEM((2 * groups, wide, length), BF16),
            pltpu.SemaphoreType.DMA((2 * groups,)),
        ],
        scalars=1,
        after=after,
    )
    grads, _ = split_refs(results[4:], counts)
    return results[:3], results[3], grads


def down_kernel(chunks, kinds, *refs):
    total = None
    for _ in range(chunks):
        matrices, acts, refs = refs[:kinds], refs[kinds : 2 * kinds], refs[2 * kinds :]
        for matrix, act in zip(matrices, acts):
            product = dot_nn(matrix[0], act[0])
            total = product if total is None else total + product
    (out_ref,) = refs
    out_ref[0] = total.astype(BF16)


def down(chunk_weights, chunk_acts, first, kinds, start, count, after):
    length = chunk_acts[0][0].shape[2]
    wide = chunk_weights[0].shape[1]
    operands, specs = [], []
    flops = 0
    for weights, acts in zip(chunk_weights, chunk_acts):
        acts = acts[1:] if kinds == 2 else acts[:1]
        operands += [weights] * kinds + list(acts)
        specs += [
            pl.BlockSpec(
                (1,) + weights.shape[1:], lambda g, n=n: (n, 0, 0), pipeline_mode=pl.Buffered(1)
            )
            for n in range(first, first + kinds)
        ]
        specs += [
            pl.BlockSpec((1, act.shape[1], length), lambda g: (start + g, 0, 0)) for act in acts
        ]
        flops += 2 * kinds * count * length * wide * acts[0].shape[1]
    return call(
        functools.partial(down_kernel, len(chunk_acts), kinds),
        "down",
        (count,),
        specs,
        [slab(wide, length)],
        [jax.ShapeDtypeStruct((count, wide, length), BF16)],
        operands,
        flops=flops,
        after=after,
    )[0]


def body(
    inputs,
    cotangent,
    segments,
    rel_bucket,
    head_order,
    rel_table,
    norm1_gain,
    norm2_gain,
    w_query,
    w_key,
    w_value,
    output_weight,
    w_gate,
    w_up,
    w_down,
):
    dp, mp = dp_size(), lax.axis_size("mp")
    x = lax.axis_index("mp")
    core, chip = lax.axis_index("core"), lax.axis_index("chip")
    chips, depth = dp // 2, dp // 4
    micro, rows, own_length, model = inputs.shape
    groups = micro * rows
    length = own_length * mp
    bucket_count, head_count = rel_table.shape
    inner = w_query.shape[1]
    head_size = inner // head_count
    block = min(256, own_length)
    q_blocks, k_blocks = own_length // block, length // block
    own_rows, own_units = w_gate.shape
    half_units = own_units // 2
    chip_rows = 2 * own_rows
    place = chip.reshape(1).astype(jnp.int32)

    micros = range(groups)
    own_place = (2 * x + core).reshape(1).astype(jnp.int32)
    role_place = own_place & 3

    def feature_major(array):
        return jnp.transpose(array.reshape(groups, own_length, model), (0, 2, 1))

    bucket_rev = jnp.concatenate([rel_bucket[::-1], jnp.full((1,), -1, jnp.int32)])
    bucket_hot = (bucket_rev[:, None] == jnp.arange(bucket_count, dtype=jnp.int32)[None, :]).astype(F32)
    head_hot = (head_order[:, None] == jnp.arange(head_count, dtype=jnp.int32)[None, :]).astype(F32)
    offset_table = jnp.dot(bucket_hot, rel_table, precision=TOP_PRECISION)
    offset_bias = jnp.dot(head_hot, offset_table.T, precision=TOP_PRECISION)
    bias_blocks = offset_bias.reshape(head_count, 2 * k_blocks, block)
    windows = jnp.concatenate([bias_blocks[:, :-1], bias_blocks[:, 1:]], axis=2)

    part = 4 * inner // (2 * mp)
    shard = jnp.concatenate([w_query, w_key, w_value, jnp.transpose(output_weight)], axis=1)
    kept = lax.dynamic_slice_in_dim(shard, (2 * x + core) * part, part, 1)
    sent = lax.dynamic_slice_in_dim(shard, (2 * x + 1 - core) * part, part, 1)
    got = swap_dp(sent, 1)
    attention_piece = either(
        core, jnp.concatenate([kept, got], axis=0), jnp.concatenate([got, kept], axis=0)
    )[None]
    ffn_shard = jnp.stack([w_gate, w_up, jnp.transpose(w_down)])
    low_half, high_half = ffn_shard[:, :, :half_units], ffn_shard[:, :, half_units:]
    kept = either(core, low_half, high_half)
    got = swap_dp(either(core, high_half, low_half), 1)
    ffn_piece = either(
        core, jnp.concatenate([kept, got], axis=1), jnp.concatenate([got, kept], axis=1)
    )
    if half_units % (7 * LANES) == 0:
        bounds = [0, half_units // 7 * 4, half_units]
    elif half_units > LANES:
        bounds = [0, LANES, half_units]
    else:
        bounds = [0, half_units]
    widths = [b - a for a, b in zip(bounds[:-1], bounds[1:])]
    chunk_stacks = []
    for a, width in zip(bounds, widths):
        flat = jnp.concatenate([ffn_piece[n, :, a : a + width] for n in range(3)], axis=1)
        chunk_stacks.append(lax.all_gather(flat, ("mp", "chip")))

    far_masks = z_masks()

    def gather_z(piece, masks, first=(), then=()):
        for mask in masks:
            piece = merge(piece, hold(swap_dp(hold(piece, *first), mask), *then))
        return piece

    own = gather_z(attention_piece, far_masks)
    arrays = feature_major(inputs)
    layer_in = [reorder(arrays, m, place, chips, False) for m in micros]
    arrays = feature_major(cotangent)
    cots = [reorder(arrays, m, place, chips, False, [*layer_in, own]) for m in micros]
    cots_far = [swap_dp(cot, 1) for cot in cots]
    table = bias_table(windows[:, :, None, :], block, cots)
    over_y, over_x = gather_xy(own, layer_in, [table])
    corner = gather_corner(over_y, over_x)
    quads = quads_of(own, over_y, over_x, corner)
    matrices = []
    for parts in quads:
        matrices += [parts, tuple(swap_dp(ref, 1) for ref in parts)]

    seg_flat = segments.reshape(groups, length)
    seg_q = lax.dynamic_slice_in_dim(seg_flat, x * own_length, own_length, 1)
    seg_parts = seg_flat.reshape(groups, mp, own_length)
    seg_k = jnp.concatenate([pick(seg_parts, x ^ k, 1) for k in range(mp)], axis=1)
    q_edges = seg_q.reshape(groups, q_blocks, block)
    k_edges = seg_k.reshape(groups, k_blocks, block)
    live = (q_edges[:, :, None, 0] <= k_edges[:, None, :, -1]) & (
        k_edges[:, None, :, 0] <= q_edges[:, :, None, -1]
    )
    infos = [
        jnp.concatenate([x.reshape(1).astype(jnp.int32), live[m].reshape(-1).astype(jnp.int32)])
        for m in micros
    ]
    seg_q_rows = [seg_q[m][None, :] for m in micros]
    seg_k_columns = [seg_k[m][:, None] for m in micros]

    gains = reorder(jnp.stack([norm1_gain, norm2_gain], axis=1)[None], 0, place, chips, False)
    gain1, gain2 = gains[:, :1], gains[:, 1:]
    normed1, qkvs, others = [], [], []
    last = cots_far
    for m in micros:
        normed, qkv, kv = project(own_place, layer_in[m], gain1, matrices, last)
        last = [normed]
        normed1.append(normed)
        qkvs.append(qkv.reshape(4 * inner, own_length))
        others.append([swap_mp(kv, k).reshape(2 * inner, own_length) for k in x_masks()])
    weights = assemble(own_place, matrices, inner, [normed1[-1]])
    last = [weights]
    contexts, lses, normed2, normed2_far = [], [], [], []
    for m in micros:
        context, lse = attend(
            infos[m], qkvs[m], others[m], seg_q_rows[m], seg_k_columns[m], table,
            block, head_size, inner, last,
        )
        contexts.append(context)
        lses.append(lse)
        last = [context]
        normed = middle_layer(layer_in[m], context, weights, gain2, last)
        last = [normed]
        normed2.append(normed)
        normed2_far.append(swap_dp(normed, 1))

    ffn_info = jnp.concatenate([place, x.reshape(1).astype(jnp.int32)])
    chunk_acts, chunk_weights, corners = [], [], []
    for stack, width in zip(chunk_stacks, widths):
        if own_rows % 4 or width % LANES:
            ordered = jnp.stack(
                [
                    jnp.stack([pick(stack, (x ^ k) * chips + block_of(chip, p, depth), 0) for p in range(chips)])
                    for k in range(mp)
                ]
            ).reshape(mp, model, 3, width)
            stack = [jnp.transpose(ordered[k], (1, 0, 2)) for k in range(mp)]
        acts, matrices_in, grads = ffn_chunk(
            ffn_info, stack, width, normed2 + normed2_far, cots + cots_far, last
        )
        last = [acts[0]] + [c[1] for c in corners]
        chunk_acts.append(acts)
        chunk_weights.append(matrices_in)
        corners.append(scatter_corner(grads, [], [acts[0]] if len(widths) == 1 else []))
    corners[0] = hold(corners[0], chunk_acts[-1][0])
    back_far = down(chunk_weights, chunk_acts, 0, 2, groups, groups, chunk_acts[-1][:1])
    from_far = swap_dp(back_far, 1)
    back_own = down(chunk_weights, chunk_acts, 0, 2, 0, groups, [back_far])
    last = [back_own]

    z_count = len(far_masks)
    grad_attn, grad_q, grad_kv, bias_grads, gain2_grads = [], [], [], [], []
    for m in micros:
        low, grad_context, gain_grads = turn(
            m, layer_in[m], contexts[m], cots[m], (back_own, from_far), gain2, weights, last
        )
        last = [low]
        grad_attn.append(low)
        gain2_grads.append(gain_grads)
        dq, bias_grad, dkv = attend_grads(
            infos[m], qkvs[m], others[m], seg_q_rows[m], seg_k_columns[m], table,
            contexts[m], lses[m], grad_context, block, head_size, last,
        )
        last = [dq]
        grad_q.append(dq)
        bias_grads.append(bias_grad)
        grad_kv.append((dkv[0], [swap_mp(dkv[k], k) for k in x_masks()]))
        if m == micros[0]:
            sums = [scatter_xy(*corners[0], [dq])]
            waiting = [hold(corner, dq) for corner in corners[1:]]
            last += [sums[0][0]] + [corner[1] for corner in waiting]
    sums[0] = scatter_z(sums[0], 0, [dq])
    last.append(sums[0][0])
    weight_grads = outer_products(
        role_place,
        (0, 3),
        [
            [(normed1[m], grad_q[m]) for m in micros],
            [(grad_attn[m], contexts[m]) for m in micros],
        ],
        None,
        last,
    )
    ffn_far = down(chunk_weights, chunk_acts, 2, 1, groups, groups, [weight_grads])
    ffn_from = swap_dp(ffn_far, 1)
    ffn_own = down(chunk_weights, chunk_acts, 2, 1, 0, groups, [ffn_far])
    sums[0] = scatter_z(sums[0], 1, [ffn_own])
    last = [ffn_own, first_of(sums[0])]
    grad_kv = [sum_rows([own, *hold(got, ffn_own)], 1, after=[ffn_own]) for own, got in grad_kv]
    weight_grads = outer_products(
        role_place,
        (1, 2),
        [[(normed1[m], (grad_kv[m], n)) for m in micros] for n in range(2)],
        weight_grads,
        last,
    )
    sums += [scatter_xy(*corner, [weight_grads]) for corner in waiting]

    half = model // 2
    split = [half, half // 2, half // 2]
    if part == inner:
        got = [swap_dp(weight_grads[2 * k + 1 : 2 * k + 2], 1) for k in range(mp)]
        quads = [
            sum_rows([weight_grads, got[k]], 2 if k == 0 else split, [2 * k, 0], 1)
            for k in range(mp)
        ]
    else:
        ordered = jnp.concatenate(
            [lax.dynamic_slice_in_dim(weight_grads, role_place[0] ^ r, 1, 0) for r in range(4)]
        )
        by_part = jnp.transpose(
            ordered.reshape(4, model, inner // part, part), (0, 2, 1, 3)
        ).reshape(mp, 2, model, part)
        near = add_low(pick(by_part, core, 1), swap_dp(pick(by_part, 1 - core, 1), 1))
        quads = []
        for k in range(mp):
            matrix = pick(near, x ^ k, 0)[None]
            sizes = [half, half] if k == 0 else split
            starts = [sum(sizes[:n]) for n in range(len(sizes))]
            quads.append(tuple(matrix[:, a : a + n] for a, n in zip(starts, sizes)))
    grad_inputs, gain1_grads = input_grads(
        place,
        [(layer_in[m], grad_attn[m], grad_q[m], grad_kv[m]) for m in micros],
        gain1,
        weights,
        chips,
        [quads[0][0]] + [parts[0] for parts in sums[1:]],
    )
    corner = scatter_corner(quads, [], [gain1_grads])
    last = [gain1_grads, corner[1]]
    sums[1:] = [scatter_z(parts, 0, [gain1_grads]) for parts in sums[1:]]
    last += [parts[0] for parts in sums[1:]]
    outputs = finish(
        place,
        [(layer_in[m], contexts[m]) for m in micros],
        (ffn_own, ffn_from),
        weights,
        chips,
        last,
    )
    sums[1:] = [scatter_z(parts, 1, [outputs]) for parts in sums[1:]]
    total = scatter_xy(*corner, [outputs])
    for stage in range(z_count):
        total = scatter_z(total, stage)
    piece = total[0]
    for stage in range(2, z_count):
        sums = [scatter_z(parts, stage) for parts in sums]
    over_x = jnp.stack([piece] + [swap_mp(piece, k) for k in x_masks()])
    kept = either(core, over_x[:, :own_rows], over_x[:, own_rows:])
    got = swap_dp(either(core, over_x[:, own_rows:], over_x[:, :own_rows]), 1)
    both = jnp.stack([kept, got], axis=1).reshape(2 * mp, own_rows, part)
    final = jnp.concatenate(
        [pick(both, (2 * x + core) ^ r, 0) for r in range(2 * mp)], axis=1
    ).astype(F32)

    sums = jnp.concatenate(sums, axis=2)
    kept = either(core, sums[:, :own_rows], sums[:, own_rows:])
    got = swap_dp(either(core, sums[:, own_rows:], sums[:, :own_rows]), 1)
    ffn_grads = either(
        core, jnp.concatenate([kept, got], axis=2), jnp.concatenate([got, kept], axis=2)
    ).astype(F32)

    bias_rows = sum(bias_grads)
    bias_tiles = sum(
        jnp.pad(bias_rows[:, :, :, t, : 2 * block - 7 + t], ((0, 0),) * 3 + ((7 - t, 0),))
        for t in range(8)
    )
    run = 2 * q_blocks - 1
    bias_flat = jnp.zeros((head_count, 2 * k_blocks - 1, 2 * block), F32)
    for k in range(mp):
        first = k_blocks - q_blocks - ((x ^ k) - x) * q_blocks
        held = lax.dynamic_slice_in_dim(bias_flat, first, run, 1)
        bias_flat = lax.dynamic_update_slice_in_dim(bias_flat, held + bias_tiles[:, k], first, 1)
    left = jnp.pad(bias_flat[:, :, :block], ((0, 0), (0, 1), (0, 0)))
    right = jnp.pad(bias_flat[:, :, block:], ((0, 0), (1, 0), (0, 0)))
    offsets_total = (left + right).reshape(head_count, 2 * k_blocks * block)
    bucket_part = jnp.dot(bucket_hot.T, offsets_total.T, precision=TOP_PRECISION)
    rel_part = jnp.dot(bucket_part, head_hot, precision=TOP_PRECISION)
    gain_parts = jnp.concatenate([gain1_grads, sum(gain2_grads)], axis=1)
    gain_parts = reorder(gain_parts[None], 0, place, chips, True)
    small = jnp.concatenate([gain_parts[:, 0], gain_parts[:, 1], rel_part.reshape(-1)])
    small = sum_all(small, [outputs])

    shape = inputs.shape

    def placed(array):
        return jnp.transpose(array, (0, 2, 1)).reshape(shape)

    return (
        placed(outputs),
        placed(grad_inputs),
        small[2 * model :].reshape(rel_table.shape),
        small[:model],
        small[model : 2 * model],
        final[:, :inner],
        final[:, inner : 2 * inner],
        final[:, 2 * inner : 3 * inner],
        jnp.transpose(final[:, 3 * inner :]),
        ffn_grads[0],
        ffn_grads[1],
        jnp.transpose(ffn_grads[2]),
    )


def solution(mesh):
    devices = mesh.devices.reshape(-1, 2, mesh.shape["mp"])
    return jax.shard_map(
        body,
        mesh=jax.sharding.Mesh(devices, DP + ("mp",)),
        in_specs=(
            P(None, DP, "mp", None),
            P(None, DP, "mp", None),
            P(None, DP, None),
            P(),
            P(),
            P(),
            P(),
            P(),
            P(DP, None),
            P(DP, None),
            P(DP, None),
            P(None, DP),
            P(DP, "mp"),
            P(DP, "mp"),
            P("mp", DP),
        ),
        out_specs=(
            P(None, DP, "mp", None),
            P(None, DP, "mp", None),
            P(),
            P(),
            P(),
            P(DP, None),
            P(DP, None),
            P(DP, None),
            P(None, DP),
            P(DP, "mp"),
            P(DP, "mp"),
            P("mp", DP),
        ),
        check_vma=False,
    )
```

time: 762 us -> 667 us (0.88)
  waiting for transfers between devices: 281 us -> 157 us
  Pallas kernels: 277 us -> 377 us
  other arithmetic: 56.9 us -> 10.9 us
  starting transfers between devices: 94.9 us -> 60.9 us
  between operations: 1.73 us -> 15.3 us
    ppermute x16 -> x14, waiting for transfers between devices: 164 us -> 57.2 us  [swap_mp(): return lax.ppermute(array, 'mp', [(i, i ^ mask) for i in range(count)])]
    pallas_call x17 -> x48, Pallas kernels: 277 us -> 377 us  [call(): pl.pallas_call(run, grid_spec=pltpu.PrefetchScalarGridSpec(num_scalar_pre...]
    ppermute x44 -> x37, waiting for transfers between devices: 117 us -> 48.5 us  [swap_dp(): return lax.ppermute(array, DP, [(i, i ^ mask) for i in range(dp_size())])]
    all_gather x0 -> x2, waiting for transfers between devices: none -> 51.2 us  [body(): chunk_stacks.append(lax.all_gather(flat, ('mp', 'chip')))]
    ppermute x44 -> x37, starting transfers between devices: 76.9 us -> 47.6 us  [swap_dp(): return lax.ppermute(array, DP, [(i, i ^ mask) for i in range(dp_size())])]
    convert_element_type x14 -> x1, other arithmetic: 23.8 us -> 0.01 us  [body(): live[m].reshape(-1).astype(jnp.int32)]
    concatenate x9 -> x6, other arithmetic: 15.8 us -> 4.64 us  [the longest x2 1.66 us: body(): jnp.concatenate([ffn_piece[n, :, a:a + width] for n in range(3)], axis=1)]
    another operation x7 -> x2, other arithmetic: 9.19 us -> 0.02 us  [the longest x1 0.01 us: body(): seg_k_columns = [seg_k[m][:, None] for m in micros]]
  transfers between devices with their start and end apart: 60 -> 53, of which waited for: 22 -> 24; matrix products, arithmetic and copies ran while one was open for 11% -> 4% of each run, Pallas kernels for 23% -> 57%
where the time goes in v3:
time: 667 us; the launch traced here: 656 us
  Pallas kernels  377 us (57%)
  waiting for transfers between devices  157 us (24%)
  starting transfers between devices  60.9 us (9%)
  local copies, waits for them, and re-layouts  33.3 us (5%)
  between operations  15.3 us (2%)
  other arithmetic  10.9 us (2%)
    pallas_call x48, Pallas kernels, call(): pl.pallas_call(run, grid_spec=pltpu.PrefetchScalarGridSpec(num_scalar_pre...  377 us
    ppermute x14, waiting for transfers between devices, swap_mp(): return lax.ppermute(array, 'mp', [(i, i ^ mask) for i in range(count)])  57.2 us
    all_gather x2, waiting for transfers between devices, body(): chunk_stacks.append(lax.all_gather(flat, ('mp', 'chip')))  51.2 us
    ppermute x37, waiting for transfers between devices, swap_dp(): return lax.ppermute(array, DP, [(i, i ^ mask) for i in range(dp_size())])  48.5 us
    ppermute x37, starting transfers between devices, swap_dp(): return lax.ppermute(array, DP, [(i, i ^ mask) for i in range(dp_size())])  47.6 us
    unnamed x90, local copies, waits for them, and re-layouts  14.6 us
  transfers between devices with their start and end apart: 53, of which 24 were waited for; matrix products, arithmetic and copies ran while one was open for 4% of the time, Pallas kernels for 57%

profile of v3, /device:TPU:0, one launch (start us, length us, event | category | flops | bytes accessed | tf_op | source)
XLA Modules:
  0.0 656.5 jit_solution(2449911320554825788)
XLA Ops:
  30.3 14.5 %collective-permute-done.2.refs_1_ = bf16[1,368,384]{2,1,0:T(8,128)(2,1)S(1)} collective-permute-done((bf16[1,368,384]{2,1,0:T(8,128)(2,1)}, bf16[1,368,384]{2,1,0:T(8,128)(2,1)S(1)}, u32[]{:S(2)}, u32[]{:S(2)}) %collective-permute-start.2) | collective-permute-done | bytes 282656 | tf_op jit(solution)/shard_map/ppermute | solution.py:30
  57.4 6.9 %bias_table.1.refs_8_ = f32[6,7,256,256]{3,2,1,0:T(8,128)} custom-call(f32[6,7,1,512]{3,2,1,0:T(1,128)} %broadcast_in_dim.2.refs_0_, bf16[1472,512]{1,0:T(8,128)(2,1)} %bitcast.169, bf16[1472,512]{1,0:T(8,128)(2,1)} %bitcast.173), custom_call_target="tpu_custom_call" | custom-call | bytes 554803 | tf_op jit(solution)/shard_map/bias_table/pallas_call | solution.py:150
  64.2 8.7 %collective-permute-done.4.refs_0_.refs_7_.refs_5_ = bf16[1,736,384]{2,1,0:T(8,128)(2,1)S(1)} collective-permute-done((bf16[1,736,384]{2,1,0:T(8,128)(2,1)}, bf16[1,736,384]{2,1,0:T(8,128)(2,1)S(1)}, u32[]{:S(2)}, u32[]{:S(2)}) %collective-permute-start.4) | collective-permute-done | bytes 565280 | tf_op jit(solution)/shard_map/ppermute | solution.py:35
  93.2 8.3 %project.2 = (bf16[1472,512]{1,0:T(8,128)(2,1)}, bf16[4,384,512]{2,1,0:T(8,128)(2,1)}, bf16[2,384,512]{2,1,0:T(8,128)(2,1)}) custom-call(s32[1]{0:T(128)} %bitcast.6.refs_0_, bf16[1472,512]{1,0:T(8,128)(2,1)} %bitcast.138, f32[1472,1]{1,0:T(8,128)} %get-tuple-element.342.refs_2_.refs_9_, bf16[1,736,384]{2,1,0:T(8,128)(2,1)} %merge.3.refs_4_.refs_3_.refs_1_, ...), custom_call_target="tpu_custom_call" | custom-call | flops 86822096 | bytes 495091 | tf_op jit(solution)/shard_map/project/pallas_call | solution.py:150
  103.7 7.9 %project.3 = (bf16[1472,512]{1,0:T(8,128)(2,1)}, bf16[4,384,512]{2,1,0:T(8,128)(2,1)}, bf16[2,384,512]{2,1,0:T(8,128)(2,1)}) custom-call(s32[1]{0:T(128)} %bitcast.6.refs_0_, bf16[1472,512]{1,0:T(8,128)(2,1)} %bitcast.145, f32[1472,1]{1,0:T(8,128)} %get-tuple-element.342.refs_2_.refs_9_, bf16[1,736,384]{2,1,0:T(8,128)(2,1)} %merge.3.refs_4_.refs_3_.refs_1_, ...), custom_call_target="tpu_custom_call" | custom-call | flops 86822096 | bytes 495091 | tf_op jit(solution)/shard_map/project/pallas_call | solution.py:150
  115.8 4.7 assemble.1.refs_9_.refs_2_.refs_6_.refs_10_.refs_7_
  120.5 18.6 %collective-permute-done.14 = bf16[2,384,512]{2,1,0:T(8,128)(2,1)S(1)} collective-permute-done((bf16[2,384,512]{2,1,0:T(8,128)(2,1)}, bf16[2,384,512]{2,1,0:T(8,128)(2,1)S(1)}, u32[]{:S(2)}, u32[]{:S(2)}) %collective-permute-start.14) | collective-permute-done | bytes 786464 | tf_op jit(solution)/shard_map/ppermute | solution.py:35
  140.0 10.2 %attend.2 = (bf16[384,512]{1,0:T(8,128)(2,1)}, f32[3,8,512]{2,1,0:T(8,128)}) custom-call(s32[9]{0:T(128)} %pad_add_fusion.3.refs_0_, bf16[1536,512]{1,0:T(8,128)(2,1)} %bitcast.162, bf16[1536,512]{1,0:T(8,128)(2,1)} %bitcast.163, bf16[1536,512]{1,0:T(8,128)(2,1)} %bitcast.164, bf16[768,512]{1,0:T(8,128)(2,1)} %bitcast.182, bf16[768,512]{1,0:T(8,128)(2,1)} %bitcast.183, ...), custom_call_target="tpu_custom_call" | custom-call | flops 161061280 | bytes 887502 | tf_op jit(solution)/shard_map/attend/pallas_call | solution.py:150
  154.6 8.6 %collective-permute-done.15 = bf16[2,384,512]{2,1,0:T(8,128)(2,1)S(1)} collective-permute-done((bf16[2,384,512]{2,1,0:T(8,128)(2,1)}, bf16[2,384,512]{2,1,0:T(8,128)(2,1)S(1)}, u32[]{:S(2)}, u32[]{:S(2)}) %collective-permute-start.15) | collective-permute-done | bytes 786464 | tf_op jit(solution)/shard_map/ppermute | solution.py:35
  164.1 10.6 %attend.3 = (bf16[384,512]{1,0:T(8,128)(2,1)}, f32[3,8,512]{2,1,0:T(8,128)}) custom-call(s32[9]{0:T(128)} %pad_add_fusion.4.refs_0_, bf16[1536,512]{1,0:T(8,128)(2,1)} %bitcast.156, bf16[1536,512]{1,0:T(8,128)(2,1)} %bitcast.157, bf16[1536,512]{1,0:T(8,128)(2,1)} %bitcast.158, bf16[768,512]{1,0:T(8,128)(2,1)} %bitcast.178, bf16[768,512]{1,0:T(8,128)(2,1)} %bitcast.179, ...), custom_call_target="tpu_custom_call" | custom-call | flops 161061280 | bytes 887502 | tf_op jit(solution)/shard_map/attend/pallas_call | solution.py:150
  174.7 4.5 middle.3.refs_5_.refs_12_
  184.9 52.6 %ffn_chunk.2 = (bf16[4,1024,512]{2,1,0:T(8,128)(2,1)}, bf16[4,1024,512]{2,1,0:T(8,128)(2,1)}, bf16[4,1024,512]{2,1,0:T(8,128)(2,1)}, bf16[3,1472,1024]{2,1,0:T(8...) custom-call(s32[2]{0:T(128)} %pad_add_fusion.5.refs_0_, ...), custom_call_target="tpu_custom_call" | custom-call | flops 1852204672 | bytes 3493069 | tf_op jit(solution)/shard_map/ffn_chunk/pallas_call | solution.py:150
  242.3 51.1 %all-gather.7.cloned.1.call-done = bf16[2944,1152]{1,0:T(8,128)(2,1)} async-done(((bf16[184,1152]{1,0:T(8,128)(2,1)}), bf16[2944,1152]{1,0:T(8,128)(2,1)}) %all-gather.7.cloned.1.call-update) | async-done | bytes 6782992 | tf_op jit(solution)/shard_map/all_gather | solution.py:1230
  293.4 41.3 %ffn_chunk.3 = (bf16[4,768,512]{2,1,0:T(8,128)(2,1)}, bf16[4,768,512]{2,1,0:T(8,128)(2,1)}, bf16[4,768,512]{2,1,0:T(8,128)(2,1)}, bf16[3,1472,768]{2,1,0:T(8,128...) custom-call(s32[2]{0:T(128)} %pad_add_fusion.5.refs_0_, ...), custom_call_target="tpu_custom_call" | custom-call | flops 1389153536 | bytes 2770534 | tf_op jit(solution)/shard_map/ffn_chunk/pallas_call | solution.py:150
  334.7 18.1 %down.4.refs_8_ = bf16[2,1472,512]{2,1,0:T(8,128)(2,1)} custom-call(bf16[3,1472,1024]{2,1,0:T(8,128)(2,1)} %get-tuple-element.115.refs_0_.refs_1_, bf16[3,1472,1024]{2,1,0:T(8,128)(2,1)} %get-tuple-element.115.refs_0_.refs_1_, bf16[4,1024,512]{2,1,0:T(8,128)(2,1)} %get-tuple-element.120.refs_2_, bf16[4,1024,512]{2,1,0:T(8,128)(2,1)} %get-tuple-element.121.refs_3_, ...), custom_call_target="tpu_custom_call" | custom-call | flops 540226368 | bytes 2467430 | tf_op jit(solution)/shard_map/down/pallas_call | solution.py:150
  352.9 4.4 add_corner.3
  361.3 17.9 %down.5.refs_3_.refs_7_ = bf16[2,1472,512]{2,1,0:T(8,128)(2,1)} custom-call(bf16[3,1472,1024]{2,1,0:T(8,128)(2,1)} %get-tuple-element.115.refs_0_.refs_1_, bf16[3,1472,1024]{2,1,0:T(8,128)(2,1)} %get-tuple-element.115.refs_0_.refs_1_, bf16[4,1024,512]{2,1,0:T(8,128)(2,1)} %get-tuple-element.120.refs_2_, bf16[4,1024,512]{2,1,0:T(8,128)(2,1)} %get-tuple-element.121.refs_3_, ...), custom_call_target="tpu_custom_call" | custom-call | flops 540226368 | bytes 2467430 | tf_op jit(solution)/shard_map/down/pallas_call | solution.py:150
  380.9 8.6 %turn.2 = (bf16[1472,512]{1,0:T(8,128)(2,1)}, bf16[384,512]{1,0:T(8,128)(2,1)}, f32[1472,1]{1,0:T(8,128)}) custom-call(bf16[1472,512]{1,0:T(8,128)(2,1)} %bitcast.140, bf16[384,512]{1,0:T(8,128)(2,1)} %get-tuple-element.111.refs_1_.refs_4_.refs_9_.refs_6_.refs_2_, bf16[1472,512]{1,0:T(8,128)(2,1)} %bitcast.172, bf16[2,1472,512]{2,1,0:T(8,128)(2,1)} %down.5.refs_3_.refs_7_, ...), custom_call_target="tpu_custom_call" | custom-call | flops 57881396 | bytes 793574 | tf_op jit(solution)/shard_map/turn/pallas_call | solution.py:150
  389.5 23.1 %attend_grads.2 = (bf16[384,512]{1,0:T(8,128)(2,1)}, f32[6,2,3,8,512]{4,3,2,1,0:T(8,128)}, bf16[2,384,512]{2,1,0:T(8,128)(2,1)}, bf16[2,384,512]{2,1,0:T(8,128)(2,1)}) custom-call(s32[9]{0:T(128)} %pad_add_fusion.3.refs_0_, bf16[1536,512]{1,0:T(8,128)(2,1)} %bitcast.165, bf16[1536,512]{1,0:T(8,128)(2,1)} %bitcast.166, bf16[1536,512]{1,0:T(8,128)(2,1)} %bitcast.167, ...), custom_call_target="tpu_custom_call" | custom-call | flops 322122560 | bytes 1034958 | tf_op jit(solution)/shard_map/attend_grads/pallas_call | solution.py:150
  412.6 5.1 sum_rows.13
  417.7 7.5 %collective-permute-start.26 = (bf16[3,368,512]{2,1,0:T(8,128)(2,1)}, bf16[3,368,512]{2,1,0:T(8,128)(2,1)S(1)}, u32[]{:S(2)}, u32[]{:S(2)}) collective-permute-start(bf16[3,368,512]{2,1,0:T(8,128)(2,1)} %get-tuple-element.152), channel_id=1, source_target_pairs={{0,8},{2,10},{4,12},{6,14},{8,0},{10,2},{12,4},{14,6},{16,24},{18,... | collective-permute-start | bytes 3391496 | tf_op jit(solution)/shard_map/ppermute | solution.py:30
  432.4 8.7 %turn.3 = (bf16[1472,512]{1,0:T(8,128)(2,1)}, bf16[384,512]{1,0:T(8,128)(2,1)}, f32[1472,1]{1,0:T(8,128)}) custom-call(bf16[1472,512]{1,0:T(8,128)(2,1)} %bitcast.147, bf16[384,512]{1,0:T(8,128)(2,1)} %get-tuple-element.114.refs_1_.refs_4_.refs_9_.refs_8_, bf16[1472,512]{1,0:T(8,128)(2,1)} %bitcast.176, bf16[2,1472,512]{2,1,0:T(8,128)(2,1)} %down.5.refs_3_.refs_7_, ...), custom_call_target="tpu_custom_call" | custom-call | flops 57881396 | bytes 793574 | tf_op jit(solution)/shard_map/turn/pallas_call | solution.py:150
  441.1 22.9 %attend_grads.3 = (bf16[384,512]{1,0:T(8,128)(2,1)}, f32[6,2,3,8,512]{4,3,2,1,0:T(8,128)}, bf16[2,384,512]{2,1,0:T(8,128)(2,1)}, bf16[2,384,512]{2,1,0:T(8,128)(2,1)}) custom-call(s32[9]{0:T(128)} %pad_add_fusion.4.refs_0_, bf16[1536,512]{1,0:T(8,128)(2,1)} %bitcast.159, bf16[1536,512]{1,0:T(8,128)(2,1)} %bitcast.160, bf16[1536,512]{1,0:T(8,128)(2,1)} %bitcast.161, ...), custom_call_target="tpu_custom_call" | custom-call | flops 322122560 | bytes 1034958 | tf_op jit(solution)/shard_map/attend_grads/pallas_call | solution.py:150
  476.6 7.7 %outer_products.2.refs_4_.refs_9_ = bf16[4,1472,384]{2,1,0:T(8,128)(2,1)} custom-call(s32[1]{0:T(128)S(6)} %and.10.refs_0_, bf16[1472,512]{1,0:T(8,128)(2,1)} %get-tuple-element.109.refs_13_.refs_1_.refs_5_, bf16[384,512]{1,0:T(8,128)(2,1)} %get-tuple-element.126.refs_7_.refs_2_.refs_3_, bf16[1472,512]{1,0:T(8,128)(2,1)} %get-tuple-element.110.refs_11_.refs_3_.refs_7_, ...), custom_call_target="tpu_custom_call" | custom-call | flops 115762792 | bytes 606208 | tf_op jit(solution)/shard_map/outer_products/pallas_call | solution.py:150
  484.3 10.1 %down.6.refs_4_ = bf16[2,1472,512]{2,1,0:T(8,128)(2,1)} custom-call(bf16[3,1472,1024]{2,1,0:T(8,128)(2,1)} %get-tuple-element.115.refs_0_.refs_1_, bf16[4,1024,512]{2,1,0:T(8,128)(2,1)} %get-tuple-element.116.refs_12_.refs_1_, bf16[3,1472,768]{2,1,0:T(8,128)(2,1)} %get-tuple-element.117.refs_4_.refs_5_.refs_2_, ...), custom_call_target="tpu_custom_call" | custom-call | flops 270113184 | bytes 1309081 | tf_op jit(solution)/shard_map/down/pallas_call | solution.py:150
  496.0 10.3 %down.7.refs_2_.refs_10_.refs_5_ = bf16[2,1472,512]{2,1,0:T(8,128)(2,1)} custom-call(bf16[3,1472,1024]{2,1,0:T(8,128)(2,1)} %get-tuple-element.115.refs_0_.refs_1_, bf16[4,1024,512]{2,1,0:T(8,128)(2,1)} %get-tuple-element.116.refs_12_.refs_1_, bf16[3,1472,768]{2,1,0:T(8,128)(2,1)} %get-tuple-element.117.refs_4_.refs_5_.refs_2_, ...), custom_call_target="tpu_custom_call" | custom-call | flops 270113184 | bytes 1309081 | tf_op jit(solution)/shard_map/down/pallas_call | solution.py:150
  514.5 7.7 %outer_products.3.refs_0_ = bf16[4,1472,384]{2,1,0:T(8,128)(2,1)} custom-call(s32[1]{0:T(128)S(6)} %and.10.refs_0_, bf16[1472,512]{1,0:T(8,128)(2,1)} %get-tuple-element.109.refs_13_.refs_1_.refs_5_, bf16[2,384,512]{2,1,0:T(8,128)(2,1)} %sum_rows.15.refs_2_.refs_6_.refs_4_, ...), custom_call_target="tpu_custom_call", output_to_operand_aliasing={{}: (9, {})} | custom-call | flops 115762792 | bytes 910950 | tf_op jit(solution)/shard_map/outer_products/pallas_call | solution.py:150
  528.1 8.1 %collective-permute-done.33.refs_2_ = bf16[3,736,384]{2,1,0:T(8,128)(2,1)S(1)} collective-permute-done((bf16[3,736,384]{2,1,0:T(8,128)(2,1)}, bf16[3,736,384]{2,1,0:T(8,128)(2,1)S(1)}, u32[]{:S(2)}, u32[]{:S(2)}) %collective-permute-start.33) | collective-permute-done | bytes 1695776 | tf_op jit(solution)/shard_map/ppermute | solution.py:35
  553.2 13.7 %input_grads.1 = (bf16[2,8,184,512]{3,2,1,0:T(8,128)(2,1)}, f32[1472,1]{1,0:T(8,128)}) custom-call(s32[1]{0:T(128)} %bitcast.refs_0_, bf16[1472,512]{1,0:T(8,128)(2,1)} %bitcast.141, bf16[1472,512]{1,0:T(8,128)(2,1)} %get-tuple-element.125.refs_12_.refs_5_.refs_2_, bf16[384,512]{1,0:T(8,128)(2,1)} %get-tuple-element.126.refs_7_.refs_2_.refs_3_, ...), custom_call_target="tpu_custom_call" | custom-call | flops 173644192 | bytes 796851 | tf_op jit(solution)/shard_map/input_grads/pallas_call | solution.py:150
  577.9 7.2 %finish.1 = bf16[2,8,184,512]{3,2,1,0:T(8,128)(2,1)} custom-call(s32[1]{0:T(128)} %bitcast.refs_0_, bf16[1472,512]{1,0:T(8,128)(2,1)} %bitcast.142, bf16[384,512]{1,0:T(8,128)(2,1)} %get-tuple-element.111.refs_1_.refs_4_.refs_9_.refs_6_.refs_2_, bf16[1472,512]{1,0:T(8,128)(2,1)} %bitcast.149, ...), custom_call_target="tpu_custom_call" | custom-call | flops 57881396 | bytes 868352 | tf_op jit(solution)/shard_map/finish/pallas_call | solution.py:150
  586.7 11.5 %collective-permute-done.49.refs_1_ = bf16[3,184,384]{2,1,0:T(8,128)(2,1)S(1)} collective-permute-done((bf16[3,184,384]{2,1,0:T(8,128)(2,1)}, bf16[3,184,384]{2,1,0:T(8,128)(2,1)S(1)}, u32[]{:S(2)}, u32[]{:S(2)}) %collective-permute-start.49) | collective-permute-done | bytes 423968 | tf_op jit(solution)/shard_map/ppermute | solution.py:30
  642.0 4.7 collective-permute-done.47
  (305 shorter events, 195.1 us)
Async XLA Ops:
  7.2 177.7 %all-gather.5.cloned.1.call-start = ((), (), s32[]{:S(2)}) async-start(), calls=%async_computation | async-start | bytes 9609216 | tf_op jit(solution)/shard_map/all_gather | solution.py:1230
  12.1 281.3 %all-gather.7.cloned.1.call-start = ((), (), s32[]{:S(2)}) async-start(), calls=%async_computation.1 | async-start | bytes 7206912 | tf_op jit(solution)/shard_map/all_gather | solution.py:1230
  28.0 16.8 %collective-permute-start.2 = (bf16[1,368,384]{2,1,0:T(8,128)(2,1)}, bf16[1,368,384]{2,1,0:T(8,128)(2,1)S(1)}, u32[]{:S(2)}, u32[]{:S(2)}) collective-permute-start(bf16[1,368,384]{2,1,0:T(8,128)(2,1)} %merge.2.refs_0_), channel_id=1, source_target_pairs={{0,8},{2,10},{4,12},{6,14},{8,0},{10,2},{12,4},{14,6},{16,24},{18,... | collective-permute-start | bytes 847880 | tf_op jit(solution)/shard_map/ppermute | solution.py:30
  47.4 25.5 %collective-permute-start.4 = (bf16[1,736,384]{2,1,0:T(8,128)(2,1)}, bf16[1,736,384]{2,1,0:T(8,128)(2,1)S(1)}, u32[]{:S(2)}, u32[]{:S(2)}) collective-permute-start(bf16[1,736,384]{2,1,0:T(8,128)(2,1)} %merge.3.refs_4_.refs_3_.refs_1_), channel_id=1, source_target_pairs={{0,1},{1,0},{2,3},{3,2},{4,5},{5,4},{6,7},{7,6},{8,9},{9,8},{10,11... | collective-permute-start | bytes 1695752 | tf_op jit(solution)/shard_map/ppermute | solution.py:35
  48.9 24.1 %collective-permute-start.3 = (bf16[1,736,384]{2,1,0:T(8,128)(2,1)}, bf16[1,736,384]{2,1,0:T(8,128)(2,1)}, u32[]{:S(2)}, u32[]{:S(2)}) collective-permute-start(bf16[1,736,384]{2,1,0:T(8,128)(2,1)} %merge.3.refs_4_.refs_3_.refs_1_), channel_id=1, source_target_pairs={{0,4},{2,6},{4,0},{6,2},{8,12},{10,14},{12,8},{14,10},{16,20},{18,... | collective-permute-start | bytes 1695752 | tf_op jit(solution)/shard_map/ppermute | solution.py:30
  50.6 33.6 %collective-permute-start.5 = (bf16[1,736,384]{2,1,0:T(8,128)(2,1)}, bf16[1,736,384]{2,1,0:T(8,128)(2,1)}, u32[]{:S(2)}, u32[]{:S(2)}) collective-permute-start(bf16[1,736,384]{2,1,0:T(8,128)(2,1)} %merge.3.refs_4_.refs_3_.refs_1_), channel_id=1, source_target_pairs={{0,2},{2,0},{4,6},{6,4},{8,10},{10,8},{12,14},{14,12},{16,18},{18,... | collective-permute-start | bytes 1695752 | tf_op jit(solution)/shard_map/ppermute | solution.py:30
  56.1 35.8 %collective-permute-start.12 = (bf16[1472,512]{1,0:T(8,128)(2,1)}, bf16[1472,512]{1,0:T(8,128)(2,1)S(1)}, u32[]{:S(2)}, u32[]{:S(2)}) collective-permute-start(bf16[1472,512]{1,0:T(8,128)(2,1)} %bitcast.168), channel_id=1, source_target_pairs={{0,2},{2,0},{4,6},{6,4},{8,10},{10,8},{12,14},{14,12},{16,18},{18,... | collective-permute-start | bytes 4521992 | tf_op jit(solution)/shard_map/ppermute | solution.py:30
  56.6 35.4 %collective-permute-start.13 = (bf16[1472,512]{1,0:T(8,128)(2,1)S(1)}, bf16[1472,512]{1,0:T(8,128)(2,1)}, u32[]{:S(2)}, u32[]{:S(2)}) collective-permute-start(bf16[1472,512]{1,0:T(8,128)(2,1)S(1)} %bitcast.177), channel_id=1, source_target_pairs={{0,2},{2,0},{4,6},{6,4},{8,10},{10,8},{12,14},{14,12},{16,18},{18,... | collective-permute-start | bytes 4521992 | tf_op jit(solution)/shard_map/ppermute | solution.py:30
  101.5 37.6 %collective-permute-start.14 = (bf16[2,384,512]{2,1,0:T(8,128)(2,1)}, bf16[2,384,512]{2,1,0:T(8,128)(2,1)S(1)}, u32[]{:S(2)}, u32[]{:S(2)}) collective-permute-start(bf16[2,384,512]{2,1,0:T(8,128)(2,1)} %get-tuple-element.108), channel_id=1, source_target_pairs={{0,1},{1,0},{2,3},{3,2},{4,5},{5,4},{6,7},{7,6},{8,9},{9,8},{10,11... | collective-permute-start | bytes 2359304 | tf_op jit(solution)/shard_map/ppermute | solution.py:35
  111.6 51.6 %collective-permute-start.15 = (bf16[2,384,512]{2,1,0:T(8,128)(2,1)}, bf16[2,384,512]{2,1,0:T(8,128)(2,1)S(1)}, u32[]{:S(2)}, u32[]{:S(2)}) collective-permute-start(bf16[2,384,512]{2,1,0:T(8,128)(2,1)} %get-tuple-element.113), channel_id=1, source_target_pairs={{0,1},{1,0},{2,3},{3,2},{4,5},{5,4},{6,7},{7,6},{8,9},{9,8},{10,11... | collective-permute-start | bytes 2359304 | tf_op jit(solution)/shard_map/ppermute | solution.py:35
  237.5 115.3 %collective-permute-start.20 = (bf16[3,368,512]{2,1,0:T(8,128)(2,1)}, bf16[3,368,512]{2,1,0:T(8,128)(2,1)}, u32[]{:S(2)}, u32[]{:S(2)}) collective-permute-start(bf16[3,368,512]{2,1,0:T(8,128)(2,1)} %get-tuple-element.130), channel_id=1, source_target_pairs={{0,1},{1,0},{2,3},{3,2},{4,5},{5,4},{6,7},{7,6},{8,9},{9,8},{10,11... | collective-permute-start | bytes 3391496 | tf_op jit(solution)/shard_map/ppermute | solution.py:35
  238.4 114.4 %collective-permute-start.21 = (bf16[3,368,512]{2,1,0:T(8,128)(2,1)}, bf16[3,368,512]{2,1,0:T(8,128)(2,1)}, u32[]{:S(2)}, u32[]{:S(2)}) collective-permute-start(bf16[3,368,512]{2,1,0:T(8,128)(2,1)} %get-tuple-element.132), channel_id=1, source_target_pairs={{0,4},{2,6},{4,0},{6,2},{8,12},{10,14},{12,8},{14,10},{16,20},{18,... | collective-permute-start | bytes 3391496 | tf_op jit(solution)/shard_map/ppermute | solution.py:30
  352.9 26.4 %collective-permute-start.19 = (bf16[2,1472,512]{2,1,0:T(8,128)(2,1)}, bf16[2,1472,512]{2,1,0:T(8,128)(2,1)S(1)}, u32[]{:S(2)}, u32[]{:S(2)}) collective-permute-start(bf16[2,1472,512]{2,1,0:T(8,128)(2,1)} %down.4.refs_8_), channel_id=1, source_target_pairs={{0,2},{2,0},{4,6},{6,4},{8,10},{10,8},{12,14},{14,12},{16,18},{18,... | collective-permute-start | bytes 9043976 | tf_op jit(solution)/shard_map/ppermute | solution.py:30
  357.3 55.3 %collective-permute-start.22 = (bf16[3,736,512]{2,1,0:T(8,128)(2,1)}, bf16[3,736,512]{2,1,0:T(8,128)(2,1)}, u32[]{:S(2)}, u32[]{:S(2)}) collective-permute-start(bf16[3,736,512]{2,1,0:T(8,128)(2,1)} %get-tuple-element.136), channel_id=1, source_target_pairs={{0,4},{2,6},{4,0},{6,2},{8,12},{10,14},{12,8},{14,10},{16,20},{18,... | collective-permute-start | bytes 6782984 | tf_op jit(solution)/shard_map/ppermute | solution.py:30
  358.8 53.8 %collective-permute-start.23 = (bf16[3,736,512]{2,1,0:T(8,128)(2,1)}, bf16[3,736,512]{2,1,0:T(8,128)(2,1)}, u32[]{:S(2)}, u32[]{:S(2)}) collective-permute-start(bf16[3,736,512]{2,1,0:T(8,128)(2,1)} %get-tuple-element.137), channel_id=1, source_target_pairs={{0,1},{1,0},{2,3},{3,2},{4,5},{5,4},{6,7},{7,6},{8,9},{9,8},{10,11... | collective-permute-start | bytes 6782984 | tf_op jit(solution)/shard_map/ppermute | solution.py:35
  359.2 69.3 %collective-permute-start.24 = (bf16[3,368,384]{2,1,0:T(8,128)(2,1)}, bf16[3,368,384]{2,1,0:T(8,128)(2,1)}, u32[]{:S(2)}, u32[]{:S(2)}) collective-permute-start(bf16[3,368,384]{2,1,0:T(8,128)(2,1)} %get-tuple-element.143), channel_id=1, source_target_pairs={{0,1},{1,0},{2,3},{3,2},{4,5},{5,4},{6,7},{7,6},{8,9},{9,8},{10,11... | collective-permute-start | bytes 2543624 | tf_op jit(solution)/shard_map/ppermute | solution.py:35
  360.8 67.7 %collective-permute-start.25 = (bf16[3,368,384]{2,1,0:T(8,128)(2,1)}, bf16[3,368,384]{2,1,0:T(8,128)(2,1)}, u32[]{:S(2)}, u32[]{:S(2)}) collective-permute-start(bf16[3,368,384]{2,1,0:T(8,128)(2,1)} %get-tuple-element.145), channel_id=1, source_target_pairs={{0,4},{2,6},{4,0},{6,2},{8,12},{10,14},{12,8},{14,10},{16,20},{18,... | collective-permute-start | bytes 2543624 | tf_op jit(solution)/shard_map/ppermute | solution.py:30
  417.7 48.3 %collective-permute-start.26 = (bf16[3,368,512]{2,1,0:T(8,128)(2,1)}, bf16[3,368,512]{2,1,0:T(8,128)(2,1)S(1)}, u32[]{:S(2)}, u32[]{:S(2)}) collective-permute-start(bf16[3,368,512]{2,1,0:T(8,128)(2,1)} %get-tuple-element.152), channel_id=1, source_target_pairs={{0,8},{2,10},{4,12},{6,14},{8,0},{10,2},{12,4},{14,6},{16,24},{18,... | collective-permute-start | bytes 3391496 | tf_op jit(solution)/shard_map/ppermute | solution.py:30
  464.0 30.5 %collective-permute-start.29 = (bf16[2,384,512]{2,1,0:T(8,128)(2,1)}, bf16[2,384,512]{2,1,0:T(8,128)(2,1)}, u32[]{:S(2)}, u32[]{:S(2)}) collective-permute-start(bf16[2,384,512]{2,1,0:T(8,128)(2,1)} %get-tuple-element.159), channel_id=1, source_target_pairs={{0,1},{1,0},{2,3},{3,2},{4,5},{5,4},{6,7},{7,6},{8,9},{9,8},{10,11... | collective-permute-start | bytes 2359304 | tf_op jit(solution)/shard_map/ppermute | solution.py:35
  464.4 41.9 %collective-permute-start.28 = (bf16[2,384,512]{2,1,0:T(8,128)(2,1)}, bf16[2,384,512]{2,1,0:T(8,128)(2,1)}, u32[]{:S(2)}, u32[]{:S(2)}) collective-permute-start(bf16[2,384,512]{2,1,0:T(8,128)(2,1)} %get-tuple-element.156), channel_id=1, source_target_pairs={{0,1},{1,0},{2,3},{3,2},{4,5},{5,4},{6,7},{7,6},{8,9},{9,8},{10,11... | collective-permute-start | bytes 2359304 | tf_op jit(solution)/shard_map/ppermute | solution.py:35
  470.4 40.3 %collective-permute-start.30 = (bf16[3,184,512]{2,1,0:T(8,128)(2,1)}, bf16[3,184,512]{2,1,0:T(8,128)(2,1)S(1)}, u32[]{:S(2)}, u32[]{:S(2)}) collective-permute-start(bf16[3,184,512]{2,1,0:T(8,128)(2,1)} %get-tuple-element.161), channel_id=1, source_target_pairs={{0,16},{2,18},{4,20},{6,22},{8,24},{10,26},{12,28},{14,30},{16,0},... | collective-permute-start | bytes 1695752 | tf_op jit(solution)/shard_map/ppermute | solution.py:30
  474.7 61.6 %collective-permute-start.33 = (bf16[3,736,384]{2,1,0:T(8,128)(2,1)}, bf16[3,736,384]{2,1,0:T(8,128)(2,1)S(1)}, u32[]{:S(2)}, u32[]{:S(2)}) collective-permute-start(bf16[3,736,384]{2,1,0:T(8,128)(2,1)} %get-tuple-element.165), channel_id=1, source_target_pairs={{0,1},{1,0},{2,3},{3,2},{4,5},{5,4},{6,7},{7,6},{8,9},{9,8},{10,11... | collective-permute-start | bytes 5087240 | tf_op jit(solution)/shard_map/ppermute | solution.py:35
  475.0 61.3 %collective-permute-start.32 = (bf16[3,736,384]{2,1,0:T(8,128)(2,1)S(1)}, bf16[3,736,384]{2,1,0:T(8,128)(2,1)}, u32[]{:S(2)}, u32[]{:S(2)}) collective-permute-start(bf16[3,736,384]{2,1,0:T(8,128)(2,1)S(1)} %copy-done.9), channel_id=1, source_target_pairs={{0,4},{2,6},{4,0},{6,2},{8,12},{10,14},{12,8},{14,10},{16,20},{18,... | collective-permute-start | bytes 5087240 | tf_op jit(solution)/shard_map/ppermute | solution.py:30
  494.4 83.4 %collective-permute-start.27 = (bf16[2,1472,512]{2,1,0:T(8,128)(2,1)}, bf16[2,1472,512]{2,1,0:T(8,128)(2,1)}, u32[]{:S(2)}, u32[]{:S(2)}) collective-permute-start(bf16[2,1472,512]{2,1,0:T(8,128)(2,1)} %down.6.refs_4_), channel_id=1, source_target_pairs={{0,2},{2,0},{4,6},{6,4},{8,10},{10,8},{12,14},{14,12},{16,18},{18,... | collective-permute-start | bytes 9043976 | tf_op jit(solution)/shard_map/ppermute | solution.py:30
  525.4 20.1 %collective-permute-start.34 = (bf16[1,1472,384]{2,1,0:T(8,128)(2,1)}, bf16[1,1472,384]{2,1,0:T(8,128)(2,1)}, u32[]{:S(2)}, u32[]{:S(2)}) collective-permute-start(bf16[1,1472,384]{2,1,0:T(8,128)(2,1)} %get-tuple-element.326), channel_id=1, source_target_pairs={{0,2},{2,0},{4,6},{6,4},{8,10},{10,8},{12,14},{14,12},{16,18},{18,... | collective-permute-start | bytes 3391496 | tf_op jit(solution)/shard_map/ppermute | solution.py:30
  525.4 25.0 %collective-permute-start.31 = (bf16[1,1472,384]{2,1,0:T(8,128)(2,1)}, bf16[1,1472,384]{2,1,0:T(8,128)(2,1)}, u32[]{:S(2)}, u32[]{:S(2)}) collective-permute-start(bf16[1,1472,384]{2,1,0:T(8,128)(2,1)} %get-tuple-element.327), channel_id=1, source_target_pairs={{0,2},{2,0},{4,6},{6,4},{8,10},{10,8},{12,14},{14,12},{16,18},{18,... | collective-permute-start | bytes 3391496 | tf_op jit(solution)/shard_map/ppermute | solution.py:30
  541.8 30.3 %collective-permute-start.37 = (bf16[3,368,384]{2,1,0:T(8,128)(2,1)}, bf16[3,368,384]{2,1,0:T(8,128)(2,1)S(1)}, u32[]{:S(2)}, u32[]{:S(2)}) collective-permute-start(bf16[3,368,384]{2,1,0:T(8,128)(2,1)} %get-tuple-element.177), channel_id=1, source_target_pairs={{0,8},{2,10},{4,12},{6,14},{8,0},{10,2},{12,4},{14,6},{16,24},{18,... | collective-permute-start | bytes 2543624 | tf_op jit(solution)/shard_map/ppermute | solution.py:30
  548.2 18.7 %collective-permute-start.35 = (bf16[1,368,384]{2,1,0:T(8,128)(2,1)}, bf16[1,368,384]{2,1,0:T(8,128)(2,1)S(1)}, u32[]{:S(2)}, u32[]{:S(2)}) collective-permute-start(bf16[1,368,384]{2,1,0:T(8,128)(2,1)} %get-tuple-element.171), channel_id=1, source_target_pairs={{0,1},{1,0},{2,3},{3,2},{4,5},{5,4},{6,7},{7,6},{8,9},{9,8},{10,11... | collective-permute-start | bytes 847880 | tf_op jit(solution)/shard_map/ppermute | solution.py:35
  548.3 18.6 %collective-permute-start.36 = (bf16[1,368,384]{2,1,0:T(8,128)(2,1)}, bf16[1,368,384]{2,1,0:T(8,128)(2,1)S(1)}, u32[]{:S(2)}, u32[]{:S(2)}) collective-permute-start(bf16[1,368,384]{2,1,0:T(8,128)(2,1)} %get-tuple-element.172), channel_id=1, source_target_pairs={{0,4},{2,6},{4,0},{6,2},{8,12},{10,14},{12,8},{14,10},{16,20},{18,... | collective-permute-start | bytes 847880 | tf_op jit(solution)/shard_map/ppermute | solution.py:30
  576.1 22.1 %collective-permute-start.49 = (bf16[3,184,384]{2,1,0:T(8,128)(2,1)}, bf16[3,184,384]{2,1,0:T(8,128)(2,1)S(1)}, u32[]{:S(2)}, u32[]{:S(2)}) collective-permute-start(bf16[3,184,384]{2,1,0:T(8,128)(2,1)} %get-tuple-element.194), channel_id=1, source_target_pairs={{0,16},{2,18},{4,20},{6,22},{8,24},{10,26},{12,28},{14,30},{16,0},... | collective-permute-start | bytes 1271816 | tf_op jit(solution)/shard_map/ppermute | solution.py:30
  605.6 23.3 %collective-permute-start.45 = (bf16[1,368,384]{2,1,0:T(8,128)(2,1)}, bf16[1,368,384]{2,1,0:T(8,128)(2,1)S(1)}, u32[]{:S(2)}, u32[]{:S(2)}) collective-permute-start(bf16[1,368,384]{2,1,0:T(8,128)(2,1)} %get-tuple-element.191), channel_id=1, source_target_pairs={{0,8},{2,10},{4,12},{6,14},{8,0},{10,2},{12,4},{14,6},{16,24},{18,... | collective-permute-start | bytes 847880 | tf_op jit(solution)/shard_map/ppermute | solution.py:30
  605.6 36.1 %collective-permute-start.50 = (bf16[3,92,896]{2,1,0:T(8,128)(2,1)S(1)}, bf16[3,92,896]{2,1,0:T(8,128)(2,1)S(1)}, u32[]{:S(2)}, u32[]{:S(2)}) collective-permute-start(bf16[3,92,896]{2,1,0:T(8,128)(2,1)S(1)} %get-tuple-element.334), channel_id=1, source_target_pairs={{0,2},{2,0},{4,6},{6,4},{8,10},{10,8},{12,14},{14,12},{16,18},{18,... | collective-permute-start | bytes 1483784 | tf_op jit(solution)/shard_map/ppermute | solution.py:30
  (63 other events, 380.2 us)
Sparse Core Ops, SparseCore 0:
  12.2 164.2 all-gather.4
  179.2 114.1 all-gather.6

commit v4 on v3

--- a/solution.py
+++ b/solution.py
@@ -16,7 +16,8 @@
 NEGATIVE = -1e30
 VMEM_BYTES = 60 * 1024 * 1024
 LANES = 128
-COST_SHARE = 0.05
+COST_SHARE = 1.0
+FIRST_SEVENTHS = 4
 
 
 DP = ("chip", "core")
@@ -44,6 +45,11 @@
     for term in terms[1:]:
         total = total + term.astype(F32)
     return total.astype(BF16)
+
+
+def trade_rows(array, core, rows):
+    low, high = array[:, :rows], array[:, rows:]
+    return either(core, low, high), swap_dp(either(core, high, low), 1)
 
 
 def first_of(parts):
@@ -101,7 +107,7 @@
         got.append((swap_mp(hold(low, *first), k), swap_dp(hold(high, *first), 2)))
     got = hold(got, *then)
     if len(got) == 1:
-        to_y, to_x = add_corner(to_y, got[0][0], quads[1][0], got[0][1])
+        to_y, to_x = add_corner(to_y, got[0][0], quads[1][0], got[0][1], then)
         return own, to_y, [to_x]
     half = own.shape[1] // 2
     low = add_low(to_y[:, :half], *[part for part, _ in got])
@@ -114,26 +120,30 @@
 
 def scatter_xy(own, to_y, to_x, then=()):
     got = [swap_dp(to_y, 2)] + [swap_mp(other, k) for k, other in zip(x_masks(), to_x)]
-    return sum_rows([own, *hold(got, *then)], 2)
+    return sum_rows([own, *hold(got, *then)], 2, after=then)
 
 
 def scatter_z(pair, stage, then=()):
     masks = z_masks()
     mask = masks[len(masks) - 1 - stage]
     got = hold(swap_dp(pair[1], mask), *then)
-    return sum_rows([pair[0], got], 1 if stage == len(masks) - 1 else 2)
-
-
-def sum_all(values, late):
-    mask = 1
-    while mask < lax.axis_size("mp"):
-        values = values + swap_mp(values, mask)
+    return sum_rows([pair[0], got], 1 if stage == len(masks) - 1 else 2, after=then)
+
+
+def doubling(count):
+    masks, mask = [], 1
+    while mask < count:
+        masks.append(mask)
         mask *= 2
-    mask = 1
-    while mask < dp_size():
-        values = values + swap_dp(hold(values, *late) if mask > 2 else values, mask)
-        mask *= 2
-    return values
+    return masks
+
+
+def beside(got, values, steps):
+    if not steps:
+        return got, values
+    swap, mask = steps.pop(0)
+    got, other = lax.optimization_barrier((got, swap(values, mask)))
+    return got, values + other
 
 
 def call(
@@ -685,7 +695,7 @@
     x_out[...] = (x_ref[...].astype(F32) + second_ref[...].astype(F32)).astype(BF16)
 
 
-def add_corner(to_y, first, to_x, second):
+def add_corner(to_y, first, to_x, second, after):
     kinds, half, width = first.shape
     upper = pl.BlockSpec((1, half, width), lambda k: (k, 0, 0))
     lower = pl.BlockSpec((1, half, width), lambda k: (k, 1, 0))
@@ -698,6 +708,7 @@
         [jax.ShapeDtypeStruct(to_y.shape, BF16), jax.ShapeDtypeStruct(to_x.shape, BF16)],
         [to_y, first, to_x, second],
         aliases={0: 0, 2: 1},
+        after=after,
     )
 
 
@@ -773,8 +784,6 @@
     q_blocks = length // block
     k_blocks = q_blocks * sources
     place_x = info_ref[0]
-    lane = lax.broadcasted_iota(jnp.int32, (block, 2 * half), 1)
-
     db_scr[...] = jnp.zeros(db_scr.shape, F32)
     for s in range(sources):
         k_scr[s * length : (s + 1) * length, :] = transposed(kv_refs[2 * s][...])
@@ -792,13 +801,6 @@
         )
         q_heads = halves(query_t, half)
         g_heads = halves(grad_out_t, half)
-        query, grad_out = transposed(query_t), transposed(grad_out_t)
-        zero = jnp.zeros(query.shape, BF16)
-        q_lanes = (jnp.where(lane < half, query, zero), jnp.where(lane < half, zero, query))
-        g_lanes = (
-            jnp.where(lane < half, grad_out, zero),
-            jnp.where(lane < half, zero, grad_out),
-        )
         seg_q = segq_ref[:, rows]
         dq_scr[...] = jnp.zeros(dq_scr.shape, F32)
         for kb in range(k_blocks):
@@ -812,8 +814,6 @@
                 keys = k_scr[key_rows, :]
                 values = v_scr[key_rows, :]
                 kept = segk_ref[key_rows, :] == seg_q
-                key_grad = dk_scr[key_rows, :]
-                value_grad = dv_scr[key_rows, :]
                 for h in range(2):
                     score = dot_nn(keys, q_heads[h]) + table_ref[h, entry]
                     score = jnp.where(kept, score, NEGATIVE)
@@ -822,20 +822,18 @@
                     grad_score = prob * (grad_prob - deltas[h])
                     db_scr[h, s, q_blocks - 1 - lb + qb] += grad_score
                     low = grad_score.astype(BF16)
-                    key_grad = key_grad + dot_nn(low, q_lanes[h])
-                    value_grad = value_grad + dot_nn(prob.astype(BF16), g_lanes[h])
-                    keys_t = kv_refs[2 * s][
-                        h * half : (h + 1) * half, lb * block : (lb + 1) * block
-                    ]
-                    dq_scr[h * half : (h + 1) * half] += dot_nn(keys_t, low)
-                dk_scr[key_rows, :] = key_grad
-                dv_scr[key_rows, :] = value_grad
+                    head = slice(h * half, (h + 1) * half)
+                    key_lanes = slice(kb * block, (kb + 1) * block)
+                    dk_scr[head, key_lanes] += dot_nt(query_t[head], low)
+                    dv_scr[head, key_lanes] += dot_nt(grad_out_t[head], prob.astype(BF16))
+                    keys_t = kv_refs[2 * s][head, lb * block : (lb + 1) * block]
+                    dq_scr[head] += dot_nn(keys_t, low)
 
         dq_ref[:, rows] = dq_scr[...].astype(BF16)
     for s in range(sources):
-        rows = slice(s * length, (s + 1) * length)
-        dkv_refs[s][0] = jnp.transpose(dk_scr[rows, :], (1, 0)).astype(BF16)
-        dkv_refs[s][1] = jnp.transpose(dv_scr[rows, :], (1, 0)).astype(BF16)
+        lanes = slice(s * length, (s + 1) * length)
+        dkv_refs[s][0] = dk_scr[:, lanes].astype(BF16)
+        dkv_refs[s][1] = dv_scr[:, lanes].astype(BF16)
 
     for h in range(2):
         for s in range(sources):
@@ -941,8 +939,8 @@
         [info, qkv, *kvs, seg_q, seg_k, table, context, lse, grad_context],
         flops=32 * inner * length * length * sources,
         scratch=[
-            pltpu.VMEM((length * sources, width), F32),
-            pltpu.VMEM((length * sources, width), F32),
+            pltpu.VMEM((width, length * sources), F32),
+            pltpu.VMEM((width, length * sources), F32),
             pltpu.VMEM((width, block), F32),
             pltpu.VMEM((length * sources, width), BF16),
             pltpu.VMEM((length * sources, width), BF16),
@@ -991,7 +989,7 @@
     return result, refs[start:]
 
 
-def ffn_kernel(counts, groups, gathered, info_ref, *refs):
+def ffn_kernel(counts, groups, gathered, stacked, info_ref, *refs):
     if gathered:
         stacks, refs = refs[:3], refs[3:]
         blocks = stacks[0].shape[0] // len(counts)
@@ -1001,20 +999,25 @@
         tile = sources[0].shape[2]
     acts_hbm, refs = refs[: 2 * groups], refs[2 * groups :]
     (hid_ref, ggi_ref, gui_ref, w_ref), refs = refs[:4], refs[4:]
-    grads, (acts, sems) = split_refs(refs, counts)
+    if stacked:
+        grads_ref, acts, sems = refs
+    else:
+        grads, (acts, sems) = split_refs(refs, counts)
     first = pl.program_id(0) == 0
 
     def fetch(n):
         return pltpu.make_async_copy(acts_hbm[n], acts.at[n], sems.at[n])
+
+    def places(source):
+        return [
+            (info_ref[1] ^ source) * blocks + block_of(info_ref[0], p, blocks // 2)
+            for p in range(blocks)
+        ]
 
     def matrix(kind, source):
         if not gathered:
             return sources[source][kind]
-        places = [
-            (info_ref[1] ^ source) * blocks + block_of(info_ref[0], p, blocks // 2)
-            for p in range(blocks)
-        ]
-        rows = [stacks[kind][place].astype(F32) for place in places]
+        rows = [stacks[kind][place].astype(F32) for place in places(source)]
         return jnp.concatenate(rows, axis=0).astype(BF16)
 
     @pl.when(first)
@@ -1050,9 +1053,17 @@
             for g in range(groups):
                 product = dot_nt(acts[left + g], right_ref[g, rows])
                 total = product if total is None else total + product
-            total = total.astype(BF16)
+            if not stacked:
+                total = total.astype(BF16)
             for n, s in enumerate(batch):
                 row = 0
+                if stacked:
+                    depth = grads_ref.shape[2]
+                    for place in places(s):
+                        part = total[row : row + depth, n * tile : (n + 1) * tile]
+                        grads_ref[place, kind] = part.astype(BF16)
+                        row += depth
+                    continue
                 for ref in grads[s]:
                     depth = ref.shape[1]
                     ref[kind] = total[row : row + depth, n * tile : (n + 1) * tile]
@@ -1063,7 +1074,7 @@
     return LANES if width % LANES == 0 else width
 
 
-def ffn_chunk(info, weights, width, normed, cot, after):
+def ffn_chunk(info, weights, width, stacked, normed, cot, after):
     groups = len(normed)
     wide, length = normed[0].shape
     gathered = not isinstance(weights, list)
@@ -1075,6 +1086,10 @@
     shapes = [(3, half, width)] * 2
     for _ in range(sources - 1):
         shapes += [(3, half, width)] + [(3, half // 2, width)] * 2
+    grad_specs = [pl.BlockSpec(shape[:2] + (tile,), lambda j, *_: (0, 0, j)) for shape in shapes]
+    if stacked:
+        shapes = [(weights.shape[0], 3, weights.shape[1], width)]
+        grad_specs = [pl.BlockSpec(shapes[0][:3] + (tile,), lambda j, *_: (0, 0, 0, j))]
     if gathered:
         weight_specs = [
             pl.BlockSpec(weights.shape[:2] + (tile,), lambda j, *_, n=n: (0, 0, n * steps + j))
@@ -1088,13 +1103,13 @@
     act_spec = pl.BlockSpec((groups, units, length), lambda j, *_: (0, j, 0))
     act_shape = jax.ShapeDtypeStruct((groups, sources * width, length), BF16)
     results = call(
-        functools.partial(ffn_kernel, counts, groups, gathered),
+        functools.partial(ffn_kernel, counts, groups, gathered, stacked),
         "ffn_chunk",
         (steps,),
         weight_specs + [pl.BlockSpec(memory_space=pl.ANY)] * (2 * groups),
         [act_spec] * 3
         + [pl.BlockSpec((3, wide, units), lambda j, *_: (0, 0, j))]
-        + [pl.BlockSpec(shape[:2] + (tile,), lambda j, *_: (0, 0, j)) for shape in shapes],
+        + grad_specs,
         [act_shape] * 3
         + [jax.ShapeDtypeStruct((3, wide, sources * width), BF16)]
         + [jax.ShapeDtypeStruct(shape, BF16) for shape in shapes],
@@ -1107,12 +1122,14 @@
         scalars=1,
         after=after,
     )
-    grads, _ = split_refs(results[4:], counts)
+    grads = results[4] if stacked else split_refs(results[4:], counts)[0]
     return results[:3], results[3], grads
 
 
-def down_kernel(chunks, kinds, *refs):
+def down_kernel(chunks, kinds, with_prior, *refs):
     total = None
+    if with_prior:
+        total, refs = refs[0][0].astype(F32), refs[1:]
     for _ in range(chunks):
         matrices, acts, refs = refs[:kinds], refs[kinds : 2 * kinds], refs[2 * kinds :]
         for matrix, act in zip(matrices, acts):
@@ -1122,10 +1139,13 @@
     out_ref[0] = total.astype(BF16)
 
 
-def down(chunk_weights, chunk_acts, first, kinds, start, count, after):
+def down(chunk_weights, chunk_acts, first, kinds, start, count, after, prior=None):
     length = chunk_acts[0][0].shape[2]
     wide = chunk_weights[0].shape[1]
     operands, specs = [], []
+    if prior is not None:
+        operands.append(prior)
+        specs.append(pl.BlockSpec((1, wide, length), lambda g: (start + g, 0, 0)))
     flops = 0
     for weights, acts in zip(chunk_weights, chunk_acts):
         acts = acts[1:] if kinds == 2 else acts[:1]
@@ -1141,7 +1161,7 @@
         ]
         flops += 2 * kinds * count * length * wide * acts[0].shape[1]
     return call(
-        functools.partial(down_kernel, len(chunk_acts), kinds),
+        functools.partial(down_kernel, len(chunk_acts), kinds, prior is not None),
         "down",
         (count,),
         specs,
@@ -1218,7 +1238,7 @@
         core, jnp.concatenate([kept, got], axis=1), jnp.concatenate([got, kept], axis=1)
     )
     if half_units % (7 * LANES) == 0:
-        bounds = [0, half_units // 7 * 4, half_units]
+        bounds = [0, half_units // 7 * FIRST_SEVENTHS, half_units]
     elif half_units > LANES:
         bounds = [0, LANES, half_units]
     else:
@@ -1293,8 +1313,11 @@
         normed2_far.append(swap_dp(normed, 1))
 
     ffn_info = jnp.concatenate([place, x.reshape(1).astype(jnp.int32)])
-    chunk_acts, chunk_weights, corners = [], [], []
+    chunk_acts, chunk_weights, chunk_grads = [], [], []
+    prior = prior_ffn = None
+    sums = []
     for stack, width in zip(chunk_stacks, widths):
+        stacked = len(chunk_acts) + 1 < len(widths)
         if own_rows % 4 or width % LANES:
             ordered = jnp.stack(
                 [
@@ -1303,17 +1326,25 @@
                 ]
             ).reshape(mp, model, 3, width)
             stack = [jnp.transpose(ordered[k], (1, 0, 2)) for k in range(mp)]
+            stacked = False
         acts, matrices_in, grads = ffn_chunk(
-            ffn_info, stack, width, normed2 + normed2_far, cots + cots_far, last
+            ffn_info, stack, width, stacked, normed2 + normed2_far, cots + cots_far, last
         )
-        last = [acts[0]] + [c[1] for c in corners]
+        last = [acts[0]]
         chunk_acts.append(acts)
         chunk_weights.append(matrices_in)
-        corners.append(scatter_corner(grads, [], [acts[0]] if len(widths) == 1 else []))
-    corners[0] = hold(corners[0], chunk_acts[-1][0])
-    back_far = down(chunk_weights, chunk_acts, 0, 2, groups, groups, chunk_acts[-1][:1])
+        if stacked:
+            sums.append(lax.psum_scatter(grads, ("mp", "chip"), scatter_dimension=0))
+        else:
+            chunk_grads.append(grads)
+        if len(chunk_acts) < len(widths):
+            prior = down(chunk_weights, chunk_acts, 0, 2, 0, 2 * groups, last)
+            prior_ffn = down(chunk_weights, chunk_acts, 2, 1, 0, 2 * groups, [prior])
+            last = [prior_ffn]
+    back = functools.partial(down, chunk_weights[-1:], chunk_acts[-1:], 0, 2)
+    back_far = back(groups, groups, last, prior)
     from_far = swap_dp(back_far, 1)
-    back_own = down(chunk_weights, chunk_acts, 0, 2, 0, groups, [back_far])
+    back_own = back(0, groups, [back_far], prior)
     last = [back_own]
 
     z_count = len(far_masks)
@@ -1330,15 +1361,14 @@
             contexts[m], lses[m], grad_context, block, head_size, last,
         )
         last = [dq]
+        if m == micros[0]:
+            moving = [scatter_corner(grads, [], last) for grads in chunk_grads]
+            last += [parts[1] for parts in moving]
         grad_q.append(dq)
         bias_grads.append(bias_grad)
         grad_kv.append((dkv[0], [swap_mp(dkv[k], k) for k in x_masks()]))
-        if m == micros[0]:
-            sums = [scatter_xy(*corners[0], [dq])]
-            waiting = [hold(corner, dq) for corner in corners[1:]]
-            last += [sums[0][0]] + [corner[1] for corner in waiting]
-    sums[0] = scatter_z(sums[0], 0, [dq])
-    last.append(sums[0][0])
+    moving = [scatter_xy(*parts, last) for parts in moving]
+    grad_kv[0] = sum_rows([grad_kv[0][0], *hold(grad_kv[0][1], dq)], 1, after=[dq])
     weight_grads = outer_products(
         role_place,
         (0, 3),
@@ -1347,22 +1377,23 @@
             [(grad_attn[m], contexts[m]) for m in micros],
         ],
         None,
-        last,
-    )
-    ffn_far = down(chunk_weights, chunk_acts, 2, 1, groups, groups, [weight_grads])
+        [dq, grad_kv[0]] + [first_of(parts) for parts in moving],
+    )
+    ffn = functools.partial(down, chunk_weights[-1:], chunk_acts[-1:], 2, 1)
+    ffn_far = ffn(groups, groups, [weight_grads], prior_ffn)
     ffn_from = swap_dp(ffn_far, 1)
-    ffn_own = down(chunk_weights, chunk_acts, 2, 1, 0, groups, [ffn_far])
-    sums[0] = scatter_z(sums[0], 1, [ffn_own])
-    last = [ffn_own, first_of(sums[0])]
-    grad_kv = [sum_rows([own, *hold(got, ffn_own)], 1, after=[ffn_own]) for own, got in grad_kv]
+    grad_kv[1:] = [
+        sum_rows([own, *hold(got, ffn_far)], 1, after=[ffn_far]) for own, got in grad_kv[1:]
+    ]
+    ffn_own = ffn(0, groups, [ffn_far, *grad_kv[1:]], prior_ffn)
+    moving = [scatter_z(parts, 0, [ffn_own]) for parts in moving]
     weight_grads = outer_products(
         role_place,
         (1, 2),
         [[(normed1[m], (grad_kv[m], n)) for m in micros] for n in range(2)],
         weight_grads,
-        last,
-    )
-    sums += [scatter_xy(*corner, [weight_grads]) for corner in waiting]
+        [ffn_own] + [first_of(parts) for parts in moving],
+    )
 
     half = model // 2
     split = [half, half // 2, half // 2]
@@ -1392,41 +1423,12 @@
         gain1,
         weights,
         chips,
-        [quads[0][0]] + [parts[0] for parts in sums[1:]],
-    )
-    corner = scatter_corner(quads, [], [gain1_grads])
-    last = [gain1_grads, corner[1]]
-    sums[1:] = [scatter_z(parts, 0, [gain1_grads]) for parts in sums[1:]]
-    last += [parts[0] for parts in sums[1:]]
-    outputs = finish(
-        place,
-        [(layer_in[m], contexts[m]) for m in micros],
-        (ffn_own, ffn_from),
-        weights,
-        chips,
-        last,
-    )
-    sums[1:] = [scatter_z(parts, 1, [outputs]) for parts in sums[1:]]
-    total = scatter_xy(*corner, [outputs])
-    for stage in range(z_count):
-        total = scatter_z(total, stage)
-    piece = total[0]
-    for stage in range(2, z_count):
-        sums = [scatter_z(parts, stage) for parts in sums]
-    over_x = jnp.stack([piece] + [swap_mp(piece, k) for k in x_masks()])
-    kept = either(core, over_x[:, :own_rows], over_x[:, own_rows:])
-    got = swap_dp(either(core, over_x[:, own_rows:], over_x[:, :own_rows]), 1)
-    both = jnp.stack([kept, got], axis=1).reshape(2 * mp, own_rows, part)
-    final = jnp.concatenate(
-        [pick(both, (2 * x + core) ^ r, 0) for r in range(2 * mp)], axis=1
-    ).astype(F32)
-
-    sums = jnp.concatenate(sums, axis=2)
-    kept = either(core, sums[:, :own_rows], sums[:, own_rows:])
-    got = swap_dp(either(core, sums[:, own_rows:], sums[:, :own_rows]), 1)
-    ffn_grads = either(
-        core, jnp.concatenate([kept, got], axis=2), jnp.concatenate([got, kept], axis=2)
-    ).astype(F32)
+        [weight_grads, quads[0][0]],
+    )
+    last = [gain1_grads]
+    corner = scatter_corner(quads, [], last)
+    sums += [scatter_z(parts, 1, last) for parts in moving]
+    traded = [trade_rows(part, core, own_rows) for part in sums] if z_count == 2 else []
 
     bias_rows = sum(bias_grads)
     bias_tiles = sum(
@@ -1445,9 +1447,46 @@
     bucket_part = jnp.dot(bucket_hot.T, offsets_total.T, precision=TOP_PRECISION)
     rel_part = jnp.dot(bucket_part, head_hot, precision=TOP_PRECISION)
     gain_parts = jnp.concatenate([gain1_grads, sum(gain2_grads)], axis=1)
-    gain_parts = reorder(gain_parts[None], 0, place, chips, True)
+    gain_parts = reorder(hold(gain_parts, corner[1])[None], 0, place, chips, True)
     small = jnp.concatenate([gain_parts[:, 0], gain_parts[:, 1], rel_part.reshape(-1)])
-    small = sum_all(small, [outputs])
+
+    small = small + swap_dp(small, 1)
+    steps = [(swap_mp, mask) for mask in doubling(mp)]
+    steps += [(swap_dp, mask) for mask in doubling(dp) if mask > 1]
+    outputs = finish(
+        place,
+        [(layer_in[m], contexts[m]) for m in micros],
+        (ffn_own, ffn_from),
+        weights,
+        chips,
+        [corner[1], first_of(sums[-1])] + [got for _, got in traded[:-1]],
+    )
+    own, to_y, to_x = corner
+    got = [swap_dp(to_y, 2)] + [swap_mp(other, k) for k, other in zip(x_masks(), to_x)]
+    total = sum_rows([own, *hold(got, outputs)], 2, after=[outputs])
+    for stage, mask in enumerate(reversed(far_masks)):
+        got, small = beside(swap_dp(total[1], mask), small, steps)
+        total = sum_rows([total[0], got], 1 if stage == z_count - 1 else 2)
+    for stage in range(2, z_count):
+        sums = [scatter_z(parts, stage) for parts in sums]
+    piece = total[0]
+    got, small = beside([swap_mp(piece, k) for k in x_masks()], small, steps)
+    over_x = jnp.stack([piece] + got)
+    kept = either(core, over_x[:, :own_rows], over_x[:, own_rows:])
+    got = swap_dp(either(core, over_x[:, own_rows:], over_x[:, :own_rows]), 1)
+    got, small = beside(got, small, steps)
+    while steps:
+        got, small = beside(got, small, steps)
+    both = jnp.stack([kept, got], axis=1).reshape(2 * mp, own_rows, part)
+    final = jnp.concatenate(
+        [pick(both, (2 * x + core) ^ r, 0) for r in range(2 * mp)], axis=1
+    ).astype(F32)
+
+    traded = traded or [trade_rows(part, core, own_rows) for part in sums]
+    kept, got = [part for part, _ in traded], [part for _, part in traded]
+    ffn_grads = either(
+        core, jnp.concatenate(kept + got, axis=2), jnp.concatenate(got + kept, axis=2)
+    ).astype(F32)
 
     shape = inputs.shape
 

time: 667 us -> 594 us (0.89)
  waiting for transfers between devices: 157 us -> 105 us
  starting transfers between devices: 60.9 us -> 46.6 us
  Pallas kernels: 377 us -> 365 us
    all_gather x2, waiting for transfers between devices: 51.2 us -> 9.4 us  [body(): chunk_stacks.append(lax.all_gather(flat, ('mp', 'chip')))]
    ppermute x37 -> x34, starting transfers between devices: 47.6 us -> 31.9 us  [swap_dp(): return lax.ppermute(array, DP, [(i, i ^ mask) for i in range(dp_size())])]
    ppermute x37 -> x34, waiting for transfers between devices: 48.5 us -> 35.1 us  [swap_dp(): return lax.ppermute(array, DP, [(i, i ^ mask) for i in range(dp_size())])]
    pallas_call x48 -> x46, Pallas kernels: 377 us -> 365 us  [call(): pl.pallas_call(run, grid_spec=pltpu.PrefetchScalarGridSpec(num_scalar_pre...]
    ppermute x14 -> x12, waiting for transfers between devices: 57.2 us -> 60 us  [swap_mp(): return lax.ppermute(array, 'mp', [(i, i ^ mask) for i in range(count)])]
    unnamed x90 -> x104, local copies, waits for them, and re-layouts: 14.6 us -> 17.3 us
    ppermute x14 -> x12, starting transfers between devices: 13.2 us -> 14.6 us  [swap_mp(): return lax.ppermute(array, 'mp', [(i, i ^ mask) for i in range(count)])]
  transfers between devices with their start and end apart: 53 -> 49, of which waited for: 24 -> 24; matrix products, arithmetic and copies ran while one was open for 4% -> 5% of each run, Pallas kernels for 57% -> 63%
where the time goes in v4:
time: 594 us; the launch traced here: 583 us
  Pallas kernels  365 us (61%)
  waiting for transfers between devices  105 us (18%)
  starting transfers between devices  46.6 us (8%)
  local copies, waits for them, and re-layouts  37.5 us (6%)
  between operations  14.9 us (3%)
  other arithmetic  12.4 us (2%)
    pallas_call x46, Pallas kernels, call(): pl.pallas_call(run, grid_spec=pltpu.PrefetchScalarGridSpec(num_scalar_pre...  365 us
    ppermute x12, waiting for transfers between devices, swap_mp(): return lax.ppermute(array, 'mp', [(i, i ^ mask) for i in range(count)])  60 us
    ppermute x34, waiting for transfers between devices, swap_dp(): return lax.ppermute(array, DP, [(i, i ^ mask) for i in range(dp_size())])  35.1 us
    ppermute x34, starting transfers between devices, swap_dp(): return lax.ppermute(array, DP, [(i, i ^ mask) for i in range(dp_size())])  31.9 us
    unnamed x104, local copies, waits for them, and re-layouts  17.3 us
    ppermute x12, starting transfers between devices, swap_mp(): return lax.ppermute(array, 'mp', [(i, i ^ mask) for i in range(count)])  14.6 us
  transfers between devices with their start and end apart: 49, of which 24 were waited for; matrix products, arithmetic and copies ran while one was open for 5% of the time, Pallas kernels for 63%

profile of v4, /device:TPU:0, one launch (start us, length us, event | category | flops | bytes accessed | tf_op | source)
XLA Modules:
  0.0 582.9 jit_solution(13084138352668232300)
XLA Ops:
  31.0 13.8 %collective-permute-done.2.refs_1_ = bf16[1,368,384]{2,1,0:T(8,128)(2,1)S(1)} collective-permute-done((bf16[1,368,384]{2,1,0:T(8,128)(2,1)}, bf16[1,368,384]{2,1,0:T(8,128)(2,1)S(1)}, u32[]{:S(2)}, u32[]{:S(2)}) %collective-permute-start.2) | collective-permute-done | bytes 282656 | tf_op jit(solution)/shard_map/ppermute | solution.py:31
  59.0 6.8 %bias_table.1.refs_8_ = f32[6,7,256,256]{3,2,1,0:T(8,128)} custom-call(f32[6,7,1,512]{3,2,1,0:T(1,128)} %broadcast_in_dim.2.refs_0_, bf16[1472,512]{1,0:T(8,128)(2,1)} %bitcast.171, bf16[1472,512]{1,0:T(8,128)(2,1)} %bitcast.165), custom_call_target="tpu_custom_call" | custom-call | bytes 11096064 | tf_op jit(solution)/shard_map/bias_table/pallas_call | solution.py:160
  65.8 7.1 %collective-permute-done.4.refs_0_.refs_7_.refs_5_ = bf16[1,736,384]{2,1,0:T(8,128)(2,1)S(1)} collective-permute-done((bf16[1,736,384]{2,1,0:T(8,128)(2,1)}, bf16[1,736,384]{2,1,0:T(8,128)(2,1)S(1)}, u32[]{:S(2)}, u32[]{:S(2)}) %collective-permute-start.4) | collective-permute-done | bytes 565280 | tf_op jit(solution)/shard_map/ppermute | solution.py:36
  93.8 9.0 %project.2 = (bf16[1472,512]{1,0:T(8,128)(2,1)}, bf16[4,384,512]{2,1,0:T(8,128)(2,1)}, bf16[2,384,512]{2,1,0:T(8,128)(2,1)}) custom-call(s32[1]{0:T(128)} %bitcast.6.refs_0_, bf16[1472,512]{1,0:T(8,128)(2,1)} %bitcast.148, f32[1472,1]{1,0:T(8,128)} %get-tuple-element.318.refs_2_.refs_9_, bf16[1,736,384]{2,1,0:T(8,128)(2,1)} %merge.3.refs_4_.refs_3_.refs_1_, ...), custom_call_target="tpu_custom_call" | custom-call | flops 1736441856 | bytes 9901828 | tf_op jit(solution)/shard_map/project/pallas_call | solution.py:160
  104.9 7.8 %project.3 = (bf16[1472,512]{1,0:T(8,128)(2,1)}, bf16[4,384,512]{2,1,0:T(8,128)(2,1)}, bf16[2,384,512]{2,1,0:T(8,128)(2,1)}) custom-call(s32[1]{0:T(128)} %bitcast.6.refs_0_, bf16[1472,512]{1,0:T(8,128)(2,1)} %bitcast.141, f32[1472,1]{1,0:T(8,128)} %get-tuple-element.318.refs_2_.refs_9_, bf16[1,736,384]{2,1,0:T(8,128)(2,1)} %merge.3.refs_4_.refs_3_.refs_1_, ...), custom_call_target="tpu_custom_call" | custom-call | flops 1736441856 | bytes 9901828 | tf_op jit(solution)/shard_map/project/pallas_call | solution.py:160
  116.7 4.7 assemble.1.refs_9_.refs_2_.refs_6_.refs_10_.refs_7_
  121.4 18.9 %collective-permute-done.14 = bf16[2,384,512]{2,1,0:T(8,128)(2,1)S(1)} collective-permute-done((bf16[2,384,512]{2,1,0:T(8,128)(2,1)}, bf16[2,384,512]{2,1,0:T(8,128)(2,1)S(1)}, u32[]{:S(2)}, u32[]{:S(2)}) %collective-permute-start.14) | collective-permute-done | bytes 786464 | tf_op jit(solution)/shard_map/ppermute | solution.py:36
  141.2 10.2 %attend.2 = (bf16[384,512]{1,0:T(8,128)(2,1)}, f32[3,8,512]{2,1,0:T(8,128)}) custom-call(s32[9]{0:T(128)} %pad_add_fusion.3.refs_0_, bf16[1536,512]{1,0:T(8,128)(2,1)} %bitcast.159, bf16[1536,512]{1,0:T(8,128)(2,1)} %bitcast.160, bf16[1536,512]{1,0:T(8,128)(2,1)} %bitcast.161, bf16[768,512]{1,0:T(8,128)(2,1)} %bitcast.187, bf16[768,512]{1,0:T(8,128)(2,1)} %bitcast.188, ...), custom_call_target="tpu_custom_call" | custom-call | flops 3221225472 | bytes 17750052 | tf_op jit(solution)/shard_map/attend/pallas_call | solution.py:160
  151.4 4.4 middle.2.refs_9_.refs_4_
  155.8 7.3 %collective-permute-done.15 = bf16[2,384,512]{2,1,0:T(8,128)(2,1)S(1)} collective-permute-done((bf16[2,384,512]{2,1,0:T(8,128)(2,1)}, bf16[2,384,512]{2,1,0:T(8,128)(2,1)S(1)}, u32[]{:S(2)}, u32[]{:S(2)}) %collective-permute-start.15) | collective-permute-done | bytes 786464 | tf_op jit(solution)/shard_map/ppermute | solution.py:36
  164.0 10.7 %attend.3 = (bf16[384,512]{1,0:T(8,128)(2,1)}, f32[3,8,512]{2,1,0:T(8,128)}) custom-call(s32[9]{0:T(128)} %pad_add_fusion.4.refs_0_, bf16[1536,512]{1,0:T(8,128)(2,1)} %bitcast.153, bf16[1536,512]{1,0:T(8,128)(2,1)} %bitcast.154, bf16[1536,512]{1,0:T(8,128)(2,1)} %bitcast.155, bf16[768,512]{1,0:T(8,128)(2,1)} %bitcast.183, bf16[768,512]{1,0:T(8,128)(2,1)} %bitcast.184, ...), custom_call_target="tpu_custom_call" | custom-call | flops 3221225472 | bytes 17750052 | tf_op jit(solution)/shard_map/attend/pallas_call | solution.py:160
  174.7 4.5 middle.3.refs_5_.refs_12_
  185.3 53.0 %ffn_chunk.2 = (bf16[4,1024,512]{2,1,0:T(8,128)(2,1)}, bf16[4,1024,512]{2,1,0:T(8,128)(2,1)}, bf16[4,1024,512]{2,1,0:T(8,128)(2,1)}, bf16[3,1472,1024]{2,1,0:T(8,128)(2,1)}, bf16[16,3,184,512]{3,2,1,0:T(8,128)(2,1)}) custom-call(s32[2]{0:T(128)} %pad_add_fusion.5.refs_0_, bf16[16,184,1536]{2,1,0:T(8,128)(2,1)} %bitcast.215, ...), custom_call_target="tpu_custom_call" | custom-call | flops 37044092928 | bytes 69861384 | tf_op jit(solution)/shard_map/ffn_chunk/pallas_call | solution.py:160
  238.3 17.9 %down.6.refs_2_.refs_0_ = bf16[4,1472,512]{2,1,0:T(8,128)(2,1)} custom-call(bf16[3,1472,1024]{2,1,0:T(8,128)(2,1)} %get-tuple-element.104.refs_0_.refs_1_, bf16[3,1472,1024]{2,1,0:T(8,128)(2,1)} %get-tuple-element.104.refs_0_.refs_1_, bf16[4,1024,512]{2,1,0:T(8,128)(2,1)} %get-tuple-element.106.refs_2_, bf16[4,1024,512]{2,1,0:T(8,128)(2,1)} %get-tuple-element.107.refs_3_, ...), custom_call_target="tpu_custom_call" | custom-call | flops 12348030976 | bytes 32505856 | tf_op jit(solution)/shard_map/down/pallas_call | solution.py:160
  256.2 10.5 %down.7.refs_12_.refs_0_ = bf16[4,1472,512]{2,1,0:T(8,128)(2,1)} custom-call(bf16[3,1472,1024]{2,1,0:T(8,128)(2,1)} %get-tuple-element.104.refs_0_.refs_1_, bf16[4,1024,512]{2,1,0:T(8,128)(2,1)} %get-tuple-element.105.refs_4_.refs_1_, bf16[4,1472,512]{2,1,0:T(8,128)(2,1)} %down.6.refs_2_.refs_0_), custom_call_target="tpu_custom_call" | custom-call | flops 6174015488 | bytes 19267584 | tf_op jit(solution)/shard_map/down/pallas_call | solution.py:160
  266.7 9.4 %all-gather.7.cloned.1.call-done = bf16[2944,1152]{1,0:T(8,128)(2,1)} async-done(((bf16[184,1152]{1,0:T(8,128)(2,1)}), bf16[2944,1152]{1,0:T(8,128)(2,1)}) %all-gather.7.cloned.1.call-update) | async-done | bytes 6782992 | tf_op jit(solution)/shard_map/all_gather | solution.py:1250
  276.0 41.1 %ffn_chunk.3 = (bf16[4,768,512]{2,1,0:T(8,128)(2,1)}, bf16[4,768,512]{2,1,0:T(8,128)(2,1)}, bf16[4,768,512]{2,1,0:T(8,128)(2,1)}, bf16[3,1472,768]{2,1,0:T(8,128...) custom-call(s32[2]{0:T(128)} %pad_add_fusion.5.refs_0_, ...), custom_call_target="tpu_custom_call" | custom-call | flops 27783069696 | bytes 55410696 | tf_op jit(solution)/shard_map/ffn_chunk/pallas_call | solution.py:160
  317.1 10.1 %down.8.refs_5_ = bf16[2,1472,512]{2,1,0:T(8,128)(2,1)} custom-call(bf16[4,1472,512]{2,1,0:T(8,128)(2,1)} %down.6.refs_2_.refs_0_, bf16[3,1472,768]{2,1,0:T(8,128)(2,1)} %get-tuple-element.108.refs_1_.refs_2_, bf16[3,1472,768]{2,1,0:T(8,128)(2,1)} %get-tuple-element.108.refs_1_.refs_2_, bf16[4,768,512]{2,1,0:T(8,128)(2,1)} %get-tuple-element.111.refs_3_, ...), custom_call_target="tpu_custom_call" | custom-call | flops 4630511616 | bytes 28901376 | tf_op jit(solution)/shard_map/down/pallas_call | solution.py:160
  329.4 10.0 %down.9.refs_3_.refs_7_ = bf16[2,1472,512]{2,1,0:T(8,128)(2,1)} custom-call(bf16[4,1472,512]{2,1,0:T(8,128)(2,1)} %down.6.refs_2_.refs_0_, bf16[3,1472,768]{2,1,0:T(8,128)(2,1)} %get-tuple-element.108.refs_1_.refs_2_, bf16[3,1472,768]{2,1,0:T(8,128)(2,1)} %get-tuple-element.108.refs_1_.refs_2_, bf16[4,768,512]{2,1,0:T(8,128)(2,1)} %get-tuple-element.111.refs_3_, ...), custom_call_target="tpu_custom_call" | custom-call | flops 4630511616 | bytes 28901376 | tf_op jit(solution)/shard_map/down/pallas_call | solution.py:160
  340.9 8.8 %turn.2 = (bf16[1472,512]{1,0:T(8,128)(2,1)}, bf16[384,512]{1,0:T(8,128)(2,1)}, f32[1472,1]{1,0:T(8,128)}) custom-call(bf16[1472,512]{1,0:T(8,128)(2,1)} %bitcast.150, bf16[384,512]{1,0:T(8,128)(2,1)} %get-tuple-element.100.refs_1_.refs_4_.refs_9_.refs_6_.refs_2_, bf16[1472,512]{1,0:T(8,128)(2,1)} %bitcast.174, bf16[2,1472,512]{2,1,0:T(8,128)(2,1)} %down.9.refs_3_.refs_7_, ...), custom_call_target="tpu_custom_call" | custom-call | flops 1157627904 | bytes 15871488 | tf_op jit(solution)/shard_map/turn/pallas_call | solution.py:160
  349.7 21.4 %attend_grads.2 = (bf16[384,512]{1,0:T(8,128)(2,1)}, f32[6,2,3,8,512]{4,3,2,1,0:T(8,128)}, bf16[2,384,512]{2,1,0:T(8,128)(2,1)}, bf16[2,384,512]{2,1,0:T(8,128)(2,1)}) custom-call(s32[9]{0:T(128)} %pad_add_fusion.3.refs_0_, bf16[1536,512]{1,0:T(8,128)(2,1)} %bitcast.162, bf16[1536,512]{1,0:T(8,128)(2,1)} %bitcast.163, bf16[1536,512]{1,0:T(8,128)(2,1)} %bitcast.164, ...), custom_call_target="tpu_custom_call" | custom-call | flops 6442450944 | bytes 20699172 | tf_op jit(solution)/shard_map/attend_grads/pallas_call | solution.py:160
  377.3 4.5 collective-permute-start.23
  383.2 9.1 %turn.3 = (bf16[1472,512]{1,0:T(8,128)(2,1)}, bf16[384,512]{1,0:T(8,128)(2,1)}, f32[1472,1]{1,0:T(8,128)}) custom-call(bf16[1472,512]{1,0:T(8,128)(2,1)} %bitcast.143, bf16[384,512]{1,0:T(8,128)(2,1)} %get-tuple-element.103.refs_1_.refs_4_.refs_9_.refs_8_, bf16[1472,512]{1,0:T(8,128)(2,1)} %bitcast.168, bf16[2,1472,512]{2,1,0:T(8,128)(2,1)} %down.9.refs_3_.refs_7_, ...), custom_call_target="tpu_custom_call" | custom-call | flops 1157627904 | bytes 15871488 | tf_op jit(solution)/shard_map/turn/pallas_call | solution.py:160
  392.3 22.1 %attend_grads.3 = (bf16[384,512]{1,0:T(8,128)(2,1)}, f32[6,2,3,8,512]{4,3,2,1,0:T(8,128)}, bf16[2,384,512]{2,1,0:T(8,128)(2,1)}, bf16[2,384,512]{2,1,0:T(8,128)(2,1)}) custom-call(s32[9]{0:T(128)} %pad_add_fusion.4.refs_0_, bf16[1536,512]{1,0:T(8,128)(2,1)} %bitcast.156, bf16[1536,512]{1,0:T(8,128)(2,1)} %bitcast.157, bf16[1536,512]{1,0:T(8,128)(2,1)} %bitcast.158, ...), custom_call_target="tpu_custom_call" | custom-call | flops 6442450944 | bytes 20699172 | tf_op jit(solution)/shard_map/attend_grads/pallas_call | solution.py:160
  415.1 10.2 %collective-permute-done.24.refs_2_ = bf16[3,736,384]{2,1,0:T(8,128)(2,1)S(1)} collective-permute-done((bf16[3,736,384]{2,1,0:T(8,128)(2,1)}, bf16[3,736,384]{2,1,0:T(8,128)(2,1)S(1)}, u32[]{:S(2)}, u32[]{:S(2)}) %collective-permute-start.24) | collective-permute-done | bytes 1695776 | tf_op jit(solution)/shard_map/ppermute | solution.py:36
  432.9 4.8 collective-permute-start.27
  444.5 7.8 %outer_products.2.refs_3_.refs_9_ = bf16[4,1472,384]{2,1,0:T(8,128)(2,1)} custom-call(s32[1]{0:T(128)S(6)} %and.10.refs_0_, bf16[1472,512]{1,0:T(8,128)(2,1)} %get-tuple-element.98.refs_13_.refs_1_.refs_5_, bf16[384,512]{1,0:T(8,128)(2,1)} %get-tuple-element.115.refs_4_.refs_7_.refs_2_.refs_3_, bf16[1472,512]{1,0:T(8,128)(2,1)} %get-tuple-element.99.refs_11_.refs_3_.refs_7_, ...), custom_call_target="tpu_custom_call" | custom-call | flops 2315255808 | bytes 12124164 | tf_op jit(solution)/shard_map/outer_products/pallas_call | solution.py:160
  452.3 6.3 %down.10.refs_2_.refs_3_ = bf16[2,1472,512]{2,1,0:T(8,128)(2,1)} custom-call(bf16[4,1472,512]{2,1,0:T(8,128)(2,1)} %down.7.refs_12_.refs_0_, bf16[3,1472,768]{2,1,0:T(8,128)(2,1)} %get-tuple-element.108.refs_1_.refs_2_, bf16[4,768,512]{2,1,0:T(8,128)(2,1)} %get-tuple-element.109.refs_5_.refs_2_, bf16[4,1472,384]{2,1,0:T(8,128)(2,1)} %outer_products.2.refs_3_.refs_9_), custom_call_target="tpu_custom_call" | custom-call | flops 2315255808 | bytes 18972672 | tf_op jit(solution)/shard_map/down/pallas_call | solution.py:160
  464.7 6.2 %down.11.refs_2_.refs_10_.refs_5_ = bf16[2,1472,512]{2,1,0:T(8,128)(2,1)} custom-call(bf16[4,1472,512]{2,1,0:T(8,128)(2,1)} %down.7.refs_12_.refs_0_, bf16[3,1472,768]{2,1,0:T(8,128)(2,1)} %get-tuple-element.108.refs_1_.refs_2_, bf16[4,768,512]{2,1,0:T(8,128)(2,1)} %get-tuple-element.109.refs_5_.refs_2_, bf16[2,1472,512]{2,1,0:T(8,128)(2,1)} %down.10.refs_2_.refs_3_, ...), custom_call_target="tpu_custom_call" | custom-call | flops 2315255808 | bytes 18972672 | tf_op jit(solution)/shard_map/down/pallas_call | solution.py:160
  474.9 8.0 %outer_products.3.refs_0_.refs_11_ = bf16[4,1472,384]{2,1,0:T(8,128)(2,1)} custom-call(s32[1]{0:T(128)S(6)} %and.10.refs_0_, bf16[1472,512]{1,0:T(8,128)(2,1)} %get-tuple-element.98.refs_13_.refs_1_.refs_5_, bf16[2,384,512]{2,1,0:T(8,128)(2,1)} %sum_rows.10.refs_10_.refs_2_.refs_6_.refs_4_, ...), custom_call_target="tpu_custom_call", output_to_operand_aliasing={{}: (9, {})} | custom-call | flops 2315255808 | bytes 18219012 | tf_op jit(solution)/shard_map/outer_products/pallas_call | solution.py:160
  499.8 13.6 %input_grads.1 = (bf16[2,8,184,512]{3,2,1,0:T(8,128)(2,1)}, f32[1472,1]{1,0:T(8,128)}) custom-call(s32[1]{0:T(128)} %bitcast.refs_0_, bf16[1472,512]{1,0:T(8,128)(2,1)} %bitcast.151, bf16[1472,512]{1,0:T(8,128)(2,1)} %get-tuple-element.114.refs_12_.refs_5_.refs_2_, bf16[384,512]{1,0:T(8,128)(2,1)} %get-tuple-element.115.refs_4_.refs_7_.refs_2_.refs_3_, ...), custom_call_target="tpu_custom_call" | custom-call | flops 3472883712 | bytes 15937028 | tf_op jit(solution)/shard_map/input_grads/pallas_call | solution.py:160
  527.7 7.2 %finish.1 = bf16[2,8,184,512]{3,2,1,0:T(8,128)(2,1)} custom-call(s32[1]{0:T(128)} %bitcast.refs_0_, bf16[1472,512]{1,0:T(8,128)(2,1)} %bitcast.152, bf16[384,512]{1,0:T(8,128)(2,1)} %get-tuple-element.100.refs_1_.refs_4_.refs_9_.refs_6_.refs_2_, bf16[1472,512]{1,0:T(8,128)(2,1)} %bitcast.145, ...), custom_call_target="tpu_custom_call" | custom-call | flops 1157627904 | bytes 17367044 | tf_op jit(solution)/shard_map/finish/pallas_call | solution.py:160
  (314 shorter events, 180.8 us)
Async XLA Ops:
  7.2 177.6 %all-gather.5.cloned.1.call-start = ((), (), s32[]{:S(2)}) async-start(), calls=%async_computation.2 | async-start | bytes 9609216 | tf_op jit(solution)/shard_map/all_gather | solution.py:1250
  12.1 264.0 %all-gather.7.cloned.1.call-start = ((), (), s32[]{:S(2)}) async-start(), calls=%async_computation.3 | async-start | bytes 7206912 | tf_op jit(solution)/shard_map/all_gather | solution.py:1250
  13.0 505.4 %reduce-scatter.2.cloned.1.call-start = ((), (), s32[]{:S(2)}) async-start(), calls=%async_computation.1 | async-start | bytes 9609216 | tf_op jit(solution)/shard_map/reduce_scatter | solution.py:1337
  14.6 11.1 %collective-permute-start.1 = (bf16[1,184,384]{2,1,0:T(8,128)(2,1)S(1)}, bf16[1,184,384]{2,1,0:T(8,128)(2,1)S(1)}, u32[]{:S(2)}, u32[]{:S(2)}) collective-permute-start(bf16[1,184,384]{2,1,0:T(8,128)(2,1)S(1)} %maximum_select_fusion.2.refs_0_), channel_id=1, source_target_pairs={{0,16},{2,18},{4,20},{6,22},{8,24},{10,26},{12,28},{14,30},{16,0},... | collective-permute-start | bytes 423944 | tf_op jit(solution)/shard_map/ppermute | solution.py:31
  28.0 16.8 %collective-permute-start.2 = (bf16[1,368,384]{2,1,0:T(8,128)(2,1)}, bf16[1,368,384]{2,1,0:T(8,128)(2,1)S(1)}, u32[]{:S(2)}, u32[]{:S(2)}) collective-permute-start(bf16[1,368,384]{2,1,0:T(8,128)(2,1)} %merge.2.refs_0_), channel_id=1, source_target_pairs={{0,8},{2,10},{4,12},{6,14},{8,0},{10,2},{12,4},{14,6},{16,24},{18,... | collective-permute-start | bytes 847880 | tf_op jit(solution)/shard_map/ppermute | solution.py:31
  47.4 25.5 %collective-permute-start.4 = (bf16[1,736,384]{2,1,0:T(8,128)(2,1)}, bf16[1,736,384]{2,1,0:T(8,128)(2,1)S(1)}, u32[]{:S(2)}, u32[]{:S(2)}) collective-permute-start(bf16[1,736,384]{2,1,0:T(8,128)(2,1)} %merge.3.refs_4_.refs_3_.refs_1_), channel_id=1, source_target_pairs={{0,1},{1,0},{2,3},{3,2},{4,5},{5,4},{6,7},{7,6},{8,9},{9,8},{10,11... | collective-permute-start | bytes 1695752 | tf_op jit(solution)/shard_map/ppermute | solution.py:36
  48.9 24.1 %collective-permute-start.3 = (bf16[1,736,384]{2,1,0:T(8,128)(2,1)}, bf16[1,736,384]{2,1,0:T(8,128)(2,1)S(1)}, u32[]{:S(2)}, u32[]{:S(2)}) collective-permute-start(bf16[1,736,384]{2,1,0:T(8,128)(2,1)} %merge.3.refs_4_.refs_3_.refs_1_), channel_id=1, source_target_pairs={{0,4},{2,6},{4,0},{6,2},{8,12},{10,14},{12,8},{14,10},{16,20},{18,... | collective-permute-start | bytes 1695752 | tf_op jit(solution)/shard_map/ppermute | solution.py:31
  56.1 36.7 %collective-permute-start.12 = (bf16[1472,512]{1,0:T(8,128)(2,1)}, bf16[1472,512]{1,0:T(8,128)(2,1)}, u32[]{:S(2)}, u32[]{:S(2)}) collective-permute-start(bf16[1472,512]{1,0:T(8,128)(2,1)} %bitcast.170), channel_id=1, source_target_pairs={{0,2},{2,0},{4,6},{6,4},{8,10},{10,8},{12,14},{14,12},{16,18},{18,... | collective-permute-start | bytes 4521992 | tf_op jit(solution)/shard_map/ppermute | solution.py:31
  56.1 36.7 %collective-permute-start.13 = (bf16[1472,512]{1,0:T(8,128)(2,1)S(1)}, bf16[1472,512]{1,0:T(8,128)(2,1)}, u32[]{:S(2)}, u32[]{:S(2)}) collective-permute-start(bf16[1472,512]{1,0:T(8,128)(2,1)S(1)} %bitcast.169), channel_id=1, source_target_pairs={{0,2},{2,0},{4,6},{6,4},{8,10},{10,8},{12,14},{14,12},{16,18},{18,... | collective-permute-start | bytes 4521992 | tf_op jit(solution)/shard_map/ppermute | solution.py:31
  56.7 25.7 %collective-permute-start.5 = (bf16[1,736,384]{2,1,0:T(8,128)(2,1)S(1)}, bf16[1,736,384]{2,1,0:T(8,128)(2,1)}, u32[]{:S(2)}, u32[]{:S(2)}) collective-permute-start(bf16[1,736,384]{2,1,0:T(8,128)(2,1)S(1)} %copy-done.2), channel_id=1, source_target_pairs={{0,2},{2,0},{4,6},{6,4},{8,10},{10,8},{12,14},{14,12},{16,18},{18,... | collective-permute-start | bytes 1695752 | tf_op jit(solution)/shard_map/ppermute | solution.py:31
  78.8 7.2 %collective-permute-start.7 = (bf16[1,368,384]{2,1,0:T(8,128)(2,1)}, bf16[1,368,384]{2,1,0:T(8,128)(2,1)S(1)}, u32[]{:S(2)}, u32[]{:S(2)}) collective-permute-start(bf16[1,368,384]{2,1,0:T(8,128)(2,1)} %rows.2), channel_id=1, source_target_pairs={{0,1},{1,0},{2,3},{3,2},{4,5},{5,4},{6,7},{7,6},{8,9},{9,8},{10,11... | collective-permute-start | bytes 847880 | tf_op jit(solution)/shard_map/ppermute | solution.py:36
  82.4 10.3 %collective-permute-start.6 = (bf16[1,736,384]{2,1,0:T(8,128)(2,1)}, bf16[1,736,384]{2,1,0:T(8,128)(2,1)S(1)}, u32[]{:S(2)}, u32[]{:S(2)}) collective-permute-start(bf16[1,736,384]{2,1,0:T(8,128)(2,1)} %copy-done.6), channel_id=1, source_target_pairs={{0,2},{2,0},{4,6},{6,4},{8,10},{10,8},{12,14},{14,12},{16,18},{18,... | collective-permute-start | bytes 1695752 | tf_op jit(solution)/shard_map/ppermute | solution.py:31
  102.8 37.5 %collective-permute-start.14 = (bf16[2,384,512]{2,1,0:T(8,128)(2,1)}, bf16[2,384,512]{2,1,0:T(8,128)(2,1)S(1)}, u32[]{:S(2)}, u32[]{:S(2)}) collective-permute-start(bf16[2,384,512]{2,1,0:T(8,128)(2,1)} %get-tuple-element.97), channel_id=1, source_target_pairs={{0,1},{1,0},{2,3},{3,2},{4,5},{5,4},{6,7},{7,6},{8,9},{9,8},{10,11... | collective-permute-start | bytes 2359304 | tf_op jit(solution)/shard_map/ppermute | solution.py:36
  112.7 50.3 %collective-permute-start.15 = (bf16[2,384,512]{2,1,0:T(8,128)(2,1)}, bf16[2,384,512]{2,1,0:T(8,128)(2,1)S(1)}, u32[]{:S(2)}, u32[]{:S(2)}) collective-permute-start(bf16[2,384,512]{2,1,0:T(8,128)(2,1)} %get-tuple-element.102), channel_id=1, source_target_pairs={{0,1},{1,0},{2,3},{3,2},{4,5},{5,4},{6,7},{7,6},{8,9},{9,8},{10,11... | collective-permute-start | bytes 2359304 | tf_op jit(solution)/shard_map/ppermute | solution.py:36
  327.2 12.1 %collective-permute-start.19 = (bf16[2,1472,512]{2,1,0:T(8,128)(2,1)}, bf16[2,1472,512]{2,1,0:T(8,128)(2,1)S(1)}, u32[]{:S(2)}, u32[]{:S(2)}) collective-permute-start(bf16[2,1472,512]{2,1,0:T(8,128)(2,1)} %down.8.refs_5_), channel_id=1, source_target_pairs={{0,2},{2,0},{4,6},{6,4},{8,10},{10,8},{12,14},{14,12},{16,18},{18,... | collective-permute-start | bytes 9043976 | tf_op jit(solution)/shard_map/ppermute | solution.py:31
  327.2 43.9 %collective-permute-start.20 = (bf16[3,368,384]{2,1,0:T(8,128)(2,1)}, bf16[3,368,384]{2,1,0:T(8,128)(2,1)S(1)}, u32[]{:S(2)}, u32[]{:S(2)}) collective-permute-start(bf16[3,368,384]{2,1,0:T(8,128)(2,1)} %get-tuple-element.118), channel_id=1, source_target_pairs={{0,1},{1,0},{2,3},{3,2},{4,5},{5,4},{6,7},{7,6},{8,9},{9,8},{10,11... | collective-permute-start | bytes 2543624 | tf_op jit(solution)/shard_map/ppermute | solution.py:36
  328.7 42.5 %collective-permute-start.21 = (bf16[3,368,384]{2,1,0:T(8,128)(2,1)}, bf16[3,368,384]{2,1,0:T(8,128)(2,1)}, u32[]{:S(2)}, u32[]{:S(2)}) collective-permute-start(bf16[3,368,384]{2,1,0:T(8,128)(2,1)} %get-tuple-element.119), channel_id=1, source_target_pairs={{0,4},{2,6},{4,0},{6,2},{8,12},{10,14},{12,8},{14,10},{16,20},{18,... | collective-permute-start | bytes 2543624 | tf_op jit(solution)/shard_map/ppermute | solution.py:31
  375.9 49.5 %collective-permute-start.24 = (bf16[3,736,384]{2,1,0:T(8,128)(2,1)}, bf16[3,736,384]{2,1,0:T(8,128)(2,1)S(1)}, u32[]{:S(2)}, u32[]{:S(2)}) collective-permute-start(bf16[3,736,384]{2,1,0:T(8,128)(2,1)} %get-tuple-element.131), channel_id=1, source_target_pairs={{0,1},{1,0},{2,3},{3,2},{4,5},{5,4},{6,7},{7,6},{8,9},{9,8},{10,11... | collective-permute-start | bytes 5087240 | tf_op jit(solution)/shard_map/ppermute | solution.py:36
  377.3 50.0 %collective-permute-start.23 = (bf16[3,736,384]{2,1,0:T(8,128)(2,1)}, bf16[3,736,384]{2,1,0:T(8,128)(2,1)S(1)}, u32[]{:S(2)}, u32[]{:S(2)}) collective-permute-start(bf16[3,736,384]{2,1,0:T(8,128)(2,1)} %get-tuple-element.123.refs_8_), channel_id=1, source_target_pairs={{0,4},{2,6},{4,0},{6,2},{8,12},{10,14},{12,8},{14,10},{16,20},{18,... | collective-permute-start | bytes 5087240 | tf_op jit(solution)/shard_map/ppermute | solution.py:31
  381.8 60.5 %collective-permute-start.22 = (bf16[2,384,512]{2,1,0:T(8,128)(2,1)}, bf16[2,384,512]{2,1,0:T(8,128)(2,1)}, u32[]{:S(2)}, u32[]{:S(2)}) collective-permute-start(bf16[2,384,512]{2,1,0:T(8,128)(2,1)} %get-tuple-element.128), channel_id=1, source_target_pairs={{0,1},{1,0},{2,3},{3,2},{4,5},{5,4},{6,7},{7,6},{8,9},{9,8},{10,11... | collective-permute-start | bytes 2359304 | tf_op jit(solution)/shard_map/ppermute | solution.py:36
  414.4 48.1 %collective-permute-start.25 = (bf16[2,384,512]{2,1,0:T(8,128)(2,1)}, bf16[2,384,512]{2,1,0:T(8,128)(2,1)}, u32[]{:S(2)}, u32[]{:S(2)}) collective-permute-start(bf16[2,384,512]{2,1,0:T(8,128)(2,1)} %get-tuple-element.136), channel_id=1, source_target_pairs={{0,1},{1,0},{2,3},{3,2},{4,5},{5,4},{6,7},{7,6},{8,9},{9,8},{10,11... | collective-permute-start | bytes 2359304 | tf_op jit(solution)/shard_map/ppermute | solution.py:36
  432.9 38.0 %collective-permute-start.27 = (bf16[3,368,384]{2,1,0:T(8,128)(2,1)}, bf16[3,368,384]{2,1,0:T(8,128)(2,1)S(1)}, u32[]{:S(2)}, u32[]{:S(2)}) collective-permute-start(bf16[3,368,384]{2,1,0:T(8,128)(2,1)} %get-tuple-element.138), channel_id=1, source_target_pairs={{0,8},{2,10},{4,12},{6,14},{8,0},{10,2},{12,4},{14,6},{16,24},{18,... | collective-permute-start | bytes 2543624 | tf_op jit(solution)/shard_map/ppermute | solution.py:31
  458.7 68.3 %collective-permute-start.26 = (bf16[2,1472,512]{2,1,0:T(8,128)(2,1)}, bf16[2,1472,512]{2,1,0:T(8,128)(2,1)}, u32[]{:S(2)}, u32[]{:S(2)}) collective-permute-start(bf16[2,1472,512]{2,1,0:T(8,128)(2,1)} %down.10.refs_2_.refs_3_), channel_id=1, source_target_pairs={{0,2},{2,0},{4,6},{6,4},{8,10},{10,8},{12,14},{14,12},{16,18},{18,... | collective-permute-start | bytes 9043976 | tf_op jit(solution)/shard_map/ppermute | solution.py:31
  485.8 10.3 %collective-permute-start.28 = (bf16[1,1472,384]{2,1,0:T(8,128)(2,1)S(1)}, bf16[1,1472,384]{2,1,0:T(8,128)(2,1)S(1)}, u32[]{:S(2)}, u32[]{:S(2)}) collective-permute-start(bf16[1,1472,384]{2,1,0:T(8,128)(2,1)S(1)} %get-tuple-element.305), channel_id=1, source_target_pairs={{0,2},{2,0},{4,6},{6,4},{8,10},{10,8},{12,14},{14,12},{16,18},{18,... | collective-permute-start | bytes 3391496 | tf_op jit(solution)/shard_map/ppermute | solution.py:31
  487.9 34.5 %collective-permute-start.32 = (bf16[3,184,384]{2,1,0:T(8,128)(2,1)}, bf16[3,184,384]{2,1,0:T(8,128)(2,1)}, u32[]{:S(2)}, u32[]{:S(2)}) collective-permute-start(bf16[3,184,384]{2,1,0:T(8,128)(2,1)} %get-tuple-element.150), channel_id=1, source_target_pairs={{0,16},{2,18},{4,20},{6,22},{8,24},{10,26},{12,28},{14,30},{16,0},... | collective-permute-start | bytes 1271816 | tf_op jit(solution)/shard_map/ppermute | solution.py:31
  494.1 19.4 %collective-permute-start.30 = (bf16[1,368,384]{2,1,0:T(8,128)(2,1)}, bf16[1,368,384]{2,1,0:T(8,128)(2,1)S(1)}, u32[]{:S(2)}, u32[]{:S(2)}) collective-permute-start(bf16[1,368,384]{2,1,0:T(8,128)(2,1)} %get-tuple-element.142), channel_id=1, source_target_pairs={{0,1},{1,0},{2,3},{3,2},{4,5},{5,4},{6,7},{7,6},{8,9},{9,8},{10,11... | collective-permute-start | bytes 847880 | tf_op jit(solution)/shard_map/ppermute | solution.py:36
  495.1 18.3 %collective-permute-start.31 = (bf16[1,368,384]{2,1,0:T(8,128)(2,1)}, bf16[1,368,384]{2,1,0:T(8,128)(2,1)S(1)}, u32[]{:S(2)}, u32[]{:S(2)}) collective-permute-start(bf16[1,368,384]{2,1,0:T(8,128)(2,1)} %get-tuple-element.143), channel_id=1, source_target_pairs={{0,4},{2,6},{4,0},{6,2},{8,12},{10,14},{12,8},{14,10},{16,20},{18,... | collective-permute-start | bytes 847880 | tf_op jit(solution)/shard_map/ppermute | solution.py:31
  516.4 18.5 %collective-permute-start.36 = (bf16[1,736,384]{2,1,0:T(8,128)(2,1)}, bf16[1,736,384]{2,1,0:T(8,128)(2,1)S(1)}, u32[]{:S(2)}, u32[]{:S(2)}) collective-permute-start(bf16[1,736,384]{2,1,0:T(8,128)(2,1)} %get-tuple-element.159), channel_id=1, source_target_pairs={{0,1},{1,0},{2,3},{3,2},{4,5},{5,4},{6,7},{7,6},{8,9},{9,8},{10,11... | collective-permute-start | bytes 1695752 | tf_op jit(solution)/shard_map/ppermute | solution.py:36
  517.4 17.5 %collective-permute-start.35 = (bf16[1,736,384]{2,1,0:T(8,128)(2,1)}, bf16[1,736,384]{2,1,0:T(8,128)(2,1)}, u32[]{:S(2)}, u32[]{:S(2)}) collective-permute-start(bf16[1,736,384]{2,1,0:T(8,128)(2,1)} %get-tuple-element.149.refs_8_), channel_id=1, source_target_pairs={{0,4},{2,6},{4,0},{6,2},{8,12},{10,14},{12,8},{14,10},{16,20},{18,... | collective-permute-start | bytes 1695752 | tf_op jit(solution)/shard_map/ppermute | solution.py:31
  526.4 38.1 %collective-permute-start.45 = (bf16[3,92,384]{2,1,0:T(8,128)(2,1)S(1)}, bf16[3,92,384]{2,1,0:T(8,128)(2,1)S(1)}, u32[]{:S(2)}, u32[]{:S(2)}) collective-permute-start(bf16[3,92,384]{2,1,0:T(8,128)(2,1)S(1)} %get-tuple-element.326), channel_id=1, source_target_pairs={{0,2},{2,0},{4,6},{6,4},{8,10},{10,8},{12,14},{14,12},{16,18},{18,... | collective-permute-start | bytes 635912 | tf_op jit(solution)/shard_map/ppermute | solution.py:31
  538.0 12.4 %collective-permute-start.37 = (bf16[1,368,384]{2,1,0:T(8,128)(2,1)}, bf16[1,368,384]{2,1,0:T(8,128)(2,1)S(1)}, u32[]{:S(2)}, u32[]{:S(2)}) collective-permute-start(bf16[1,368,384]{2,1,0:T(8,128)(2,1)} %get-tuple-element.162), channel_id=1, source_target_pairs={{0,8},{2,10},{4,12},{6,14},{8,0},{10,2},{12,4},{14,6},{16,24},{18,... | collective-permute-start | bytes 847880 | tf_op jit(solution)/shard_map/ppermute | solution.py:31
  552.9 8.2 %collective-permute-start.39 = (bf16[1,184,384]{2,1,0:T(8,128)(2,1)}, bf16[1,184,384]{2,1,0:T(8,128)(2,1)S(1)}, u32[]{:S(2)}, u32[]{:S(2)}) collective-permute-start(bf16[1,184,384]{2,1,0:T(8,128)(2,1)} %get-tuple-element.166), channel_id=1, source_target_pairs={{0,16},{2,18},{4,20},{6,22},{8,24},{10,26},{12,28},{14,30},{16,0},... | collective-permute-start | bytes 423944 | tf_op jit(solution)/shard_map/ppermute | solution.py:31
  (66 other events, 313.7 us)
Sparse Core Ops, SparseCore 0:
  12.2 163.7 all-gather.4
  178.7 97.3 all-gather.6
  281.8 188.1 reduce-scatter.1

commit v5 on v4

--- a/solution.py
+++ b/solution.py
@@ -1367,7 +1367,6 @@
         grad_q.append(dq)
         bias_grads.append(bias_grad)
         grad_kv.append((dkv[0], [swap_mp(dkv[k], k) for k in x_masks()]))
-    moving = [scatter_xy(*parts, last) for parts in moving]
     grad_kv[0] = sum_rows([grad_kv[0][0], *hold(grad_kv[0][1], dq)], 1, after=[dq])
     weight_grads = outer_products(
         role_place,
@@ -1377,7 +1376,7 @@
             [(grad_attn[m], contexts[m]) for m in micros],
         ],
         None,
-        [dq, grad_kv[0]] + [first_of(parts) for parts in moving],
+        [dq, grad_kv[0]],
     )
     ffn = functools.partial(down, chunk_weights[-1:], chunk_acts[-1:], 2, 1)
     ffn_far = ffn(groups, groups, [weight_grads], prior_ffn)
@@ -1386,13 +1385,13 @@
         sum_rows([own, *hold(got, ffn_far)], 1, after=[ffn_far]) for own, got in grad_kv[1:]
     ]
     ffn_own = ffn(0, groups, [ffn_far, *grad_kv[1:]], prior_ffn)
-    moving = [scatter_z(parts, 0, [ffn_own]) for parts in moving]
+    from_y = [swap_dp(to_y, 2) for _, to_y, _ in moving]
     weight_grads = outer_products(
         role_place,
         (1, 2),
         [[(normed1[m], (grad_kv[m], n)) for m in micros] for n in range(2)],
         weight_grads,
-        [ffn_own] + [first_of(parts) for parts in moving],
+        [ffn_own],
     )
 
     half = model // 2
@@ -1417,18 +1416,23 @@
             sizes = [half, half] if k == 0 else split
             starts = [sum(sizes[:n]) for n in range(len(sizes))]
             quads.append(tuple(matrix[:, a : a + n] for a, n in zip(starts, sizes)))
+    xy_sums = []
+    for (own, _, to_x), got in zip(moving, from_y):
+        to_x = hold(to_x, *grad_kv[1:])
+        got = [got] + [swap_mp(other, k) for k, other in zip(x_masks(), to_x)]
+        xy_sums.append(sum_rows([own, *hold(got, quads[0][0])], 2, after=[quads[0][0]]))
     grad_inputs, gain1_grads = input_grads(
         place,
         [(layer_in[m], grad_attn[m], grad_q[m], grad_kv[m]) for m in micros],
         gain1,
         weights,
         chips,
-        [weight_grads, quads[0][0]],
+        [weight_grads, quads[0][0]] + [parts[0] for parts in xy_sums],
     )
     last = [gain1_grads]
     corner = scatter_corner(quads, [], last)
-    sums += [scatter_z(parts, 1, last) for parts in moving]
     traded = [trade_rows(part, core, own_rows) for part in sums] if z_count == 2 else []
+    moving = [scatter_z(parts, 0, last) for parts in xy_sums]
 
     bias_rows = sum(bias_grads)
     bias_tiles = sum(
@@ -1459,16 +1463,18 @@
         (ffn_own, ffn_from),
         weights,
         chips,
-        [corner[1], first_of(sums[-1])] + [got for _, got in traded[:-1]],
+        [corner[1]] + [first_of(parts) for parts in moving] + [got for _, got in traded],
     )
     own, to_y, to_x = corner
     got = [swap_dp(to_y, 2)] + [swap_mp(other, k) for k, other in zip(x_masks(), to_x)]
     total = sum_rows([own, *hold(got, outputs)], 2, after=[outputs])
+    moving = [scatter_z(parts, 1, [outputs]) for parts in moving]
     for stage, mask in enumerate(reversed(far_masks)):
         got, small = beside(swap_dp(total[1], mask), small, steps)
-        total = sum_rows([total[0], got], 1 if stage == z_count - 1 else 2)
+        waited = moving if stage == z_count - 1 and z_count == 2 else []
+        total = sum_rows([total[0], got], 1 if stage == z_count - 1 else 2, after=waited)
     for stage in range(2, z_count):
-        sums = [scatter_z(parts, stage) for parts in sums]
+        moving = [scatter_z(parts, stage) for parts in moving]
     piece = total[0]
     got, small = beside([swap_mp(piece, k) for k in x_masks()], small, steps)
     over_x = jnp.stack([piece] + got)
@@ -1482,7 +1488,8 @@
         [pick(both, (2 * x + core) ^ r, 0) for r in range(2 * mp)], axis=1
     ).astype(F32)
 
-    traded = traded or [trade_rows(part, core, own_rows) for part in sums]
+    late = moving if traded else sums + moving
+    traded = traded + [trade_rows(part, core, own_rows) for part in late]
     kept, got = [part for part, _ in traded], [part for _, part in traded]
     ffn_grads = either(
         core, jnp.concatenate(kept + got, axis=2), jnp.concatenate(got + kept, axis=2)

time: 594 us -> 590 us (level)
    unnamed x104 -> x102, local copies, waits for them, and re-layouts: 17.3 us -> 13.2 us
  transfers between devices with their start and end apart: 49 -> 49, of which waited for: 24 -> 21; matrix products, arithmetic and copies ran while one was open for 5% -> 5% of each run, Pallas kernels for 63% -> 63%
where the time goes in v5:
time: 590 us; the launch traced here: 579 us
  Pallas kernels  365 us (62%)
  waiting for transfers between devices  108 us (18%)
  starting transfers between devices  44.7 us (8%)
  local copies, waits for them, and re-layouts  32.5 us (6%)
  between operations  14.9 us (3%)
  other arithmetic  11.5 us (2%)
    pallas_call x46, Pallas kernels, call(): pl.pallas_call(run, grid_spec=pltpu.PrefetchScalarGridSpec(num_scalar_pre...  365 us
    ppermute x12, waiting for transfers between devices, swap_mp(): return lax.ppermute(array, 'mp', [(i, i ^ mask) for i in range(count)])  61.3 us
    ppermute x34, waiting for transfers between devices, swap_dp(): return lax.ppermute(array, DP, [(i, i ^ mask) for i in range(dp_size())])  39.3 us
    ppermute x34, starting transfers between devices, swap_dp(): return lax.ppermute(array, DP, [(i, i ^ mask) for i in range(dp_size())])  29.2 us
    ppermute x12, starting transfers between devices, swap_mp(): return lax.ppermute(array, 'mp', [(i, i ^ mask) for i in range(count)])  15.4 us
    unnamed x102, local copies, waits for them, and re-layouts  13.2 us
  transfers between devices with their start and end apart: 49, of which 21 were waited for; matrix products, arithmetic and copies ran while one was open for 5% of the time, Pallas kernels for 63%

profile of v5, /device:TPU:0, one launch (start us, length us, event | category | flops | bytes accessed | tf_op | source)
XLA Modules:
  0.0 578.7 jit_solution(2319703485071915409)
XLA Ops:
  31.0 13.9 %collective-permute-done.2.refs_1_ = bf16[1,368,384]{2,1,0:T(8,128)(2,1)S(1)} collective-permute-done((bf16[1,368,384]{2,1,0:T(8,128)(2,1)}, bf16[1,368,384]{2,1,0:T(8,128)(2,1)S(1)}, u32[]{:S(2)}, u32[]{:S(2)}) %collective-permute-start.2) | collective-permute-done | bytes 282656 | tf_op jit(solution)/shard_map/ppermute | solution.py:31
  59.0 6.9 %bias_table.1.refs_8_ = f32[6,7,256,256]{3,2,1,0:T(8,128)} custom-call(f32[6,7,1,512]{3,2,1,0:T(1,128)} %broadcast_in_dim.2.refs_0_, bf16[1472,512]{1,0:T(8,128)(2,1)} %bitcast.174, bf16[1472,512]{1,0:T(8,128)(2,1)} %bitcast.168), custom_call_target="tpu_custom_call" | custom-call | bytes 11096064 | tf_op jit(solution)/shard_map/bias_table/pallas_call | solution.py:160
  65.9 7.1 %collective-permute-done.4.refs_0_.refs_7_.refs_5_ = bf16[1,736,384]{2,1,0:T(8,128)(2,1)S(1)} collective-permute-done((bf16[1,736,384]{2,1,0:T(8,128)(2,1)}, bf16[1,736,384]{2,1,0:T(8,128)(2,1)S(1)}, u32[]{:S(2)}, u32[]{:S(2)}) %collective-permute-start.4) | collective-permute-done | bytes 565280 | tf_op jit(solution)/shard_map/ppermute | solution.py:36
  93.8 9.0 %project.2 = (bf16[1472,512]{1,0:T(8,128)(2,1)}, bf16[4,384,512]{2,1,0:T(8,128)(2,1)}, bf16[2,384,512]{2,1,0:T(8,128)(2,1)}) custom-call(s32[1]{0:T(128)} %bitcast.6.refs_0_, bf16[1472,512]{1,0:T(8,128)(2,1)} %bitcast.148, f32[1472,1]{1,0:T(8,128)} %get-tuple-element.320.refs_2_.refs_9_, bf16[1,736,384]{2,1,0:T(8,128)(2,1)} %merge.3.refs_4_.refs_3_.refs_1_, ...), custom_call_target="tpu_custom_call" | custom-call | flops 1736441856 | bytes 9901828 | tf_op jit(solution)/shard_map/project/pallas_call | solution.py:160
  104.9 7.8 %project.3 = (bf16[1472,512]{1,0:T(8,128)(2,1)}, bf16[4,384,512]{2,1,0:T(8,128)(2,1)}, bf16[2,384,512]{2,1,0:T(8,128)(2,1)}) custom-call(s32[1]{0:T(128)} %bitcast.6.refs_0_, bf16[1472,512]{1,0:T(8,128)(2,1)} %bitcast.141, f32[1472,1]{1,0:T(8,128)} %get-tuple-element.320.refs_2_.refs_9_, bf16[1,736,384]{2,1,0:T(8,128)(2,1)} %merge.3.refs_4_.refs_3_.refs_1_, ...), custom_call_target="tpu_custom_call" | custom-call | flops 1736441856 | bytes 9901828 | tf_op jit(solution)/shard_map/project/pallas_call | solution.py:160
  116.7 4.7 assemble.1.refs_9_.refs_2_.refs_6_.refs_10_.refs_7_
  121.4 18.9 %collective-permute-done.14 = bf16[2,384,512]{2,1,0:T(8,128)(2,1)S(1)} collective-permute-done((bf16[2,384,512]{2,1,0:T(8,128)(2,1)}, bf16[2,384,512]{2,1,0:T(8,128)(2,1)S(1)}, u32[]{:S(2)}, u32[]{:S(2)}) %collective-permute-start.14) | collective-permute-done | bytes 786464 | tf_op jit(solution)/shard_map/ppermute | solution.py:36
  141.2 10.2 %attend.2 = (bf16[384,512]{1,0:T(8,128)(2,1)}, f32[3,8,512]{2,1,0:T(8,128)}) custom-call(s32[9]{0:T(128)} %pad_add_fusion.3.refs_0_, bf16[1536,512]{1,0:T(8,128)(2,1)} %bitcast.162, bf16[1536,512]{1,0:T(8,128)(2,1)} %bitcast.163, bf16[1536,512]{1,0:T(8,128)(2,1)} %bitcast.164, bf16[768,512]{1,0:T(8,128)(2,1)} %bitcast.188, bf16[768,512]{1,0:T(8,128)(2,1)} %bitcast.189, ...), custom_call_target="tpu_custom_call" | custom-call | flops 3221225472 | bytes 17750052 | tf_op jit(solution)/shard_map/attend/pallas_call | solution.py:160
  151.5 4.4 middle.2.refs_9_.refs_4_
  155.9 7.2 %collective-permute-done.15 = bf16[2,384,512]{2,1,0:T(8,128)(2,1)S(1)} collective-permute-done((bf16[2,384,512]{2,1,0:T(8,128)(2,1)}, bf16[2,384,512]{2,1,0:T(8,128)(2,1)S(1)}, u32[]{:S(2)}, u32[]{:S(2)}) %collective-permute-start.15) | collective-permute-done | bytes 786464 | tf_op jit(solution)/shard_map/ppermute | solution.py:36
  164.0 10.7 %attend.3 = (bf16[384,512]{1,0:T(8,128)(2,1)}, f32[3,8,512]{2,1,0:T(8,128)}) custom-call(s32[9]{0:T(128)} %pad_add_fusion.4.refs_0_, bf16[1536,512]{1,0:T(8,128)(2,1)} %bitcast.156, bf16[1536,512]{1,0:T(8,128)(2,1)} %bitcast.157, bf16[1536,512]{1,0:T(8,128)(2,1)} %bitcast.158, bf16[768,512]{1,0:T(8,128)(2,1)} %bitcast.184, bf16[768,512]{1,0:T(8,128)(2,1)} %bitcast.185, ...), custom_call_target="tpu_custom_call" | custom-call | flops 3221225472 | bytes 17750052 | tf_op jit(solution)/shard_map/attend/pallas_call | solution.py:160
  174.7 4.5 middle.3.refs_5_.refs_12_
  187.1 52.9 %ffn_chunk.2 = (bf16[4,1024,512]{2,1,0:T(8,128)(2,1)}, bf16[4,1024,512]{2,1,0:T(8,128)(2,1)}, bf16[4,1024,512]{2,1,0:T(8,128)(2,1)}, bf16[3,1472,1024]{2,1,0:T(8,128)(2,1)}, bf16[16,3,184,512]{3,2,1,0:T(8,128)(2,1)}) custom-call(s32[2]{0:T(128)} %pad_add_fusion.5.refs_0_, bf16[16,184,1536]{2,1,0:T(8,128)(2,1)} %bitcast.216, ...), custom_call_target="tpu_custom_call" | custom-call | flops 37044092928 | bytes 69861384 | tf_op jit(solution)/shard_map/ffn_chunk/pallas_call | solution.py:160
  240.1 17.9 %down.6.refs_2_.refs_0_ = bf16[4,1472,512]{2,1,0:T(8,128)(2,1)} custom-call(bf16[3,1472,1024]{2,1,0:T(8,128)(2,1)} %get-tuple-element.105.refs_0_.refs_1_, bf16[3,1472,1024]{2,1,0:T(8,128)(2,1)} %get-tuple-element.105.refs_0_.refs_1_, bf16[4,1024,512]{2,1,0:T(8,128)(2,1)} %get-tuple-element.107.refs_2_, bf16[4,1024,512]{2,1,0:T(8,128)(2,1)} %get-tuple-element.108.refs_3_, ...), custom_call_target="tpu_custom_call" | custom-call | flops 12348030976 | bytes 32505856 | tf_op jit(solution)/shard_map/down/pallas_call | solution.py:160
  257.9 10.4 %down.7.refs_12_.refs_0_ = bf16[4,1472,512]{2,1,0:T(8,128)(2,1)} custom-call(bf16[3,1472,1024]{2,1,0:T(8,128)(2,1)} %get-tuple-element.105.refs_0_.refs_1_, bf16[4,1024,512]{2,1,0:T(8,128)(2,1)} %get-tuple-element.106.refs_4_.refs_1_, bf16[4,1472,512]{2,1,0:T(8,128)(2,1)} %down.6.refs_2_.refs_0_), custom_call_target="tpu_custom_call" | custom-call | flops 6174015488 | bytes 19267584 | tf_op jit(solution)/shard_map/down/pallas_call | solution.py:160
  268.4 7.8 %all-gather.7.cloned.1.call-done = bf16[2944,1152]{1,0:T(8,128)(2,1)} async-done(((bf16[184,1152]{1,0:T(8,128)(2,1)}), bf16[2944,1152]{1,0:T(8,128)(2,1)}) %all-gather.7.cloned.1.call-update) | async-done | bytes 6782992 | tf_op jit(solution)/shard_map/all_gather | solution.py:1250
  276.2 41.2 %ffn_chunk.3 = (bf16[4,768,512]{2,1,0:T(8,128)(2,1)}, bf16[4,768,512]{2,1,0:T(8,128)(2,1)}, bf16[4,768,512]{2,1,0:T(8,128)(2,1)}, bf16[3,1472,768]{2,1,0:T(8,128...) custom-call(s32[2]{0:T(128)} %pad_add_fusion.5.refs_0_, ...), custom_call_target="tpu_custom_call" | custom-call | flops 27783069696 | bytes 55410696 | tf_op jit(solution)/shard_map/ffn_chunk/pallas_call | solution.py:160
  317.4 10.1 %down.8.refs_5_ = bf16[2,1472,512]{2,1,0:T(8,128)(2,1)} custom-call(bf16[4,1472,512]{2,1,0:T(8,128)(2,1)} %down.6.refs_2_.refs_0_, bf16[3,1472,768]{2,1,0:T(8,128)(2,1)} %get-tuple-element.109.refs_1_.refs_2_, bf16[3,1472,768]{2,1,0:T(8,128)(2,1)} %get-tuple-element.109.refs_1_.refs_2_, bf16[4,768,512]{2,1,0:T(8,128)(2,1)} %get-tuple-element.112.refs_3_, ...), custom_call_target="tpu_custom_call" | custom-call | flops 4630511616 | bytes 28901376 | tf_op jit(solution)/shard_map/down/pallas_call | solution.py:160
  329.5 9.9 %down.9.refs_3_.refs_7_ = bf16[2,1472,512]{2,1,0:T(8,128)(2,1)} custom-call(bf16[4,1472,512]{2,1,0:T(8,128)(2,1)} %down.6.refs_2_.refs_0_, bf16[3,1472,768]{2,1,0:T(8,128)(2,1)} %get-tuple-element.109.refs_1_.refs_2_, bf16[3,1472,768]{2,1,0:T(8,128)(2,1)} %get-tuple-element.109.refs_1_.refs_2_, bf16[4,768,512]{2,1,0:T(8,128)(2,1)} %get-tuple-element.112.refs_3_, ...), custom_call_target="tpu_custom_call" | custom-call | flops 4630511616 | bytes 28901376 | tf_op jit(solution)/shard_map/down/pallas_call | solution.py:160
  341.1 8.8 %turn.2 = (bf16[1472,512]{1,0:T(8,128)(2,1)}, bf16[384,512]{1,0:T(8,128)(2,1)}, f32[1472,1]{1,0:T(8,128)}) custom-call(bf16[1472,512]{1,0:T(8,128)(2,1)} %bitcast.150, bf16[384,512]{1,0:T(8,128)(2,1)} %get-tuple-element.101.refs_1_.refs_4_.refs_9_.refs_6_.refs_2_, bf16[1472,512]{1,0:T(8,128)(2,1)} %bitcast.177, bf16[2,1472,512]{2,1,0:T(8,128)(2,1)} %down.9.refs_3_.refs_7_, ...), custom_call_target="tpu_custom_call" | custom-call | flops 1157627904 | bytes 15871488 | tf_op jit(solution)/shard_map/turn/pallas_call | solution.py:160
  349.8 21.4 %attend_grads.2 = (bf16[384,512]{1,0:T(8,128)(2,1)}, f32[6,2,3,8,512]{4,3,2,1,0:T(8,128)}, bf16[2,384,512]{2,1,0:T(8,128)(2,1)}, bf16[2,384,512]{2,1,0:T(8,128)(2,1)}) custom-call(s32[9]{0:T(128)} %pad_add_fusion.3.refs_0_, bf16[1536,512]{1,0:T(8,128)(2,1)} %bitcast.165, bf16[1536,512]{1,0:T(8,128)(2,1)} %bitcast.166, bf16[1536,512]{1,0:T(8,128)(2,1)} %bitcast.167, ...), custom_call_target="tpu_custom_call" | custom-call | flops 6442450944 | bytes 20699172 | tf_op jit(solution)/shard_map/attend_grads/pallas_call | solution.py:160
  376.8 9.2 %turn.3 = (bf16[1472,512]{1,0:T(8,128)(2,1)}, bf16[384,512]{1,0:T(8,128)(2,1)}, f32[1472,1]{1,0:T(8,128)}) custom-call(bf16[1472,512]{1,0:T(8,128)(2,1)} %bitcast.143, bf16[384,512]{1,0:T(8,128)(2,1)} %get-tuple-element.104.refs_1_.refs_4_.refs_9_.refs_8_, bf16[1472,512]{1,0:T(8,128)(2,1)} %bitcast.171, bf16[2,1472,512]{2,1,0:T(8,128)(2,1)} %down.9.refs_3_.refs_7_, ...), custom_call_target="tpu_custom_call" | custom-call | flops 1157627904 | bytes 15871488 | tf_op jit(solution)/shard_map/turn/pallas_call | solution.py:160
  386.1 21.5 %attend_grads.3 = (bf16[384,512]{1,0:T(8,128)(2,1)}, f32[6,2,3,8,512]{4,3,2,1,0:T(8,128)}, bf16[2,384,512]{2,1,0:T(8,128)(2,1)}, bf16[2,384,512]{2,1,0:T(8,128)(2,1)}) custom-call(s32[9]{0:T(128)} %pad_add_fusion.4.refs_0_, bf16[1536,512]{1,0:T(8,128)(2,1)} %bitcast.159, bf16[1536,512]{1,0:T(8,128)(2,1)} %bitcast.160, bf16[1536,512]{1,0:T(8,128)(2,1)} %bitcast.161, ...), custom_call_target="tpu_custom_call" | custom-call | flops 6442450944 | bytes 20699172 | tf_op jit(solution)/shard_map/attend_grads/pallas_call | solution.py:160
  411.9 7.8 %outer_products.2.refs_3_.refs_9_ = bf16[4,1472,384]{2,1,0:T(8,128)(2,1)} custom-call(s32[1]{0:T(128)S(6)} %and.10.refs_0_, bf16[1472,512]{1,0:T(8,128)(2,1)} %get-tuple-element.99.refs_13_.refs_1_.refs_5_, bf16[384,512]{1,0:T(8,128)(2,1)} %get-tuple-element.116.refs_4_.refs_7_.refs_2_.refs_3_, ...), custom_call_target="tpu_custom_call" | custom-call | flops 2315255808 | bytes 12124164 | tf_op jit(solution)/shard_map/outer_products/pallas_call | solution.py:160
  419.7 6.3 %down.10.refs_2_.refs_3_ = bf16[2,1472,512]{2,1,0:T(8,128)(2,1)} custom-call(bf16[4,1472,512]{2,1,0:T(8,128)(2,1)} %down.7.refs_12_.refs_0_, bf16[3,1472,768]{2,1,0:T(8,128)(2,1)} %get-tuple-element.109.refs_1_.refs_2_, bf16[4,768,512]{2,1,0:T(8,128)(2,1)} %get-tuple-element.110.refs_5_.refs_2_, bf16[4,1472,384]{2,1,0:T(8,128)(2,1)} %outer_products.2.refs_3_.refs_9_), custom_call_target="tpu_custom_call" | custom-call | flops 2315255808 | bytes 18972672 | tf_op jit(solution)/shard_map/down/pallas_call | solution.py:160
  426.0 5.8 %collective-permute-start.24 = (bf16[2,1472,512]{2,1,0:T(8,128)(2,1)}, bf16[2,1472,512]{2,1,0:T(8,128)(2,1)}, u32[]{:S(2)}, u32[]{:S(2)}) collective-permute-start(bf16[2,1472,512]{2,1,0:T(8,128)(2,1)} %down.10.refs_2_.refs_3_), channel_id=1, source_target_pairs={{0,2},{2,0},{4,6},{6,4},{8,10},{10,8},{12,14},{14,12},{16,18},{18,... | collective-permute-start | bytes 9043976 | tf_op jit(solution)/shard_map/ppermute | solution.py:31
  434.9 6.3 %down.11.refs_10_.refs_5_ = bf16[2,1472,512]{2,1,0:T(8,128)(2,1)} custom-call(bf16[4,1472,512]{2,1,0:T(8,128)(2,1)} %down.7.refs_12_.refs_0_, bf16[3,1472,768]{2,1,0:T(8,128)(2,1)} %get-tuple-element.109.refs_1_.refs_2_, bf16[4,768,512]{2,1,0:T(8,128)(2,1)} %get-tuple-element.110.refs_5_.refs_2_, bf16[2,1472,512]{2,1,0:T(8,128)(2,1)} %down.10.refs_2_.refs_3_, ...), custom_call_target="tpu_custom_call" | custom-call | flops 2315255808 | bytes 18972672 | tf_op jit(solution)/shard_map/down/pallas_call | solution.py:160
  441.2 8.0 %outer_products.3.refs_0_.refs_11_ = bf16[4,1472,384]{2,1,0:T(8,128)(2,1)} custom-call(s32[1]{0:T(128)S(6)} %and.10.refs_0_, bf16[1472,512]{1,0:T(8,128)(2,1)} %get-tuple-element.99.refs_13_.refs_1_.refs_5_, bf16[2,384,512]{2,1,0:T(8,128)(2,1)} %sum_rows.10.refs_10_.refs_2_.refs_6_.refs_4_, ...), custom_call_target="tpu_custom_call", output_to_operand_aliasing={{}: (9, {})} | custom-call | flops 2315255808 | bytes 18219012 | tf_op jit(solution)/shard_map/outer_products/pallas_call | solution.py:160
  459.0 18.3 %collective-permute-done.30.refs_2_ = bf16[3,736,384]{2,1,0:T(8,128)(2,1)} collective-permute-done((bf16[3,736,384]{2,1,0:T(8,128)(2,1)}, bf16[3,736,384]{2,1,0:T(8,128)(2,1)}, u32[]{:S(2)}, u32[]{:S(2)}) %collective-permute-start.30) | collective-permute-done | bytes 1695776 | tf_op jit(solution)/shard_map/ppermute | solution.py:36
  487.7 13.6 %input_grads.1 = (bf16[2,8,184,512]{3,2,1,0:T(8,128)(2,1)}, f32[1472,1]{1,0:T(8,128)}) custom-call(s32[1]{0:T(128)} %bitcast.refs_0_, bf16[1472,512]{1,0:T(8,128)(2,1)} %bitcast.151, bf16[1472,512]{1,0:T(8,128)(2,1)} %get-tuple-element.115.refs_12_.refs_5_.refs_2_, bf16[384,512]{1,0:T(8,128)(2,1)} %get-tuple-element.116.refs_4_.refs_7_.refs_2_.refs_3_, ...), custom_call_target="tpu_custom_call" | custom-call | flops 3472883712 | bytes 15937028 | tf_op jit(solution)/shard_map/input_grads/pallas_call | solution.py:160
  521.1 7.2 %finish.1 = bf16[2,8,184,512]{3,2,1,0:T(8,128)(2,1)} custom-call(s32[1]{0:T(128)} %bitcast.refs_0_, bf16[1472,512]{1,0:T(8,128)(2,1)} %bitcast.152, bf16[384,512]{1,0:T(8,128)(2,1)} %get-tuple-element.101.refs_1_.refs_4_.refs_9_.refs_6_.refs_2_, bf16[1472,512]{1,0:T(8,128)(2,1)} %bitcast.145, ...), custom_call_target="tpu_custom_call" | custom-call | flops 1157627904 | bytes 17367044 | tf_op jit(solution)/shard_map/finish/pallas_call | solution.py:160
  552.0 4.7 collective-permute-done.38.refs_1_
  (312 shorter events, 169.3 us)
Async XLA Ops:
  7.2 179.4 %all-gather.5.cloned.1.call-start = ((), (), s32[]{:S(2)}) async-start(), calls=%async_computation.2 | async-start | bytes 9609216 | tf_op jit(solution)/shard_map/all_gather | solution.py:1250
  12.1 264.1 %all-gather.7.cloned.1.call-start = ((), (), s32[]{:S(2)}) async-start(), calls=%async_computation.3 | async-start | bytes 7206912 | tf_op jit(solution)/shard_map/all_gather | solution.py:1250
  13.0 500.1 %reduce-scatter.2.cloned.1.call-start = ((), (), s32[]{:S(2)}) async-start(), calls=%async_computation.1 | async-start | bytes 9609216 | tf_op jit(solution)/shard_map/reduce_scatter | solution.py:1337
  14.6 11.1 %collective-permute-start.1 = (bf16[1,184,384]{2,1,0:T(8,128)(2,1)S(1)}, bf16[1,184,384]{2,1,0:T(8,128)(2,1)S(1)}, u32[]{:S(2)}, u32[]{:S(2)}) collective-permute-start(bf16[1,184,384]{2,1,0:T(8,128)(2,1)S(1)} %maximum_select_fusion.2.refs_0_), channel_id=1, source_target_pairs={{0,16},{2,18},{4,20},{6,22},{8,24},{10,26},{12,28},{14,30},{16,0},... | collective-permute-start | bytes 423944 | tf_op jit(solution)/shard_map/ppermute | solution.py:31
  28.0 16.8 %collective-permute-start.2 = (bf16[1,368,384]{2,1,0:T(8,128)(2,1)}, bf16[1,368,384]{2,1,0:T(8,128)(2,1)S(1)}, u32[]{:S(2)}, u32[]{:S(2)}) collective-permute-start(bf16[1,368,384]{2,1,0:T(8,128)(2,1)} %merge.2.refs_0_), channel_id=1, source_target_pairs={{0,8},{2,10},{4,12},{6,14},{8,0},{10,2},{12,4},{14,6},{16,24},{18,... | collective-permute-start | bytes 847880 | tf_op jit(solution)/shard_map/ppermute | solution.py:31
  47.4 25.5 %collective-permute-start.4 = (bf16[1,736,384]{2,1,0:T(8,128)(2,1)}, bf16[1,736,384]{2,1,0:T(8,128)(2,1)S(1)}, u32[]{:S(2)}, u32[]{:S(2)}) collective-permute-start(bf16[1,736,384]{2,1,0:T(8,128)(2,1)} %merge.3.refs_4_.refs_3_.refs_1_), channel_id=1, source_target_pairs={{0,1},{1,0},{2,3},{3,2},{4,5},{5,4},{6,7},{7,6},{8,9},{9,8},{10,11... | collective-permute-start | bytes 1695752 | tf_op jit(solution)/shard_map/ppermute | solution.py:36
  48.9 24.1 %collective-permute-start.3 = (bf16[1,736,384]{2,1,0:T(8,128)(2,1)}, bf16[1,736,384]{2,1,0:T(8,128)(2,1)S(1)}, u32[]{:S(2)}, u32[]{:S(2)}) collective-permute-start(bf16[1,736,384]{2,1,0:T(8,128)(2,1)} %merge.3.refs_4_.refs_3_.refs_1_), channel_id=1, source_target_pairs={{0,4},{2,6},{4,0},{6,2},{8,12},{10,14},{12,8},{14,10},{16,20},{18,... | collective-permute-start | bytes 1695752 | tf_op jit(solution)/shard_map/ppermute | solution.py:31
  56.1 36.7 %collective-permute-start.12 = (bf16[1472,512]{1,0:T(8,128)(2,1)}, bf16[1472,512]{1,0:T(8,128)(2,1)}, u32[]{:S(2)}, u32[]{:S(2)}) collective-permute-start(bf16[1472,512]{1,0:T(8,128)(2,1)} %bitcast.173), channel_id=1, source_target_pairs={{0,2},{2,0},{4,6},{6,4},{8,10},{10,8},{12,14},{14,12},{16,18},{18,... | collective-permute-start | bytes 4521992 | tf_op jit(solution)/shard_map/ppermute | solution.py:31
  56.1 36.7 %collective-permute-start.13 = (bf16[1472,512]{1,0:T(8,128)(2,1)S(1)}, bf16[1472,512]{1,0:T(8,128)(2,1)}, u32[]{:S(2)}, u32[]{:S(2)}) collective-permute-start(bf16[1472,512]{1,0:T(8,128)(2,1)S(1)} %bitcast.172), channel_id=1, source_target_pairs={{0,2},{2,0},{4,6},{6,4},{8,10},{10,8},{12,14},{14,12},{16,18},{18,... | collective-permute-start | bytes 4521992 | tf_op jit(solution)/shard_map/ppermute | solution.py:31
  56.7 25.7 %collective-permute-start.5 = (bf16[1,736,384]{2,1,0:T(8,128)(2,1)S(1)}, bf16[1,736,384]{2,1,0:T(8,128)(2,1)}, u32[]{:S(2)}, u32[]{:S(2)}) collective-permute-start(bf16[1,736,384]{2,1,0:T(8,128)(2,1)S(1)} %copy-done.2), channel_id=1, source_target_pairs={{0,2},{2,0},{4,6},{6,4},{8,10},{10,8},{12,14},{14,12},{16,18},{18,... | collective-permute-start | bytes 1695752 | tf_op jit(solution)/shard_map/ppermute | solution.py:31
  78.8 7.2 %collective-permute-start.7 = (bf16[1,368,384]{2,1,0:T(8,128)(2,1)}, bf16[1,368,384]{2,1,0:T(8,128)(2,1)S(1)}, u32[]{:S(2)}, u32[]{:S(2)}) collective-permute-start(bf16[1,368,384]{2,1,0:T(8,128)(2,1)} %rows.2), channel_id=1, source_target_pairs={{0,1},{1,0},{2,3},{3,2},{4,5},{5,4},{6,7},{7,6},{8,9},{9,8},{10,11... | collective-permute-start | bytes 847880 | tf_op jit(solution)/shard_map/ppermute | solution.py:36
  82.4 10.3 %collective-permute-start.6 = (bf16[1,736,384]{2,1,0:T(8,128)(2,1)}, bf16[1,736,384]{2,1,0:T(8,128)(2,1)S(1)}, u32[]{:S(2)}, u32[]{:S(2)}) collective-permute-start(bf16[1,736,384]{2,1,0:T(8,128)(2,1)} %copy-done.6), channel_id=1, source_target_pairs={{0,2},{2,0},{4,6},{6,4},{8,10},{10,8},{12,14},{14,12},{16,18},{18,... | collective-permute-start | bytes 1695752 | tf_op jit(solution)/shard_map/ppermute | solution.py:31
  102.8 37.5 %collective-permute-start.14 = (bf16[2,384,512]{2,1,0:T(8,128)(2,1)}, bf16[2,384,512]{2,1,0:T(8,128)(2,1)S(1)}, u32[]{:S(2)}, u32[]{:S(2)}) collective-permute-start(bf16[2,384,512]{2,1,0:T(8,128)(2,1)} %get-tuple-element.98), channel_id=1, source_target_pairs={{0,1},{1,0},{2,3},{3,2},{4,5},{5,4},{6,7},{7,6},{8,9},{9,8},{10,11... | collective-permute-start | bytes 2359304 | tf_op jit(solution)/shard_map/ppermute | solution.py:36
  112.8 50.3 %collective-permute-start.15 = (bf16[2,384,512]{2,1,0:T(8,128)(2,1)}, bf16[2,384,512]{2,1,0:T(8,128)(2,1)S(1)}, u32[]{:S(2)}, u32[]{:S(2)}) collective-permute-start(bf16[2,384,512]{2,1,0:T(8,128)(2,1)} %get-tuple-element.103), channel_id=1, source_target_pairs={{0,1},{1,0},{2,3},{3,2},{4,5},{5,4},{6,7},{7,6},{8,9},{9,8},{10,11... | collective-permute-start | bytes 2359304 | tf_op jit(solution)/shard_map/ppermute | solution.py:36
  327.5 12.0 %collective-permute-start.19 = (bf16[2,1472,512]{2,1,0:T(8,128)(2,1)}, bf16[2,1472,512]{2,1,0:T(8,128)(2,1)S(1)}, u32[]{:S(2)}, u32[]{:S(2)}) collective-permute-start(bf16[2,1472,512]{2,1,0:T(8,128)(2,1)} %down.8.refs_5_), channel_id=1, source_target_pairs={{0,2},{2,0},{4,6},{6,4},{8,10},{10,8},{12,14},{14,12},{16,18},{18,... | collective-permute-start | bytes 9043976 | tf_op jit(solution)/shard_map/ppermute | solution.py:31
  327.5 43.8 %collective-permute-start.20 = (bf16[3,368,384]{2,1,0:T(8,128)(2,1)}, bf16[3,368,384]{2,1,0:T(8,128)(2,1)S(1)}, u32[]{:S(2)}, u32[]{:S(2)}) collective-permute-start(bf16[3,368,384]{2,1,0:T(8,128)(2,1)} %get-tuple-element.119), channel_id=1, source_target_pairs={{0,1},{1,0},{2,3},{3,2},{4,5},{5,4},{6,7},{7,6},{8,9},{9,8},{10,11... | collective-permute-start | bytes 2543624 | tf_op jit(solution)/shard_map/ppermute | solution.py:36
  328.9 42.3 %collective-permute-start.21 = (bf16[3,368,384]{2,1,0:T(8,128)(2,1)}, bf16[3,368,384]{2,1,0:T(8,128)(2,1)}, u32[]{:S(2)}, u32[]{:S(2)}) collective-permute-start(bf16[3,368,384]{2,1,0:T(8,128)(2,1)} %get-tuple-element.120), channel_id=1, source_target_pairs={{0,4},{2,6},{4,0},{6,2},{8,12},{10,14},{12,8},{14,10},{16,20},{18,... | collective-permute-start | bytes 2543624 | tf_op jit(solution)/shard_map/ppermute | solution.py:31
  371.3 38.4 %collective-permute-start.22 = (bf16[2,384,512]{2,1,0:T(8,128)(2,1)}, bf16[2,384,512]{2,1,0:T(8,128)(2,1)}, u32[]{:S(2)}, u32[]{:S(2)}) collective-permute-start(bf16[2,384,512]{2,1,0:T(8,128)(2,1)} %get-tuple-element.129), channel_id=1, source_target_pairs={{0,1},{1,0},{2,3},{3,2},{4,5},{5,4},{6,7},{7,6},{8,9},{9,8},{10,11... | collective-permute-start | bytes 2359304 | tf_op jit(solution)/shard_map/ppermute | solution.py:36
  407.6 24.2 %collective-permute-start.23 = (bf16[2,384,512]{2,1,0:T(8,128)(2,1)}, bf16[2,384,512]{2,1,0:T(8,128)(2,1)}, u32[]{:S(2)}, u32[]{:S(2)}) collective-permute-start(bf16[2,384,512]{2,1,0:T(8,128)(2,1)} %get-tuple-element.132), channel_id=1, source_target_pairs={{0,1},{1,0},{2,3},{3,2},{4,5},{5,4},{6,7},{7,6},{8,9},{9,8},{10,11... | collective-permute-start | bytes 2359304 | tf_op jit(solution)/shard_map/ppermute | solution.py:36
  408.5 50.4 %collective-permute-start.29 = (bf16[3,736,384]{2,1,0:T(8,128)(2,1)S(1)}, bf16[3,736,384]{2,1,0:T(8,128)(2,1)S(1)}, u32[]{:S(2)}, u32[]{:S(2)}) collective-permute-start(bf16[3,736,384]{2,1,0:T(8,128)(2,1)S(1)} %copy-done.9), channel_id=1, source_target_pairs={{0,4},{2,6},{4,0},{6,2},{8,12},{10,14},{12,8},{14,10},{16,20},{18,... | collective-permute-start | bytes 5087240 | tf_op jit(solution)/shard_map/ppermute | solution.py:31
  426.0 94.4 %collective-permute-start.24 = (bf16[2,1472,512]{2,1,0:T(8,128)(2,1)}, bf16[2,1472,512]{2,1,0:T(8,128)(2,1)}, u32[]{:S(2)}, u32[]{:S(2)}) collective-permute-start(bf16[2,1472,512]{2,1,0:T(8,128)(2,1)} %down.10.refs_2_.refs_3_), channel_id=1, source_target_pairs={{0,2},{2,0},{4,6},{6,4},{8,10},{10,8},{12,14},{14,12},{16,18},{18,... | collective-permute-start | bytes 9043976 | tf_op jit(solution)/shard_map/ppermute | solution.py:31
  434.0 43.3 %collective-permute-start.30 = (bf16[3,736,384]{2,1,0:T(8,128)(2,1)}, bf16[3,736,384]{2,1,0:T(8,128)(2,1)}, u32[]{:S(2)}, u32[]{:S(2)}) collective-permute-start(bf16[3,736,384]{2,1,0:T(8,128)(2,1)} %get-tuple-element.140), channel_id=1, source_target_pairs={{0,1},{1,0},{2,3},{3,2},{4,5},{5,4},{6,7},{7,6},{8,9},{9,8},{10,11... | collective-permute-start | bytes 5087240 | tf_op jit(solution)/shard_map/ppermute | solution.py:36
  454.7 27.7 %collective-permute-start.26 = (bf16[1,1472,384]{2,1,0:T(8,128)(2,1)}, bf16[1,1472,384]{2,1,0:T(8,128)(2,1)}, u32[]{:S(2)}, u32[]{:S(2)}) collective-permute-start(bf16[1,1472,384]{2,1,0:T(8,128)(2,1)} %get-tuple-element.306), channel_id=1, source_target_pairs={{0,2},{2,0},{4,6},{6,4},{8,10},{10,8},{12,14},{14,12},{16,18},{18,... | collective-permute-start | bytes 3391496 | tf_op jit(solution)/shard_map/ppermute | solution.py:31
  481.7 24.0 %collective-permute-start.31 = (bf16[3,368,384]{2,1,0:T(8,128)(2,1)}, bf16[3,368,384]{2,1,0:T(8,128)(2,1)S(1)}, u32[]{:S(2)}, u32[]{:S(2)}) collective-permute-start(bf16[3,368,384]{2,1,0:T(8,128)(2,1)} %get-tuple-element.149), channel_id=1, source_target_pairs={{0,8},{2,10},{4,12},{6,14},{8,0},{10,2},{12,4},{14,6},{16,24},{18,... | collective-permute-start | bytes 2543624 | tf_op jit(solution)/shard_map/ppermute | solution.py:31
  485.0 16.3 %collective-permute-start.27 = (bf16[1,368,384]{2,1,0:T(8,128)(2,1)}, bf16[1,368,384]{2,1,0:T(8,128)(2,1)S(1)}, u32[]{:S(2)}, u32[]{:S(2)}) collective-permute-start(bf16[1,368,384]{2,1,0:T(8,128)(2,1)} %get-tuple-element.135), channel_id=1, source_target_pairs={{0,1},{1,0},{2,3},{3,2},{4,5},{5,4},{6,7},{7,6},{8,9},{9,8},{10,11... | collective-permute-start | bytes 847880 | tf_op jit(solution)/shard_map/ppermute | solution.py:36
  485.9 15.4 %collective-permute-start.28 = (bf16[1,368,384]{2,1,0:T(8,128)(2,1)}, bf16[1,368,384]{2,1,0:T(8,128)(2,1)S(1)}, u32[]{:S(2)}, u32[]{:S(2)}) collective-permute-start(bf16[1,368,384]{2,1,0:T(8,128)(2,1)} %get-tuple-element.136), channel_id=1, source_target_pairs={{0,4},{2,6},{4,0},{6,2},{8,12},{10,14},{12,8},{14,10},{16,20},{18,... | collective-permute-start | bytes 847880 | tf_op jit(solution)/shard_map/ppermute | solution.py:31
  504.2 29.4 %collective-permute-start.35 = (bf16[1,736,384]{2,1,0:T(8,128)(2,1)}, bf16[1,736,384]{2,1,0:T(8,128)(2,1)S(1)}, u32[]{:S(2)}, u32[]{:S(2)}) collective-permute-start(bf16[1,736,384]{2,1,0:T(8,128)(2,1)} %get-tuple-element.159), channel_id=1, source_target_pairs={{0,1},{1,0},{2,3},{3,2},{4,5},{5,4},{6,7},{7,6},{8,9},{9,8},{10,11... | collective-permute-start | bytes 1695752 | tf_op jit(solution)/shard_map/ppermute | solution.py:36
  505.4 28.2 %collective-permute-start.34 = (bf16[1,736,384]{2,1,0:T(8,128)(2,1)}, bf16[1,736,384]{2,1,0:T(8,128)(2,1)}, u32[]{:S(2)}, u32[]{:S(2)}) collective-permute-start(bf16[1,736,384]{2,1,0:T(8,128)(2,1)} %get-tuple-element.148.refs_8_), channel_id=1, source_target_pairs={{0,4},{2,6},{4,0},{6,2},{8,12},{10,14},{12,8},{14,10},{16,20},{18,... | collective-permute-start | bytes 1695752 | tf_op jit(solution)/shard_map/ppermute | solution.py:31
  509.7 21.0 %collective-permute-start.40 = (bf16[3,184,384]{2,1,0:T(8,128)(2,1)}, bf16[3,184,384]{2,1,0:T(8,128)(2,1)}, u32[]{:S(2)}, u32[]{:S(2)}) collective-permute-start(bf16[3,184,384]{2,1,0:T(8,128)(2,1)} %get-tuple-element.170), channel_id=1, source_target_pairs={{0,16},{2,18},{4,20},{6,22},{8,24},{10,26},{12,28},{14,30},{16,0},... | collective-permute-start | bytes 1271816 | tf_op jit(solution)/shard_map/ppermute | solution.py:31
  536.7 8.7 %collective-permute-start.36 = (bf16[1,368,384]{2,1,0:T(8,128)(2,1)}, bf16[1,368,384]{2,1,0:T(8,128)(2,1)S(1)}, u32[]{:S(2)}, u32[]{:S(2)}) collective-permute-start(bf16[1,368,384]{2,1,0:T(8,128)(2,1)} %get-tuple-element.162), channel_id=1, source_target_pairs={{0,8},{2,10},{4,12},{6,14},{8,0},{10,2},{12,4},{14,6},{16,24},{18,... | collective-permute-start | bytes 847880 | tf_op jit(solution)/shard_map/ppermute | solution.py:31
  536.9 23.6 %collective-permute-start.45 = (bf16[3,92,384]{2,1,0:T(8,128)(2,1)S(1)}, bf16[3,92,384]{2,1,0:T(8,128)(2,1)S(1)}, u32[]{:S(2)}, u32[]{:S(2)}) collective-permute-start(bf16[3,92,384]{2,1,0:T(8,128)(2,1)S(1)} %get-tuple-element.328), channel_id=1, source_target_pairs={{0,2},{2,0},{4,6},{6,4},{8,10},{10,8},{12,14},{14,12},{16,18},{18,... | collective-permute-start | bytes 635912 | tf_op jit(solution)/shard_map/ppermute | solution.py:31
  547.9 8.7 %collective-permute-start.38 = (bf16[1,184,384]{2,1,0:T(8,128)(2,1)}, bf16[1,184,384]{2,1,0:T(8,128)(2,1)S(1)}, u32[]{:S(2)}, u32[]{:S(2)}) collective-permute-start(bf16[1,184,384]{2,1,0:T(8,128)(2,1)} %get-tuple-element.166), channel_id=1, source_target_pairs={{0,16},{2,18},{4,20},{6,22},{8,24},{10,26},{12,28},{14,30},{16,0},... | collective-permute-start | bytes 423944 | tf_op jit(solution)/shard_map/ppermute | solution.py:31
  (65 other events, 361.0 us)
Sparse Core Ops, SparseCore 0:
  12.2 163.9 all-gather.4
  178.9 97.2 all-gather.6
  281.9 184.7 reduce-scatter.1
